TPU v7x, 32 devices: a whole 2x2x4 slice. The times are simulated.
32 devices in a mesh: groups: 2 (over y), row: 4 (over z), col: 2 (over x), sub: 2 (over core).
Axes of the slice: x: 2, y: 2, z: 4, core: 2. Of those that a mesh axis runs over, the one named last changes fastest.
Arguments:
- stream_in: bfloat16 [4096, 5376], P(('groups', 'row'), ('col', 'sub')), parts along dimension 0, may hold values from -6 to 6
- in_gain: float32 [5376], replicated, may hold values from 0.1 to 1.9
- query_weight: bfloat16 [5376, 4096], P('row', ('col', 'sub')), may hold values from -0.078125 to 0.078125
- key_matrix: bfloat16 [5376, 2048], P('row', ('col', 'sub')), may hold values from -0.078125 to 0.078125
- value_matrix: bfloat16 [5376, 2048], P('row', ('col', 'sub')), may hold values from -0.078125 to 0.078125
- query_gain: float32 [128], replicated, may hold values from 0.45 to 10, as said below
- key_norm_gain: float32 [128], replicated, may hold values from 0.45 to 10, as said below
- output_weight: bfloat16 [4096, 5376], P('row', ('col', 'sub')), may hold values from -3 to 3
- post_gain: float32 [5376], P(('col', 'sub')), may hold values from 0.1 to 1.9
Outputs:
- stream_out: bfloat16 [4096, 5376], P(('groups', 'row'), ('col', 'sub')), parts along dimension 0
There are 2 independent parts, one for each index of `groups`. A program takes and returns all parts, laid end to end along the dimension named above; an argument that names none is the same for every part. Nothing has to cross between parts.
Inputs may be any that keep to these rules, and one draw needn't show every extreme that they name: `query_gain`: positive. `key_norm_gain`: positive.
All inputs are finite; a program needn't handle non-finite values.
Results may differ from a plain program's by a relative error of at most 0.014.
The roundings to bfloat16 on the way count: a program that leaves them out, or rounds other values in their place, can miss the bound.
Values may be sent and summed in bfloat16 or wider, within the bound.
No kernel may reach another device: no remote copies, remote signals or barrier semaphores. Data moves between devices by JAX's collectives and lax.ppermute only.
A program may use at most 128 MiB of HBM per device.

v0:
```python
import jax
import jax.numpy as jnp
from jax import lax
from jax.sharding import PartitionSpec as P

MODEL_WIDTH = 5376
QUERY_HEAD_COUNT = 32
WINDOW_LENGTH = 1024


EPSILON = 1e-06


def shifted(x, axis, by):
    count = lax.axis_size(axis)
    pairs = [(i, i + by) for i in range(count) if 0 <= i + by < count]
    return lax.ppermute(x, axis, pairs)


def root_mean_scale(values, gain):
    return values * lax.rsqrt(jnp.mean(values * values, axis=-1, keepdims=True) + EPSILON) * gain


def apply_rotary(tensor, token_positions):
    half_dim = tensor.shape[-1] // 2
    inverse = 10000.0 ** (-(jnp.arange(half_dim, dtype=jnp.float32) * 2.0) / tensor.shape[-1])
    angles = token_positions[:, None] * inverse[None, :]
    cosine = jnp.cos(angles)[:, None, :]
    sine_part = jnp.sin(angles)[:, None, :]
    first_half = tensor[..., :half_dim]
    second_half = tensor[..., half_dim:]
    return jnp.concatenate(
        [
            first_half * cosine - second_half * sine_part,
            second_half * cosine + first_half * sine_part,
        ],
        axis=-1,
    )


def on_device(
    stream_in,
    in_gain,
    query_weight,
    key_matrix,
    value_matrix,
    query_gain,
    key_norm_gain,
    output_weight,
    post_gain,
):
    token_rows = lax.all_gather(stream_in, ("col", "sub"), axis=1, tiled=True)
    tokens = token_rows.shape[0]
    normed = root_mean_scale(token_rows.astype(jnp.float32), in_gain).astype(jnp.bfloat16)

    def add_panel(panel_piece):
        return jnp.dot(normed, panel_piece, preferred_element_type=jnp.float32)

    query_proj = add_panel(lax.all_gather(query_weight, "row", axis=0, tiled=True))
    projected_keys = add_panel(lax.all_gather(key_matrix, "row", axis=0, tiled=True))
    projected_values = add_panel(lax.all_gather(value_matrix, "row", axis=0, tiled=True))
    head_size = query_gain.shape[0]
    query_heads = query_weight.shape[1] // head_size
    pair_heads = key_matrix.shape[1] // head_size
    group_count = query_heads // pair_heads
    scale_factor = float(MODEL_WIDTH // QUERY_HEAD_COUNT) ** (-0.5)
    row_index = lax.axis_index("row")
    query_places = row_index * tokens + jnp.arange(tokens, dtype=jnp.int32)
    query_rot = apply_rotary(
        root_mean_scale(query_proj.reshape(tokens, query_heads, head_size), query_gain),
        query_places.astype(jnp.float32),
    ).astype(jnp.bfloat16)
    rotary_keys = apply_rotary(
        root_mean_scale(projected_keys.reshape(tokens, pair_heads, head_size), key_norm_gain),
        query_places.astype(jnp.float32),
    ).astype(jnp.bfloat16)
    keys_flat = rotary_keys.reshape(tokens, pair_heads * head_size)
    values_flat = projected_values.astype(jnp.bfloat16)
    shards_back = min(WINDOW_LENGTH // tokens, lax.axis_size("row") - 1)
    band_length = (shards_back + 1) * tokens
    key_parts = [keys_flat]
    value_parts = [values_flat]
    for offset in range(1, shards_back + 1):
        keys_prior, values_prior = shifted((keys_flat, values_flat), "row", offset)
        key_parts = [keys_prior] + key_parts
        value_parts = [values_prior] + value_parts
    keys_band = jnp.concatenate(key_parts, axis=0)
    values_band = jnp.concatenate(value_parts, axis=0)
    key_places = (row_index - shards_back) * tokens + jnp.arange(band_length, dtype=jnp.int32)
    distance = query_places[:, None] - key_places[None, :]
    visible = (distance >= 0) & (distance < WINDOW_LENGTH) & (key_places[None, :] >= 0)
    grouped = query_rot.reshape(tokens, pair_heads, group_count, head_size)
    scores = (
        jnp.einsum(
            "qhgd,shd->hgqs",
            grouped,
            keys_band.reshape(band_length, pair_heads, head_size),
            preferred_element_type=jnp.float32,
        )
        * scale_factor
    )
    scores = jnp.where(visible, scores, -1e30)
    row_max = jnp.max(scores, axis=-1, keepdims=True)
    exponent = jnp.exp(scores - row_max)
    weights = (exponent / jnp.sum(exponent, axis=-1, keepdims=True)).astype(jnp.bfloat16)
    attended = jnp.einsum(
        "hgqs,shd->qhgd",
        weights,
        values_band.reshape(band_length, pair_heads, head_size),
        preferred_element_type=jnp.float32,
    )
    heads_out = attended.reshape(tokens, query_heads * head_size).astype(jnp.bfloat16)
    head_rows = lax.all_gather(heads_out, ("col", "sub"), axis=1, tiled=True)
    branch = jnp.dot(
        head_rows,
        lax.all_gather(output_weight, "row", axis=0, tiled=True),
        preferred_element_type=jnp.float32,
    )
    squares = lax.psum(jnp.sum(branch * branch, axis=-1), ("col", "sub"))
    scaled = branch * lax.rsqrt(squares[:, None] / MODEL_WIDTH + EPSILON) * post_gain
    return (stream_in.astype(jnp.float32) + scaled).astype(jnp.bfloat16)


def solution(mesh):
    placed = (
        P(("groups", "row"), ("col", "sub")),
        P(),
        P("row", ("col", "sub")),
        P("row", ("col", "sub")),
        P("row", ("col", "sub")),
        P(),
        P(),
        P("row", ("col", "sub")),
        P(("col", "sub")),
    )
    return jax.shard_map(
        on_device,
        mesh=mesh,
        in_specs=placed,
        out_specs=P(("groups", "row"), ("col", "sub")),
        check_vma=False,
    )
```

profile of v0, /device:TPU:0, one launch (start us, length us, event | category | flops | bytes accessed | tf_op | source)
XLA Modules:
  0.0 759.2 jit_solution(18262040499544532429)
XLA Ops:
  6.5 0.7 all-gather.7.cloned.1.call-update
  7.3 0.7 all-gather.11.cloned.1.call-update
  10.0 1.0 multiply_cosine_fusion
  11.0 42.6 %all-gather.7.cloned.1.call-done = bf16[512,5376]{0,1:T(8,128)(2,1)} async-done(((bf16[512,1344]{0,1:T(8,128)(2,1)}), bf16[512,5376]{0,1:T(8,128)(2,1)}) %all-gather.7.cloned.1.call-update) | async-done | bytes 5505040 | tf_op jit(solution)/shard_map/all_gather | solution.py:52
  53.6 3.8 fusion.6
  57.3 100.2 %all-gather.11.cloned.1.call-done = bf16[5376,512]{1,0:T(8,128)(2,1)} async-done(((bf16[1344,512]{1,0:T(8,128)(2,1)}), bf16[5376,512]{1,0:T(8,128)(2,1)}) %all-gather.11.cloned.1.call-update) | async-done | bytes 5505040 | tf_op jit(solution)/shard_map/all_gather | solution.py:60
  157.6 7.6 %multiply_reduce_fusion.2 = (f32[512,4]{0,1:T(4,128)S(1)}, f32[512,512]{0,1:T(8,128)S(1)}) fusion(bf16[5376,512]{1,0:T(8,128)(2,1)} %all-gather.11.cloned.1.call-done, bf16[512,5376]{0,1:T(8,128)(2,1)} %all-gather.7.cloned.1.call-done, f32[5376]{0:T(1024)S(1)} %copy-done.6, f32[512]{0:T(512)S(1)} %add_rsqrt_fusion.3), kind=kOutput, calls=%fused_computation.35 | convolution fusion | flops 2830104576 | bytes 12090368 | tf_op jit(solution)/shard_map/dot_general | solution.py:57
  166.8 2.7 collective-permute-start.2
  169.5 2.1 collective-permute-start.3
  171.7 106.5 %all-gather.9.cloned.1.call-done = bf16[5376,512]{1,0:T(8,128)(2,1)} async-done(((bf16[1344,512]{1,0:T(8,128)(2,1)}), bf16[5376,512]{1,0:T(8,128)(2,1)}) %all-gather.9.cloned.1.call-update) | async-done | bytes 5505040 | tf_op jit(solution)/shard_map/all_gather | solution.py:61
  278.1 7.4 convolution_convert_fusion
  285.5 5.2 collective-permute-start
  290.7 16.1 %collective-permute-start.1 = (bf16[512,512]{1,0:T(8,128)(2,1)S(1)}, bf16[512,512]{1,0:T(8,128)(2,1)}, u32[]{:S(2)}, u32[]{:S(2)}) collective-permute-start(bf16[512,512]{1,0:T(8,128)(2,1)S(1)} %convolution_convert_fusion), channel_id=1, source_target_pairs={{0,4},{4,8},{8,12},{1,5},{5,9},{9,13},{2,6},{6,10},{10,14},{3,7},{... | collective-permute-start | bytes 1572872 | tf_op jit(solution)/shard_map/ppermute | solution.py:17
  306.9 1.9 fusion.12
  308.8 1.0 copy.34
  309.8 1.0 copy.35
  310.8 18.4 %collective-permute-done.1 = bf16[512,512]{1,0:T(8,128)(2,1)} collective-permute-done((bf16[512,512]{1,0:T(8,128)(2,1)S(1)}, bf16[512,512]{1,0:T(8,128)(2,1)}, u32[]{:S(2)}, u32[]{:S(2)}) %collective-permute-start.1) | collective-permute-done | bytes 524320 | tf_op jit(solution)/shard_map/ppermute | solution.py:17
  329.2 1.3 pad_maximum_fusion
  330.5 1.6 copy.45
  332.1 160.2 %all-gather.13.cloned.1.call-done = bf16[5376,1024]{1,0:T(8,128)(2,1)} async-done(((bf16[1344,1024]{1,0:T(8,128)(2,1)}), bf16[5376,1024]{1,0:T(8,128)(2,1)}) %all-gather.13.cloned.1.call-update) | async-done | bytes 11010064 | tf_op jit(solution)/shard_map/all_gather | solution.py:59
  492.3 11.7 %convolution_bitcast_fusion = f32[64,8,8,128]{3,1,2,0:T(8,128)S(1)} fusion(bf16[5376,1024]{1,0:T(8,128)(2,1)} %all-gather.13.cloned.1.call-done, bf16[512,5376]{0,1:T(8,128)(2,1)} %all-gather.7.cloned.1.call-done, f32[5376]{0:T(1024)S(1)} %copy-done.6, f32[512]{0:T(512)S(1)} %add_rsqrt_fusion.3), kind=kOutput, calls=%fused_computation.25 | convolution fusion | flops 5648154624 | bytes 18635776 | tf_op jit(solution)/shard_map/dot_general | solution.py:57
  505.4 1.1 multiply_multiply_fusion
  506.5 0.9 subtract_convert_fusion
  507.6 0.7 copy-done.1
  508.5 14.3 %fusion.14 = f32[4,1536,512,2]{2,1,3,0:T(8,128)} fusion(bf16[512,4,128]{2,0,1:T(8,128)(2,1)S(1)} %maximum_convert_fusion, bf16[512,4,128]{2,0,1:T(8,128)(2,1)S(1)} %copy-done.2, bf16[512,4,128]{2,0,1:T(8,128)(2,1)S(1)} %copy-done.1, bf16[512,4,2,64]{3,0,2,1:T(8,128)(2,1)S(1)} %bitcast.48, bf16[512,4,2,64]{3,0,2,1:T(8,128)(2,1)S(1)} %bitcast.50), kind=kOutput, calls=%fused_computation.36 | convolution fusion | flops 1617428480 | bytes 27787264 | tf_op jit(solution)/shard_map/qhgd,shd->hgqs/dot_general | solution.py:94
  522.8 10.5 %fusion.30 = f32[4,2,512]{2,1,0:T(2,128)S(1)} fusion(pred[512,1536]{0,1:T(8,128)(4,1)} %fusion.12, bf16[512,4,128]{2,0,1:T(8,128)(2,1)S(1)} %maximum_convert_fusion, bf16[512,4,128]{2,0,1:T(8,128)(2,1)} %copy.35, bf16[512,4,128]{2,0,1:T(8,128)(2,1)S(1)} %copy-done.1, bf16[512,4,2,64]{3,0,2,1:T(8,128)(2,1)S(1)} %bitcast.49, ...), kind=kOutput, calls=%fused_computation.56 | convolution fusion | flops 1642595840 | bytes 3424256 | tf_op jit(solution)/shard_map/sub | solution.py:104
  533.3 15.3 %fusion.13 = bf16[4,128,2,512]{3,1,2,0:T(8,128)(2,1)} fusion(bf16[1536,4,128,1]{0,2,3,1:T(8,128)(2,1)} %bitcast.52, f32[4,2,512]{2,1,0:T(2,128)S(1)} %fusion.30, f32[4,1536,512,2]{2,1,3,0:T(8,128)} %fusion.14, pred[512,1536]{0,1:T(8,128)(4,1)} %fusion.12), kind=kOutput, calls=%fused_computation.28 | convolution fusion | flops 1642599936 | bytes 28590080 | tf_op jit(solution)/shard_map/hgqs,shd->qhgd/dot_general | solution.py:106
  548.7 149.4 %all-gather.17.cloned.1.call-done = bf16[4096,1344]{0,1:T(8,128)(2,1)} async-done(((bf16[1024,1344]{0,1:T(8,128)(2,1)}), bf16[4096,1344]{0,1:T(8,128)(2,1)}) %all-gather.17.cloned.1.call-update) | async-done | bytes 11010064 | tf_op jit(solution)/shard_map/all_gather | solution.py:116
  698.1 34.1 %all-gather.15.cloned.1.call-done = bf16[512,4096]{0,1:T(8,128)(2,1)} async-done(((bf16[512,1024]{0,1:T(8,128)(2,1)}), bf16[512,4096]{0,1:T(8,128)(2,1)}) %all-gather.15.cloned.1.call-update) | async-done | bytes 4194320 | tf_op jit(solution)/shard_map/all_gather | solution.py:113
  732.2 10.9 %multiply_reduce_fusion = (f32[512]{0:T(512)S(1)}, f32[512,1344]{0,1:T(8,128)}) fusion(bf16[4096,1344]{0,1:T(8,128)(2,1)} %all-gather.17.cloned.1.call-done, bf16[512,4096]{0,1:T(8,128)(2,1)} %all-gather.15.cloned.1.call-done), kind=kOutput, calls=%fused_computation.20 | convolution fusion | flops 5638520320 | bytes 17958912 | tf_op jit(solution)/shard_map/dot_general | solution.py:114
  743.2 5.9 psum.7
  749.0 3.3 add_convert_fusion
  (46 shorter events, 5.4 us)
Async XLA Ops:
  6.5 47.0 %all-gather.7.cloned.1.call-start = ((), (), s32[]{:S(2)}) async-start(), calls=%async_computation | async-start | bytes 6881280 | tf_op jit(solution)/shard_map/all_gather | solution.py:52
  7.3 150.3 %all-gather.11.cloned.1.call-start = ((), (), s32[]{:S(2)}) async-start(), calls=%async_computation.2 | async-start | bytes 6881280 | tf_op jit(solution)/shard_map/all_gather | solution.py:60
  8.0 270.1 %all-gather.9.cloned.1.call-start = ((), (), s32[]{:S(2)}) async-start(), calls=%async_computation.1 | async-start | bytes 6881280 | tf_op jit(solution)/shard_map/all_gather | solution.py:61
  8.7 483.5 %all-gather.13.cloned.1.call-start = ((), (), s32[]{:S(2)}) async-start(), calls=%async_computation.3 | async-start | bytes 13762560 | tf_op jit(solution)/shard_map/all_gather | solution.py:59
  9.3 688.8 %all-gather.17.cloned.1.call-start = ((), (), s32[]{:S(2)}) async-start(), calls=%async_computation.5 | async-start | bytes 13762560 | tf_op jit(solution)/shard_map/all_gather | solution.py:116
  9.9 147.7 %copy-start.6 = (f32[5376]{0:T(1024)S(1)}, f32[5376]{0:T(1024)}, u32[]{:S(2)}) copy-start(f32[5376]{0:T(1024)} %param.10) | copy-start | bytes 64516
  9.9 722.3 %all-gather.15.cloned.1.call-start = ((), (), s32[]{:S(2)}) async-start(), calls=%async_computation.4 | async-start | bytes 5242880 | tf_op jit(solution)/shard_map/all_gather | solution.py:113
  57.3 108.2 %copy-start.4 = (f32[128]{0:T(128)S(1)}, f32[128]{0:T(128)}, u32[]{:S(2)}) copy-start(f32[128]{0:T(128)} %param.15) | copy-start | bytes 1540
  166.8 142.0 %collective-permute-start.2 = (bf16[512,512]{0,1:T(8,128)(2,1)S(1)}, bf16[512,512]{0,1:T(8,128)(2,1)S(1)}, u32[]{:S(2)}, u32[]{:S(2)}) collective-permute-start(bf16[512,512]{0,1:T(8,128)(2,1)S(1)} %bitcast.55), channel_id=1, source_target_pairs={{0,8},{4,12},{1,9},{5,13},{2,10},{6,14},{3,11},{7,15},{16,24},{20,... | collective-permute-start | bytes 1572872 | tf_op jit(solution)/shard_map/ppermute | solution.py:17
  169.5 140.3 %collective-permute-start.3 = (bf16[512,512]{0,1:T(8,128)(2,1)S(1)}, bf16[512,512]{0,1:T(8,128)(2,1)S(1)}, u32[]{:S(2)}, u32[]{:S(2)}) collective-permute-start(bf16[512,512]{0,1:T(8,128)(2,1)S(1)} %bitcast.56), channel_id=1, source_target_pairs={{0,4},{4,8},{8,12},{1,5},{5,9},{9,13},{2,6},{6,10},{10,14},{3,7},{... | collective-permute-start | bytes 1572872 | tf_op jit(solution)/shard_map/ppermute | solution.py:17
  285.5 25.3 %collective-permute-start = (bf16[512,512]{1,0:T(8,128)(2,1)S(1)}, bf16[512,512]{1,0:T(8,128)(2,1)}, u32[]{:S(2)}, u32[]{:S(2)}) collective-permute-start(bf16[512,512]{1,0:T(8,128)(2,1)S(1)} %convolution_convert_fusion), channel_id=1, source_target_pairs={{0,8},{4,12},{1,9},{5,13},{2,10},{6,14},{3,11},{7,15},{16,24},{20,... | collective-permute-start | bytes 1572872 | tf_op jit(solution)/shard_map/ppermute | solution.py:17
  290.7 38.5 %collective-permute-start.1 = (bf16[512,512]{1,0:T(8,128)(2,1)S(1)}, bf16[512,512]{1,0:T(8,128)(2,1)}, u32[]{:S(2)}, u32[]{:S(2)}) collective-permute-start(bf16[512,512]{1,0:T(8,128)(2,1)S(1)} %convolution_convert_fusion), channel_id=1, source_target_pairs={{0,4},{4,8},{8,12},{1,5},{5,9},{9,13},{2,6},{6,10},{10,14},{3,7},{... | collective-permute-start | bytes 1572872 | tf_op jit(solution)/shard_map/ppermute | solution.py:17
  504.0 1.4 copy-start.5
  507.3 1.0 copy-start.1
  507.3 1.2 copy-start.2
  548.6 200.4 %copy-start = (bf16[512,1344]{0,1:T(8,128)(2,1)S(1)}, bf16[512,1344]{0,1:T(8,128)(2,1)}, u32[]{:S(2)}) copy-start(bf16[512,1344]{0,1:T(8,128)(2,1)} %param.9) | copy-start | bytes 4128772
  548.6 200.4 %copy-start.3 = (f32[1344]{0:T(1024)S(1)}, f32[1344]{0:T(1024)}, u32[]{:S(2)}) copy-start(f32[1344]{0:T(1024)} %param.17) | copy-start | bytes 16132
Sparse Core Ops, SparseCore 0:
  8.9 44.6 all-gather.6
  55.1 102.3 all-gather.10
  159.1 118.9 all-gather.8
  279.6 212.6 all-gather.12
  493.7 204.3 all-gather.16
  699.5 32.6 all-gather.14
where the time goes:
time: 760 us; the launch traced here: 759 us
  waiting for transfers between devices  614 us (81%)
  matrix products  77.7 us (10%)
  starting transfers between devices  26.3 us (3%)
  other arithmetic  15 us (2%)
  between operations  13.7 us (2%)
    all_gather x1, waiting for transfers between devices, on_device(): lax.all_gather(query_weight, 'row', axis=0, tiled=True)  160 us
    all_gather x1, waiting for transfers between devices, on_device(): lax.all_gather(output_weight, 'row', axis=0, tiled=True)  149 us
    all_gather x1, waiting for transfers between devices, on_device(): lax.all_gather(value_matrix, 'row', axis=0, tiled=True)  106 us
    all_gather x1, waiting for transfers between devices, on_device(): lax.all_gather(key_matrix, 'row', axis=0, tiled=True)  100 us
    all_gather x1, waiting for transfers between devices, on_device(): token_rows = lax.all_gather(stream_in, ('col', 'sub'), axis=1, tiled=True)  42.6 us
    all_gather x1, waiting for transfers between devices, on_device(): head_rows = lax.all_gather(heads_out, ('col', 'sub'), axis=1, tiled=True)  34.1 us
    dot_general x3, matrix products, add_panel(): return jnp.dot(normed, panel_piece, preferred_element_type=jnp.float32)  26.7 us
    ppermute x4, starting transfers between devices, shifted(): return lax.ppermute(x, axis, pairs)  26.2 us
  transfers between devices with their start and end apart: 10, of which 7 were waited for; matrix products, arithmetic and copies ran while one was open for 11% of the time, Pallas kernels for 0%

commit v1 on v0

--- a/solution.py
+++ b/solution.py
@@ -1,6 +1,10 @@
+import functools
+
 import jax
 import jax.numpy as jnp
 from jax import lax
+from jax.experimental import pallas as pl
+from jax.experimental.pallas import tpu as pltpu
 from jax.sharding import PartitionSpec as P
 
 MODEL_WIDTH = 5376
@@ -9,6 +13,9 @@
 
 
 EPSILON = 1e-06
+MIDDLE = (1, 2)
+ENDS = (0, 3)
+VMEM_BYTES = 60 * 1024 * 1024
 
 
 def shifted(x, axis, by):
@@ -21,12 +28,17 @@
     return values * lax.rsqrt(jnp.mean(values * values, axis=-1, keepdims=True) + EPSILON) * gain
 
 
+def rotary_tables(token_positions, size):
+    half_dim = size // 2
+    inverse = 10000.0 ** (-(jnp.arange(half_dim, dtype=jnp.float32) * 2.0) / size)
+    angles = token_positions[:, None] * inverse[None, :]
+    return jnp.cos(angles), jnp.sin(angles)
+
+
 def apply_rotary(tensor, token_positions):
     half_dim = tensor.shape[-1] // 2
-    inverse = 10000.0 ** (-(jnp.arange(half_dim, dtype=jnp.float32) * 2.0) / tensor.shape[-1])
-    angles = token_positions[:, None] * inverse[None, :]
-    cosine = jnp.cos(angles)[:, None, :]
-    sine_part = jnp.sin(angles)[:, None, :]
+    cosine, sine_part = rotary_tables(token_positions, tensor.shape[-1])
+    cosine, sine_part = cosine[:, None, :], sine_part[:, None, :]
     first_half = tensor[..., :half_dim]
     second_half = tensor[..., half_dim:]
     return jnp.concatenate(
@@ -38,7 +50,7 @@
     )
 
 
-def on_device(
+def general_form(
     stream_in,
     in_gain,
     query_weight,
@@ -121,6 +133,368 @@
     return (stream_in.astype(jnp.float32) + scaled).astype(jnp.bfloat16)
 
 
+def swapped(x, axis, rows):
+    if axis == "groups":
+        count = lax.axis_size("row")
+        pairs = [(count * i + r, count * (1 - i) + r) for r in rows for i in range(2)]
+        return lax.ppermute(x, ("groups", "row"), pairs)
+    pairs = [(2 * r + i, 2 * r + 1 - i) for r in rows for i in range(2)]
+    return lax.ppermute(x, ("row", axis), pairs)
+
+
+def project_kernel(
+    x0, x1, x2, x3, gain, weight, q_gain, k_gain, cosine, sine, q_out, k_out, v_out, total, scale
+):
+    pieces = (x0, x1, x2, x3)
+    step = pl.program_id(0)
+    head = q_gain.shape[-1]
+
+    @pl.when(step == 0)
+    def _():
+        squares = sum(
+            jnp.sum(jnp.square(p[...].astype(jnp.float32)), axis=-1, keepdims=True) for p in pieces
+        )
+        scale[...] = lax.rsqrt(squares / MODEL_WIDTH + EPSILON)
+
+    for index, piece in enumerate(pieces):
+
+        @pl.when(step == index)
+        def _(index=index, piece=piece):
+            normed = (piece[...].astype(jnp.float32) * scale[...] * gain[index : index + 1, :]).astype(
+                jnp.bfloat16
+            )
+            half = weight.shape[-1]
+            for part in range(2):
+                product = jnp.dot(normed, weight[0, part], preferred_element_type=jnp.float32)
+                columns = slice(part * half, (part + 1) * half)
+                if index == 0:
+                    total[:, columns] = product
+                else:
+                    total[:, columns] += product
+
+    @pl.when(step == len(pieces) - 1)
+    def _():
+        cos, sin = cosine[...], sine[...]
+
+        def rotated(columns, head_gain):
+            values = total[:, columns]
+            values = (
+                values
+                * lax.rsqrt(jnp.mean(values * values, axis=-1, keepdims=True) + EPSILON)
+                * head_gain[...]
+            )
+            return (values * cos + pltpu.roll(values, head // 2, 1) * sin).astype(jnp.bfloat16)
+
+        q_width, k_width = q_out.shape[-1], k_out.shape[-1]
+        for start in range(0, q_width, head):
+            q_out[:, start : start + head] = rotated(slice(start, start + head), q_gain)
+        for start in range(0, k_width, head):
+            k_out[:, start : start + head] = rotated(
+                slice(q_width + start, q_width + start + head), k_gain
+            )
+        v_out[...] = total[:, q_width + k_width :].astype(jnp.bfloat16)
+
+
+def project(pieces, gain, weight, q_gain, k_gain, cosine, sine):
+    tokens, depth = pieces[0].shape
+    width = weight.shape[-1]
+    head = q_gain.shape[-1]
+    whole = lambda shape: pl.BlockSpec(shape, lambda k: (0,) * len(shape))
+    return pl.pallas_call(
+        project_kernel,
+        grid=(4,),
+        in_specs=[whole((tokens, depth))] * 4
+        + [
+            whole((4, depth)),
+            pl.BlockSpec((1, 2, depth, width), lambda k: (k, 0, 0, 0)),
+            whole((1, head)),
+            whole((1, head)),
+            whole((tokens, head)),
+            whole((tokens, head)),
+        ],
+        out_specs=[
+            whole((tokens, width)),
+            whole((tokens, width // 2)),
+            whole((tokens, width // 2)),
+        ],
+        out_shape=[
+            jax.ShapeDtypeStruct((tokens, width), jnp.bfloat16),
+            jax.ShapeDtypeStruct((tokens, width // 2), jnp.bfloat16),
+            jax.ShapeDtypeStruct((tokens, width // 2), jnp.bfloat16),
+        ],
+        scratch_shapes=[
+            pltpu.VMEM((tokens, 2 * width), jnp.float32),
+            pltpu.VMEM((tokens, 1), jnp.float32),
+        ],
+        compiler_params=pltpu.CompilerParams(vmem_limit_bytes=VMEM_BYTES),
+        cost_estimate=pl.CostEstimate(
+            flops=2 * tokens * 4 * depth * 2 * width,
+            bytes_accessed=2 * (4 * tokens * depth + 8 * depth * width + 2 * tokens * width),
+            transcendentals=0,
+        ),
+    )(*pieces, gain, weight, q_gain, k_gain, cosine, sine)
+
+
+def attend_kernel(band, scale, table, q_ref, k0, k1, k2, k3, v0, v1, v2, v3, out, keys, values):
+    tokens, tile = k0.shape[0], q_ref.shape[0]
+    head = 128
+    step = pl.program_id(0)
+
+    @pl.when(step == 0)
+    def _():
+        for index, (k, v) in enumerate(((k0, v0), (k1, v1), (k2, v2), (k3, v3))):
+            rows = pl.ds(pl.multiple_of(table[index + 1] * tokens, tokens), tokens)
+            keys[rows, :] = k[...]
+            values[rows, :] = v[...]
+
+    first = table[0] * tokens + step * tile
+    start = pl.multiple_of(
+        jnp.clip(first + tile - band, 0, keys.shape[0] - band), tile
+    )
+    rows = pl.ds(start, band)
+    distance = (
+        (first - start)
+        + lax.broadcasted_iota(jnp.int32, (tile, band), 0)
+        - lax.broadcasted_iota(jnp.int32, (tile, band), 1)
+    )
+    visible = (distance >= 0) & (distance < WINDOW_LENGTH)
+    group = (q_ref.shape[1] // head) // (keys.shape[1] // head)
+    for index in range(q_ref.shape[1] // head):
+        q = q_ref[:, index * head : (index + 1) * head]
+        kv_columns = slice((index // group) * head, (index // group + 1) * head)
+        scores = lax.dot_general(
+            q, keys[rows, kv_columns], (((1,), (1,)), ((), ())), preferred_element_type=jnp.float32
+        )
+        scores = jnp.where(visible, scores * scale, -1e30)
+        exponent = jnp.exp(scores - jnp.max(scores, axis=-1, keepdims=True))
+        weights = exponent * (1.0 / jnp.sum(exponent, axis=-1, keepdims=True))
+        out[:, index * head : (index + 1) * head] = jnp.dot(
+            weights.astype(jnp.bfloat16), values[rows, kv_columns], preferred_element_type=jnp.float32
+        ).astype(jnp.bfloat16)
+
+
+def attend(table, q, ks, vs):
+    tokens, q_width = q.shape
+    kv_width = ks[0].shape[1]
+    tile = tokens // 2
+    band = min(WINDOW_LENGTH + tile, 4 * tokens)
+    whole = lambda shape: pl.BlockSpec(shape, lambda t, *_: (0,) * len(shape))
+    return pl.pallas_call(
+        functools.partial(attend_kernel, band, float(MODEL_WIDTH // QUERY_HEAD_COUNT) ** (-0.5)),
+        grid_spec=pltpu.PrefetchScalarGridSpec(
+            num_scalar_prefetch=1,
+            grid=(2,),
+            in_specs=[pl.BlockSpec((tile, q_width), lambda t, *_: (t, 0))]
+            + [whole((tokens, kv_width))] * 8,
+            out_specs=pl.BlockSpec((tile, q_width), lambda t, *_: (t, 0)),
+            scratch_shapes=[
+                pltpu.VMEM((4 * tokens, kv_width), jnp.bfloat16),
+                pltpu.VMEM((4 * tokens, kv_width), jnp.bfloat16),
+            ],
+        ),
+        out_shape=jax.ShapeDtypeStruct((tokens, q_width), jnp.bfloat16),
+        compiler_params=pltpu.CompilerParams(vmem_limit_bytes=VMEM_BYTES),
+        cost_estimate=pl.CostEstimate(
+            flops=4 * tokens * band * q_width,
+            bytes_accessed=2 * (2 * tokens * q_width + 8 * tokens * kv_width),
+            transcendentals=tokens * band * (q_width // 128),
+        ),
+    )(table, q, *ks, *vs)
+
+
+def output_kernel(*refs):
+    *parts, weight, out = refs
+    step = pl.program_id(0)
+    for index, part in enumerate(parts):
+
+        @pl.when(step == index)
+        def _(index=index, part=part):
+            product = jnp.dot(part[...], weight[0], preferred_element_type=jnp.float32)
+            if index == 0:
+                out[...] = product
+            else:
+                out[...] += product
+
+
+def output_product(parts, weight):
+    tokens, depth = parts[0].shape
+    width = weight.shape[-1]
+    whole = lambda shape: pl.BlockSpec(shape, lambda k: (0,) * len(shape))
+    return pl.pallas_call(
+        output_kernel,
+        grid=(len(parts),),
+        in_specs=[whole((tokens, depth))] * len(parts)
+        + [pl.BlockSpec((1, depth, width), lambda k: (k, 0, 0))],
+        out_specs=whole((tokens, width)),
+        out_shape=jax.ShapeDtypeStruct((tokens, width), jnp.float32),
+        compiler_params=pltpu.CompilerParams(vmem_limit_bytes=VMEM_BYTES),
+        cost_estimate=pl.CostEstimate(
+            flops=2 * tokens * depth * len(parts) * width,
+            bytes_accessed=2 * len(parts) * (tokens + width) * depth + 4 * tokens * width,
+            transcendentals=0,
+        ),
+    )(*parts, weight)
+
+
+def middle_form(
+    stream_in,
+    in_gain,
+    query_weight,
+    key_matrix,
+    value_matrix,
+    query_gain,
+    key_norm_gain,
+    output_weight,
+    post_gain,
+):
+    tokens, features = stream_in.shape
+    head = query_gain.shape[0]
+    row = lax.axis_index("row")
+    group = lax.axis_index("groups")
+    place = lax.axis_index("col") * 2 + lax.axis_index("sub")
+    upper = (row >= 2).astype(jnp.int32)
+    in_middle = (row == 1) | (row == 2)
+    own_block, near_block, cross_block, far_block = row, 3 * upper, 3 - row, 3 - 3 * upper
+    slot = lambda block: jnp.bitwise_xor(place, block)
+
+    half = query_weight.shape[1] // 2
+    quarter = key_matrix.shape[1] // 2
+
+    def side(which):
+        queries = lax.dynamic_slice_in_dim(query_weight, which * half, half, axis=1)
+        keys = lax.dynamic_slice_in_dim(key_matrix, which * quarter, quarter, axis=1)
+        values = lax.dynamic_slice_in_dim(value_matrix, which * quarter, quarter, axis=1)
+        return queries, jnp.concatenate([keys, values], axis=1)
+
+    own_queries, own_pairs = side(upper)
+    other_queries, other_pairs = side(1 - upper)
+    own_side = jnp.where(group == 0, own_queries, own_pairs)
+    other_side = jnp.where(group == 0, other_queries, other_pairs)
+
+    x_near = lax.ppermute(stream_in, "row", [(0, 1), (3, 2)])
+    x_cross = lax.ppermute(stream_in, "row", [(1, 2), (2, 1)])
+    w_near = lax.ppermute(own_side, "row", [(0, 1), (3, 2)])
+    w_cross = lax.ppermute(other_side, "row", [(1, 2), (2, 1)])
+    w_far = lax.ppermute(other_side, "row", [(0, 2), (3, 1)])
+    x_far = lax.ppermute(x_near, "row", [(1, 2), (2, 1)])
+
+    weight = jnp.zeros((4, 2) + own_side.shape, jnp.bfloat16)
+
+    def put(buffer, piece, *index):
+        return lax.dynamic_update_slice(buffer, piece[None, None], (*index, 0, 0))
+
+    weight = put(weight, own_queries, slot(own_block), 0)
+    weight = put(weight, own_pairs, slot(own_block), 1)
+    for piece, block in ((w_near, near_block), (w_cross, cross_block), (w_far, far_block)):
+        weight = put(weight, piece, slot(block), group)
+        weight = put(weight, swapped(piece, "groups", MIDDLE), slot(block), 1 - group)
+
+    depth = output_weight.shape[0] // 2
+    mine = lax.dynamic_slice_in_dim(output_weight, group * depth, depth, axis=0)
+    o_pair = lax.ppermute(mine, "row", [(0, 1), (1, 0), (2, 3), (3, 2)])
+    o_cross = lax.ppermute(mine, "row", [(1, 2), (2, 1)])
+    o_far = lax.ppermute(o_pair, "row", [(1, 2), (2, 1)])
+    o_end_cross = lax.ppermute(o_cross, "row", [(1, 0), (2, 3)])
+    o_end_far = lax.ppermute(o_far, "row", [(1, 0), (2, 3)])
+    out_weight = jnp.zeros((5, 2) + mine.shape, jnp.bfloat16)
+    for part in range(2):
+        out_weight = put(
+            out_weight,
+            output_weight[part * depth : (part + 1) * depth],
+            slot(row),
+            jnp.bitwise_xor(part, upper),
+        )
+    opposite = 3 - row
+    pair_block = jnp.bitwise_xor(row, 1)
+    cross_held = jnp.where(in_middle, slot(3 - row), 4)
+    far_held = jnp.where(in_middle, slot(3 - pair_block), 4)
+    end_cross_held = jnp.where(in_middle, 4, slot(3 - pair_block))
+    end_far_held = jnp.where(in_middle, 4, slot(3 - row))
+    for piece, where, rows in (
+        (o_pair, slot(pair_block), MIDDLE + ENDS),
+        (o_cross, cross_held, MIDDLE),
+        (o_far, far_held, MIDDLE),
+        (o_end_cross, end_cross_held, ENDS),
+        (o_end_far, end_far_held, ENDS),
+    ):
+        out_weight = put(out_weight, piece, where, jnp.bitwise_xor(group, upper))
+        out_weight = put(
+            out_weight, swapped(piece, "groups", rows), where, jnp.bitwise_xor(1 - group, upper)
+        )
+
+    positions = jnp.arange(4 * tokens, dtype=jnp.int32).astype(jnp.float32)
+    cosine, sine = rotary_tables(positions, head)
+    cosine = jnp.concatenate([cosine, cosine], axis=1)
+    sine = jnp.concatenate([-sine, sine], axis=1)
+    gain_rows = in_gain.reshape(4, features)
+    gain = jnp.concatenate(
+        [lax.dynamic_slice_in_dim(gain_rows, slot(j), 1, axis=0) for j in range(4)], axis=0
+    )
+
+    def projected(piece, block):
+        across = swapped(piece, "col", MIDDLE)
+        pieces = (piece, swapped(piece, "sub", MIDDLE), across, swapped(across, "sub", MIDDLE))
+        return project(
+            pieces,
+            gain,
+            weight,
+            query_gain[None],
+            key_norm_gain[None],
+            lax.dynamic_slice_in_dim(cosine, block * tokens, tokens, axis=0),
+            lax.dynamic_slice_in_dim(sine, block * tokens, tokens, axis=0),
+        )
+
+    blocks = (own_block, near_block, cross_block, far_block)
+    triples = [projected(p, b) for p, b in zip((stream_in, x_near, x_cross, x_far), blocks)]
+    ks = [t[1] for t in triples]
+    vs = [t[2] for t in triples]
+
+    def attended(index):
+        table = jnp.stack([blocks[index], *blocks]).astype(jnp.int32)
+        return attend(table, triples[index][0], ks, vs)
+
+    to_far = lax.ppermute(attended(3), "row", [(1, 3), (2, 0)])
+    to_near = lax.ppermute(attended(1), "row", [(1, 0), (2, 3)])
+    to_cross = lax.ppermute(attended(2), "row", [(1, 2), (2, 1)])
+    this_side = jnp.where(in_middle, attended(0), to_near)
+    that_side = jnp.where(in_middle, to_cross, to_far)
+    everywhere = MIDDLE + ENDS
+    this_across = swapped(this_side, "col", everywhere)
+    that_across = swapped(that_side, "col", everywhere)
+    parts = (
+        this_side,
+        that_side,
+        swapped(this_side, "sub", everywhere),
+        swapped(that_side, "sub", everywhere),
+        this_across,
+        that_across,
+        swapped(this_across, "sub", everywhere),
+        swapped(that_across, "sub", everywhere),
+    )
+    branch = output_product(parts, out_weight.reshape((10,) + mine.shape))
+
+    squares = jnp.sum(branch * branch, axis=-1)
+    squares = squares + swapped(squares, "sub", everywhere)
+    squares = squares + swapped(squares, "col", everywhere)
+    scaled = branch * lax.rsqrt(squares[:, None] / MODEL_WIDTH + EPSILON) * post_gain
+    return (stream_in.astype(jnp.float32) + scaled).astype(jnp.bfloat16)
+
+
+def on_device(*args):
+    stream_in, _, query_weight, key_matrix, value_matrix, query_gain, *_ = args
+    sizes = tuple(lax.axis_size(name) for name in ("groups", "row", "col", "sub"))
+    tokens, head = stream_in.shape[0], query_gain.shape[0]
+    fits = (
+        sizes == (2, 4, 2, 2)
+        and head == 128
+        and tokens % 256 == 0
+        and key_matrix.shape[1] % (2 * head) == 0
+        and query_weight.shape[1] == 2 * key_matrix.shape[1]
+        and value_matrix.shape[1] == key_matrix.shape[1]
+    )
+    return middle_form(*args) if fits else general_form(*args)
+
+
 def solution(mesh):
     placed = (
         P(("groups", "row"), ("col", "sub")),

time: 760 us -> 503 us (0.66)
  the two profiles are of different devices: /device:TPU:0 before, /device:TPU:11 now
where the time goes in v1:
time: 503 us; the launch traced here: 494 us
  waiting for transfers between devices  141 us (28%)
  local copies, waits for them, and re-layouts  123 us (24%)
  Pallas kernels  113 us (22%)
  starting transfers between devices  97.4 us (19%)
  other arithmetic  19.2 us (4%)
    ppermute x8, waiting for transfers between devices, swapped(): return lax.ppermute(x, ('groups', 'row'), pairs)  68.2 us
    pallas_call x4, Pallas kernels, project(): pl.pallas_call(project_kernel, grid=(4,), in_specs=[whole((tokens, depth)...  58.8 us
    ppermute x20, starting transfers between devices, swapped(): return lax.ppermute(x, ('row', axis), pairs)  43.1 us
    pallas_call x4, Pallas kernels, attend(): pl.pallas_call(functools.partial(attend_kernel, band, float(MODEL_WIDTH /...  40.8 us
    dynamic_update_slice x19, local copies, waits for them, and re-layouts, put(): return lax.dynamic_update_slice(buffer, piece[None, None], (*index, 0, 0))  31.4 us
    ppermute x12, local copies, waits for them, and re-layouts, swapped(): return lax.ppermute(x, ('row', axis), pairs)  30.4 us
    ppermute x1, waiting for transfers between devices, middle_form(): o_pair = lax.ppermute(mine, 'row', [(0, 1), (1, 0), (2, 3), (3, 2)])  28.2 us
    ppermute x20, waiting for transfers between devices, swapped(): return lax.ppermute(x, ('row', axis), pairs)  23.9 us
  transfers between devices with their start and end apart: 42, of which 11 were waited for; matrix products, arithmetic and copies ran while one was open for 27% of the time, Pallas kernels for 20%

profile of v1, /device:TPU:11, one launch (start us, length us, event | category | flops | bytes accessed | tf_op | source)
XLA Modules:
  0.0 494.4 jit_solution(13029380666247745877)
XLA Ops:
  11.2 4.3 constant_dynamic-slice_fusion
  18.7 3.2 collective-permute-start.32
  22.1 3.7 multiply_sine_fusion
  29.2 7.4 %collective-permute-done.1 = bf16[512,1344]{0,1:T(8,128)(2,1)} collective-permute-done((bf16[512,1344]{0,1:T(8,128)(2,1)}, bf16[512,1344]{0,1:T(8,128)(2,1)}, u32[]{:S(2)}, u32[]{:S(2)}) %collective-permute-start.1) | collective-permute-done | bytes 1376288 | tf_op jit(solution)/shard_map/ppermute | solution.py:142
  37.9 5.7 %collective-permute-done.3 = bf16[1344,512]{1,0:T(8,128)(2,1)} collective-permute-done((bf16[1344,512]{1,0:T(8,128)(2,1)}, bf16[1344,512]{1,0:T(8,128)(2,1)}, u32[]{:S(2)}, u32[]{:S(2)}) %collective-permute-start.3) | collective-permute-done | bytes 1376288 | tf_op jit(solution)/shard_map/ppermute | solution.py:376
  44.9 28.2 %collective-permute-done.30 = bf16[512,1344]{0,1:T(8,128)(2,1)} collective-permute-done((bf16[512,1344]{0,1:T(8,128)(2,1)}, bf16[512,1344]{0,1:T(8,128)(2,1)}, u32[]{:S(2)}, u32[]{:S(2)}) %collective-permute-start.30) | collective-permute-done | bytes 1376288 | tf_op jit(solution)/shard_map/ppermute | solution.py:394
  73.1 3.2 collective-permute-start.13
  88.5 5.1 %broadcast_in_dim.82 = bf16[4,2,1344,512]{3,2,1,0:T(8,128)(2,1)} broadcast(bf16[]{:T(256)} %constant.45.clone.1), dimensions={} | broadcast | bytes 11010050 | tf_op jit(solution)/shard_map/broadcast_in_dim | solution.py:381
  94.8 3.4 collective-permute-start.4
  99.4 6.3 %broadcast_in_dim.93 = bf16[5,2,512,1344]{3,2,1,0:T(8,128)(2,1)} broadcast(bf16[]{:T(256)} %constant.45.clone.1), dimensions={} | broadcast | bytes 13762562 | tf_op jit(solution)/shard_map/broadcast_in_dim | solution.py:399
  117.6 14.6 %collective-permute-done.9 = bf16[512,1344]{0,1:T(8,128)(2,1)} collective-permute-done((bf16[512,1344]{0,1:T(8,128)(2,1)}, bf16[512,1344]{0,1:T(8,128)(2,1)}, u32[]{:S(2)}, u32[]{:S(2)}) %collective-permute-start.9) | collective-permute-done | bytes 1376288 | tf_op jit(solution)/shard_map/ppermute | solution.py:374
  158.1 15.0 %collective-permute-done.6 = bf16[1344,512]{1,0:T(8,128)(2,1)} collective-permute-done((bf16[1344,512]{1,0:T(8,128)(2,1)}, bf16[1344,512]{1,0:T(8,128)(2,1)}, u32[]{:S(2)}, u32[]{:S(2)}) %collective-permute-start.6) | collective-permute-done | bytes 1376288 | tf_op jit(solution)/shard_map/ppermute | solution.py:140
  173.1 4.2 collective-permute-start.14
  177.3 25.3 %collective-permute-done.8 = bf16[1344,512]{1,0:T(8,128)(2,1)} collective-permute-done((bf16[1344,512]{1,0:T(8,128)(2,1)}, bf16[1344,512]{1,0:T(8,128)(2,1)}, u32[]{:S(2)}, u32[]{:S(2)}) %collective-permute-start.8) | collective-permute-done | bytes 1376288 | tf_op jit(solution)/shard_map/ppermute | solution.py:140
  202.6 3.2 collective-permute-start.17
  211.5 20.6 %collective-permute-done.31 = bf16[512,1344]{0,1:T(8,128)(2,1)S(1)} collective-permute-done((bf16[512,1344]{0,1:T(8,128)(2,1)}, bf16[512,1344]{0,1:T(8,128)(2,1)S(1)}, u32[]{:S(2)}, u32[]{:S(2)}) %collective-permute-start.31) | collective-permute-done | bytes 1376288 | tf_op jit(solution)/shard_map/ppermute | solution.py:140
  242.1 3.3 collective-permute-start.34
  253.4 4.0 collective-permute-start.12
  257.4 7.3 %collective-permute-done.33 = bf16[512,1344]{0,1:T(8,128)(2,1)} collective-permute-done((bf16[512,1344]{0,1:T(8,128)(2,1)}, bf16[512,1344]{0,1:T(8,128)(2,1)}, u32[]{:S(2)}, u32[]{:S(2)}) %collective-permute-start.33) | collective-permute-done | bytes 1376288 | tf_op jit(solution)/shard_map/ppermute | solution.py:140
  264.7 4.3 collective-permute-start.16
  275.8 14.6 %shard_map.91 = (bf16[512,512]{1,0:T(8,128)(2,1)}, bf16[512,256]{1,0:T(8,128)(2,1)}, bf16[512,256]{1,0:T(8,128)(2,1)}) custom-call(bf16[512,1344]{1,0:T(8,128)(2,1)} %copy.59.x0, bf16[512,1344]{1,0:T(8,128)(2,1)} %copy.60.x1, bf16[512,1344]{1,0:T(8,128)(2,1)} %copy.61.x2, bf16[512,1344]{1,0:T(8,128)(2,1)} %copy.62.x3, f32[4,1344]{1,0:T(4,128)} %pad_maximum_fusion.1.gain, ...), custom_call_target="tpu_custom_call" | custom-call | flops 5637144576 | bytes 17563648 | tf_op jit(solution)/shard_map/pallas_call | solution.py:203
  326.7 14.6 %shard_map.92 = (bf16[512,512]{1,0:T(8,128)(2,1)}, bf16[512,256]{1,0:T(8,128)(2,1)}, bf16[512,256]{1,0:T(8,128)(2,1)}) custom-call(bf16[512,1344]{1,0:T(8,128)(2,1)} %copy.63.x0, bf16[512,1344]{1,0:T(8,128)(2,1)} %copy.64.x1, bf16[512,1344]{1,0:T(8,128)(2,1)} %copy.65.x2, bf16[512,1344]{1,0:T(8,128)(2,1)} %copy.66.x3, f32[4,1344]{1,0:T(4,128)} %pad_maximum_fusion.1.gain, ...), custom_call_target="tpu_custom_call" | custom-call | flops 5637144576 | bytes 17563648 | tf_op jit(solution)/shard_map/pallas_call | solution.py:203
  341.3 14.8 %shard_map.93 = (bf16[512,512]{1,0:T(8,128)(2,1)}, bf16[512,256]{1,0:T(8,128)(2,1)}, bf16[512,256]{1,0:T(8,128)(2,1)}) custom-call(bf16[512,1344]{1,0:T(8,128)(2,1)} %copy.67.x0, bf16[512,1344]{1,0:T(8,128)(2,1)} %copy.68.x1, bf16[512,1344]{1,0:T(8,128)(2,1)} %copy.69.x2, bf16[512,1344]{1,0:T(8,128)(2,1)} %copy.70.x3, f32[4,1344]{1,0:T(4,128)} %pad_maximum_fusion.1.gain, ...), custom_call_target="tpu_custom_call" | custom-call | flops 5637144576 | bytes 17563648 | tf_op jit(solution)/shard_map/pallas_call | solution.py:203
  365.5 14.8 %shard_map.94 = (bf16[512,512]{1,0:T(8,128)(2,1)}, bf16[512,256]{1,0:T(8,128)(2,1)}, bf16[512,256]{1,0:T(8,128)(2,1)}) custom-call(bf16[512,1344]{1,0:T(8,128)(2,1)} %copy.71.x0, bf16[512,1344]{1,0:T(8,128)(2,1)} %copy.72.x1, bf16[512,1344]{1,0:T(8,128)(2,1)} %copy.73.x2, bf16[512,1344]{1,0:T(8,128)(2,1)} %copy.74.x3, f32[4,1344]{1,0:T(4,128)} %pad_maximum_fusion.1.gain, ...), custom_call_target="tpu_custom_call" | custom-call | flops 5637144576 | bytes 17563648 | tf_op jit(solution)/shard_map/pallas_call | solution.py:203
  380.3 10.1 %shard_map.96 = bf16[512,512]{1,0:T(8,128)(2,1)} custom-call(s32[5]{0:T(128)} %stack.21.table, bf16[512,512]{1,0:T(8,128)(2,1)} %get-tuple-element.26.q_ref, bf16[512,256]{1,0:T(8,128)(2,1)} %get-tuple-element.18.k0, bf16[512,256]{1,0:T(8,128)(2,1)} %get-tuple-element.19.k1, bf16[512,256]{1,0:T(8,128)(2,1)} %get-tuple-element.20.k2, ...), custom_call_target="tpu_custom_call" | custom-call | flops 1342177280 | bytes 3145728 | tf_op jit(solution)/shard_map/pallas_call | solution.py:282
  392.5 10.5 %shard_map.97 = bf16[512,512]{1,0:T(8,128)(2,1)} custom-call(s32[5]{0:T(128)} %stack.22.table, bf16[512,512]{1,0:T(8,128)(2,1)} %get-tuple-element.27.q_ref, bf16[512,256]{1,0:T(8,128)(2,1)} %get-tuple-element.18.k0, bf16[512,256]{1,0:T(8,128)(2,1)} %get-tuple-element.19.k1, bf16[512,256]{1,0:T(8,128)(2,1)} %get-tuple-element.20.k2, ...), custom_call_target="tpu_custom_call" | custom-call | flops 1342177280 | bytes 3145728 | tf_op jit(solution)/shard_map/pallas_call | solution.py:282
  406.1 10.1 %shard_map.98 = bf16[512,512]{1,0:T(8,128)(2,1)} custom-call(s32[5]{0:T(128)} %stack.23.table, bf16[512,512]{1,0:T(8,128)(2,1)} %get-tuple-element.28.q_ref, bf16[512,256]{1,0:T(8,128)(2,1)} %get-tuple-element.18.k0, bf16[512,256]{1,0:T(8,128)(2,1)} %get-tuple-element.19.k1, bf16[512,256]{1,0:T(8,128)(2,1)} %get-tuple-element.20.k2, ...), custom_call_target="tpu_custom_call" | custom-call | flops 1342177280 | bytes 3145728 | tf_op jit(solution)/shard_map/pallas_call | solution.py:282
  425.6 10.2 %shard_map.95 = bf16[512,512]{1,0:T(8,128)(2,1)} custom-call(s32[5]{0:T(128)} %stack.20.table, bf16[512,512]{1,0:T(8,128)(2,1)} %get-tuple-element.17.q_ref, bf16[512,256]{1,0:T(8,128)(2,1)} %get-tuple-element.18.k0, bf16[512,256]{1,0:T(8,128)(2,1)} %get-tuple-element.19.k1, bf16[512,256]{1,0:T(8,128)(2,1)} %get-tuple-element.20.k2, ...), custom_call_target="tpu_custom_call" | custom-call | flops 1342177280 | bytes 3145728 | tf_op jit(solution)/shard_map/pallas_call | solution.py:282
  443.9 6.3 %collective-permute-done.26.refs_4_ = bf16[512,512]{1,0:T(8,128)(2,1)} collective-permute-done((bf16[512,512]{1,0:T(8,128)(2,1)S(1)}, bf16[512,512]{1,0:T(8,128)(2,1)}, u32[]{:S(2)}, u32[]{:S(2)}) %collective-permute-start.26) | collective-permute-done | bytes 524320 | tf_op jit(solution)/shard_map/ppermute | solution.py:142
  452.3 9.0 %collective-permute-done.27.refs_5_ = bf16[512,512]{1,0:T(8,128)(2,1)} collective-permute-done((bf16[512,512]{1,0:T(8,128)(2,1)}, bf16[512,512]{1,0:T(8,128)(2,1)}, u32[]{:S(2)}, u32[]{:S(2)}) %collective-permute-start.27) | collective-permute-done | bytes 524320 | tf_op jit(solution)/shard_map/ppermute | solution.py:142
  467.0 13.6 %shard_map.99 = f32[512,1344]{1,0:T(8,128)} custom-call(bf16[512,512]{1,0:T(8,128)(2,1)} %copy-done.7, bf16[512,512]{1,0:T(8,128)(2,1)} %broadcast_select_fusion.1.refs_1_, bf16[512,512]{1,0:T(8,128)(2,1)} %collective-permute-done.24.refs_2_, bf16[512,512]{1,0:T(8,128)(2,1)} %collective-permute-done.25.refs_3_, ...), custom_call_target="tpu_custom_call" | custom-call | flops 5637144576 | bytes 17956864 | tf_op jit(solution)/shard_map/pallas_call | solution.py:323
  488.4 3.3 add_convert_fusion
  (156 shorter events, 189.5 us)
Async XLA Ops:
  0.0 27.2 %collective-permute-start = (bf16[512,1344]{0,1:T(8,128)(2,1)}, bf16[512,1344]{0,1:T(8,128)(2,1)}, u32[]{:S(2)}, u32[]{:S(2)}) collective-permute-start(bf16[512,1344]{0,1:T(8,128)(2,1)} %param.9), channel_id=1, source_target_pairs={{4,5},{5,4},{8,9},{9,8},{6,7},{7,6},{10,11},{11,10},{20,21},{21,20... | collective-permute-start | bytes 4128776 | tf_op jit(solution)/shard_map/ppermute | solution.py:142
  2.6 34.0 %collective-permute-start.1 = (bf16[512,1344]{0,1:T(8,128)(2,1)}, bf16[512,1344]{0,1:T(8,128)(2,1)}, u32[]{:S(2)}, u32[]{:S(2)}) collective-permute-start(bf16[512,1344]{0,1:T(8,128)(2,1)} %param.9), channel_id=1, source_target_pairs={{4,6},{6,4},{8,10},{10,8},{5,7},{7,5},{9,11},{11,9},{20,22},{22,20... | collective-permute-start | bytes 4128776 | tf_op jit(solution)/shard_map/ppermute | solution.py:142
  9.9 33.7 %collective-permute-start.3 = (bf16[1344,512]{1,0:T(8,128)(2,1)}, bf16[1344,512]{1,0:T(8,128)(2,1)}, u32[]{:S(2)}, u32[]{:S(2)}) collective-permute-start(bf16[1344,512]{1,0:T(8,128)(2,1)} %get-tuple-element.33), channel_id=1, source_target_pairs={{0,4},{12,8},{1,5},{13,9},{2,6},{14,10},{3,7},{15,11},{16,20},{28,... | collective-permute-start | bytes 4128776 | tf_op jit(solution)/shard_map/ppermute | solution.py:376
  15.5 57.6 %collective-permute-start.30 = (bf16[512,1344]{0,1:T(8,128)(2,1)}, bf16[512,1344]{0,1:T(8,128)(2,1)}, u32[]{:S(2)}, u32[]{:S(2)}) collective-permute-start(bf16[512,1344]{0,1:T(8,128)(2,1)} %get-tuple-element.29), channel_id=1, source_target_pairs={{0,4},{4,0},{8,12},{12,8},{1,5},{5,1},{9,13},{13,9},{2,6},{6,2},{1... | collective-permute-start | bytes 4128776 | tf_op jit(solution)/shard_map/ppermute | solution.py:394
  18.7 76.1 %collective-permute-start.32 = (bf16[512,1344]{0,1:T(8,128)(2,1)}, bf16[512,1344]{0,1:T(8,128)(2,1)}, u32[]{:S(2)}, u32[]{:S(2)}) collective-permute-start(bf16[512,1344]{0,1:T(8,128)(2,1)} %get-tuple-element.29), channel_id=1, source_target_pairs={{4,8},{8,4},{5,9},{9,5},{6,10},{10,6},{7,11},{11,7},{20,24},{24,20... | collective-permute-start | bytes 4128776 | tf_op jit(solution)/shard_map/ppermute | solution.py:395
  27.2 110.6 %collective-permute-start.5 = (bf16[1344,512]{1,0:T(8,128)(2,1)}, bf16[1344,512]{1,0:T(8,128)(2,1)}, u32[]{:S(2)}, u32[]{:S(2)}) collective-permute-start(bf16[1344,512]{1,0:T(8,128)(2,1)} %get-tuple-element.32), channel_id=1, source_target_pairs={{4,8},{8,4},{5,9},{9,5},{6,10},{10,6},{7,11},{11,7},{20,24},{24,20... | collective-permute-start | bytes 4128776 | tf_op jit(solution)/shard_map/ppermute | solution.py:377
  36.6 103.1 %collective-permute-start.7 = (bf16[1344,512]{1,0:T(8,128)(2,1)}, bf16[1344,512]{1,0:T(8,128)(2,1)}, u32[]{:S(2)}, u32[]{:S(2)}) collective-permute-start(bf16[1344,512]{1,0:T(8,128)(2,1)} %get-tuple-element.32), channel_id=1, source_target_pairs={{0,8},{12,4},{1,9},{13,5},{2,10},{14,6},{3,11},{15,7},{16,24},{28,... | collective-permute-start | bytes 4128776 | tf_op jit(solution)/shard_map/ppermute | solution.py:378
  43.6 88.5 %collective-permute-start.9 = (bf16[512,1344]{0,1:T(8,128)(2,1)}, bf16[512,1344]{0,1:T(8,128)(2,1)}, u32[]{:S(2)}, u32[]{:S(2)}) collective-permute-start(bf16[512,1344]{0,1:T(8,128)(2,1)} %param.9), channel_id=1, source_target_pairs={{0,4},{12,8},{1,5},{13,9},{2,6},{14,10},{3,7},{15,11},{16,20},{28,... | collective-permute-start | bytes 4128776 | tf_op jit(solution)/shard_map/ppermute | solution.py:374
  73.1 69.7 %collective-permute-start.13 = (bf16[512,1344]{0,1:T(8,128)(2,1)}, bf16[512,1344]{0,1:T(8,128)(2,1)}, u32[]{:S(2)}, u32[]{:S(2)}) collective-permute-start(bf16[512,1344]{0,1:T(8,128)(2,1)} %param.9), channel_id=1, source_target_pairs={{4,8},{8,4},{5,9},{9,5},{6,10},{10,6},{7,11},{11,7},{20,24},{24,20... | collective-permute-start | bytes 4128776 | tf_op jit(solution)/shard_map/ppermute | solution.py:375
  94.8 55.3 %collective-permute-start.4 = (bf16[1344,512]{1,0:T(8,128)(2,1)}, bf16[1344,512]{1,0:T(8,128)(2,1)}, u32[]{:S(2)}, u32[]{:S(2)}) collective-permute-start(bf16[1344,512]{1,0:T(8,128)(2,1)} %collective-permute-done.3), channel_id=1, source_target_pairs={{4,20},{20,4},{8,24},{24,8},{5,21},{21,5},{9,25},{25,9},{6,22},{22... | collective-permute-start | bytes 4128776 | tf_op jit(solution)/shard_map/ppermute | solution.py:140
  137.7 70.6 %collective-permute-start.10 = (bf16[512,1344]{0,1:T(8,128)(2,1)}, bf16[512,1344]{0,1:T(8,128)(2,1)}, u32[]{:S(2)}, u32[]{:S(2)}) collective-permute-start(bf16[512,1344]{0,1:T(8,128)(2,1)} %collective-permute-done.9), channel_id=1, source_target_pairs={{4,5},{5,4},{8,9},{9,8},{6,7},{7,6},{10,11},{11,10},{20,21},{21,20... | collective-permute-start | bytes 4128776 | tf_op jit(solution)/shard_map/ppermute | solution.py:142
  139.7 33.5 %collective-permute-start.6 = (bf16[1344,512]{1,0:T(8,128)(2,1)}, bf16[1344,512]{1,0:T(8,128)(2,1)}, u32[]{:S(2)}, u32[]{:S(2)}) collective-permute-start(bf16[1344,512]{1,0:T(8,128)(2,1)} %collective-permute-done.5), channel_id=1, source_target_pairs={{4,20},{20,4},{8,24},{24,8},{5,21},{21,5},{9,25},{25,9},{6,22},{22... | collective-permute-start | bytes 4128776 | tf_op jit(solution)/shard_map/ppermute | solution.py:140
  142.8 59.8 %collective-permute-start.8 = (bf16[1344,512]{1,0:T(8,128)(2,1)}, bf16[1344,512]{1,0:T(8,128)(2,1)}, u32[]{:S(2)}, u32[]{:S(2)}) collective-permute-start(bf16[1344,512]{1,0:T(8,128)(2,1)} %collective-permute-done.7), channel_id=1, source_target_pairs={{4,20},{20,4},{8,24},{24,8},{5,21},{21,5},{9,25},{25,9},{6,22},{22... | collective-permute-start | bytes 4128776 | tf_op jit(solution)/shard_map/ppermute | solution.py:140
  150.0 82.1 %collective-permute-start.31 = (bf16[512,1344]{0,1:T(8,128)(2,1)}, bf16[512,1344]{0,1:T(8,128)(2,1)S(1)}, u32[]{:S(2)}, u32[]{:S(2)}) collective-permute-start(bf16[512,1344]{0,1:T(8,128)(2,1)} %collective-permute-done.30), channel_id=1, source_target_pairs={{4,20},{20,4},{8,24},{24,8},{0,16},{16,0},{12,28},{28,12},{5,21},{... | collective-permute-start | bytes 4128776 | tf_op jit(solution)/shard_map/ppermute | solution.py:140
  155.2 86.9 %collective-permute-start.11 = (bf16[512,1344]{0,1:T(8,128)(2,1)}, bf16[512,1344]{0,1:T(8,128)(2,1)}, u32[]{:S(2)}, u32[]{:S(2)}) collective-permute-start(bf16[512,1344]{0,1:T(8,128)(2,1)} %collective-permute-done.9), channel_id=1, source_target_pairs={{4,6},{6,4},{8,10},{10,8},{5,7},{7,5},{9,11},{11,9},{20,22},{22,20... | collective-permute-start | bytes 4128776 | tf_op jit(solution)/shard_map/ppermute | solution.py:142
  173.1 72.3 %collective-permute-start.14 = (bf16[512,1344]{0,1:T(8,128)(2,1)}, bf16[512,1344]{0,1:T(8,128)(2,1)}, u32[]{:S(2)}, u32[]{:S(2)}) collective-permute-start(bf16[512,1344]{0,1:T(8,128)(2,1)} %collective-permute-done.13), channel_id=1, source_target_pairs={{4,5},{5,4},{8,9},{9,8},{6,7},{7,6},{10,11},{11,10},{20,21},{21,20... | collective-permute-start | bytes 4128776 | tf_op jit(solution)/shard_map/ppermute | solution.py:142
  202.6 45.2 %collective-permute-start.17 = (bf16[512,1344]{0,1:T(8,128)(2,1)}, bf16[512,1344]{0,1:T(8,128)(2,1)}, u32[]{:S(2)}, u32[]{:S(2)}) collective-permute-start(bf16[512,1344]{0,1:T(8,128)(2,1)} %collective-permute-done.9), channel_id=1, source_target_pairs={{4,8},{8,4},{5,9},{9,5},{6,10},{10,6},{7,11},{11,7},{20,24},{24,20... | collective-permute-start | bytes 4128776 | tf_op jit(solution)/shard_map/ppermute | solution.py:379
  208.4 45.0 %collective-permute-start.15 = (bf16[512,1344]{0,1:T(8,128)(2,1)}, bf16[512,1344]{0,1:T(8,128)(2,1)}, u32[]{:S(2)}, u32[]{:S(2)}) collective-permute-start(bf16[512,1344]{0,1:T(8,128)(2,1)} %collective-permute-done.13), channel_id=1, source_target_pairs={{4,6},{6,4},{8,10},{10,8},{5,7},{7,5},{9,11},{11,9},{20,22},{22,20... | collective-permute-start | bytes 4128776 | tf_op jit(solution)/shard_map/ppermute | solution.py:142
  232.1 32.6 %collective-permute-start.33 = (bf16[512,1344]{0,1:T(8,128)(2,1)}, bf16[512,1344]{0,1:T(8,128)(2,1)}, u32[]{:S(2)}, u32[]{:S(2)}) collective-permute-start(bf16[512,1344]{0,1:T(8,128)(2,1)} %collective-permute-done.32), channel_id=1, source_target_pairs={{4,20},{20,4},{8,24},{24,8},{5,21},{21,5},{9,25},{25,9},{6,22},{22... | collective-permute-start | bytes 4128776 | tf_op jit(solution)/shard_map/ppermute | solution.py:140
  242.1 48.3 %collective-permute-start.34 = (bf16[512,1344]{0,1:T(8,128)(2,1)}, bf16[512,1344]{0,1:T(8,128)(2,1)}, u32[]{:S(2)}, u32[]{:S(2)}) collective-permute-start(bf16[512,1344]{0,1:T(8,128)(2,1)} %collective-permute-done.30), channel_id=1, source_target_pairs={{4,8},{8,4},{5,9},{9,5},{6,10},{10,6},{7,11},{11,7},{20,24},{24,20... | collective-permute-start | bytes 4128776 | tf_op jit(solution)/shard_map/ppermute | solution.py:396
  245.4 47.1 %collective-permute-start.36 = (bf16[512,1344]{0,1:T(8,128)(2,1)}, bf16[512,1344]{0,1:T(8,128)(2,1)}, u32[]{:S(2)}, u32[]{:S(2)}) collective-permute-start(bf16[512,1344]{0,1:T(8,128)(2,1)} %collective-permute-done.32), channel_id=1, source_target_pairs={{4,0},{8,12},{5,1},{9,13},{6,2},{10,14},{7,3},{11,15},{20,16},{24,... | collective-permute-start | bytes 4128776 | tf_op jit(solution)/shard_map/ppermute | solution.py:397
  247.8 47.8 %collective-permute-start.19 = (bf16[512,1344]{0,1:T(8,128)(2,1)}, bf16[512,1344]{0,1:T(8,128)(2,1)}, u32[]{:S(2)}, u32[]{:S(2)}) collective-permute-start(bf16[512,1344]{0,1:T(8,128)(2,1)} %collective-permute-done.17), channel_id=1, source_target_pairs={{4,6},{6,4},{8,10},{10,8},{5,7},{7,5},{9,11},{11,9},{20,22},{22,20... | collective-permute-start | bytes 4128776 | tf_op jit(solution)/shard_map/ppermute | solution.py:142
  253.4 63.6 %collective-permute-start.12 = (bf16[512,1344]{0,1:T(8,128)(2,1)}, bf16[512,1344]{0,1:T(8,128)(2,1)}, u32[]{:S(2)}, u32[]{:S(2)}) collective-permute-start(bf16[512,1344]{0,1:T(8,128)(2,1)} %collective-permute-done.11), channel_id=1, source_target_pairs={{4,5},{5,4},{8,9},{9,8},{6,7},{7,6},{10,11},{11,10},{20,21},{21,20... | collective-permute-start | bytes 4128776 | tf_op jit(solution)/shard_map/ppermute | solution.py:142
  264.7 56.6 %collective-permute-start.16 = (bf16[512,1344]{0,1:T(8,128)(2,1)}, bf16[512,1344]{0,1:T(8,128)(2,1)}, u32[]{:S(2)}, u32[]{:S(2)}) collective-permute-start(bf16[512,1344]{0,1:T(8,128)(2,1)} %collective-permute-done.15), channel_id=1, source_target_pairs={{4,5},{5,4},{8,9},{9,8},{6,7},{7,6},{10,11},{11,10},{20,21},{21,20... | collective-permute-start | bytes 4128776 | tf_op jit(solution)/shard_map/ppermute | solution.py:142
  290.4 70.0 %collective-permute-start.18 = (bf16[512,1344]{0,1:T(8,128)(2,1)}, bf16[512,1344]{0,1:T(8,128)(2,1)}, u32[]{:S(2)}, u32[]{:S(2)}) collective-permute-start(bf16[512,1344]{0,1:T(8,128)(2,1)} %collective-permute-done.17), channel_id=1, source_target_pairs={{4,5},{5,4},{8,9},{9,8},{6,7},{7,6},{10,11},{11,10},{20,21},{21,20... | collective-permute-start | bytes 4128776 | tf_op jit(solution)/shard_map/ppermute | solution.py:142
  292.5 63.6 %collective-permute-start.35 = (bf16[512,1344]{0,1:T(8,128)(2,1)}, bf16[512,1344]{0,1:T(8,128)(2,1)}, u32[]{:S(2)}, u32[]{:S(2)}) collective-permute-start(bf16[512,1344]{0,1:T(8,128)(2,1)} %collective-permute-done.34), channel_id=1, source_target_pairs={{4,20},{20,4},{8,24},{24,8},{5,21},{21,5},{9,25},{25,9},{6,22},{22... | collective-permute-start | bytes 4128776 | tf_op jit(solution)/shard_map/ppermute | solution.py:140
  295.6 67.4 %collective-permute-start.20 = (bf16[512,1344]{0,1:T(8,128)(2,1)}, bf16[512,1344]{0,1:T(8,128)(2,1)}, u32[]{:S(2)}, u32[]{:S(2)}) collective-permute-start(bf16[512,1344]{0,1:T(8,128)(2,1)} %collective-permute-done.19), channel_id=1, source_target_pairs={{4,5},{5,4},{8,9},{9,8},{6,7},{7,6},{10,11},{11,10},{20,21},{21,20... | collective-permute-start | bytes 4128776 | tf_op jit(solution)/shard_map/ppermute | solution.py:142
  317.0 102.4 %collective-permute-start.37 = (bf16[512,1344]{0,1:T(8,128)(2,1)}, bf16[512,1344]{0,1:T(8,128)(2,1)}, u32[]{:S(2)}, u32[]{:S(2)}) collective-permute-start(bf16[512,1344]{0,1:T(8,128)(2,1)} %collective-permute-done.36), channel_id=1, source_target_pairs={{0,16},{16,0},{12,28},{28,12},{1,17},{17,1},{13,29},{29,13},{2,18}... | collective-permute-start | bytes 4128776 | tf_op jit(solution)/shard_map/ppermute | solution.py:140
  321.3 100.7 %collective-permute-start.38 = (bf16[512,1344]{0,1:T(8,128)(2,1)}, bf16[512,1344]{0,1:T(8,128)(2,1)}, u32[]{:S(2)}, u32[]{:S(2)}) collective-permute-start(bf16[512,1344]{0,1:T(8,128)(2,1)} %collective-permute-done.34), channel_id=1, source_target_pairs={{4,0},{8,12},{5,1},{9,13},{6,2},{10,14},{7,3},{11,15},{20,16},{24,... | collective-permute-start | bytes 4128776 | tf_op jit(solution)/shard_map/ppermute | solution.py:398
  390.4 45.4 %collective-permute-start.21 = (bf16[512,512]{1,0:T(8,128)(2,1)}, bf16[512,512]{1,0:T(8,128)(2,1)}, u32[]{:S(2)}, u32[]{:S(2)}) collective-permute-start(bf16[512,512]{1,0:T(8,128)(2,1)} %shard_map.96), channel_id=1, source_target_pairs={{4,0},{8,12},{5,1},{9,13},{6,2},{10,14},{7,3},{11,15},{20,16},{24,... | collective-permute-start | bytes 1572872 | tf_op jit(solution)/shard_map/ppermute | solution.py:457
  402.9 35.5 %collective-permute-start.22 = (bf16[512,512]{1,0:T(8,128)(2,1)}, bf16[512,512]{1,0:T(8,128)(2,1)}, u32[]{:S(2)}, u32[]{:S(2)}) collective-permute-start(bf16[512,512]{1,0:T(8,128)(2,1)} %shard_map.97), channel_id=1, source_target_pairs={{4,8},{8,4},{5,9},{9,5},{6,10},{10,6},{7,11},{11,7},{20,24},{24,20... | collective-permute-start | bytes 1572872 | tf_op jit(solution)/shard_map/ppermute | solution.py:458
  423.8 40.2 %collective-permute-start.39 = (bf16[512,1344]{0,1:T(8,128)(2,1)}, bf16[512,1344]{0,1:T(8,128)(2,1)}, u32[]{:S(2)}, u32[]{:S(2)}) collective-permute-start(bf16[512,1344]{0,1:T(8,128)(2,1)} %collective-permute-done.38), channel_id=1, source_target_pairs={{0,16},{16,0},{12,28},{28,12},{1,17},{17,1},{13,29},{29,13},{2,18}... | collective-permute-start | bytes 4128776 | tf_op jit(solution)/shard_map/ppermute | solution.py:140
  (21 other events, 206.7 us)

commit v2 on v0

--- a/solution.py
+++ b/solution.py
@@ -1,6 +1,10 @@
+import functools
+
 import jax
 import jax.numpy as jnp
 from jax import lax
+from jax.experimental import pallas as pl
+from jax.experimental.pallas import tpu as pltpu
 from jax.sharding import PartitionSpec as P
 
 MODEL_WIDTH = 5376
@@ -9,6 +13,9 @@
 
 
 EPSILON = 1e-06
+MIDDLE = (1, 2)
+ENDS = (0, 3)
+VMEM_BYTES = 60 * 1024 * 1024
 
 
 def shifted(x, axis, by):
@@ -21,12 +28,17 @@
     return values * lax.rsqrt(jnp.mean(values * values, axis=-1, keepdims=True) + EPSILON) * gain
 
 
+def rotary_tables(token_positions, size):
+    half_dim = size // 2
+    inverse = 10000.0 ** (-(jnp.arange(half_dim, dtype=jnp.float32) * 2.0) / size)
+    angles = token_positions[:, None] * inverse[None, :]
+    return jnp.cos(angles), jnp.sin(angles)
+
+
 def apply_rotary(tensor, token_positions):
     half_dim = tensor.shape[-1] // 2
-    inverse = 10000.0 ** (-(jnp.arange(half_dim, dtype=jnp.float32) * 2.0) / tensor.shape[-1])
-    angles = token_positions[:, None] * inverse[None, :]
-    cosine = jnp.cos(angles)[:, None, :]
-    sine_part = jnp.sin(angles)[:, None, :]
+    cosine, sine_part = rotary_tables(token_positions, tensor.shape[-1])
+    cosine, sine_part = cosine[:, None, :], sine_part[:, None, :]
     first_half = tensor[..., :half_dim]
     second_half = tensor[..., half_dim:]
     return jnp.concatenate(
@@ -38,7 +50,7 @@
     )
 
 
-def on_device(
+def general_form(
     stream_in,
     in_gain,
     query_weight,
@@ -121,6 +133,538 @@
     return (stream_in.astype(jnp.float32) + scaled).astype(jnp.bfloat16)
 
 
+def swapped(x, axis, rows):
+    if axis == "groups":
+        count = lax.axis_size("row")
+        pairs = [(count * i + r, count * (1 - i) + r) for r in rows for i in range(2)]
+        return lax.ppermute(x, ("groups", "row"), pairs)
+    pairs = [(2 * r + i, 2 * r + 1 - i) for r in rows for i in range(2)]
+    return lax.ppermute(x, ("row", axis), pairs)
+
+
+def after(x, *earlier):
+    return lax.optimization_barrier((x, *earlier))[0]
+
+
+def settle(*values):
+    return lax.optimization_barrier(values)
+
+
+def whole(shape):
+    return pl.BlockSpec(shape, lambda *_: (0,) * len(shape))
+
+
+ANYWHERE = pl.BlockSpec(memory_space=pl.ANY)
+
+
+def norm_kernel(table, *refs):
+    *pieces, gain, out = refs[-6:]
+    depth = pieces[0].shape[1]
+    squares = sum(
+        jnp.sum(jnp.square(p[0].astype(jnp.float32)), axis=0, keepdims=True) for p in pieces
+    )
+    scale = lax.rsqrt(squares / MODEL_WIDTH + EPSILON)
+    for index, piece in enumerate(pieces):
+        rows = pl.ds(pl.multiple_of(table[index] * depth, depth), depth)
+        out[0, rows, :] = (piece[0].astype(jnp.float32) * scale * gain[index]).astype(jnp.bfloat16)
+
+
+def norm_block(table, pieces, which, gain, index, held):
+    _, depth, tokens = pieces[0].shape
+    lanes = tokens // 2
+    shape = (4, 4 * depth, tokens)
+    before = () if held is None else (held,)
+    return pl.pallas_call(
+        norm_kernel,
+        grid_spec=pltpu.PrefetchScalarGridSpec(
+            num_scalar_prefetch=1,
+            grid=(tokens // lanes,),
+            in_specs=[ANYWHERE] * len(before)
+            + [pl.BlockSpec((1, depth, lanes), lambda t, *_: (which, 0, t))] * 4
+            + [whole((4, depth, 1))],
+            out_specs=pl.BlockSpec((1, 4 * depth, lanes), lambda t, *_: (index, 0, t)),
+        ),
+        out_shape=jax.ShapeDtypeStruct(shape, jnp.bfloat16),
+        input_output_aliases={1: 0} if before else {},
+        compiler_params=pltpu.CompilerParams(vmem_limit_bytes=VMEM_BYTES),
+        cost_estimate=pl.CostEstimate(
+            flops=40 * depth * tokens, bytes_accessed=16 * depth * tokens, transcendentals=0
+        ),
+    )(table, *before, *pieces, gain)
+
+
+def order_pieces(table, pieces, ordered):
+    base = 0
+    for index, piece in enumerate(pieces):
+        depth, width = piece.shape
+        rows = pl.ds(pl.multiple_of(table[2 * index], 16), depth)
+        columns = pl.ds(pl.multiple_of(table[2 * index + 1], width), width)
+        ordered[rows, columns] = piece[...]
+
+
+def project_early_kernel(count, table, normed, *refs):
+    pieces, out, ordered = refs[:count], refs[-2], refs[-1]
+
+    @pl.when(pl.program_id(0) == 0)
+    def _():
+        order_pieces(table, pieces, ordered)
+
+    out[0] = lax.dot_general(
+        ordered[...], normed[0], (((0,), (0,)), ((), ())), preferred_element_type=jnp.float32
+    )
+
+
+def project_early(table, normed, pieces, first, blocks, held):
+    _, features, tokens = normed.shape
+    width = 2 * pieces[0].shape[1]
+    before = () if held is None else (held,)
+    return pl.pallas_call(
+        functools.partial(project_early_kernel, len(pieces)),
+        grid_spec=pltpu.PrefetchScalarGridSpec(
+            num_scalar_prefetch=1,
+            grid=(blocks,),
+            in_specs=[pl.BlockSpec((1, features // 2, tokens), lambda i, t: (first + i, 0, 0))]
+            + [whole(p.shape) for p in pieces]
+            + [ANYWHERE] * len(before),
+            out_specs=pl.BlockSpec((1, width, tokens), lambda i, t: (first + i, 0, 0)),
+            scratch_shapes=[pltpu.VMEM((features // 2, width), jnp.bfloat16)],
+        ),
+        out_shape=jax.ShapeDtypeStruct((4, width, tokens), jnp.float32),
+        input_output_aliases={2 + len(pieces): 0} if before else {},
+        compiler_params=pltpu.CompilerParams(vmem_limit_bytes=VMEM_BYTES),
+        cost_estimate=pl.CostEstimate(
+            flops=2 * blocks * tokens * features // 2 * width,
+            bytes_accessed=blocks * features * tokens + features * width + 4 * blocks * width * tokens,
+            transcendentals=0,
+        ),
+    )(table, normed, *pieces, *before)
+
+
+def project_late_kernel(count, table, normed, *refs):
+    pieces, refs = refs[:count], refs[count:]
+    early, q_gain, k_gain, cosine, sine, q_out, k_out, v_out, total, ordered = refs
+
+    @pl.when(pl.program_id(0) == 0)
+    def _():
+        order_pieces(table, pieces, ordered)
+
+    total[...] = early[0] + lax.dot_general(
+        ordered[...], normed[0], (((0,), (0,)), ((), ())), preferred_element_type=jnp.float32
+    )
+    head = q_gain.shape[0]
+    half = head // 2
+    width = q_out.shape[1]
+    cos, sin = cosine[...], sine[...]
+
+    def rotated(start, head_gain):
+        values = total[start : start + head, :]
+        values = (
+            values
+            * lax.rsqrt(jnp.mean(values * values, axis=0, keepdims=True) + EPSILON)
+            * head_gain[...]
+        )
+        first, second = values[:half], values[half:]
+        return jnp.concatenate(
+            [first * cos - second * sin, second * cos + first * sin], axis=0
+        ).astype(jnp.bfloat16)
+
+    for start in range(0, width, head):
+        q_out[0, start : start + head, :] = rotated(start, q_gain)
+    for start in range(0, width // 2, head):
+        k_out[:, start : start + head] = rotated(width + start, k_gain).T
+    v_out[...] = total[width + width // 2 :, :].astype(jnp.bfloat16)
+
+
+def project_late(table, normed, pieces, early, extras):
+    blocks, features, tokens = normed.shape
+    width = early.shape[1] // 2
+    head = extras[0].shape[0]
+    half = head // 2
+    count = len(pieces)
+    turn = pl.BlockSpec((half, tokens), lambda i, t: (0, t[2 * count + i]))
+    return pl.pallas_call(
+        functools.partial(project_late_kernel, count),
+        grid_spec=pltpu.PrefetchScalarGridSpec(
+            num_scalar_prefetch=1,
+            grid=(blocks,),
+            in_specs=[pl.BlockSpec((1, features // 2, tokens), lambda i, t: (i, 1, 0))]
+            + [whole(p.shape) for p in pieces]
+            + [
+                pl.BlockSpec((1, 2 * width, tokens), lambda i, t: (i, 0, 0)),
+                whole((head, 1)),
+                whole((head, 1)),
+                turn,
+                turn,
+            ],
+            out_specs=[
+                pl.BlockSpec((1, width, tokens), lambda i, t: (i, 0, 0)),
+                pl.BlockSpec((tokens, width // 2), lambda i, t: (t[2 * count + i], 0)),
+                pl.BlockSpec((width // 2, tokens), lambda i, t: (0, t[2 * count + i])),
+            ],
+            scratch_shapes=[
+                pltpu.VMEM((2 * width, tokens), jnp.float32),
+                pltpu.VMEM((features // 2, 2 * width), jnp.bfloat16),
+            ],
+        ),
+        out_shape=[
+            jax.ShapeDtypeStruct((blocks, width, tokens), jnp.bfloat16),
+            jax.ShapeDtypeStruct((blocks * tokens, width // 2), jnp.bfloat16),
+            jax.ShapeDtypeStruct((width // 2, blocks * tokens), jnp.bfloat16),
+        ],
+        compiler_params=pltpu.CompilerParams(vmem_limit_bytes=VMEM_BYTES),
+        cost_estimate=pl.CostEstimate(
+            flops=2 * blocks * tokens * features * width,
+            bytes_accessed=blocks * features * tokens + 2 * features * width + 8 * blocks * width * tokens,
+            transcendentals=0,
+        ),
+    )(table, normed, *pieces, early, *extras)
+
+
+def attend_kernel(band, scale, table, q_ref, keys, values, *refs):
+    out, mask = refs[-2:]
+    head = 128
+    tile = out.shape[1]
+    first = table[0] * (2 * tile) + pl.program_id(0) * tile
+    start = pl.multiple_of(jnp.clip(first + tile - band, 0, keys.shape[0] - band), tile)
+    places = lax.broadcasted_iota(jnp.int32, (band, tile), 1)
+    distance = (first - start) + places - lax.broadcasted_iota(jnp.int32, (band, tile), 0)
+    hidden = jnp.where((distance >= 0) & (distance < WINDOW_LENGTH), 0.0, -1e30)
+    mask[:, :tile] = hidden
+    mask[:, tile:] = hidden
+    pairs = keys.shape[1] // head
+    factor = scale * 1.4426950408889634
+    chunks = [slice(a, min(a + tile, band)) for a in range(0, band, tile)]
+
+    def pair_of(ref, index):
+        return [slice((2 * index + i) * head, (2 * index + i + 1) * head) for i in range(2)]
+
+    def query(index):
+        return jnp.concatenate([q_ref[0, rows, :] for rows in pair_of(q_ref, index)], axis=1)
+
+    def within(chunk):
+        return pl.ds(pl.multiple_of(start + chunk.start, tile), chunk.stop - chunk.start)
+
+    def score(index, chunk, queries):
+        columns = slice(index * head, (index + 1) * head)
+        return mask[chunk, :] + jnp.dot(
+            keys[within(chunk), columns], queries, preferred_element_type=jnp.float32
+        )
+
+    queries = query(0)
+    scores = [score(0, chunk, queries) for chunk in chunks]
+    for index in range(pairs):
+        top = functools.reduce(
+            jnp.maximum, [jnp.max(part, axis=0, keepdims=True) for part in scores]
+        )
+        queries = query(index + 1) if index + 1 < pairs else None
+        exponents, upcoming, total = [], [], 0.0
+        for chunk, part in zip(chunks, scores):
+            exponent = jnp.exp2((part - top) * factor)
+            exponents.append(exponent)
+            total = total + jnp.sum(exponent, axis=0, keepdims=True)
+            if queries is not None:
+                upcoming.append(score(index + 1, chunk, queries))
+        inverse = 1.0 / total
+        result = 0.0
+        rows = slice(index * head, (index + 1) * head)
+        for chunk, exponent in zip(chunks, exponents):
+            result = result + jnp.dot(
+                values[rows, within(chunk)],
+                (exponent * inverse).astype(jnp.bfloat16),
+                preferred_element_type=jnp.float32,
+            )
+        for i, here in enumerate(pair_of(out, index)):
+            out[here, :] = result[:, i * tile : (i + 1) * tile].astype(jnp.bfloat16)
+        scores = upcoming
+
+
+def attend(block, index, queries, keys, values, earlier):
+    _, width, tokens = queries.shape
+    tile = tokens // 2
+    band = min(WINDOW_LENGTH + tile, keys.shape[0])
+    return pl.pallas_call(
+        functools.partial(attend_kernel, band, float(MODEL_WIDTH // QUERY_HEAD_COUNT) ** (-0.5)),
+        grid_spec=pltpu.PrefetchScalarGridSpec(
+            num_scalar_prefetch=1,
+            grid=(2,),
+            in_specs=[
+                pl.BlockSpec((1, width, tile), lambda t, *_: (index, 0, t)),
+                whole(keys.shape),
+                whole(values.shape),
+            ]
+            + [ANYWHERE] * len(earlier),
+            out_specs=pl.BlockSpec((width, tile), lambda t, *_: (0, t)),
+            scratch_shapes=[pltpu.VMEM((band, 2 * tile), jnp.float32)],
+        ),
+        out_shape=jax.ShapeDtypeStruct((width, tokens), jnp.bfloat16),
+        compiler_params=pltpu.CompilerParams(vmem_limit_bytes=VMEM_BYTES),
+        cost_estimate=pl.CostEstimate(
+            flops=4 * tokens * band * width,
+            bytes_accessed=4 * tokens * width + 4 * keys.shape[0] * keys.shape[1],
+            transcendentals=tokens * band * (width // 128),
+        ),
+    )(block[None], queries, keys, values, *earlier)
+
+
+def output_kernel(count, full, table, *refs):
+    parts, pieces, (out, squares, held, row_held) = refs[:8], refs[8 : 8 + count], refs[8 + count :]
+    depth = parts[0].shape[0]
+    step = pl.program_id(0)
+
+    @pl.when(step == 0)
+    def _():
+        for index, part in enumerate(parts):
+            held[index * depth : (index + 1) * depth, :] = part[...]
+        squares[...] = jnp.zeros_like(squares)
+
+    for index, piece in enumerate(pieces):
+
+        @pl.when(table[index] < full)
+        def _(index=index, piece=piece):
+            there = pl.ds(pl.multiple_of(table[index], 128), piece.shape[1])
+            row_held[:, there] = piece[...]
+
+    product = jnp.dot(row_held[...], held[...], preferred_element_type=jnp.float32)
+    out[...] = product
+    squares[...] += jnp.sum(jnp.square(product), axis=0, keepdims=True)
+
+
+def output_product(table, parts, pieces):
+    depth, tokens = parts[0].shape
+    width = pieces[0][0].shape[0]
+    full = 8 * depth
+    tile = width // 4
+
+    def rows(index, column, columns):
+        return pl.BlockSpec(
+            (tile, columns), lambda t, table: (jnp.where(table[index] < full, t, 0), column)
+        )
+
+    return pl.pallas_call(
+        functools.partial(output_kernel, len(pieces), full),
+        grid_spec=pltpu.PrefetchScalarGridSpec(
+            num_scalar_prefetch=1,
+            grid=(width // tile,),
+            in_specs=[whole((depth, tokens))] * 8
+            + [rows(index, column, columns) for index, (_, column, columns) in enumerate(pieces)],
+            out_specs=[pl.BlockSpec((tile, tokens), lambda t, *_: (t, 0)), whole((1, tokens))],
+            scratch_shapes=[
+                pltpu.VMEM((full, tokens), jnp.bfloat16),
+                pltpu.VMEM((tile, full), jnp.bfloat16),
+            ],
+        ),
+        out_shape=[
+            jax.ShapeDtypeStruct((width, tokens), jnp.float32),
+            jax.ShapeDtypeStruct((1, tokens), jnp.float32),
+        ],
+        compiler_params=pltpu.CompilerParams(vmem_limit_bytes=VMEM_BYTES),
+        cost_estimate=pl.CostEstimate(
+            flops=2 * tokens * full * width,
+            bytes_accessed=2 * full * (tokens + width) + 4 * tokens * width,
+            transcendentals=0,
+        ),
+    )(table, *parts, *(piece for piece, _, _ in pieces))
+
+
+def middle_form(
+    stream_in,
+    in_gain,
+    query_weight,
+    key_matrix,
+    value_matrix,
+    query_gain,
+    key_norm_gain,
+    output_weight,
+    post_gain,
+):
+    stream = stream_in.T
+    features, tokens = stream.shape
+    head = query_gain.shape[0]
+    row = lax.axis_index("row")
+    group = lax.axis_index("groups")
+    place = lax.axis_index("col") * 2 + lax.axis_index("sub")
+    upper = (row >= 2).astype(jnp.int32)
+    in_middle = (row == 1) | (row == 2)
+    near_block, cross_block, far_block = 3 * upper, 3 - row, 3 - 3 * upper
+    blocks = (row, near_block, cross_block, far_block)
+    slot = lambda block: jnp.bitwise_xor(place, block)
+    ints = lambda *values: jnp.stack([jnp.asarray(v, jnp.int32) for v in values])
+    everywhere = MIDDLE + ENDS
+    inward = [(0, 1), (3, 2)]
+    across = [(1, 2), (2, 1)]
+    outward = [(1, 0), (2, 3)]
+
+    half = query_weight.shape[1] // 2
+    quarter = key_matrix.shape[1] // 2
+
+    def side(which):
+        queries = lax.dynamic_slice_in_dim(query_weight, which * half, half, axis=1)
+        keys = lax.dynamic_slice_in_dim(key_matrix, which * quarter, quarter, axis=1)
+        values = lax.dynamic_slice_in_dim(value_matrix, which * quarter, quarter, axis=1)
+        return queries, jnp.concatenate([keys, values], axis=1)
+
+    own_queries, own_pairs = side(upper)
+    own_side = jnp.where(group == 0, own_queries, own_pairs)
+    other_side = jnp.where(group == 0, *side(1 - upper))
+    turned = output_weight.T
+    depth = turned.shape[1] // 2
+    mine = lax.dynamic_slice_in_dim(turned, group * depth, depth, axis=1)
+    theirs = lax.dynamic_slice_in_dim(turned, (1 - group) * depth, depth, axis=1)
+
+    gain_rows = in_gain.reshape(4, features)
+    gain = jnp.concatenate(
+        [lax.dynamic_slice_in_dim(gain_rows, slot(j), 1, axis=0) for j in range(4)], axis=0
+    )[:, :, None]
+    arrival = lambda block: jnp.where(
+        block == row, 0, jnp.where(block == near_block, 1, jnp.where(block == far_block, 2, 3))
+    )
+    order = ints(*(arrival(slot(j)) for j in range(4)))
+
+    x_cross = lax.ppermute(stream, "row", across)
+    x_near = lax.ppermute(stream, "row", inward)
+    own_col = swapped(stream, "col", MIDDLE)
+    own_sub = swapped(stream, "sub", MIDDLE)
+    x_cross, x_near, own_col, own_sub, own_side, other_side, mine = settle(
+        x_cross, x_near, own_col, own_sub, own_side, other_side, mine
+    )
+
+    x_far = lax.ppermute(x_near, "row", across)
+    w_near = lax.ppermute(own_side, "row", inward)
+    x_pair = jnp.stack([x_near, x_cross])
+    pair_col = swapped(x_pair, "col", MIDDLE)
+    own_both = swapped(own_col, "sub", MIDDLE)
+    pair_sub = swapped(x_pair, "sub", MIDDLE)
+    own_pieces = (stream[None], own_sub[None], own_col[None], own_both[None])
+    normed = norm_block(order, own_pieces, 0, gain, 0, None)
+    x_far, w_near, other_side, mine, normed = settle(x_far, w_near, other_side, mine, normed)
+    w_cross = lax.ppermute(other_side, "row", across)
+    o_in = lax.ppermute(mine, "row", inward)
+    w_near_y = swapped(w_near, "groups", MIDDLE)
+    far_sub = swapped(x_far, "sub", MIDDLE)
+    w_cross, o_in, w_near_y, pair_col, x_far, pair_sub, normed, other_side, turned, mine, theirs = settle(
+        w_cross, o_in, w_near_y, pair_col, x_far, pair_sub, normed, other_side, turned, mine, theirs
+    )
+
+    w_far = lax.ppermute(other_side, "row", [(0, 2), (3, 1)])
+    far_col = swapped(x_far, "col", MIDDLE)
+    w_cross_y = swapped(w_cross, "groups", MIDDLE)
+    pair_both = swapped(pair_col, "sub", MIDDLE)
+    o_out = lax.ppermute(turned, "row", outward)
+    pair_pieces = (x_pair, pair_sub, pair_col, pair_both)
+    normed = norm_block(order, pair_pieces, 0, gain, 1, normed)
+    normed = norm_block(order, pair_pieces, 1, gain, 2, normed)
+    early_table = ints(0, 0, 0, half, features, group * half, features, (1 - group) * half)
+    early_pieces = (own_queries, own_pairs, w_near, w_near_y)
+    total = project_early(early_table, normed, early_pieces, 0, 3, None)
+    w_far, far_col, w_cross_y, total, mine, o_in, theirs = settle(
+        w_far, far_col, w_cross_y, total, mine, o_in, theirs
+    )
+
+    cut = depth // 2
+    w_far_y = swapped(w_far, "groups", MIDDLE)
+    far_both = swapped(far_col, "sub", MIDDLE)
+    o_cross = lax.ppermute(mine, "row", across)
+    o_far_1 = lax.ppermute(o_in[:, :cut], "row", across)
+    o_far_2 = lax.ppermute(o_in[:, cut:], "row", across)
+    o_in_rest = lax.ppermute(theirs, "row", inward)
+    far_pieces = (x_far[None], far_sub[None], far_col[None], far_both[None])
+    normed = norm_block(order, far_pieces, 0, gain, 3, normed)
+    total = project_early(early_table, normed, early_pieces, 3, 1, total)
+    positions = jnp.arange(4 * tokens, dtype=jnp.int32).astype(jnp.float32)
+    cosine, sine = rotary_tables(positions, head)
+    here, there = group * half, (1 - group) * half
+    queries, keys, values = project_late(
+        ints(0, here, 0, there, features, here, features, there, *blocks),
+        normed,
+        (w_far, w_far_y, w_cross, w_cross_y),
+        total,
+        (query_gain[:, None], key_norm_gain[:, None], cosine.T, sine.T),
+    )
+
+    def attended(index, *earlier):
+        return attend(blocks[index].astype(jnp.int32), index, queries, keys, values, earlier)
+
+    queries, o_cross = settle(queries, o_cross)
+    o_cross_y = swapped(o_cross, "groups", MIDDLE)
+    o_end_cross = lax.ppermute(o_cross, "row", outward)
+    cross_part = attended(2)
+    to_cross = lax.ppermute(cross_part, "row", across)
+    far_part = attended(3, cross_part)
+    to_far = lax.ppermute(far_part, "row", [(1, 3), (2, 0)])
+    near_part = attended(1, far_part, o_far_1)
+    to_near = lax.ppermute(near_part, "row", outward)
+    o_far_1_y = swapped(after(o_far_1, near_part), "groups", MIDDLE)
+    o_end_far_1 = lax.ppermute(after(o_far_1, near_part), "row", outward)
+    own_part = attended(0, near_part, o_far_2, o_cross_y, to_cross)
+    o_far_2_y = swapped(after(o_far_2, own_part), "groups", MIDDLE)
+    o_end_far_2 = lax.ppermute(after(o_far_2, own_part), "row", outward)
+    this_side = jnp.where(in_middle, own_part, to_near)
+    this_across = swapped(this_side, "col", everywhere)
+    that_side = jnp.where(in_middle, to_cross, to_far)
+    that_across = swapped(that_side, "col", everywhere)
+    o_end_cross_y = swapped(after(o_end_cross, own_part), "groups", ENDS)
+    o_end_far_1_y = swapped(after(o_end_far_1, this_side), "groups", ENDS)
+    o_end_far_2_y = swapped(o_end_far_2, "groups", ENDS)
+    o_far, o_far_y = (o_far_1, o_far_2), (o_far_1_y, o_far_2_y)
+    o_end_far, o_end_far_y = (o_end_far_1, o_end_far_2), (o_end_far_1_y, o_end_far_2_y)
+
+    pair_block = jnp.bitwise_xor(row, 1)
+    out_pieces, out_table = [], []
+
+    def put(piece, column, columns, block, which, offset, here):
+        spot = (2 * slot(block) + jnp.bitwise_xor(which, upper)) * depth + offset
+        out_pieces.append((piece, column, columns))
+        out_table.append(spot if here is None else jnp.where(here, spot, 8 * depth))
+
+    for part in range(2):
+        put(turned, part, depth, row, part, 0, None)
+        put(o_out, part, depth, pair_block, part, 0, ~in_middle)
+    put(o_in, 0, depth, pair_block, group, 0, in_middle)
+    put(o_in_rest, 0, depth, pair_block, 1 - group, 0, in_middle)
+    put(o_cross, 0, depth, 3 - row, group, 0, in_middle)
+    put(o_cross_y, 0, depth, 3 - row, 1 - group, 0, in_middle)
+    put(o_end_cross, 0, depth, 3 - pair_block, group, 0, ~in_middle)
+    put(o_end_cross_y, 0, depth, 3 - pair_block, 1 - group, 0, ~in_middle)
+    for index, (piece, piece_y, end_piece, end_piece_y) in enumerate(
+        zip(o_far, o_far_y, o_end_far, o_end_far_y)
+    ):
+        put(piece, 0, cut, 3 - pair_block, group, index * cut, in_middle)
+        put(piece_y, 0, cut, 3 - pair_block, 1 - group, index * cut, in_middle)
+        put(end_piece, 0, cut, 3 - row, group, index * cut, ~in_middle)
+        put(end_piece_y, 0, cut, 3 - row, 1 - group, index * cut, ~in_middle)
+
+    parts = (
+        this_side,
+        that_side,
+        swapped(this_side, "sub", everywhere),
+        swapped(that_side, "sub", everywhere),
+        this_across,
+        that_across,
+        swapped(this_across, "sub", everywhere),
+        swapped(that_across, "sub", everywhere),
+    )
+    branch, squares = output_product(ints(*out_table), parts, out_pieces)
+    squares = squares + swapped(squares, "sub", everywhere)
+    squares = squares + swapped(squares, "col", everywhere)
+    scaled = branch * lax.rsqrt(squares / MODEL_WIDTH + EPSILON) * post_gain[:, None]
+    return (stream.astype(jnp.float32) + scaled).astype(jnp.bfloat16).T
+
+
+def on_device(*args):
+    stream_in, _, query_weight, key_matrix, value_matrix, query_gain, *_ = args
+    sizes = tuple(lax.axis_size(name) for name in ("groups", "row", "col", "sub"))
+    tokens, head = stream_in.shape[0], query_gain.shape[0]
+    fits = (
+        sizes == (2, 4, 2, 2)
+        and head == 128
+        and tokens % 256 == 0
+        and key_matrix.shape[1] % (2 * head) == 0
+        and query_weight.shape[1] == 2 * key_matrix.shape[1]
+        and value_matrix.shape[1] == key_matrix.shape[1]
+    )
+    return middle_form(*args) if fits else general_form(*args)
+
+
 def solution(mesh):
     placed = (
         P(("groups", "row"), ("col", "sub")),

time: 760 us -> 374 us (0.49)
  waiting for transfers between devices: 614 us -> 129 us
  Pallas kernels: 0 us -> 116 us
  matrix products: 77.7 us -> 0 us
  starting transfers between devices: 26.3 us -> 95 us
  between operations: 13.7 us -> 0.63 us
  local copies, waits for them, and re-layouts: 6.05 us -> 17.9 us
    all_gather x6 -> x0, waiting for transfers between devices: 593 us -> none  [the longest x1 160 us: on_device(): lax.all_gather(query_weight, 'row', axis=0, tiled=True)]
    pallas_call x0 -> x12, Pallas kernels: none -> 116 us  [the longest x4 28.2 us: norm_block(): pl.pallas_call(norm_kernel, grid_spec=pltpu.PrefetchScalarGridSpec(num_sc...]
    ppermute x4 -> x44, waiting for transfers between devices: 18.4 us -> 129 us  [the longest x9 29.4 us: swapped(): return lax.ppermute(x, ('groups', 'row'), pairs)]
    ppermute x4 -> x44, starting transfers between devices: 26.2 us -> 95 us  [the longest x17 21 us: swapped(): return lax.ppermute(x, ('row', axis), pairs)]
    dot_general x6 -> x0, matrix products: 67.2 us -> none  [the longest x3 26.7 us: add_panel(): return jnp.dot(normed, panel_piece, preferred_element_type=jnp.float32)]
    sub x1 -> x0, matrix products: 10.5 us -> none  [on_device(): exponent = jnp.exp(scores - row_max)]
  transfers between devices with their start and end apart: 10 -> 44, of which waited for: 7 -> 12; matrix products, arithmetic and copies ran while one was open for 11% -> 6% of each run, Pallas kernels for 0% -> 27%
where the time goes in v2:
time: 374 us; the launch traced here: 373 us
  waiting for transfers between devices  129 us (34%)
  Pallas kernels  116 us (31%)
  starting transfers between devices  95 us (25%)
  local copies, waits for them, and re-layouts  17.9 us (5%)
  other arithmetic  14.9 us (4%)
    ppermute x9, waiting for transfers between devices, swapped(): return lax.ppermute(x, ('groups', 'row'), pairs)  29.4 us
    pallas_call x4, Pallas kernels, norm_block(): pl.pallas_call(norm_kernel, grid_spec=pltpu.PrefetchScalarGridSpec(num_sc...  28.2 us
    pallas_call x4, Pallas kernels, attend(): pl.pallas_call(functools.partial(attend_kernel, band, float(MODEL_WIDTH /...  27.5 us
    ppermute x1, waiting for transfers between devices, middle_form(): o_in = lax.ppermute(mine, 'row', inward)  26.2 us
    pallas_call x2, Pallas kernels, project_early(): pl.pallas_call(functools.partial(project_early_kernel, len(pieces)), grid...  24.5 us
    ppermute x17, starting transfers between devices, swapped(): return lax.ppermute(x, ('row', axis), pairs)  21 us
    pallas_call x1, Pallas kernels, project_late(): pl.pallas_call(functools.partial(project_late_kernel, count), grid_spec=p...  21 us
    ppermute x1, waiting for transfers between devices, middle_form(): x_near = lax.ppermute(stream, 'row', inward)  17.2 us
  transfers between devices with their start and end apart: 44, of which 12 were waited for; matrix products, arithmetic and copies ran while one was open for 6% of the time, Pallas kernels for 27%

profile of v2, /device:TPU:0, one launch (start us, length us, event | category | flops | bytes accessed | tf_op | source)
XLA Modules:
  0.0 373.0 jit_solution(13652027713311150752)
XLA Ops:
  0.7 8.8 %collective-permute-start.1 = (bf16[1344,512]{1,0:T(8,128)(2,1)}, bf16[1344,512]{1,0:T(8,128)(2,1)}, u32[]{:S(2)}, u32[]{:S(2)}) collective-permute-start(bf16[1344,512]{1,0:T(8,128)(2,1)} %bitcast.57), channel_id=1, source_target_pairs={{0,4},{12,8},{1,5},{13,9},{2,6},{14,10},{3,7},{15,11},{16,20},{28,... | collective-permute-start | bytes 4128776 | tf_op jit(solution)/shard_map/ppermute | solution.py:524
  12.1 3.6 dynamic-slice_bitcast_fusion
  17.5 3.2 broadcast_select_fusion
  20.7 17.2 %collective-permute-done.1 = bf16[1344,512]{1,0:T(8,128)(2,1)} collective-permute-done((bf16[1344,512]{1,0:T(8,128)(2,1)}, bf16[1344,512]{1,0:T(8,128)(2,1)}, u32[]{:S(2)}, u32[]{:S(2)}) %collective-permute-start.1) | collective-permute-done | bytes 1376288 | tf_op jit(solution)/shard_map/ppermute | solution.py:524
  39.6 7.4 %collective-permute-start.5 = (bf16[1344,512]{1,0:T(8,128)(2,1)}, bf16[1344,512]{1,0:T(8,128)(2,1)}, u32[]{:S(2)}, u32[]{:S(2)}) collective-permute-start(bf16[1344,512]{1,0:T(8,128)(2,1)} %get-tuple-element.47), channel_id=1, source_target_pairs={{0,4},{12,8},{1,5},{13,9},{2,6},{14,10},{3,7},{15,11},{16,20},{28,... | collective-permute-start | bytes 4128776 | tf_op jit(solution)/shard_map/ppermute | solution.py:532
  58.7 7.1 %shard_map.91.refs_0_ = bf16[4,5376,512]{2,1,0:T(8,128)(2,1)} custom-call(s32[4]{0:T(128)} %pad_add_fusion.table, bf16[1,1344,512]{2,1,0:T(8,128)(2,1)} %bitcast.60, bf16[1,1344,512]{2,1,0:T(8,128)(2,1)} %bitcast.61, bf16[1,1344,512]{2,1,0:T(8,128)(2,1)} %bitcast.32.refs_2_, bf16[1,1344,512]{2,1,0:T(8,128)(2,1)} %bitcast.33.refs_3_, ...), custom_call_target="tpu_custom_call" | custom-call | flops 27525120 | bytes 11010048 | tf_op jit(solution)/shard_map/pallas_call | solution.py:177
  65.7 8.5 %collective-permute-done.5.refs_2_ = bf16[1344,512]{1,0:T(8,128)(2,1)} collective-permute-done((bf16[1344,512]{1,0:T(8,128)(2,1)}, bf16[1344,512]{1,0:T(8,128)(2,1)}, u32[]{:S(2)}, u32[]{:S(2)}) %collective-permute-start.5) | collective-permute-done | bytes 1376288 | tf_op jit(solution)/shard_map/ppermute | solution.py:532
  76.0 6.2 %collective-permute-start.8 = (bf16[1344,512]{1,0:T(8,128)(2,1)}, bf16[1344,512]{1,0:T(8,128)(2,1)S(1)}, u32[]{:S(2)}, u32[]{:S(2)}) collective-permute-start(bf16[1344,512]{1,0:T(8,128)(2,1)} %get-tuple-element.73), channel_id=1, source_target_pairs={{0,4},{12,8},{1,5},{13,9},{2,6},{14,10},{3,7},{15,11},{16,20},{28,... | collective-permute-start | bytes 4128776 | tf_op jit(solution)/shard_map/ppermute | solution.py:541
  82.9 26.2 %collective-permute-done.8.refs_12_ = bf16[1344,512]{1,0:T(8,128)(2,1)S(1)} collective-permute-done((bf16[1344,512]{1,0:T(8,128)(2,1)}, bf16[1344,512]{1,0:T(8,128)(2,1)S(1)}, u32[]{:S(2)}, u32[]{:S(2)}) %collective-permute-start.8) | collective-permute-done | bytes 1376288 | tf_op jit(solution)/shard_map/ppermute | solution.py:541
  111.5 7.8 %collective-permute-start.14 = (bf16[1344,512]{1,0:T(8,128)(2,1)}, bf16[1344,512]{1,0:T(8,128)(2,1)}, u32[]{:S(2)}, u32[]{:S(2)}) collective-permute-start(bf16[1344,512]{1,0:T(8,128)(2,1)} %get-tuple-element.62), channel_id=1, source_target_pairs={{0,8},{12,4},{1,9},{13,5},{2,10},{14,6},{3,11},{15,7},{16,24},{28,... | collective-permute-start | bytes 4128776 | tf_op jit(solution)/shard_map/ppermute | solution.py:548
  126.8 7.1 %shard_map.92.refs_0_ = bf16[4,5376,512]{2,1,0:T(8,128)(2,1)} custom-call(s32[4]{0:T(128)} %pad_add_fusion.table, bf16[4,5376,512]{2,1,0:T(8,128)(2,1)} %shard_map.91.refs_0_, bf16[2,1344,512]{2,1,0:T(8,128)(2,1)} %copy-done.1, bf16[2,1344,512]{2,1,0:T(8,128)(2,1)} %collective-permute-done.11.refs_2_, ...), custom_call_target="tpu_custom_call", output_to_operand_aliasing={{}: (1, {})} | custom-call | flops 27525120 | bytes 11010048 | tf_op jit(solution)/shard_map/pallas_call | solution.py:177
  133.9 7.0 %shard_map.93.normed.refs_0_ = bf16[4,5376,512]{2,1,0:T(8,128)(2,1)} custom-call(s32[4]{0:T(128)} %pad_add_fusion.table, bf16[4,5376,512]{2,1,0:T(8,128)(2,1)} %shard_map.92.refs_0_, bf16[2,1344,512]{2,1,0:T(8,128)(2,1)} %copy-done.1, bf16[2,1344,512]{2,1,0:T(8,128)(2,1)} %collective-permute-done.11.refs_2_, ...), custom_call_target="tpu_custom_call", output_to_operand_aliasing={{}: (1, {})} | custom-call | flops 27525120 | bytes 11010048 | tf_op jit(solution)/shard_map/pallas_call | solution.py:177
  140.9 15.6 %shard_map.94.refs_4_ = f32[4,1024,512]{2,1,0:T(8,128)} custom-call(s32[8]{0:T(128)} %stack.140.table, bf16[4,5376,512]{2,1,0:T(8,128)(2,1)} %shard_map.93.normed.refs_0_, bf16[1344,512]{1,0:T(8,128)(2,1)} %get-tuple-element.88.refs_0_, bf16[1344,512]{1,0:T(8,128)(2,1)} %get-tuple-element.92.refs_1_, bf16[1344,512]{1,0:T(8,128)(2,1)} %collective-permute-done.5.refs_2_, ...), custom_call_target="tpu_custom_call" | custom-call | flops 8455716864 | bytes 20054016 | tf_op jit(solution)/shard_map/pallas_call | solution.py:221
  163.6 2.8 multiply_sine_fusion
  168.2 2.5 fusion.1
  171.4 12.4 %collective-permute-start.33 = (bf16[1344,512]{1,0:T(8,128)(2,1)}, bf16[1344,512]{1,0:T(8,128)(2,1)}, u32[]{:S(2)}, u32[]{:S(2)}) collective-permute-start(bf16[1344,512]{1,0:T(8,128)(2,1)} %get-tuple-element.80), channel_id=1, source_target_pairs={{0,4},{12,8},{1,5},{13,9},{2,6},{14,10},{3,7},{15,11},{16,20},{28,... | collective-permute-start | bytes 4128776 | tf_op jit(solution)/shard_map/ppermute | solution.py:569
  183.8 7.0 %shard_map.95.normed = bf16[4,5376,512]{2,1,0:T(8,128)(2,1)} custom-call(s32[4]{0:T(128)} %pad_add_fusion.table, bf16[4,5376,512]{2,1,0:T(8,128)(2,1)} %shard_map.93.normed.refs_0_, bf16[1,1344,512]{2,1,0:T(8,128)(2,1)} %bitcast.39.refs_1_, bf16[1,1344,512]{2,1,0:T(8,128)(2,1)} %bitcast.40.refs_2_, ...), custom_call_target="tpu_custom_call", output_to_operand_aliasing={{}: (1, {})} | custom-call | flops 27525120 | bytes 11010048 | tf_op jit(solution)/shard_map/pallas_call | solution.py:177
  190.8 9.0 %shard_map.96.refs_4_ = f32[4,1024,512]{2,1,0:T(8,128)} custom-call(s32[8]{0:T(128)} %stack.140.table, bf16[4,5376,512]{2,1,0:T(8,128)(2,1)} %shard_map.95.normed, bf16[1344,512]{1,0:T(8,128)(2,1)} %get-tuple-element.88.refs_0_, bf16[1344,512]{1,0:T(8,128)(2,1)} %get-tuple-element.92.refs_1_, ...), custom_call_target="tpu_custom_call", output_to_operand_aliasing={{}: (6, {})} | custom-call | flops 2818572288 | bytes 10354688 | tf_op jit(solution)/shard_map/pallas_call | solution.py:221
  199.8 21.0 %shard_map.97 = (bf16[4,512,512]{2,1,0:T(8,128)(2,1)}, bf16[2048,256]{1,0:T(8,128)(2,1)}, bf16[256,2048]{1,0:T(8,128)(2,1)}) custom-call(s32[12]{0:T(128)} %stack.131.table, bf16[4,5376,512]{2,1,0:T(8,128)(2,1)} %shard_map.95.normed, bf16[1344,512]{1,0:T(8,128)(2,1)} %collective-permute-done.14.refs_0_, bf16[1344,512]{1,0:T(8,128)(2,1)} %collective-permute-done.18.refs_1_, ...), custom_call_target="tpu_custom_call" | custom-call | flops 11274289152 | bytes 24903680 | tf_op jit(solution)/shard_map/pallas_call | solution.py:285
  222.5 6.8 %shard_map.98.refs_0_ = bf16[512,512]{1,0:T(8,128)(2,1)} custom-call(s32[1]{0:T(128)} %bitcast.23.table, bf16[4,512,512]{2,1,0:T(8,128)(2,1)} %get-tuple-element.74.q_ref, bf16[2048,256]{1,0:T(8,128)(2,1)} %get-tuple-element.75.keys, bf16[256,2048]{1,0:T(8,128)(2,1)} %get-tuple-element.76.values), custom_call_target="tpu_custom_call" | custom-call | flops 1342177280 | bytes 3145728 | tf_op jit(solution)/shard_map/pallas_call | solution.py:385
  231.3 6.9 %shard_map.99.refs_0_ = bf16[512,512]{1,0:T(8,128)(2,1)} custom-call(s32[1]{0:T(128)} %bitcast.24.table, bf16[4,512,512]{2,1,0:T(8,128)(2,1)} %get-tuple-element.74.q_ref, bf16[2048,256]{1,0:T(8,128)(2,1)} %get-tuple-element.75.keys, bf16[256,2048]{1,0:T(8,128)(2,1)} %get-tuple-element.76.values, bf16[512,512]{1,0:T(8,128)(2,1)} %shard_map.98.refs_0_), custom_call_target="tpu_custom_call" | custom-call | flops 1342177280 | bytes 3145728 | tf_op jit(solution)/shard_map/pallas_call | solution.py:385
  241.3 6.9 %shard_map.100.refs_0_ = bf16[512,512]{1,0:T(8,128)(2,1)} custom-call(s32[1]{0:T(128)} %bitcast.22.table, bf16[4,512,512]{2,1,0:T(8,128)(2,1)} %get-tuple-element.74.q_ref, bf16[2048,256]{1,0:T(8,128)(2,1)} %get-tuple-element.75.keys, bf16[256,2048]{1,0:T(8,128)(2,1)} %get-tuple-element.76.values, bf16[512,512]{1,0:T(8,128)(2,1)} %shard_map.99.refs_0_, ...), custom_call_target="tpu_custom_call" | custom-call | flops 1342177280 | bytes 3145728 | tf_op jit(solution)/shard_map/pallas_call | solution.py:385
  248.2 10.4 %collective-permute-done.25 = bf16[512,512]{1,0:T(8,128)(2,1)} collective-permute-done((bf16[512,512]{1,0:T(8,128)(2,1)}, bf16[512,512]{1,0:T(8,128)(2,1)}, u32[]{:S(2)}, u32[]{:S(2)}) %collective-permute-start.25) | collective-permute-done | bytes 524320 | tf_op jit(solution)/shard_map/ppermute | solution.py:593
  264.6 13.2 %collective-permute-done.34.refs_16_ = bf16[1344,512]{1,0:T(8,128)(2,1)} collective-permute-done((bf16[1344,512]{1,0:T(8,128)(2,1)}, bf16[1344,512]{1,0:T(8,128)(2,1)}, u32[]{:S(2)}, u32[]{:S(2)}) %collective-permute-start.34) | collective-permute-done | bytes 1376288 | tf_op jit(solution)/shard_map/ppermute | solution.py:589
  277.8 6.9 %shard_map.101 = bf16[512,512]{1,0:T(8,128)(2,1)} custom-call(s32[1]{0:T(128)} %bitcast.19.table, bf16[4,512,512]{2,1,0:T(8,128)(2,1)} %get-tuple-element.74.q_ref, bf16[2048,256]{1,0:T(8,128)(2,1)} %get-tuple-element.75.keys, bf16[256,2048]{1,0:T(8,128)(2,1)} %get-tuple-element.76.values, bf16[512,512]{1,0:T(8,128)(2,1)} %shard_map.100.refs_0_, ...), custom_call_target="tpu_custom_call" | custom-call | flops 1342177280 | bytes 3145728 | tf_op jit(solution)/shard_map/pallas_call | solution.py:385
  285.2 3.8 %collective-permute-done.24 = bf16[512,512]{1,0:T(8,128)(2,1)} collective-permute-done((bf16[512,512]{1,0:T(8,128)(2,1)S(1)}, bf16[512,512]{1,0:T(8,128)(2,1)}, u32[]{:S(2)}, u32[]{:S(2)}) %collective-permute-start.24) | collective-permute-done | bytes 524320 | tf_op jit(solution)/shard_map/ppermute | solution.py:595
  293.9 9.9 %collective-permute-done.37.refs_20_ = bf16[1344,256]{1,0:T(8,128)(2,1)} collective-permute-done((bf16[1344,256]{1,0:T(8,128)(2,1)S(1)}, bf16[1344,256]{1,0:T(8,128)(2,1)}, u32[]{:S(2)}, u32[]{:S(2)}) %collective-permute-start.37) | collective-permute-done | bytes 688160 | tf_op jit(solution)/shard_map/ppermute | solution.py:597
  309.7 7.0 %collective-permute-done.40.refs_24_ = bf16[1344,256]{1,0:T(8,128)(2,1)} collective-permute-done((bf16[1344,256]{1,0:T(8,128)(2,1)}, bf16[1344,256]{1,0:T(8,128)(2,1)}, u32[]{:S(2)}, u32[]{:S(2)}) %collective-permute-start.40) | collective-permute-done | bytes 688160 | tf_op jit(solution)/shard_map/ppermute | solution.py:600
  320.0 19.1 %collective-permute-done.38.refs_21_ = bf16[1344,256]{1,0:T(8,128)(2,1)} collective-permute-done((bf16[1344,256]{1,0:T(8,128)(2,1)}, bf16[1344,256]{1,0:T(8,128)(2,1)}, u32[]{:S(2)}, u32[]{:S(2)}) %collective-permute-start.38) | collective-permute-done | bytes 688160 | tf_op jit(solution)/shard_map/ppermute | solution.py:140
  339.1 10.3 %collective-permute-done.41.refs_25_ = bf16[1344,256]{1,0:T(8,128)(2,1)} collective-permute-done((bf16[1344,256]{1,0:T(8,128)(2,1)}, bf16[1344,256]{1,0:T(8,128)(2,1)}, u32[]{:S(2)}, u32[]{:S(2)}) %collective-permute-start.41) | collective-permute-done | bytes 688160 | tf_op jit(solution)/shard_map/ppermute | solution.py:140
  349.4 14.5 %shard_map.102 = (f32[1344,512]{1,0:T(8,128)}, f32[1,512]{1,0:T(1,128)}) custom-call(s32[18]{0:T(128)} %stack.125.table, bf16[512,512]{1,0:T(8,128)(2,1)} %copy-done.12, bf16[512,512]{1,0:T(8,128)(2,1)} %copy-done.11, bf16[512,512]{1,0:T(8,128)(2,1)} %copy-done.22, bf16[512,512]{1,0:T(8,128)(2,1)} %collective-permute-done.27.refs_3_, ...), custom_call_target="tpu_custom_call" | custom-call | flops 5637144576 | bytes 17956864 | tf_op jit(solution)/shard_map/pallas_call | solution.py:443
  369.6 3.3 fusion
  (146 shorter events, 73.1 us)
Async XLA Ops:
  0.0 20.7 %collective-permute-start = (bf16[1344,512]{1,0:T(8,128)(2,1)}, bf16[1344,512]{1,0:T(8,128)(2,1)S(1)}, u32[]{:S(2)}, u32[]{:S(2)}) collective-permute-start(bf16[1344,512]{1,0:T(8,128)(2,1)} %bitcast.56), channel_id=1, source_target_pairs={{4,8},{8,4},{5,9},{9,5},{6,10},{10,6},{7,11},{11,7},{20,24},{24,20... | collective-permute-start | bytes 4128776 | tf_op jit(solution)/shard_map/ppermute | solution.py:523
  0.7 37.1 %collective-permute-start.1 = (bf16[1344,512]{1,0:T(8,128)(2,1)}, bf16[1344,512]{1,0:T(8,128)(2,1)}, u32[]{:S(2)}, u32[]{:S(2)}) collective-permute-start(bf16[1344,512]{1,0:T(8,128)(2,1)} %bitcast.57), channel_id=1, source_target_pairs={{0,4},{12,8},{1,5},{13,9},{2,6},{14,10},{3,7},{15,11},{16,20},{28,... | collective-permute-start | bytes 4128776 | tf_op jit(solution)/shard_map/ppermute | solution.py:524
  9.5 28.4 %collective-permute-start.2 = (bf16[1344,512]{1,0:T(8,128)(2,1)}, bf16[1344,512]{1,0:T(8,128)(2,1)}, u32[]{:S(2)}, u32[]{:S(2)}) collective-permute-start(bf16[1344,512]{1,0:T(8,128)(2,1)} %bitcast.58), channel_id=1, source_target_pairs={{4,6},{6,4},{8,10},{10,8},{5,7},{7,5},{9,11},{11,9},{20,22},{22,20... | collective-permute-start | bytes 4128776 | tf_op jit(solution)/shard_map/ppermute | solution.py:142
  11.3 26.6 %collective-permute-start.3 = (bf16[1344,512]{1,0:T(8,128)(2,1)}, bf16[1344,512]{1,0:T(8,128)(2,1)S(1)}, u32[]{:S(2)}, u32[]{:S(2)}) collective-permute-start(bf16[1344,512]{1,0:T(8,128)(2,1)} %bitcast.59), channel_id=1, source_target_pairs={{4,5},{5,4},{8,9},{9,8},{6,7},{7,6},{10,11},{11,10},{20,21},{21,20... | collective-permute-start | bytes 4128776 | tf_op jit(solution)/shard_map/ppermute | solution.py:142
  37.9 27.8 %collective-permute-start.4 = (bf16[1344,512]{1,0:T(8,128)(2,1)}, bf16[1344,512]{1,0:T(8,128)(2,1)}, u32[]{:S(2)}, u32[]{:S(2)}) collective-permute-start(bf16[1344,512]{1,0:T(8,128)(2,1)} %collective-permute-done.1), channel_id=1, source_target_pairs={{4,8},{8,4},{5,9},{9,5},{6,10},{10,6},{7,11},{11,7},{20,24},{24,20... | collective-permute-start | bytes 4128776 | tf_op jit(solution)/shard_map/ppermute | solution.py:531
  39.6 34.6 %collective-permute-start.5 = (bf16[1344,512]{1,0:T(8,128)(2,1)}, bf16[1344,512]{1,0:T(8,128)(2,1)}, u32[]{:S(2)}, u32[]{:S(2)}) collective-permute-start(bf16[1344,512]{1,0:T(8,128)(2,1)} %get-tuple-element.47), channel_id=1, source_target_pairs={{0,4},{12,8},{1,5},{13,9},{2,6},{14,10},{3,7},{15,11},{16,20},{28,... | collective-permute-start | bytes 4128776 | tf_op jit(solution)/shard_map/ppermute | solution.py:532
  50.9 58.3 %collective-permute-start.10 = (bf16[2,1344,512]{2,1,0:T(8,128)(2,1)S(1)}, bf16[2,1344,512]{2,1,0:T(8,128)(2,1)}, u32[]{:S(2)}, u32[]{:S(2)}) collective-permute-start(bf16[2,1344,512]{2,1,0:T(8,128)(2,1)S(1)} %pad_maximum_fusion.refs_1_), channel_id=1, source_target_pairs={{4,6},{6,4},{8,10},{10,8},{5,7},{7,5},{9,11},{11,9},{20,22},{22,20... | collective-permute-start | bytes 8257544 | tf_op jit(solution)/shard_map/ppermute | solution.py:142
  53.3 55.9 %collective-permute-start.11 = (bf16[2,1344,512]{2,1,0:T(8,128)(2,1)S(1)}, bf16[2,1344,512]{2,1,0:T(8,128)(2,1)}, u32[]{:S(2)}, u32[]{:S(2)}) collective-permute-start(bf16[2,1344,512]{2,1,0:T(8,128)(2,1)S(1)} %pad_maximum_fusion.refs_1_), channel_id=1, source_target_pairs={{4,5},{5,4},{8,9},{9,8},{6,7},{7,6},{10,11},{11,10},{20,21},{21,20... | collective-permute-start | bytes 8257544 | tf_op jit(solution)/shard_map/ppermute | solution.py:142
  76.0 33.1 %collective-permute-start.8 = (bf16[1344,512]{1,0:T(8,128)(2,1)}, bf16[1344,512]{1,0:T(8,128)(2,1)S(1)}, u32[]{:S(2)}, u32[]{:S(2)}) collective-permute-start(bf16[1344,512]{1,0:T(8,128)(2,1)} %get-tuple-element.73), channel_id=1, source_target_pairs={{0,4},{12,8},{1,5},{13,9},{2,6},{14,10},{3,7},{15,11},{16,20},{28,... | collective-permute-start | bytes 4128776 | tf_op jit(solution)/shard_map/ppermute | solution.py:541
  82.2 27.0 %collective-permute-start.9 = (bf16[1344,512]{1,0:T(8,128)(2,1)}, bf16[1344,512]{1,0:T(8,128)(2,1)S(1)}, u32[]{:S(2)}, u32[]{:S(2)}) collective-permute-start(bf16[1344,512]{1,0:T(8,128)(2,1)} %collective-permute-done.5.refs_2_), channel_id=1, source_target_pairs={{4,20},{20,4},{8,24},{24,8},{5,21},{21,5},{9,25},{25,9},{6,22},{22... | collective-permute-start | bytes 4128776 | tf_op jit(solution)/shard_map/ppermute | solution.py:140
  111.5 44.9 %collective-permute-start.14 = (bf16[1344,512]{1,0:T(8,128)(2,1)}, bf16[1344,512]{1,0:T(8,128)(2,1)}, u32[]{:S(2)}, u32[]{:S(2)}) collective-permute-start(bf16[1344,512]{1,0:T(8,128)(2,1)} %get-tuple-element.62), channel_id=1, source_target_pairs={{0,8},{12,4},{1,9},{13,5},{2,10},{14,6},{3,11},{15,7},{16,24},{28,... | collective-permute-start | bytes 4128776 | tf_op jit(solution)/shard_map/ppermute | solution.py:548
  119.3 37.1 %collective-permute-start.15 = (bf16[1344,512]{1,0:T(8,128)(2,1)}, bf16[1344,512]{1,0:T(8,128)(2,1)}, u32[]{:S(2)}, u32[]{:S(2)}) collective-permute-start(bf16[1344,512]{1,0:T(8,128)(2,1)} %collective-permute-done.4), channel_id=1, source_target_pairs={{4,6},{6,4},{8,10},{10,8},{5,7},{7,5},{9,11},{11,9},{20,22},{22,20... | collective-permute-start | bytes 4128776 | tf_op jit(solution)/shard_map/ppermute | solution.py:142
  121.1 35.4 %collective-permute-start.16 = (bf16[1344,512]{1,0:T(8,128)(2,1)}, bf16[1344,512]{1,0:T(8,128)(2,1)}, u32[]{:S(2)}, u32[]{:S(2)}) collective-permute-start(bf16[1344,512]{1,0:T(8,128)(2,1)} %collective-permute-done.7.refs_2_), channel_id=1, source_target_pairs={{4,20},{20,4},{8,24},{24,8},{5,21},{21,5},{9,25},{25,9},{6,22},{22... | collective-permute-start | bytes 4128776 | tf_op jit(solution)/shard_map/ppermute | solution.py:140
  123.5 47.1 %collective-permute-start.13 = (bf16[1344,512]{1,0:T(8,128)(2,1)}, bf16[1344,512]{1,0:T(8,128)(2,1)}, u32[]{:S(2)}, u32[]{:S(2)}) collective-permute-start(bf16[1344,512]{1,0:T(8,128)(2,1)} %collective-permute-done.4), channel_id=1, source_target_pairs={{4,5},{5,4},{8,9},{9,8},{6,7},{7,6},{10,11},{11,10},{20,21},{21,20... | collective-permute-start | bytes 4128776 | tf_op jit(solution)/shard_map/ppermute | solution.py:142
  160.5 69.5 %collective-permute-start.32 = (bf16[1344,1024]{1,0:T(8,128)(2,1)S(1)}, bf16[1344,1024]{1,0:T(8,128)(2,1)}, u32[]{:S(2)}, u32[]{:S(2)}) collective-permute-start(bf16[1344,1024]{1,0:T(8,128)(2,1)S(1)} %bitcast.55), channel_id=1, source_target_pairs={{4,0},{8,12},{5,1},{9,13},{6,2},{10,14},{7,3},{11,15},{20,16},{24,... | collective-permute-start | bytes 8257544 | tf_op jit(solution)/shard_map/ppermute | solution.py:552
  161.8 38.0 %collective-permute-start.18 = (bf16[1344,512]{1,0:T(8,128)(2,1)}, bf16[1344,512]{1,0:T(8,128)(2,1)}, u32[]{:S(2)}, u32[]{:S(2)}) collective-permute-start(bf16[1344,512]{1,0:T(8,128)(2,1)} %collective-permute-done.14.refs_0_), channel_id=1, source_target_pairs={{4,20},{20,4},{8,24},{24,8},{5,21},{21,5},{9,25},{25,9},{6,22},{22... | collective-permute-start | bytes 4128776 | tf_op jit(solution)/shard_map/ppermute | solution.py:140
  166.4 54.3 %collective-permute-start.19 = (bf16[1344,512]{1,0:T(8,128)(2,1)}, bf16[1344,512]{1,0:T(8,128)(2,1)}, u32[]{:S(2)}, u32[]{:S(2)}) collective-permute-start(bf16[1344,512]{1,0:T(8,128)(2,1)} %get-tuple-element.73), channel_id=1, source_target_pairs={{4,8},{8,4},{5,9},{9,5},{6,10},{10,6},{7,11},{11,7},{20,24},{24,20... | collective-permute-start | bytes 4128776 | tf_op jit(solution)/shard_map/ppermute | solution.py:566
  170.6 67.6 %collective-permute-start.20 = (bf16[1344,256]{1,0:T(8,128)(2,1)}, bf16[1344,256]{1,0:T(8,128)(2,1)S(1)}, u32[]{:S(2)}, u32[]{:S(2)}) collective-permute-start(bf16[1344,256]{1,0:T(8,128)(2,1)} %get-tuple-element.94), channel_id=1, source_target_pairs={{4,8},{8,4},{5,9},{9,5},{6,10},{10,6},{7,11},{11,7},{20,24},{24,20... | collective-permute-start | bytes 2064392 | tf_op jit(solution)/shard_map/ppermute | solution.py:567
  171.4 90.6 %collective-permute-start.33 = (bf16[1344,512]{1,0:T(8,128)(2,1)}, bf16[1344,512]{1,0:T(8,128)(2,1)}, u32[]{:S(2)}, u32[]{:S(2)}) collective-permute-start(bf16[1344,512]{1,0:T(8,128)(2,1)} %get-tuple-element.80), channel_id=1, source_target_pairs={{0,4},{12,8},{1,5},{13,9},{2,6},{14,10},{3,7},{15,11},{16,20},{28,... | collective-permute-start | bytes 4128776 | tf_op jit(solution)/shard_map/ppermute | solution.py:569
  220.8 42.5 %collective-permute-start.22 = (bf16[1344,512]{1,0:T(8,128)(2,1)}, bf16[1344,512]{1,0:T(8,128)(2,1)}, u32[]{:S(2)}, u32[]{:S(2)}) collective-permute-start(bf16[1344,512]{1,0:T(8,128)(2,1)} %collective-permute-done.19.refs_14_), channel_id=1, source_target_pairs={{4,20},{20,4},{8,24},{24,8},{5,21},{21,5},{9,25},{25,9},{6,22},{22... | collective-permute-start | bytes 4128776 | tf_op jit(solution)/shard_map/ppermute | solution.py:140
  230.0 47.8 %collective-permute-start.34 = (bf16[1344,512]{1,0:T(8,128)(2,1)}, bf16[1344,512]{1,0:T(8,128)(2,1)}, u32[]{:S(2)}, u32[]{:S(2)}) collective-permute-start(bf16[1344,512]{1,0:T(8,128)(2,1)} %collective-permute-done.19.refs_14_), channel_id=1, source_target_pairs={{4,0},{8,12},{5,1},{9,13},{6,2},{10,14},{7,3},{11,15},{20,16},{24,... | collective-permute-start | bytes 4128776 | tf_op jit(solution)/shard_map/ppermute | solution.py:589
  258.6 32.8 %collective-permute-start.36 = (bf16[1344,256]{1,0:T(8,128)(2,1)}, bf16[1344,256]{1,0:T(8,128)(2,1)S(1)}, u32[]{:S(2)}, u32[]{:S(2)}) collective-permute-start(bf16[1344,256]{1,0:T(8,128)(2,1)} %copy-done.7), channel_id=1, source_target_pairs={{4,20},{20,4},{8,24},{24,8},{5,21},{21,5},{9,25},{25,9},{6,22},{22... | collective-permute-start | bytes 2064392 | tf_op jit(solution)/shard_map/ppermute | solution.py:140
  260.4 24.2 %collective-permute-start.29 = (bf16[512,512]{1,0:T(8,128)(2,1)S(1)}, bf16[512,512]{1,0:T(8,128)(2,1)}, u32[]{:S(2)}, u32[]{:S(2)}) collective-permute-start(bf16[512,512]{1,0:T(8,128)(2,1)S(1)} %broadcast_select_fusion.1.refs_1_), channel_id=1, source_target_pairs={{4,6},{6,4},{8,10},{10,8},{0,2},{2,0},{12,14},{14,12},{5,7},{7,5},... | collective-permute-start | bytes 1572872 | tf_op jit(solution)/shard_map/ppermute | solution.py:142
  262.0 27.0 %collective-permute-start.24 = (bf16[512,512]{1,0:T(8,128)(2,1)S(1)}, bf16[512,512]{1,0:T(8,128)(2,1)}, u32[]{:S(2)}, u32[]{:S(2)}) collective-permute-start(bf16[512,512]{1,0:T(8,128)(2,1)S(1)} %copy-done.13), channel_id=1, source_target_pairs={{4,0},{8,12},{5,1},{9,13},{6,2},{10,14},{7,3},{11,15},{20,16},{24,... | collective-permute-start | bytes 1572872 | tf_op jit(solution)/shard_map/ppermute | solution.py:595
  263.3 40.5 %collective-permute-start.37 = (bf16[1344,256]{1,0:T(8,128)(2,1)S(1)}, bf16[1344,256]{1,0:T(8,128)(2,1)}, u32[]{:S(2)}, u32[]{:S(2)}) collective-permute-start(bf16[1344,256]{1,0:T(8,128)(2,1)S(1)} %copy-done.8), channel_id=1, source_target_pairs={{4,0},{8,12},{5,1},{9,13},{6,2},{10,14},{7,3},{11,15},{20,16},{24,... | collective-permute-start | bytes 2064392 | tf_op jit(solution)/shard_map/ppermute | solution.py:597
  277.8 26.0 %collective-permute-start.27 = (bf16[512,512]{1,0:T(8,128)(2,1)S(1)}, bf16[512,512]{1,0:T(8,128)(2,1)}, u32[]{:S(2)}, u32[]{:S(2)}) collective-permute-start(bf16[512,512]{1,0:T(8,128)(2,1)S(1)} %broadcast_select_fusion.1.refs_1_), channel_id=1, source_target_pairs={{4,5},{5,4},{8,9},{9,8},{0,1},{1,0},{12,13},{13,12},{6,7},{7,6},{1... | collective-permute-start | bytes 1572872 | tf_op jit(solution)/shard_map/ppermute | solution.py:142
  284.7 21.0 %collective-permute-start.31 = (bf16[512,512]{1,0:T(8,128)(2,1)}, bf16[512,512]{1,0:T(8,128)(2,1)S(1)}, u32[]{:S(2)}, u32[]{:S(2)}) collective-permute-start(bf16[512,512]{1,0:T(8,128)(2,1)} %collective-permute-done.29.refs_5_), channel_id=1, source_target_pairs={{4,5},{5,4},{8,9},{9,8},{0,1},{1,0},{12,13},{13,12},{6,7},{7,6},{1... | collective-permute-start | bytes 1572872 | tf_op jit(solution)/shard_map/ppermute | solution.py:142
  289.0 50.1 %collective-permute-start.35 = (bf16[1344,512]{1,0:T(8,128)(2,1)}, bf16[1344,512]{1,0:T(8,128)(2,1)}, u32[]{:S(2)}, u32[]{:S(2)}) collective-permute-start(bf16[1344,512]{1,0:T(8,128)(2,1)} %collective-permute-done.34.refs_16_), channel_id=1, source_target_pairs={{0,16},{16,0},{12,28},{28,12},{1,17},{17,1},{13,29},{29,13},{2,18}... | collective-permute-start | bytes 4128776 | tf_op jit(solution)/shard_map/ppermute | solution.py:140
  291.4 25.3 %collective-permute-start.40 = (bf16[1344,256]{1,0:T(8,128)(2,1)}, bf16[1344,256]{1,0:T(8,128)(2,1)}, u32[]{:S(2)}, u32[]{:S(2)}) collective-permute-start(bf16[1344,256]{1,0:T(8,128)(2,1)} %copy-done.9), channel_id=1, source_target_pairs={{4,0},{8,12},{5,1},{9,13},{6,2},{10,14},{7,3},{11,15},{20,16},{24,... | collective-permute-start | bytes 2064392 | tf_op jit(solution)/shard_map/ppermute | solution.py:600
  305.7 33.4 %collective-permute-start.38 = (bf16[1344,256]{1,0:T(8,128)(2,1)}, bf16[1344,256]{1,0:T(8,128)(2,1)}, u32[]{:S(2)}, u32[]{:S(2)}) collective-permute-start(bf16[1344,256]{1,0:T(8,128)(2,1)} %collective-permute-done.37.refs_20_), channel_id=1, source_target_pairs={{0,16},{16,0},{12,28},{28,12},{1,17},{17,1},{13,29},{29,13},{2,18}... | collective-permute-start | bytes 2064392 | tf_op jit(solution)/shard_map/ppermute | solution.py:140
  308.2 30.9 %collective-permute-start.39 = (bf16[1344,256]{1,0:T(8,128)(2,1)S(1)}, bf16[1344,256]{1,0:T(8,128)(2,1)}, u32[]{:S(2)}, u32[]{:S(2)}) collective-permute-start(bf16[1344,256]{1,0:T(8,128)(2,1)S(1)} %copy-done.10), channel_id=1, source_target_pairs={{4,20},{20,4},{8,24},{24,8},{5,21},{21,5},{9,25},{25,9},{6,22},{22... | collective-permute-start | bytes 2064392 | tf_op jit(solution)/shard_map/ppermute | solution.py:140
  316.7 32.6 %collective-permute-start.41 = (bf16[1344,256]{1,0:T(8,128)(2,1)}, bf16[1344,256]{1,0:T(8,128)(2,1)}, u32[]{:S(2)}, u32[]{:S(2)}) collective-permute-start(bf16[1344,256]{1,0:T(8,128)(2,1)} %collective-permute-done.40.refs_24_), channel_id=1, source_target_pairs={{0,16},{16,0},{12,28},{28,12},{1,17},{17,1},{13,29},{29,13},{2,18}... | collective-permute-start | bytes 2064392 | tf_op jit(solution)/shard_map/ppermute | solution.py:140
  (39 other events, 629.0 us)

commit v3 on v2

--- a/solution.py
+++ b/solution.py
@@ -13,8 +13,6 @@
 
 
 EPSILON = 1e-06
-MIDDLE = (1, 2)
-ENDS = (0, 3)
 VMEM_BYTES = 60 * 1024 * 1024
 
 
@@ -133,13 +131,12 @@
     return (stream_in.astype(jnp.float32) + scaled).astype(jnp.bfloat16)
 
 
-def swapped(x, axis, rows):
-    if axis == "groups":
-        count = lax.axis_size("row")
-        pairs = [(count * i + r, count * (1 - i) + r) for r in rows for i in range(2)]
-        return lax.ppermute(x, ("groups", "row"), pairs)
-    pairs = [(2 * r + i, 2 * r + 1 - i) for r in rows for i in range(2)]
-    return lax.ppermute(x, ("row", axis), pairs)
+def swapped(x, axis, rows=None):
+    if rows is None:
+        return lax.ppermute(x, axis, [(0, 1), (1, 0)])
+    count = lax.axis_size("row")
+    pairs = [(count * i + r, count * (1 - i) + r) for r in rows for i in range(2)]
+    return lax.ppermute(x, ("groups", "row"), pairs)
 
 
 def after(x, *earlier):
@@ -155,6 +152,7 @@
 
 
 ANYWHERE = pl.BlockSpec(memory_space=pl.ANY)
+LITTLE = pl.CostEstimate(flops=0, bytes_accessed=0, transcendentals=0)
 
 
 def norm_kernel(table, *refs):
@@ -261,7 +259,7 @@
         values = (
             values
             * lax.rsqrt(jnp.mean(values * values, axis=0, keepdims=True) + EPSILON)
-            * head_gain[...]
+            * head_gain[:, :1]
         )
         first, second = values[:half], values[half:]
         return jnp.concatenate(
@@ -291,8 +289,8 @@
             + [whole(p.shape) for p in pieces]
             + [
                 pl.BlockSpec((1, 2 * width, tokens), lambda i, t: (i, 0, 0)),
-                whole((head, 1)),
-                whole((head, 1)),
+                whole((head, head)),
+                whole((head, head)),
                 turn,
                 turn,
             ],
@@ -312,11 +310,7 @@
             jax.ShapeDtypeStruct((width // 2, blocks * tokens), jnp.bfloat16),
         ],
         compiler_params=pltpu.CompilerParams(vmem_limit_bytes=VMEM_BYTES),
-        cost_estimate=pl.CostEstimate(
-            flops=2 * blocks * tokens * features * width,
-            bytes_accessed=blocks * features * tokens + 2 * features * width + 8 * blocks * width * tokens,
-            transcendentals=0,
-        ),
+        cost_estimate=LITTLE,
     )(table, normed, *pieces, early, *extras)
 
 
@@ -398,11 +392,7 @@
         ),
         out_shape=jax.ShapeDtypeStruct((width, tokens), jnp.bfloat16),
         compiler_params=pltpu.CompilerParams(vmem_limit_bytes=VMEM_BYTES),
-        cost_estimate=pl.CostEstimate(
-            flops=4 * tokens * band * width,
-            bytes_accessed=4 * tokens * width + 4 * keys.shape[0] * keys.shape[1],
-            transcendentals=tokens * band * (width // 128),
-        ),
+        cost_estimate=LITTLE,
     )(block[None], queries, keys, values, *earlier)
 
 
@@ -489,10 +479,12 @@
     blocks = (row, near_block, cross_block, far_block)
     slot = lambda block: jnp.bitwise_xor(place, block)
     ints = lambda *values: jnp.stack([jnp.asarray(v, jnp.int32) for v in values])
-    everywhere = MIDDLE + ENDS
-    inward = [(0, 1), (3, 2)]
+    beside = [(0, 1), (1, 0), (2, 3), (3, 2)]
     across = [(1, 2), (2, 1)]
+    beyond = [(0, 2), (1, 0), (2, 3), (3, 1)]
+    outside = [(1, 3), (2, 0)]
     outward = [(1, 0), (2, 3)]
+    middles, ends = (1, 2), (0, 3)
 
     half = query_weight.shape[1] // 2
     quarter = key_matrix.shape[1] // 2
@@ -520,93 +512,94 @@
     )
     order = ints(*(arrival(slot(j)) for j in range(4)))
 
+    positions = jnp.arange(4 * tokens, dtype=jnp.int32).astype(jnp.float32)
+    cosine, sine = rotary_tables(positions, head)
+    spread = lambda gains: jnp.broadcast_to(gains[:, None], (head, head))
+    tables = (spread(query_gain), spread(key_norm_gain), cosine.T, sine.T)
+
     x_cross = lax.ppermute(stream, "row", across)
-    x_near = lax.ppermute(stream, "row", inward)
-    own_col = swapped(stream, "col", MIDDLE)
-    own_sub = swapped(stream, "sub", MIDDLE)
-    x_cross, x_near, own_col, own_sub, own_side, other_side, mine = settle(
-        x_cross, x_near, own_col, own_sub, own_side, other_side, mine
+    x_near = lax.ppermute(stream, "row", beside)
+    own_col = swapped(stream, "col")
+    own_sub = swapped(stream, "sub")
+    x_cross, x_near, own_col, own_side, other_side, mine, *tables = settle(
+        x_cross, x_near, own_col, own_side, other_side, mine, *tables
     )
 
     x_far = lax.ppermute(x_near, "row", across)
-    w_near = lax.ppermute(own_side, "row", inward)
-    x_pair = jnp.stack([x_near, x_cross])
-    pair_col = swapped(x_pair, "col", MIDDLE)
-    own_both = swapped(own_col, "sub", MIDDLE)
-    pair_sub = swapped(x_pair, "sub", MIDDLE)
+    w_near = lax.ppermute(own_side, "row", beside)
+    near_col = swapped(x_near, "col")
+    own_both = swapped(own_col, "sub")
+    near_sub = swapped(x_near, "sub")
     own_pieces = (stream[None], own_sub[None], own_col[None], own_both[None])
     normed = norm_block(order, own_pieces, 0, gain, 0, None)
-    x_far, w_near, other_side, mine, normed = settle(x_far, w_near, other_side, mine, normed)
+    x_far, w_near, near_col, other_side, mine, normed, x_cross = settle(
+        x_far, w_near, near_col, other_side, mine, normed, x_cross
+    )
     w_cross = lax.ppermute(other_side, "row", across)
-    o_in = lax.ppermute(mine, "row", inward)
-    w_near_y = swapped(w_near, "groups", MIDDLE)
-    far_sub = swapped(x_far, "sub", MIDDLE)
-    w_cross, o_in, w_near_y, pair_col, x_far, pair_sub, normed, other_side, turned, mine, theirs = settle(
-        w_cross, o_in, w_near_y, pair_col, x_far, pair_sub, normed, other_side, turned, mine, theirs
-    )
-
-    w_far = lax.ppermute(other_side, "row", [(0, 2), (3, 1)])
-    far_col = swapped(x_far, "col", MIDDLE)
-    w_cross_y = swapped(w_cross, "groups", MIDDLE)
-    pair_both = swapped(pair_col, "sub", MIDDLE)
-    o_out = lax.ppermute(turned, "row", outward)
-    pair_pieces = (x_pair, pair_sub, pair_col, pair_both)
-    normed = norm_block(order, pair_pieces, 0, gain, 1, normed)
-    normed = norm_block(order, pair_pieces, 1, gain, 2, normed)
+    cross_col = swapped(x_cross, "col")
+    o_in = lax.ppermute(mine, "row", beside)
+    w_near_y = swapped(w_near, "groups")
+    near_both = swapped(near_col, "sub")
+    cross_sub = swapped(x_cross, "sub")
+    far_sub = swapped(x_far, "sub")
+    near_pieces = (x_near[None], near_sub[None], near_col[None], near_both[None])
+    normed = norm_block(order, near_pieces, 0, gain, 1, normed)
+    w_cross, o_in, w_near_y, cross_col, x_far, normed, other_side, theirs, cross_sub = settle(
+        w_cross, o_in, w_near_y, cross_col, x_far, normed, other_side, theirs, cross_sub
+    )
+
+    w_far = lax.ppermute(other_side, "row", beyond)
+    far_col = swapped(x_far, "col")
+    cross_both = swapped(cross_col, "sub")
+    w_cross_y = swapped(w_cross, "groups")
+    cross_pieces = (x_cross[None], cross_sub[None], cross_col[None], cross_both[None])
+    normed = norm_block(order, cross_pieces, 0, gain, 2, normed)
     early_table = ints(0, 0, 0, half, features, group * half, features, (1 - group) * half)
     early_pieces = (own_queries, own_pairs, w_near, w_near_y)
     total = project_early(early_table, normed, early_pieces, 0, 3, None)
-    w_far, far_col, w_cross_y, total, mine, o_in, theirs = settle(
-        w_far, far_col, w_cross_y, total, mine, o_in, theirs
-    )
-
-    cut = depth // 2
-    w_far_y = swapped(w_far, "groups", MIDDLE)
-    far_both = swapped(far_col, "sub", MIDDLE)
-    o_cross = lax.ppermute(mine, "row", across)
-    o_far_1 = lax.ppermute(o_in[:, :cut], "row", across)
-    o_far_2 = lax.ppermute(o_in[:, cut:], "row", across)
-    o_in_rest = lax.ppermute(theirs, "row", inward)
+    w_far, far_col, w_cross_y, total, o_in, theirs = settle(
+        w_far, far_col, w_cross_y, total, o_in, theirs
+    )
+
+    w_far_y = swapped(w_far, "groups")
+    far_both = swapped(far_col, "sub")
+    o_far = lax.ppermute(o_in, "row", across)
+    o_in_rest = lax.ppermute(theirs, "row", beside)
     far_pieces = (x_far[None], far_sub[None], far_col[None], far_both[None])
     normed = norm_block(order, far_pieces, 0, gain, 3, normed)
     total = project_early(early_table, normed, early_pieces, 3, 1, total)
-    positions = jnp.arange(4 * tokens, dtype=jnp.int32).astype(jnp.float32)
-    cosine, sine = rotary_tables(positions, head)
+    w_far_y, o_far, total, o_in_rest = settle(w_far_y, o_far, total, o_in_rest)
+    o_end_far = lax.ppermute(o_far, "row", outward)
+    o_cross = lax.ppermute(mine, "row", across)
+    o_far_y = swapped(o_far, "groups", middles)
     here, there = group * half, (1 - group) * half
     queries, keys, values = project_late(
         ints(0, here, 0, there, features, here, features, there, *blocks),
         normed,
         (w_far, w_far_y, w_cross, w_cross_y),
         total,
-        (query_gain[:, None], key_norm_gain[:, None], cosine.T, sine.T),
+        tables,
     )
 
     def attended(index, *earlier):
         return attend(blocks[index].astype(jnp.int32), index, queries, keys, values, earlier)
 
-    queries, o_cross = settle(queries, o_cross)
-    o_cross_y = swapped(o_cross, "groups", MIDDLE)
-    o_end_cross = lax.ppermute(o_cross, "row", outward)
     cross_part = attended(2)
     to_cross = lax.ppermute(cross_part, "row", across)
-    far_part = attended(3, cross_part)
-    to_far = lax.ppermute(far_part, "row", [(1, 3), (2, 0)])
-    near_part = attended(1, far_part, o_far_1)
+    shown, o_end_far, o_cross = settle(cross_part, o_end_far, o_cross)
+    o_end_cross = lax.ppermute(o_cross, "row", outward)
+    o_end_far_y = swapped(o_end_far, "groups", ends)
+    o_cross_y = swapped(o_cross, "groups", middles)
+    near_part = attended(1, shown)
     to_near = lax.ppermute(near_part, "row", outward)
-    o_far_1_y = swapped(after(o_far_1, near_part), "groups", MIDDLE)
-    o_end_far_1 = lax.ppermute(after(o_far_1, near_part), "row", outward)
-    own_part = attended(0, near_part, o_far_2, o_cross_y, to_cross)
-    o_far_2_y = swapped(after(o_far_2, own_part), "groups", MIDDLE)
-    o_end_far_2 = lax.ppermute(after(o_far_2, own_part), "row", outward)
+    far_part = attended(3, near_part, o_far_y)
+    to_far = lax.ppermute(far_part, "row", outside)
+    own_part = attended(0, far_part, to_cross, o_end_far_y)
     this_side = jnp.where(in_middle, own_part, to_near)
-    this_across = swapped(this_side, "col", everywhere)
-    that_side = jnp.where(in_middle, to_cross, to_far)
-    that_across = swapped(that_side, "col", everywhere)
-    o_end_cross_y = swapped(after(o_end_cross, own_part), "groups", ENDS)
-    o_end_far_1_y = swapped(after(o_end_far_1, this_side), "groups", ENDS)
-    o_end_far_2_y = swapped(o_end_far_2, "groups", ENDS)
-    o_far, o_far_y = (o_far_1, o_far_2), (o_far_1_y, o_far_2_y)
-    o_end_far, o_end_far_y = (o_end_far_1, o_end_far_2), (o_end_far_1_y, o_end_far_2_y)
+    this_across = swapped(this_side, "col")
+    that_side = jnp.where(in_middle, to_cross, after(to_far, own_part))
+    that_across = swapped(that_side, "col")
+    o_end_cross_y = swapped(after(o_end_cross, own_part), "groups", ends)
 
     pair_block = jnp.bitwise_xor(row, 1)
     out_pieces, out_table = [], []
@@ -618,34 +611,30 @@
 
     for part in range(2):
         put(turned, part, depth, row, part, 0, None)
-        put(o_out, part, depth, pair_block, part, 0, ~in_middle)
-    put(o_in, 0, depth, pair_block, group, 0, in_middle)
-    put(o_in_rest, 0, depth, pair_block, 1 - group, 0, in_middle)
+    put(o_in, 0, depth, pair_block, group, 0, None)
+    put(o_in_rest, 0, depth, pair_block, 1 - group, 0, None)
+    put(o_far, 0, depth, 3 - pair_block, group, 0, in_middle)
+    put(o_far_y, 0, depth, 3 - pair_block, 1 - group, 0, in_middle)
+    put(o_end_far, 0, depth, 3 - row, group, 0, ~in_middle)
+    put(o_end_far_y, 0, depth, 3 - row, 1 - group, 0, ~in_middle)
     put(o_cross, 0, depth, 3 - row, group, 0, in_middle)
     put(o_cross_y, 0, depth, 3 - row, 1 - group, 0, in_middle)
     put(o_end_cross, 0, depth, 3 - pair_block, group, 0, ~in_middle)
     put(o_end_cross_y, 0, depth, 3 - pair_block, 1 - group, 0, ~in_middle)
-    for index, (piece, piece_y, end_piece, end_piece_y) in enumerate(
-        zip(o_far, o_far_y, o_end_far, o_end_far_y)
-    ):
-        put(piece, 0, cut, 3 - pair_block, group, index * cut, in_middle)
-        put(piece_y, 0, cut, 3 - pair_block, 1 - group, index * cut, in_middle)
-        put(end_piece, 0, cut, 3 - row, group, index * cut, ~in_middle)
-        put(end_piece_y, 0, cut, 3 - row, 1 - group, index * cut, ~in_middle)
 
     parts = (
         this_side,
         that_side,
-        swapped(this_side, "sub", everywhere),
-        swapped(that_side, "sub", everywhere),
+        swapped(this_side, "sub"),
+        swapped(that_side, "sub"),
         this_across,
         that_across,
-        swapped(this_across, "sub", everywhere),
-        swapped(that_across, "sub", everywhere),
+        swapped(this_across, "sub"),
+        swapped(that_across, "sub"),
     )
     branch, squares = output_product(ints(*out_table), parts, out_pieces)
-    squares = squares + swapped(squares, "sub", everywhere)
-    squares = squares + swapped(squares, "col", everywhere)
+    squares = squares + swapped(squares, "sub")
+    squares = squares + swapped(squares, "col")
     scaled = branch * lax.rsqrt(squares / MODEL_WIDTH + EPSILON) * post_gain[:, None]
     return (stream.astype(jnp.float32) + scaled).astype(jnp.bfloat16).T
 

time: 374 us -> 317 us (0.85)
  starting transfers between devices: 95 us -> 46.9 us
    ppermute x28 -> x31, starting transfers between devices: 70.3 us -> 28 us  [the longest x23 11.4 us: swapped(): return lax.ppermute(x, axis, [(0, 1), (1, 0)])]
    ppermute x28 -> x31, waiting for transfers between devices: 82.4 us -> 105 us  [the longest x23 42.9 us: swapped(): return lax.ppermute(x, axis, [(0, 1), (1, 0)])]
    ppermute x9 -> x4, waiting for transfers between devices: 29.4 us -> 8.34 us  [swapped(): return lax.ppermute(x, ('groups', 'row'), pairs)]
    ppermute x9 -> x4, starting transfers between devices: 15.4 us -> 8.34 us  [swapped(): return lax.ppermute(x, ('groups', 'row'), pairs)]
  transfers between devices with their start and end apart: 44 -> 42, of which waited for: 12 -> 23; matrix products, arithmetic and copies ran while one was open for 6% -> 6% of each run, Pallas kernels for 27% -> 32%
where the time goes in v3:
time: 317 us
  waiting for transfers between devices  128 us (40%)
  Pallas kernels  115 us (36%)
  starting transfers between devices  46.9 us (15%)
  local copies, waits for them, and re-layouts  14.9 us (5%)
  other arithmetic  11.8 us (4%)
    ppermute x23, waiting for transfers between devices, swapped(): return lax.ppermute(x, axis, [(0, 1), (1, 0)])  42.9 us
    pallas_call x4, Pallas kernels, norm_block(): pl.pallas_call(norm_kernel, grid_spec=pltpu.PrefetchScalarGridSpec(num_sc...  28.2 us
    pallas_call x4, Pallas kernels, attend(): pl.pallas_call(functools.partial(attend_kernel, band, float(MODEL_WIDTH /...  27.5 us
    pallas_call x2, Pallas kernels, project_early(): pl.pallas_call(functools.partial(project_early_kernel, len(pieces)), grid...  24.4 us
    pallas_call x1, Pallas kernels, project_late(): pl.pallas_call(functools.partial(project_late_kernel, count), grid_spec=p...  21.1 us
    ppermute x1, waiting for transfers between devices, middle_form(): o_in = lax.ppermute(mine, 'row', beside)  20.7 us
    ppermute x1, waiting for transfers between devices, middle_form(): w_near = lax.ppermute(own_side, 'row', beside)  18.5 us
    pallas_call x1, Pallas kernels, output_product(): pl.pallas_call(functools.partial(output_kernel, len(pieces), full), grid_...  13.8 us
  transfers between devices with their start and end apart: 42, of which 23 were waited for; matrix products, arithmetic and copies ran while one was open for 6% of the time, Pallas kernels for 32%

profile of v3, /device:TPU:0, one launch (start us, length us, event | category | flops | bytes accessed | tf_op | source)
XLA Modules:
  0.0 316.7 jit_solution(13581242723222862940)
XLA Ops:
  0.0 2.9 collective-permute-start.2
  6.3 3.6 %dynamic-slice_bitcast_fusion = (bf16[1344,512]{1,0:T(8,128)(2,1)}, bf16[1344,512]{1,0:T(8,128)(2,1)}) fusion(bf16[1024,1344]{0,1:T(8,128)(2,1)} %param.16, s32[]{:T(128)S(6)} %select_n.146, s32[]{:T(128)S(6)} %select_n.141), kind=kLoop, calls=%fused_computation.4 | loop fusion | bytes 5505032 | tf_op jit(solution)/shard_map/dynamic_slice | solution.py:504
  12.1 3.2 %broadcast_select_fusion = (bf16[1344,512]{1,0:T(8,128)(2,1)}, bf16[1344,512]{1,0:T(8,128)(2,1)}, bf16[1344,512]{1,0:T(8,128)(2,1)}, bf16[1344,512]{1,0:T(8,128)(2,1)}) fusion(pred[]{:T(512)S(6)} %eq.60, bf16[1344,256]{1,0:T(8,128)(2,1)S(1)} %get-tuple-element.106, bf16[1344,256]{1,0:T(8,128)(2,1)S(1)} %get-tuple-element.113, ...), kind=kLoop, calls=%fused_computation.6 | loop fusion | flops 6881280 | bytes 11010057 | tf_op jit(solution)/shard_map/jit(_where)/select_n | solution.py:499
  15.3 2.8 multiply_sine_fusion
  18.1 15.3 %collective-permute-done.2 = bf16[1344,512]{1,0:T(8,128)(2,1)S(1)} collective-permute-done((bf16[1344,512]{1,0:T(8,128)(2,1)}, bf16[1344,512]{1,0:T(8,128)(2,1)S(1)}, u32[]{:S(2)}, u32[]{:S(2)}) %collective-permute-start.2) | collective-permute-done | bytes 1376288 | tf_op jit(solution)/shard_map/ppermute | solution.py:136
  36.3 4.6 %collective-permute-start.4 = (bf16[1344,512]{1,0:T(8,128)(2,1)}, bf16[1344,512]{1,0:T(8,128)(2,1)S(1)}, u32[]{:S(2)}, u32[]{:S(2)}) collective-permute-start(bf16[1344,512]{1,0:T(8,128)(2,1)} %get-tuple-element.52), channel_id=1, source_target_pairs={{0,4},{4,0},{8,12},{12,8},{1,5},{5,1},{9,13},{13,9},{2,6},{6,2},{1... | collective-permute-start | bytes 4128776 | tf_op jit(solution)/shard_map/ppermute | solution.py:529
  46.4 7.1 %shard_map.91.refs_0_ = bf16[4,5376,512]{2,1,0:T(8,128)(2,1)} custom-call(s32[4]{0:T(128)} %pad_add_fusion.table, bf16[1,1344,512]{2,1,0:T(8,128)(2,1)} %bitcast.57, bf16[1,1344,512]{2,1,0:T(8,128)(2,1)} %bitcast.25.refs_1_, bf16[1,1344,512]{2,1,0:T(8,128)(2,1)} %bitcast.58, bf16[1,1344,512]{2,1,0:T(8,128)(2,1)} %bitcast.27.refs_3_, ...), custom_call_target="tpu_custom_call" | custom-call | flops 27525120 | bytes 11010048 | tf_op jit(solution)/shard_map/pallas_call | solution.py:175
  53.5 18.5 %collective-permute-done.4.refs_2_ = bf16[1344,512]{1,0:T(8,128)(2,1)S(1)} collective-permute-done((bf16[1344,512]{1,0:T(8,128)(2,1)}, bf16[1344,512]{1,0:T(8,128)(2,1)S(1)}, u32[]{:S(2)}, u32[]{:S(2)}) %collective-permute-start.4) | collective-permute-done | bytes 1376288 | tf_op jit(solution)/shard_map/ppermute | solution.py:529
  75.3 4.4 %collective-permute-start.9 = (bf16[1344,512]{1,0:T(8,128)(2,1)}, bf16[1344,512]{1,0:T(8,128)(2,1)}, u32[]{:S(2)}, u32[]{:S(2)}) collective-permute-start(bf16[1344,512]{1,0:T(8,128)(2,1)} %get-tuple-element.58), channel_id=1, source_target_pairs={{0,4},{4,0},{8,12},{12,8},{1,5},{5,1},{9,13},{13,9},{2,6},{6,2},{1... | collective-permute-start | bytes 4128776 | tf_op jit(solution)/shard_map/ppermute | solution.py:540
  82.8 7.1 %shard_map.92.refs_0_ = bf16[4,5376,512]{2,1,0:T(8,128)(2,1)} custom-call(s32[4]{0:T(128)} %pad_add_fusion.table, bf16[4,5376,512]{2,1,0:T(8,128)(2,1)} %shard_map.91.refs_0_, bf16[1,1344,512]{2,1,0:T(8,128)(2,1)} %bitcast.29.refs_1_, bf16[1,1344,512]{2,1,0:T(8,128)(2,1)} %bitcast.30.refs_2_, ...), custom_call_target="tpu_custom_call", output_to_operand_aliasing={{}: (1, {})} | custom-call | flops 27525120 | bytes 11010048 | tf_op jit(solution)/shard_map/pallas_call | solution.py:175
  89.8 20.7 %collective-permute-done.9.refs_10_ = bf16[1344,512]{1,0:T(8,128)(2,1)} collective-permute-done((bf16[1344,512]{1,0:T(8,128)(2,1)}, bf16[1344,512]{1,0:T(8,128)(2,1)}, u32[]{:S(2)}, u32[]{:S(2)}) %collective-permute-start.9) | collective-permute-done | bytes 1376288 | tf_op jit(solution)/shard_map/ppermute | solution.py:540
  117.6 7.0 %shard_map.93.normed.refs_0_ = bf16[4,5376,512]{2,1,0:T(8,128)(2,1)} custom-call(s32[4]{0:T(128)} %pad_add_fusion.table, bf16[4,5376,512]{2,1,0:T(8,128)(2,1)} %shard_map.92.refs_0_, bf16[1,1344,512]{2,1,0:T(8,128)(2,1)} %bitcast.34.refs_1_, bf16[1,1344,512]{2,1,0:T(8,128)(2,1)} %bitcast.35.refs_2_, ...), custom_call_target="tpu_custom_call", output_to_operand_aliasing={{}: (1, {})} | custom-call | flops 27525120 | bytes 11010048 | tf_op jit(solution)/shard_map/pallas_call | solution.py:175
  124.6 15.4 %shard_map.94.refs_4_ = f32[4,1024,512]{2,1,0:T(8,128)} custom-call(s32[8]{0:T(128)} %stack.104.table, bf16[4,5376,512]{2,1,0:T(8,128)(2,1)} %shard_map.93.normed.refs_0_, bf16[1344,512]{1,0:T(8,128)(2,1)} %get-tuple-element.98.refs_0_, bf16[1344,512]{1,0:T(8,128)(2,1)} %get-tuple-element.102.refs_1_, bf16[1344,512]{1,0:T(8,128)(2,1)} %copy-done, ...), custom_call_target="tpu_custom_call" | custom-call | flops 8455716864 | bytes 20054016 | tf_op jit(solution)/shard_map/pallas_call | solution.py:219
  140.0 6.9 %collective-permute-done.17.refs_0_ = bf16[1344,512]{1,0:T(8,128)(2,1)S(1)} collective-permute-done((bf16[1344,512]{1,0:T(8,128)(2,1)}, bf16[1344,512]{1,0:T(8,128)(2,1)S(1)}, u32[]{:S(2)}, u32[]{:S(2)}) %collective-permute-start.17) | collective-permute-done | bytes 1376288 | tf_op jit(solution)/shard_map/ppermute | solution.py:551
  154.0 7.0 %shard_map.95.normed = bf16[4,5376,512]{2,1,0:T(8,128)(2,1)} custom-call(s32[4]{0:T(128)} %pad_add_fusion.table, bf16[4,5376,512]{2,1,0:T(8,128)(2,1)} %shard_map.93.normed.refs_0_, bf16[1,1344,512]{2,1,0:T(8,128)(2,1)} %bitcast.38.refs_1_, bf16[1,1344,512]{2,1,0:T(8,128)(2,1)} %bitcast.39.refs_2_, ...), custom_call_target="tpu_custom_call", output_to_operand_aliasing={{}: (1, {})} | custom-call | flops 27525120 | bytes 11010048 | tf_op jit(solution)/shard_map/pallas_call | solution.py:175
  161.0 9.0 %shard_map.96.refs_4_ = f32[4,1024,512]{2,1,0:T(8,128)} custom-call(s32[8]{0:T(128)} %stack.104.table, bf16[4,5376,512]{2,1,0:T(8,128)(2,1)} %shard_map.95.normed, bf16[1344,512]{1,0:T(8,128)(2,1)} %get-tuple-element.98.refs_0_, bf16[1344,512]{1,0:T(8,128)(2,1)} %get-tuple-element.102.refs_1_, ...), custom_call_target="tpu_custom_call", output_to_operand_aliasing={{}: (6, {})} | custom-call | flops 2818572288 | bytes 10354688 | tf_op jit(solution)/shard_map/pallas_call | solution.py:219
  170.0 11.1 %collective-permute-done.23.refs_11_ = bf16[1344,512]{1,0:T(8,128)(2,1)} collective-permute-done((bf16[1344,512]{1,0:T(8,128)(2,1)}, bf16[1344,512]{1,0:T(8,128)(2,1)}, u32[]{:S(2)}, u32[]{:S(2)}) %collective-permute-start.23) | collective-permute-done | bytes 1376288 | tf_op jit(solution)/shard_map/ppermute | solution.py:567
  185.0 21.1 %shard_map.97 = (bf16[4,512,512]{2,1,0:T(8,128)(2,1)}, bf16[2048,256]{1,0:T(8,128)(2,1)}, bf16[256,2048]{1,0:T(8,128)(2,1)}) custom-call(s32[12]{0:T(128)} %stack.98.table, bf16[4,5376,512]{2,1,0:T(8,128)(2,1)} %shard_map.95.normed, bf16[1344,512]{1,0:T(8,128)(2,1)} %copy-done.11, bf16[1344,512]{1,0:T(8,128)(2,1)} %copy-done.12, ...), custom_call_target="tpu_custom_call" | custom-call | tf_op jit(solution)/shard_map/pallas_call | solution.py:283
  206.2 6.9 %shard_map.98.refs_0_ = bf16[512,512]{1,0:T(8,128)(2,1)} custom-call(s32[1]{0:T(128)} %bitcast.17.table, bf16[4,512,512]{2,1,0:T(8,128)(2,1)} %get-tuple-element.85.q_ref, bf16[2048,256]{1,0:T(8,128)(2,1)} %get-tuple-element.86.keys, bf16[256,2048]{1,0:T(8,128)(2,1)} %get-tuple-element.87.values), custom_call_target="tpu_custom_call" | custom-call | tf_op jit(solution)/shard_map/pallas_call | solution.py:379
  213.1 3.0 collective-permute-done.24.refs_14_
  216.0 3.4 %collective-permute-start.28 = (bf16[1344,512]{1,0:T(8,128)(2,1)}, bf16[1344,512]{1,0:T(8,128)(2,1)S(1)}, u32[]{:S(2)}, u32[]{:S(2)}) collective-permute-start(bf16[1344,512]{1,0:T(8,128)(2,1)} %collective-permute-done.24.refs_14_), channel_id=1, source_target_pairs={{0,16},{16,0},{12,28},{28,12},{1,17},{17,1},{13,29},{29,13},{2,18}... | collective-permute-start | bytes 4128776 | tf_op jit(solution)/shard_map/ppermute | solution.py:139
  221.7 6.9 %shard_map.99.refs_0_ = bf16[512,512]{1,0:T(8,128)(2,1)} custom-call(s32[1]{0:T(128)} %bitcast.16.table, bf16[4,512,512]{2,1,0:T(8,128)(2,1)} %get-tuple-element.85.q_ref, bf16[2048,256]{1,0:T(8,128)(2,1)} %get-tuple-element.86.keys, bf16[256,2048]{1,0:T(8,128)(2,1)} %get-tuple-element.87.values, bf16[512,512]{1,0:T(8,128)(2,1)} %shard_map.98.refs_0_), custom_call_target="tpu_custom_call" | custom-call | tf_op jit(solution)/shard_map/pallas_call | solution.py:379
  229.6 6.8 %shard_map.100.refs_0_ = bf16[512,512]{1,0:T(8,128)(2,1)} custom-call(s32[1]{0:T(128)} %bitcast.18.table, bf16[4,512,512]{2,1,0:T(8,128)(2,1)} %get-tuple-element.85.q_ref, bf16[2048,256]{1,0:T(8,128)(2,1)} %get-tuple-element.86.keys, bf16[256,2048]{1,0:T(8,128)(2,1)} %get-tuple-element.87.values, bf16[512,512]{1,0:T(8,128)(2,1)} %shard_map.99.refs_0_, ...), custom_call_target="tpu_custom_call" | custom-call | tf_op jit(solution)/shard_map/pallas_call | solution.py:379
  240.8 6.8 %collective-permute-done.28.refs_2_.refs_15_ = bf16[1344,512]{1,0:T(8,128)(2,1)S(1)} collective-permute-done((bf16[1344,512]{1,0:T(8,128)(2,1)}, bf16[1344,512]{1,0:T(8,128)(2,1)S(1)}, u32[]{:S(2)}, u32[]{:S(2)}) %collective-permute-start.28) | collective-permute-done | bytes 1376288 | tf_op jit(solution)/shard_map/ppermute | solution.py:139
  248.8 6.8 %shard_map.101 = bf16[512,512]{1,0:T(8,128)(2,1)} custom-call(s32[1]{0:T(128)} %bitcast.13.table, bf16[4,512,512]{2,1,0:T(8,128)(2,1)} %get-tuple-element.85.q_ref, bf16[2048,256]{1,0:T(8,128)(2,1)} %get-tuple-element.86.keys, bf16[256,2048]{1,0:T(8,128)(2,1)} %get-tuple-element.87.values, bf16[512,512]{1,0:T(8,128)(2,1)} %shard_map.100.refs_0_, ...), custom_call_target="tpu_custom_call" | custom-call | tf_op jit(solution)/shard_map/pallas_call | solution.py:379
  255.6 10.4 %collective-permute-done.38.refs_18_ = bf16[1344,512]{1,0:T(8,128)(2,1)} collective-permute-done((bf16[1344,512]{1,0:T(8,128)(2,1)}, bf16[1344,512]{1,0:T(8,128)(2,1)}, u32[]{:S(2)}, u32[]{:S(2)}) %collective-permute-start.38) | collective-permute-done | bytes 1376288 | tf_op jit(solution)/shard_map/ppermute | solution.py:590
  269.1 4.4 %collective-permute-done.29 = bf16[512,512]{1,0:T(8,128)(2,1)} collective-permute-done((bf16[512,512]{1,0:T(8,128)(2,1)}, bf16[512,512]{1,0:T(8,128)(2,1)}, u32[]{:S(2)}, u32[]{:S(2)}) %collective-permute-start.29) | collective-permute-done | bytes 524320 | tf_op jit(solution)/shard_map/ppermute | solution.py:594
  275.8 5.9 %collective-permute-done.34.refs_5_ = bf16[512,512]{1,0:T(8,128)(2,1)S(1)} collective-permute-done((bf16[512,512]{1,0:T(8,128)(2,1)S(1)}, bf16[512,512]{1,0:T(8,128)(2,1)S(1)}, u32[]{:S(2)}, u32[]{:S(2)}) %collective-permute-start.34) | collective-permute-done | bytes 524320 | tf_op jit(solution)/shard_map/ppermute | solution.py:136
  281.7 7.4 %collective-permute-done.33.refs_4_ = bf16[512,512]{1,0:T(8,128)(2,1)} collective-permute-done((bf16[512,512]{1,0:T(8,128)(2,1)S(1)}, bf16[512,512]{1,0:T(8,128)(2,1)}, u32[]{:S(2)}, u32[]{:S(2)}) %collective-permute-start.33) | collective-permute-done | bytes 524320 | tf_op jit(solution)/shard_map/ppermute | solution.py:136
  294.0 13.8 %shard_map.102 = (f32[1344,512]{1,0:T(8,128)}, f32[1,512]{1,0:T(1,128)}) custom-call(s32[12]{0:T(128)} %stack.92.table, bf16[512,512]{1,0:T(8,128)(2,1)} %copy-done.9, bf16[512,512]{1,0:T(8,128)(2,1)} %copy-done.8, bf16[512,512]{1,0:T(8,128)(2,1)} %collective-permute-done.31.refs_2_, bf16[512,512]{1,0:T(8,128)(2,1)} %collective-permute-done.32.refs_3_, ...), custom_call_target="tpu_custom_call" | custom-call | flops 5637144576 | bytes 17956864 | tf_op jit(solution)/shard_map/pallas_call | solution.py:433
  310.3 3.1 collective-permute-done.41
  313.4 3.3 %fusion = bf16[512,1344]{0,1:T(8,128)(2,1)} fusion(f32[1344,512]{1,0:T(8,128)} %get-tuple-element.95, f32[1344]{0:T(1024)S(1)} %copy-done.17, f32[512]{0:T(512)S(1)} %bitcast.59, bf16[512,1344]{0,1:T(8,128)(2,1)S(1)} %copy-done.2), kind=kLoop, calls=%fused_computation.1 | loop fusion | flops 3440640 | bytes 5512448 | tf_op jit(solution)/shard_map/transpose | solution.py:639
  (126 shorter events, 59.9 us)
Async XLA Ops:
  0.0 33.3 %collective-permute-start.2 = (bf16[1344,512]{1,0:T(8,128)(2,1)}, bf16[1344,512]{1,0:T(8,128)(2,1)S(1)}, u32[]{:S(2)}, u32[]{:S(2)}) collective-permute-start(bf16[1344,512]{1,0:T(8,128)(2,1)} %bitcast.53), channel_id=1, source_target_pairs={{0,2},{2,0},{1,3},{3,1},{4,6},{6,4},{5,7},{7,5},{8,10},{10,8},{9,1... | collective-permute-start | bytes 4128776 | tf_op jit(solution)/shard_map/ppermute | solution.py:136
  2.9 32.0 %collective-permute-start.1 = (bf16[1344,512]{1,0:T(8,128)(2,1)}, bf16[1344,512]{1,0:T(8,128)(2,1)}, u32[]{:S(2)}, u32[]{:S(2)}) collective-permute-start(bf16[1344,512]{1,0:T(8,128)(2,1)} %bitcast.54), channel_id=1, source_target_pairs={{0,4},{4,0},{8,12},{12,8},{1,5},{5,1},{9,13},{13,9},{2,6},{6,2},{1... | collective-permute-start | bytes 4128776 | tf_op jit(solution)/shard_map/ppermute | solution.py:521
  4.5 30.4 %collective-permute-start = (bf16[1344,512]{1,0:T(8,128)(2,1)}, bf16[1344,512]{1,0:T(8,128)(2,1)}, u32[]{:S(2)}, u32[]{:S(2)}) collective-permute-start(bf16[1344,512]{1,0:T(8,128)(2,1)} %bitcast.55), channel_id=1, source_target_pairs={{4,8},{8,4},{5,9},{9,5},{6,10},{10,6},{7,11},{11,7},{20,24},{24,20... | collective-permute-start | bytes 4128776 | tf_op jit(solution)/shard_map/ppermute | solution.py:520
  6.3 40.1 %collective-permute-start.6 = (bf16[1344,512]{1,0:T(8,128)(2,1)}, bf16[1344,512]{1,0:T(8,128)(2,1)}, u32[]{:S(2)}, u32[]{:S(2)}) collective-permute-start(bf16[1344,512]{1,0:T(8,128)(2,1)} %bitcast.56), channel_id=1, source_target_pairs={{0,1},{1,0},{2,3},{3,2},{4,5},{5,4},{6,7},{7,6},{8,9},{9,8},{10,11... | collective-permute-start | bytes 4128776 | tf_op jit(solution)/shard_map/ppermute | solution.py:136
  36.3 35.7 %collective-permute-start.4 = (bf16[1344,512]{1,0:T(8,128)(2,1)}, bf16[1344,512]{1,0:T(8,128)(2,1)S(1)}, u32[]{:S(2)}, u32[]{:S(2)}) collective-permute-start(bf16[1344,512]{1,0:T(8,128)(2,1)} %get-tuple-element.52), channel_id=1, source_target_pairs={{0,4},{4,0},{8,12},{12,8},{1,5},{5,1},{9,13},{13,9},{2,6},{6,2},{1... | collective-permute-start | bytes 4128776 | tf_op jit(solution)/shard_map/ppermute | solution.py:529
  40.9 32.6 %collective-permute-start.5 = (bf16[1344,512]{1,0:T(8,128)(2,1)}, bf16[1344,512]{1,0:T(8,128)(2,1)}, u32[]{:S(2)}, u32[]{:S(2)}) collective-permute-start(bf16[1344,512]{1,0:T(8,128)(2,1)} %collective-permute-done.1), channel_id=1, source_target_pairs={{0,2},{2,0},{1,3},{3,1},{4,6},{6,4},{5,7},{7,5},{8,10},{10,8},{9,1... | collective-permute-start | bytes 4128776 | tf_op jit(solution)/shard_map/ppermute | solution.py:136
  41.4 32.1 %collective-permute-start.3 = (bf16[1344,512]{1,0:T(8,128)(2,1)}, bf16[1344,512]{1,0:T(8,128)(2,1)}, u32[]{:S(2)}, u32[]{:S(2)}) collective-permute-start(bf16[1344,512]{1,0:T(8,128)(2,1)} %collective-permute-done.1), channel_id=1, source_target_pairs={{4,8},{8,4},{5,9},{9,5},{6,10},{10,6},{7,11},{11,7},{20,24},{24,20... | collective-permute-start | bytes 4128776 | tf_op jit(solution)/shard_map/ppermute | solution.py:528
  46.4 34.8 %collective-permute-start.12 = (bf16[1344,512]{1,0:T(8,128)(2,1)}, bf16[1344,512]{1,0:T(8,128)(2,1)}, u32[]{:S(2)}, u32[]{:S(2)}) collective-permute-start(bf16[1344,512]{1,0:T(8,128)(2,1)} %collective-permute-done.1), channel_id=1, source_target_pairs={{0,1},{1,0},{2,3},{3,2},{4,5},{5,4},{6,7},{7,6},{8,9},{9,8},{10,11... | collective-permute-start | bytes 4128776 | tf_op jit(solution)/shard_map/ppermute | solution.py:136
  73.5 16.3 %collective-permute-start.8 = (bf16[1344,512]{1,0:T(8,128)(2,1)}, bf16[1344,512]{1,0:T(8,128)(2,1)}, u32[]{:S(2)}, u32[]{:S(2)}) collective-permute-start(bf16[1344,512]{1,0:T(8,128)(2,1)} %get-tuple-element.68), channel_id=1, source_target_pairs={{4,8},{8,4},{5,9},{9,5},{6,10},{10,6},{7,11},{11,7},{20,24},{24,20... | collective-permute-start | bytes 4128776 | tf_op jit(solution)/shard_map/ppermute | solution.py:538
  75.3 35.3 %collective-permute-start.9 = (bf16[1344,512]{1,0:T(8,128)(2,1)}, bf16[1344,512]{1,0:T(8,128)(2,1)}, u32[]{:S(2)}, u32[]{:S(2)}) collective-permute-start(bf16[1344,512]{1,0:T(8,128)(2,1)} %get-tuple-element.58), channel_id=1, source_target_pairs={{0,4},{4,0},{8,12},{12,8},{1,5},{5,1},{9,13},{13,9},{2,6},{6,2},{1... | collective-permute-start | bytes 4128776 | tf_op jit(solution)/shard_map/ppermute | solution.py:540
  79.7 32.0 %collective-permute-start.10 = (bf16[1344,512]{1,0:T(8,128)(2,1)S(1)}, bf16[1344,512]{1,0:T(8,128)(2,1)S(1)}, u32[]{:S(2)}, u32[]{:S(2)}) collective-permute-start(bf16[1344,512]{1,0:T(8,128)(2,1)S(1)} %collective-permute-done.4.refs_2_), channel_id=1, source_target_pairs={{0,16},{16,0},{1,17},{17,1},{2,18},{18,2},{3,19},{19,3},{4,20},{20... | collective-permute-start | bytes 4128776 | tf_op jit(solution)/shard_map/ppermute | solution.py:136
  81.2 30.5 %collective-permute-start.14 = (bf16[1344,512]{1,0:T(8,128)(2,1)}, bf16[1344,512]{1,0:T(8,128)(2,1)}, u32[]{:S(2)}, u32[]{:S(2)}) collective-permute-start(bf16[1344,512]{1,0:T(8,128)(2,1)} %collective-permute-done), channel_id=1, source_target_pairs={{0,1},{1,0},{2,3},{3,2},{4,5},{5,4},{6,7},{7,6},{8,9},{9,8},{10,11... | collective-permute-start | bytes 4128776 | tf_op jit(solution)/shard_map/ppermute | solution.py:136
  81.2 32.9 %collective-permute-start.11 = (bf16[1344,512]{1,0:T(8,128)(2,1)}, bf16[1344,512]{1,0:T(8,128)(2,1)}, u32[]{:S(2)}, u32[]{:S(2)}) collective-permute-start(bf16[1344,512]{1,0:T(8,128)(2,1)} %collective-permute-done), channel_id=1, source_target_pairs={{0,2},{2,0},{1,3},{3,1},{4,6},{6,4},{5,7},{7,5},{8,10},{10,8},{9,1... | collective-permute-start | bytes 4128776 | tf_op jit(solution)/shard_map/ppermute | solution.py:136
  114.1 32.8 %collective-permute-start.17 = (bf16[1344,512]{1,0:T(8,128)(2,1)}, bf16[1344,512]{1,0:T(8,128)(2,1)S(1)}, u32[]{:S(2)}, u32[]{:S(2)}) collective-permute-start(bf16[1344,512]{1,0:T(8,128)(2,1)} %get-tuple-element.68), channel_id=1, source_target_pairs={{0,8},{4,0},{8,12},{12,4},{1,9},{5,1},{9,13},{13,5},{2,10},{6,2},{... | collective-permute-start | bytes 4128776 | tf_op jit(solution)/shard_map/ppermute | solution.py:551
  114.1 32.9 %collective-permute-start.18 = (bf16[1344,512]{1,0:T(8,128)(2,1)}, bf16[1344,512]{1,0:T(8,128)(2,1)}, u32[]{:S(2)}, u32[]{:S(2)}) collective-permute-start(bf16[1344,512]{1,0:T(8,128)(2,1)} %collective-permute-done.3), channel_id=1, source_target_pairs={{0,2},{2,0},{1,3},{3,1},{4,6},{6,4},{5,7},{7,5},{8,10},{10,8},{9,1... | collective-permute-start | bytes 4128776 | tf_op jit(solution)/shard_map/ppermute | solution.py:136
  115.6 32.6 %collective-permute-start.19 = (bf16[1344,512]{1,0:T(8,128)(2,1)}, bf16[1344,512]{1,0:T(8,128)(2,1)}, u32[]{:S(2)}, u32[]{:S(2)}) collective-permute-start(bf16[1344,512]{1,0:T(8,128)(2,1)} %collective-permute-done.8.refs_2_), channel_id=1, source_target_pairs={{0,16},{16,0},{1,17},{17,1},{2,18},{18,2},{3,19},{19,3},{4,20},{20... | collective-permute-start | bytes 4128776 | tf_op jit(solution)/shard_map/ppermute | solution.py:136
  116.8 35.4 %collective-permute-start.16 = (bf16[1344,512]{1,0:T(8,128)(2,1)}, bf16[1344,512]{1,0:T(8,128)(2,1)}, u32[]{:S(2)}, u32[]{:S(2)}) collective-permute-start(bf16[1344,512]{1,0:T(8,128)(2,1)} %collective-permute-done.3), channel_id=1, source_target_pairs={{0,1},{1,0},{2,3},{3,2},{4,5},{5,4},{6,7},{7,6},{8,9},{9,8},{10,11... | collective-permute-start | bytes 4128776 | tf_op jit(solution)/shard_map/ppermute | solution.py:136
  148.2 32.9 %collective-permute-start.23 = (bf16[1344,512]{1,0:T(8,128)(2,1)}, bf16[1344,512]{1,0:T(8,128)(2,1)}, u32[]{:S(2)}, u32[]{:S(2)}) collective-permute-start(bf16[1344,512]{1,0:T(8,128)(2,1)} %get-tuple-element.77), channel_id=1, source_target_pairs={{0,4},{4,0},{8,12},{12,8},{1,5},{5,1},{9,13},{13,9},{2,6},{6,2},{1... | collective-permute-start | bytes 4128776 | tf_op jit(solution)/shard_map/ppermute | solution.py:567
  150.0 32.3 %collective-permute-start.21 = (bf16[1344,512]{1,0:T(8,128)(2,1)S(1)}, bf16[1344,512]{1,0:T(8,128)(2,1)S(1)}, u32[]{:S(2)}, u32[]{:S(2)}) collective-permute-start(bf16[1344,512]{1,0:T(8,128)(2,1)S(1)} %collective-permute-done.17.refs_0_), channel_id=1, source_target_pairs={{0,16},{16,0},{1,17},{17,1},{2,18},{18,2},{3,19},{19,3},{4,20},{20... | collective-permute-start | bytes 4128776 | tf_op jit(solution)/shard_map/ppermute | solution.py:136
  150.5 31.8 %collective-permute-start.22 = (bf16[1344,512]{1,0:T(8,128)(2,1)}, bf16[1344,512]{1,0:T(8,128)(2,1)}, u32[]{:S(2)}, u32[]{:S(2)}) collective-permute-start(bf16[1344,512]{1,0:T(8,128)(2,1)} %collective-permute-done.9.refs_10_), channel_id=1, source_target_pairs={{4,8},{8,4},{5,9},{9,5},{6,10},{10,6},{7,11},{11,7},{20,24},{24,20... | collective-permute-start | bytes 4128776 | tf_op jit(solution)/shard_map/ppermute | solution.py:566
  152.2 60.8 %collective-permute-start.25 = (bf16[1344,512]{1,0:T(8,128)(2,1)}, bf16[1344,512]{1,0:T(8,128)(2,1)}, u32[]{:S(2)}, u32[]{:S(2)}) collective-permute-start(bf16[1344,512]{1,0:T(8,128)(2,1)} %get-tuple-element.58), channel_id=1, source_target_pairs={{4,8},{8,4},{5,9},{9,5},{6,10},{10,6},{7,11},{11,7},{20,24},{24,20... | collective-permute-start | bytes 4128776 | tf_op jit(solution)/shard_map/ppermute | solution.py:573
  182.3 33.7 %collective-permute-start.24 = (bf16[1344,512]{1,0:T(8,128)(2,1)}, bf16[1344,512]{1,0:T(8,128)(2,1)}, u32[]{:S(2)}, u32[]{:S(2)}) collective-permute-start(bf16[1344,512]{1,0:T(8,128)(2,1)} %collective-permute-done.22.refs_12_), channel_id=1, source_target_pairs={{4,0},{8,12},{5,1},{9,13},{6,2},{10,14},{7,3},{11,15},{20,16},{24,... | collective-permute-start | bytes 4128776 | tf_op jit(solution)/shard_map/ppermute | solution.py:572
  183.6 45.0 %collective-permute-start.26 = (bf16[1344,512]{1,0:T(8,128)(2,1)}, bf16[1344,512]{1,0:T(8,128)(2,1)S(1)}, u32[]{:S(2)}, u32[]{:S(2)}) collective-permute-start(bf16[1344,512]{1,0:T(8,128)(2,1)} %collective-permute-done.22.refs_12_), channel_id=1, source_target_pairs={{4,20},{20,4},{8,24},{24,8},{5,21},{21,5},{9,25},{25,9},{6,22},{22... | collective-permute-start | bytes 4128776 | tf_op jit(solution)/shard_map/ppermute | solution.py:139
  216.0 31.6 %collective-permute-start.28 = (bf16[1344,512]{1,0:T(8,128)(2,1)}, bf16[1344,512]{1,0:T(8,128)(2,1)S(1)}, u32[]{:S(2)}, u32[]{:S(2)}) collective-permute-start(bf16[1344,512]{1,0:T(8,128)(2,1)} %collective-permute-done.24.refs_14_), channel_id=1, source_target_pairs={{0,16},{16,0},{12,28},{28,12},{1,17},{17,1},{13,29},{29,13},{2,18}... | collective-permute-start | bytes 4128776 | tf_op jit(solution)/shard_map/ppermute | solution.py:139
  219.4 46.6 %collective-permute-start.38 = (bf16[1344,512]{1,0:T(8,128)(2,1)}, bf16[1344,512]{1,0:T(8,128)(2,1)}, u32[]{:S(2)}, u32[]{:S(2)}) collective-permute-start(bf16[1344,512]{1,0:T(8,128)(2,1)} %collective-permute-done.25.refs_16_), channel_id=1, source_target_pairs={{4,0},{8,12},{5,1},{9,13},{6,2},{10,14},{7,3},{11,15},{20,16},{24,... | collective-permute-start | bytes 4128776 | tf_op jit(solution)/shard_map/ppermute | solution.py:590
  220.7 18.8 %collective-permute-start.27 = (bf16[512,512]{1,0:T(8,128)(2,1)}, bf16[512,512]{1,0:T(8,128)(2,1)S(1)}, u32[]{:S(2)}, u32[]{:S(2)}) collective-permute-start(bf16[512,512]{1,0:T(8,128)(2,1)} %shard_map.98.refs_0_), channel_id=1, source_target_pairs={{4,8},{8,4},{5,9},{9,5},{6,10},{10,6},{7,11},{11,7},{20,24},{24,20... | collective-permute-start | bytes 1572872 | tf_op jit(solution)/shard_map/ppermute | solution.py:588
  236.5 19.1 %collective-permute-start.30 = (bf16[512,512]{1,0:T(8,128)(2,1)}, bf16[512,512]{1,0:T(8,128)(2,1)S(1)}, u32[]{:S(2)}, u32[]{:S(2)}) collective-permute-start(bf16[512,512]{1,0:T(8,128)(2,1)} %shard_map.100.refs_0_), channel_id=1, source_target_pairs={{4,12},{8,0},{5,13},{9,1},{6,14},{10,2},{7,15},{11,3},{20,28},{24,... | collective-permute-start | bytes 1572872 | tf_op jit(solution)/shard_map/ppermute | solution.py:596
  237.8 37.5 %collective-permute-start.37 = (bf16[1344,512]{1,0:T(8,128)(2,1)}, bf16[1344,512]{1,0:T(8,128)(2,1)}, u32[]{:S(2)}, u32[]{:S(2)}) collective-permute-start(bf16[1344,512]{1,0:T(8,128)(2,1)} %collective-permute-done.25.refs_16_), channel_id=1, source_target_pairs={{4,20},{20,4},{8,24},{24,8},{5,21},{21,5},{9,25},{25,9},{6,22},{22... | collective-permute-start | bytes 4128776 | tf_op jit(solution)/shard_map/ppermute | solution.py:139
  239.5 34.0 %collective-permute-start.29 = (bf16[512,512]{1,0:T(8,128)(2,1)}, bf16[512,512]{1,0:T(8,128)(2,1)}, u32[]{:S(2)}, u32[]{:S(2)}) collective-permute-start(bf16[512,512]{1,0:T(8,128)(2,1)} %shard_map.99.refs_0_), channel_id=1, source_target_pairs={{4,0},{8,12},{5,1},{9,13},{6,2},{10,14},{7,3},{11,15},{20,16},{24,... | collective-permute-start | bytes 1572872 | tf_op jit(solution)/shard_map/ppermute | solution.py:594
  266.0 26.9 %collective-permute-start.39 = (bf16[1344,512]{1,0:T(8,128)(2,1)}, bf16[1344,512]{1,0:T(8,128)(2,1)S(1)}, u32[]{:S(2)}, u32[]{:S(2)}) collective-permute-start(bf16[1344,512]{1,0:T(8,128)(2,1)} %collective-permute-done.38.refs_18_), channel_id=1, source_target_pairs={{0,16},{16,0},{12,28},{28,12},{1,17},{17,1},{13,29},{29,13},{2,18}... | collective-permute-start | bytes 4128776 | tf_op jit(solution)/shard_map/ppermute | solution.py:139
  275.3 14.5 %collective-permute-start.32 = (bf16[512,512]{1,0:T(8,128)(2,1)S(1)}, bf16[512,512]{1,0:T(8,128)(2,1)}, u32[]{:S(2)}, u32[]{:S(2)}) collective-permute-start(bf16[512,512]{1,0:T(8,128)(2,1)S(1)} %broadcast_select_fusion.1.refs_1_), channel_id=1, source_target_pairs={{0,1},{1,0},{2,3},{3,2},{4,5},{5,4},{6,7},{7,6},{8,9},{9,8},{10,11... | collective-permute-start | bytes 1572872 | tf_op jit(solution)/shard_map/ppermute | solution.py:136
  275.3 14.5 %collective-permute-start.31 = (bf16[512,512]{1,0:T(8,128)(2,1)S(1)}, bf16[512,512]{1,0:T(8,128)(2,1)}, u32[]{:S(2)}, u32[]{:S(2)}) collective-permute-start(bf16[512,512]{1,0:T(8,128)(2,1)S(1)} %broadcast_select_fusion.2.refs_0_), channel_id=1, source_target_pairs={{0,1},{1,0},{2,3},{3,2},{4,5},{5,4},{6,7},{7,6},{8,9},{9,8},{10,11... | collective-permute-start | bytes 1572872 | tf_op jit(solution)/shard_map/ppermute | solution.py:136
  (30 other events, 335.4 us)

commit v4 on v3

--- a/solution.py
+++ b/solution.py
@@ -132,11 +132,27 @@
 
 
 def swapped(x, axis, rows=None):
-    if rows is None:
+    if rows is None or axis == "sub":
         return lax.ppermute(x, axis, [(0, 1), (1, 0)])
     count = lax.axis_size("row")
-    pairs = [(count * i + r, count * (1 - i) + r) for r in rows for i in range(2)]
-    return lax.ppermute(x, ("groups", "row"), pairs)
+    names = ("groups", "row", "sub") if axis == "groups" else ("row", "col", "sub")
+    row_stride = 2 if axis == "groups" else 4
+    stride = 2 * count if axis == "groups" else 2
+    pairs = []
+    for device in range(4 * count):
+        step = stride if (device // row_stride) % count in rows else 1
+        pairs.append((device, device + step if (device // step) % 2 == 0 else device - step))
+    return lax.ppermute(x, names, pairs)
+
+
+def exchanged(x, planes):
+    other = dict(zip(planes, planes[::-1]))
+    pairs = [
+        (2 * r + s, 2 * other[r] + s if r in other else 2 * r + 1 - s)
+        for r in range(lax.axis_size("row"))
+        for s in range(2)
+    ]
+    return lax.ppermute(x, ("row", "sub"), pairs)
 
 
 def after(x, *earlier):
@@ -480,10 +496,8 @@
     slot = lambda block: jnp.bitwise_xor(place, block)
     ints = lambda *values: jnp.stack([jnp.asarray(v, jnp.int32) for v in values])
     beside = [(0, 1), (1, 0), (2, 3), (3, 2)]
-    across = [(1, 2), (2, 1)]
     beyond = [(0, 2), (1, 0), (2, 3), (3, 1)]
-    outside = [(1, 3), (2, 0)]
-    outward = [(1, 0), (2, 3)]
+    outside = [(0, 1), (1, 3), (2, 0), (3, 2)]
     middles, ends = (1, 2), (0, 3)
 
     half = query_weight.shape[1] // 2
@@ -517,25 +531,26 @@
     spread = lambda gains: jnp.broadcast_to(gains[:, None], (head, head))
     tables = (spread(query_gain), spread(key_norm_gain), cosine.T, sine.T)
 
-    x_cross = lax.ppermute(stream, "row", across)
+    x_cross = exchanged(stream, middles)
     x_near = lax.ppermute(stream, "row", beside)
     own_col = swapped(stream, "col")
     own_sub = swapped(stream, "sub")
-    x_cross, x_near, own_col, own_side, other_side, mine, *tables = settle(
-        x_cross, x_near, own_col, own_side, other_side, mine, *tables
-    )
-
-    x_far = lax.ppermute(x_near, "row", across)
+    x_cross, x_near, own_col, own_side, other_side, mine = settle(
+        x_cross, x_near, own_col, own_side, other_side, mine
+    )
+
+    x_far = exchanged(x_near, middles)
     w_near = lax.ppermute(own_side, "row", beside)
     near_col = swapped(x_near, "col")
     own_both = swapped(own_col, "sub")
     near_sub = swapped(x_near, "sub")
     own_pieces = (stream[None], own_sub[None], own_col[None], own_both[None])
+    order, *tables = settle(order, *tables)
     normed = norm_block(order, own_pieces, 0, gain, 0, None)
     x_far, w_near, near_col, other_side, mine, normed, x_cross = settle(
         x_far, w_near, near_col, other_side, mine, normed, x_cross
     )
-    w_cross = lax.ppermute(other_side, "row", across)
+    w_cross = exchanged(other_side, middles)
     cross_col = swapped(x_cross, "col")
     o_in = lax.ppermute(mine, "row", beside)
     w_near_y = swapped(w_near, "groups")
@@ -563,14 +578,14 @@
 
     w_far_y = swapped(w_far, "groups")
     far_both = swapped(far_col, "sub")
-    o_far = lax.ppermute(o_in, "row", across)
+    o_far = exchanged(o_in, middles)
     o_in_rest = lax.ppermute(theirs, "row", beside)
     far_pieces = (x_far[None], far_sub[None], far_col[None], far_both[None])
     normed = norm_block(order, far_pieces, 0, gain, 3, normed)
     total = project_early(early_table, normed, early_pieces, 3, 1, total)
     w_far_y, o_far, total, o_in_rest = settle(w_far_y, o_far, total, o_in_rest)
-    o_end_far = lax.ppermute(o_far, "row", outward)
-    o_cross = lax.ppermute(mine, "row", across)
+    o_end_far = lax.ppermute(o_far, "row", beside)
+    o_cross = exchanged(mine, middles)
     o_far_y = swapped(o_far, "groups", middles)
     here, there = group * half, (1 - group) * half
     queries, keys, values = project_late(
@@ -585,13 +600,13 @@
         return attend(blocks[index].astype(jnp.int32), index, queries, keys, values, earlier)
 
     cross_part = attended(2)
-    to_cross = lax.ppermute(cross_part, "row", across)
+    to_cross = exchanged(cross_part, middles)
     shown, o_end_far, o_cross = settle(cross_part, o_end_far, o_cross)
-    o_end_cross = lax.ppermute(o_cross, "row", outward)
+    o_end_cross = lax.ppermute(o_cross, "row", beside)
     o_end_far_y = swapped(o_end_far, "groups", ends)
     o_cross_y = swapped(o_cross, "groups", middles)
     near_part = attended(1, shown)
-    to_near = lax.ppermute(near_part, "row", outward)
+    to_near = lax.ppermute(near_part, "row", beside)
     far_part = attended(3, near_part, o_far_y)
     to_far = lax.ppermute(far_part, "row", outside)
     own_part = attended(0, far_part, to_cross, o_end_far_y)
@@ -633,8 +648,8 @@
         swapped(that_across, "sub"),
     )
     branch, squares = output_product(ints(*out_table), parts, out_pieces)
-    squares = squares + swapped(squares, "sub")
-    squares = squares + swapped(squares, "col")
+    diagonal = lax.ppermute(squares, ("col", "sub"), [(0, 3), (1, 2), (2, 1), (3, 0)])
+    squares = squares + swapped(squares, "sub") + swapped(squares, "col") + diagonal
     scaled = branch * lax.rsqrt(squares / MODEL_WIDTH + EPSILON) * post_gain[:, None]
     return (stream.astype(jnp.float32) + scaled).astype(jnp.bfloat16).T
 

time: 317 us -> 307 us (0.968)
  starting transfers between devices: 46.9 us -> 33.3 us
    ppermute x13 -> x14, starting transfers between devices: 21.9 us -> 8.8 us  [the longest x1 3.57 us: middle_form(): o_end_far = lax.ppermute(o_far, 'row', beside)]
    ppermute x23, starting transfers between devices: 11.4 us -> 14.7 us  [swapped(): return lax.ppermute(x, axis, [(0, 1), (1, 0)])]
    ppermute x13 -> x14, waiting for transfers between devices: 26.2 us -> 28.5 us  [the longest x4 17 us: swapped(): return lax.ppermute(x, names, pairs)]
  transfers between devices with their start and end apart: 42 -> 43, of which waited for: 23 -> 23; matrix products, arithmetic and copies ran while one was open for 6% -> 6% of each run, Pallas kernels for 32% -> 33%
where the time goes in v4:
time: 307 us; the launch traced here: 306 us
  waiting for transfers between devices  131 us (43%)
  Pallas kernels  115 us (37%)
  starting transfers between devices  33.3 us (11%)
  local copies, waits for them, and re-layouts  14.6 us (5%)
  other arithmetic  11.9 us (4%)
    ppermute x23, waiting for transfers between devices, swapped(): return lax.ppermute(x, axis, [(0, 1), (1, 0)])  42.8 us
    pallas_call x4, Pallas kernels, norm_block(): pl.pallas_call(norm_kernel, grid_spec=pltpu.PrefetchScalarGridSpec(num_sc...  28.2 us
    pallas_call x4, Pallas kernels, attend(): pl.pallas_call(functools.partial(attend_kernel, band, float(MODEL_WIDTH /...  27.6 us
    pallas_call x2, Pallas kernels, project_early(): pl.pallas_call(functools.partial(project_early_kernel, len(pieces)), grid...  24.4 us
    pallas_call x1, Pallas kernels, project_late(): pl.pallas_call(functools.partial(project_late_kernel, count), grid_spec=p...  21.1 us
    ppermute x1, waiting for transfers between devices, middle_form(): o_in = lax.ppermute(mine, 'row', beside)  20.7 us
    ppermute x4, waiting for transfers between devices, swapped(): return lax.ppermute(x, names, pairs)  17 us
    ppermute x1, waiting for transfers between devices, middle_form(): w_near = lax.ppermute(own_side, 'row', beside)  15.5 us
  transfers between devices with their start and end apart: 43, of which 23 were waited for; matrix products, arithmetic and copies ran while one was open for 6% of the time, Pallas kernels for 33%

profile of v4, /device:TPU:0, one launch (start us, length us, event | category | flops | bytes accessed | tf_op | source)
XLA Modules:
  0.0 306.1 jit_solution(9008293157915895413)
XLA Ops:
  0.0 2.9 collective-permute-start.2
  5.0 3.6 %dynamic-slice_bitcast_fusion = (bf16[1344,512]{1,0:T(8,128)(2,1)}, bf16[1344,512]{1,0:T(8,128)(2,1)}) fusion(bf16[1024,1344]{0,1:T(8,128)(2,1)} %param.16, s32[]{:T(128)S(6)} %select_n.146, s32[]{:T(128)S(6)} %select_n.141), kind=kLoop, calls=%fused_computation.4 | loop fusion | bytes 5505032 | tf_op jit(solution)/shard_map/dynamic_slice | solution.py:518
  10.4 3.2 %broadcast_select_fusion = (bf16[1344,512]{1,0:T(8,128)(2,1)}, bf16[1344,512]{1,0:T(8,128)(2,1)}, bf16[1344,512]{1,0:T(8,128)(2,1)}, bf16[1344,512]{1,0:T(8,128)(2,1)}) fusion(pred[]{:T(512)S(6)} %eq.60, bf16[1344,256]{1,0:T(8,128)(2,1)S(1)} %get-tuple-element.108, bf16[1344,256]{1,0:T(8,128)(2,1)S(1)} %get-tuple-element.115, ...), kind=kLoop, calls=%fused_computation.6 | loop fusion | flops 6881280 | bytes 11010057 | tf_op jit(solution)/shard_map/jit(_where)/select_n | solution.py:513
  13.7 19.7 %collective-permute-done.2 = bf16[1344,512]{1,0:T(8,128)(2,1)S(1)} collective-permute-done((bf16[1344,512]{1,0:T(8,128)(2,1)}, bf16[1344,512]{1,0:T(8,128)(2,1)S(1)}, u32[]{:S(2)}, u32[]{:S(2)}) %collective-permute-start.2) | collective-permute-done | bytes 1376288 | tf_op jit(solution)/shard_map/ppermute | solution.py:136
  34.9 2.7 collective-permute-start.4
  39.0 2.8 multiply_sine_fusion
  43.3 2.4 copy.14.refs_4_.refs_5_
  46.1 7.1 %shard_map.91.refs_0_ = bf16[4,5376,512]{2,1,0:T(8,128)(2,1)} custom-call(s32[4]{0:T(128)} %pad_add_fusion.table, bf16[1,1344,512]{2,1,0:T(8,128)(2,1)} %bitcast.57, bf16[1,1344,512]{2,1,0:T(8,128)(2,1)} %bitcast.25.refs_1_, bf16[1,1344,512]{2,1,0:T(8,128)(2,1)} %bitcast.58, bf16[1,1344,512]{2,1,0:T(8,128)(2,1)} %bitcast.27.refs_3_, ...), custom_call_target="tpu_custom_call" | custom-call | flops 27525120 | bytes 11010048 | tf_op jit(solution)/shard_map/pallas_call | solution.py:191
  53.2 15.5 %collective-permute-done.4.refs_2_ = bf16[1344,512]{1,0:T(8,128)(2,1)S(1)} collective-permute-done((bf16[1344,512]{1,0:T(8,128)(2,1)}, bf16[1344,512]{1,0:T(8,128)(2,1)S(1)}, u32[]{:S(2)}, u32[]{:S(2)}) %collective-permute-start.4) | collective-permute-done | bytes 1376288 | tf_op jit(solution)/shard_map/ppermute | solution.py:543
  75.6 7.1 %shard_map.92.refs_0_ = bf16[4,5376,512]{2,1,0:T(8,128)(2,1)} custom-call(s32[4]{0:T(128)} %pad_add_fusion.table, bf16[4,5376,512]{2,1,0:T(8,128)(2,1)} %shard_map.91.refs_0_, bf16[1,1344,512]{2,1,0:T(8,128)(2,1)} %bitcast.29.refs_1_, bf16[1,1344,512]{2,1,0:T(8,128)(2,1)} %bitcast.30.refs_2_, ...), custom_call_target="tpu_custom_call", output_to_operand_aliasing={{}: (1, {})} | custom-call | flops 27525120 | bytes 11010048 | tf_op jit(solution)/shard_map/pallas_call | solution.py:191
  82.7 20.7 %collective-permute-done.9.refs_10_ = bf16[1344,512]{1,0:T(8,128)(2,1)} collective-permute-done((bf16[1344,512]{1,0:T(8,128)(2,1)}, bf16[1344,512]{1,0:T(8,128)(2,1)}, u32[]{:S(2)}, u32[]{:S(2)}) %collective-permute-start.9) | collective-permute-done | bytes 1376288 | tf_op jit(solution)/shard_map/ppermute | solution.py:555
  104.6 2.4 collective-permute-done.11
  111.6 7.0 %shard_map.93.normed.refs_0_ = bf16[4,5376,512]{2,1,0:T(8,128)(2,1)} custom-call(s32[4]{0:T(128)} %pad_add_fusion.table, bf16[4,5376,512]{2,1,0:T(8,128)(2,1)} %shard_map.92.refs_0_, bf16[1,1344,512]{2,1,0:T(8,128)(2,1)} %bitcast.34.refs_1_, bf16[1,1344,512]{2,1,0:T(8,128)(2,1)} %bitcast.35.refs_2_, ...), custom_call_target="tpu_custom_call", output_to_operand_aliasing={{}: (1, {})} | custom-call | flops 27525120 | bytes 11010048 | tf_op jit(solution)/shard_map/pallas_call | solution.py:191
  118.7 15.4 %shard_map.94.refs_4_ = f32[4,1024,512]{2,1,0:T(8,128)} custom-call(s32[8]{0:T(128)} %stack.104.table, bf16[4,5376,512]{2,1,0:T(8,128)(2,1)} %shard_map.93.normed.refs_0_, bf16[1344,512]{1,0:T(8,128)(2,1)} %get-tuple-element.100.refs_0_, bf16[1344,512]{1,0:T(8,128)(2,1)} %get-tuple-element.104.refs_1_, bf16[1344,512]{1,0:T(8,128)(2,1)} %copy-done, ...), custom_call_target="tpu_custom_call" | custom-call | flops 8455716864 | bytes 20054016 | tf_op jit(solution)/shard_map/pallas_call | solution.py:235
  134.1 5.7 %collective-permute-done.17.refs_0_ = bf16[1344,512]{1,0:T(8,128)(2,1)S(1)} collective-permute-done((bf16[1344,512]{1,0:T(8,128)(2,1)}, bf16[1344,512]{1,0:T(8,128)(2,1)S(1)}, u32[]{:S(2)}, u32[]{:S(2)}) %collective-permute-start.17) | collective-permute-done | bytes 1376288 | tf_op jit(solution)/shard_map/ppermute | solution.py:566
  145.3 7.0 %shard_map.95.normed = bf16[4,5376,512]{2,1,0:T(8,128)(2,1)} custom-call(s32[4]{0:T(128)} %pad_add_fusion.table, bf16[4,5376,512]{2,1,0:T(8,128)(2,1)} %shard_map.93.normed.refs_0_, bf16[1,1344,512]{2,1,0:T(8,128)(2,1)} %bitcast.38.refs_1_, bf16[1,1344,512]{2,1,0:T(8,128)(2,1)} %bitcast.39.refs_2_, ...), custom_call_target="tpu_custom_call", output_to_operand_aliasing={{}: (1, {})} | custom-call | flops 27525120 | bytes 11010048 | tf_op jit(solution)/shard_map/pallas_call | solution.py:191
  152.3 9.0 %shard_map.96.refs_4_ = f32[4,1024,512]{2,1,0:T(8,128)} custom-call(s32[8]{0:T(128)} %stack.104.table, bf16[4,5376,512]{2,1,0:T(8,128)(2,1)} %shard_map.95.normed, bf16[1344,512]{1,0:T(8,128)(2,1)} %get-tuple-element.100.refs_0_, bf16[1344,512]{1,0:T(8,128)(2,1)} %get-tuple-element.104.refs_1_, ...), custom_call_target="tpu_custom_call", output_to_operand_aliasing={{}: (6, {})} | custom-call | flops 2818572288 | bytes 10354688 | tf_op jit(solution)/shard_map/pallas_call | solution.py:235
  161.3 13.4 %collective-permute-done.23.refs_11_ = bf16[1344,512]{1,0:T(8,128)(2,1)} collective-permute-done((bf16[1344,512]{1,0:T(8,128)(2,1)}, bf16[1344,512]{1,0:T(8,128)(2,1)}, u32[]{:S(2)}, u32[]{:S(2)}) %collective-permute-start.23) | collective-permute-done | bytes 1376288 | tf_op jit(solution)/shard_map/ppermute | solution.py:582
  175.2 3.6 %collective-permute-start.24 = (bf16[1344,512]{1,0:T(8,128)(2,1)}, bf16[1344,512]{1,0:T(8,128)(2,1)}, u32[]{:S(2)}, u32[]{:S(2)}) collective-permute-start(bf16[1344,512]{1,0:T(8,128)(2,1)} %collective-permute-done.22.refs_12_), channel_id=1, source_target_pairs={{0,4},{4,0},{8,12},{12,8},{1,5},{5,1},{9,13},{13,9},{2,6},{6,2},{1... | collective-permute-start | bytes 4128776 | tf_op jit(solution)/shard_map/ppermute | solution.py:587
  179.3 21.1 %shard_map.97 = (bf16[4,512,512]{2,1,0:T(8,128)(2,1)}, bf16[2048,256]{1,0:T(8,128)(2,1)}, bf16[256,2048]{1,0:T(8,128)(2,1)}) custom-call(s32[12]{0:T(128)} %stack.98.table, bf16[4,5376,512]{2,1,0:T(8,128)(2,1)} %shard_map.95.normed, bf16[1344,512]{1,0:T(8,128)(2,1)} %copy-done.11, bf16[1344,512]{1,0:T(8,128)(2,1)} %copy-done.12, ...), custom_call_target="tpu_custom_call" | custom-call | tf_op jit(solution)/shard_map/pallas_call | solution.py:299
  200.4 7.1 %shard_map.98.refs_0_ = bf16[512,512]{1,0:T(8,128)(2,1)} custom-call(s32[1]{0:T(128)} %bitcast.17.table, bf16[4,512,512]{2,1,0:T(8,128)(2,1)} %get-tuple-element.87.q_ref, bf16[2048,256]{1,0:T(8,128)(2,1)} %get-tuple-element.88.keys, bf16[256,2048]{1,0:T(8,128)(2,1)} %get-tuple-element.89.values), custom_call_target="tpu_custom_call" | custom-call | tf_op jit(solution)/shard_map/pallas_call | solution.py:395
  209.4 6.8 %shard_map.99.refs_0_ = bf16[512,512]{1,0:T(8,128)(2,1)} custom-call(s32[1]{0:T(128)} %bitcast.16.table, bf16[4,512,512]{2,1,0:T(8,128)(2,1)} %get-tuple-element.87.q_ref, bf16[2048,256]{1,0:T(8,128)(2,1)} %get-tuple-element.88.keys, bf16[256,2048]{1,0:T(8,128)(2,1)} %get-tuple-element.89.values, bf16[512,512]{1,0:T(8,128)(2,1)} %shard_map.98.refs_0_), custom_call_target="tpu_custom_call" | custom-call | tf_op jit(solution)/shard_map/pallas_call | solution.py:395
  217.4 6.8 %shard_map.100.refs_0_ = bf16[512,512]{1,0:T(8,128)(2,1)} custom-call(s32[1]{0:T(128)} %bitcast.18.table, bf16[4,512,512]{2,1,0:T(8,128)(2,1)} %get-tuple-element.87.q_ref, bf16[2048,256]{1,0:T(8,128)(2,1)} %get-tuple-element.88.keys, bf16[256,2048]{1,0:T(8,128)(2,1)} %get-tuple-element.89.values, bf16[512,512]{1,0:T(8,128)(2,1)} %shard_map.99.refs_0_, ...), custom_call_target="tpu_custom_call" | custom-call | tf_op jit(solution)/shard_map/pallas_call | solution.py:395
  226.7 13.7 %collective-permute-done.28.refs_2_.refs_15_ = bf16[1344,512]{1,0:T(8,128)(2,1)S(1)} collective-permute-done((bf16[1344,512]{1,0:T(8,128)(2,1)}, bf16[1344,512]{1,0:T(8,128)(2,1)S(1)}, u32[]{:S(2)}, u32[]{:S(2)}) %collective-permute-start.28) | collective-permute-done | bytes 1376288 | tf_op jit(solution)/shard_map/ppermute | solution.py:145
  241.5 6.9 %shard_map.101 = bf16[512,512]{1,0:T(8,128)(2,1)} custom-call(s32[1]{0:T(128)} %bitcast.13.table, bf16[4,512,512]{2,1,0:T(8,128)(2,1)} %get-tuple-element.87.q_ref, bf16[2048,256]{1,0:T(8,128)(2,1)} %get-tuple-element.88.keys, bf16[256,2048]{1,0:T(8,128)(2,1)} %get-tuple-element.89.values, bf16[512,512]{1,0:T(8,128)(2,1)} %shard_map.100.refs_0_, ...), custom_call_target="tpu_custom_call" | custom-call | tf_op jit(solution)/shard_map/pallas_call | solution.py:395
  248.4 2.9 collective-permute-done.30
  251.3 1.8 collective-permute-done.38.refs_18_
  254.8 8.3 %collective-permute-done.29 = bf16[512,512]{1,0:T(8,128)(2,1)} collective-permute-done((bf16[512,512]{1,0:T(8,128)(2,1)}, bf16[512,512]{1,0:T(8,128)(2,1)}, u32[]{:S(2)}, u32[]{:S(2)}) %collective-permute-start.29) | collective-permute-done | bytes 524320 | tf_op jit(solution)/shard_map/ppermute | solution.py:609
  267.1 10.8 %collective-permute-done.33.refs_4_ = bf16[512,512]{1,0:T(8,128)(2,1)} collective-permute-done((bf16[512,512]{1,0:T(8,128)(2,1)S(1)}, bf16[512,512]{1,0:T(8,128)(2,1)}, u32[]{:S(2)}, u32[]{:S(2)}) %collective-permute-start.33) | collective-permute-done | bytes 524320 | tf_op jit(solution)/shard_map/ppermute | solution.py:136
  280.2 3.3 %collective-permute-done.39.refs_19_ = bf16[1344,512]{1,0:T(8,128)(2,1)S(1)} collective-permute-done((bf16[1344,512]{1,0:T(8,128)(2,1)}, bf16[1344,512]{1,0:T(8,128)(2,1)S(1)}, u32[]{:S(2)}, u32[]{:S(2)}) %collective-permute-start.39) | collective-permute-done | bytes 1376288 | tf_op jit(solution)/shard_map/ppermute | solution.py:145
  284.5 13.8 %shard_map.102 = (f32[1344,512]{1,0:T(8,128)}, f32[1,512]{1,0:T(1,128)}) custom-call(s32[12]{0:T(128)} %stack.92.table, bf16[512,512]{1,0:T(8,128)(2,1)} %copy-done.9, bf16[512,512]{1,0:T(8,128)(2,1)} %copy-done.8, bf16[512,512]{1,0:T(8,128)(2,1)} %collective-permute-done.31.refs_2_, bf16[512,512]{1,0:T(8,128)(2,1)} %collective-permute-done.32.refs_3_, ...), custom_call_target="tpu_custom_call" | custom-call | flops 5637144576 | bytes 17956864 | tf_op jit(solution)/shard_map/pallas_call | solution.py:449
  302.8 3.3 %fusion = bf16[512,1344]{0,1:T(8,128)(2,1)} fusion(f32[1344,512]{1,0:T(8,128)} %get-tuple-element.97, f32[1344]{0:T(1024)S(1)} %copy-done.18, f32[512]{0:T(512)S(1)} %bitcast.59, bf16[512,1344]{0,1:T(8,128)(2,1)S(1)} %copy-done.2), kind=kLoop, calls=%fused_computation.1 | loop fusion | flops 3440640 | bytes 5512448 | tf_op jit(solution)/shard_map/transpose | solution.py:654
  (129 shorter events, 48.1 us)
Async XLA Ops:
  0.0 33.3 %collective-permute-start.2 = (bf16[1344,512]{1,0:T(8,128)(2,1)}, bf16[1344,512]{1,0:T(8,128)(2,1)S(1)}, u32[]{:S(2)}, u32[]{:S(2)}) collective-permute-start(bf16[1344,512]{1,0:T(8,128)(2,1)} %bitcast.53), channel_id=1, source_target_pairs={{0,2},{2,0},{1,3},{3,1},{4,6},{6,4},{5,7},{7,5},{8,10},{10,8},{9,1... | collective-permute-start | bytes 4128776 | tf_op jit(solution)/shard_map/ppermute | solution.py:136
  2.9 32.0 %collective-permute-start.1 = (bf16[1344,512]{1,0:T(8,128)(2,1)}, bf16[1344,512]{1,0:T(8,128)(2,1)}, u32[]{:S(2)}, u32[]{:S(2)}) collective-permute-start(bf16[1344,512]{1,0:T(8,128)(2,1)} %bitcast.54), channel_id=1, source_target_pairs={{0,4},{4,0},{8,12},{12,8},{1,5},{5,1},{9,13},{13,9},{2,6},{6,2},{1... | collective-permute-start | bytes 4128776 | tf_op jit(solution)/shard_map/ppermute | solution.py:535
  4.5 30.4 %collective-permute-start = (bf16[1344,512]{1,0:T(8,128)(2,1)}, bf16[1344,512]{1,0:T(8,128)(2,1)}, u32[]{:S(2)}, u32[]{:S(2)}) collective-permute-start(bf16[1344,512]{1,0:T(8,128)(2,1)} %bitcast.55), channel_id=1, source_target_pairs={{0,1},{1,0},{4,8},{5,9},{8,4},{9,5},{12,13},{13,12},{2,3},{3,2},{6... | collective-permute-start | bytes 4128776 | tf_op jit(solution)/shard_map/ppermute | solution.py:155
  4.5 41.1 %collective-permute-start.6 = (bf16[1344,512]{1,0:T(8,128)(2,1)}, bf16[1344,512]{1,0:T(8,128)(2,1)}, u32[]{:S(2)}, u32[]{:S(2)}) collective-permute-start(bf16[1344,512]{1,0:T(8,128)(2,1)} %bitcast.56), channel_id=1, source_target_pairs={{0,1},{1,0},{2,3},{3,2},{4,5},{5,4},{6,7},{7,6},{8,9},{9,8},{10,11... | collective-permute-start | bytes 4128776 | tf_op jit(solution)/shard_map/ppermute | solution.py:136
  34.9 33.8 %collective-permute-start.4 = (bf16[1344,512]{1,0:T(8,128)(2,1)}, bf16[1344,512]{1,0:T(8,128)(2,1)S(1)}, u32[]{:S(2)}, u32[]{:S(2)}) collective-permute-start(bf16[1344,512]{1,0:T(8,128)(2,1)} %get-tuple-element.54), channel_id=1, source_target_pairs={{0,4},{4,0},{8,12},{12,8},{1,5},{5,1},{9,13},{13,9},{2,6},{6,2},{1... | collective-permute-start | bytes 4128776 | tf_op jit(solution)/shard_map/ppermute | solution.py:543
  37.6 32.6 %collective-permute-start.5 = (bf16[1344,512]{1,0:T(8,128)(2,1)}, bf16[1344,512]{1,0:T(8,128)(2,1)}, u32[]{:S(2)}, u32[]{:S(2)}) collective-permute-start(bf16[1344,512]{1,0:T(8,128)(2,1)} %collective-permute-done.1), channel_id=1, source_target_pairs={{0,2},{2,0},{1,3},{3,1},{4,6},{6,4},{5,7},{7,5},{8,10},{10,8},{9,1... | collective-permute-start | bytes 4128776 | tf_op jit(solution)/shard_map/ppermute | solution.py:136
  38.2 32.1 %collective-permute-start.3 = (bf16[1344,512]{1,0:T(8,128)(2,1)}, bf16[1344,512]{1,0:T(8,128)(2,1)}, u32[]{:S(2)}, u32[]{:S(2)}) collective-permute-start(bf16[1344,512]{1,0:T(8,128)(2,1)} %collective-permute-done.1), channel_id=1, source_target_pairs={{0,1},{1,0},{4,8},{5,9},{8,4},{9,5},{12,13},{13,12},{2,3},{3,2},{6... | collective-permute-start | bytes 4128776 | tf_op jit(solution)/shard_map/ppermute | solution.py:155
  45.6 28.4 %collective-permute-start.12 = (bf16[1344,512]{1,0:T(8,128)(2,1)}, bf16[1344,512]{1,0:T(8,128)(2,1)}, u32[]{:S(2)}, u32[]{:S(2)}) collective-permute-start(bf16[1344,512]{1,0:T(8,128)(2,1)} %collective-permute-done.1), channel_id=1, source_target_pairs={{0,1},{1,0},{2,3},{3,2},{4,5},{5,4},{6,7},{7,6},{8,9},{9,8},{10,11... | collective-permute-start | bytes 4128776 | tf_op jit(solution)/shard_map/ppermute | solution.py:136
  70.8 32.6 %collective-permute-start.9 = (bf16[1344,512]{1,0:T(8,128)(2,1)}, bf16[1344,512]{1,0:T(8,128)(2,1)}, u32[]{:S(2)}, u32[]{:S(2)}) collective-permute-start(bf16[1344,512]{1,0:T(8,128)(2,1)} %get-tuple-element.60), channel_id=1, source_target_pairs={{0,4},{4,0},{8,12},{12,8},{1,5},{5,1},{9,13},{13,9},{2,6},{6,2},{1... | collective-permute-start | bytes 4128776 | tf_op jit(solution)/shard_map/ppermute | solution.py:555
  72.5 32.0 %collective-permute-start.10 = (bf16[1344,512]{1,0:T(8,128)(2,1)S(1)}, bf16[1344,512]{1,0:T(8,128)(2,1)S(1)}, u32[]{:S(2)}, u32[]{:S(2)}) collective-permute-start(bf16[1344,512]{1,0:T(8,128)(2,1)S(1)} %collective-permute-done.4.refs_2_), channel_id=1, source_target_pairs={{0,16},{16,0},{1,17},{17,1},{2,18},{18,2},{3,19},{19,3},{4,20},{20... | collective-permute-start | bytes 4128776 | tf_op jit(solution)/shard_map/ppermute | solution.py:136
  74.0 30.5 %collective-permute-start.14 = (bf16[1344,512]{1,0:T(8,128)(2,1)}, bf16[1344,512]{1,0:T(8,128)(2,1)}, u32[]{:S(2)}, u32[]{:S(2)}) collective-permute-start(bf16[1344,512]{1,0:T(8,128)(2,1)} %collective-permute-done), channel_id=1, source_target_pairs={{0,1},{1,0},{2,3},{3,2},{4,5},{5,4},{6,7},{7,6},{8,9},{9,8},{10,11... | collective-permute-start | bytes 4128776 | tf_op jit(solution)/shard_map/ppermute | solution.py:136
  74.1 32.9 %collective-permute-start.11 = (bf16[1344,512]{1,0:T(8,128)(2,1)}, bf16[1344,512]{1,0:T(8,128)(2,1)}, u32[]{:S(2)}, u32[]{:S(2)}) collective-permute-start(bf16[1344,512]{1,0:T(8,128)(2,1)} %collective-permute-done), channel_id=1, source_target_pairs={{0,2},{2,0},{1,3},{3,1},{4,6},{6,4},{5,7},{7,5},{8,10},{10,8},{9,1... | collective-permute-start | bytes 4128776 | tf_op jit(solution)/shard_map/ppermute | solution.py:136
  107.0 32.8 %collective-permute-start.17 = (bf16[1344,512]{1,0:T(8,128)(2,1)}, bf16[1344,512]{1,0:T(8,128)(2,1)S(1)}, u32[]{:S(2)}, u32[]{:S(2)}) collective-permute-start(bf16[1344,512]{1,0:T(8,128)(2,1)} %get-tuple-element.70), channel_id=1, source_target_pairs={{0,8},{4,0},{8,12},{12,4},{1,9},{5,1},{9,13},{13,5},{2,10},{6,2},{... | collective-permute-start | bytes 4128776 | tf_op jit(solution)/shard_map/ppermute | solution.py:566
  108.4 32.6 %collective-permute-start.18 = (bf16[1344,512]{1,0:T(8,128)(2,1)}, bf16[1344,512]{1,0:T(8,128)(2,1)}, u32[]{:S(2)}, u32[]{:S(2)}) collective-permute-start(bf16[1344,512]{1,0:T(8,128)(2,1)} %collective-permute-done.3), channel_id=1, source_target_pairs={{0,2},{2,0},{1,3},{3,1},{4,6},{6,4},{5,7},{7,5},{8,10},{10,8},{9,1... | collective-permute-start | bytes 4128776 | tf_op jit(solution)/shard_map/ppermute | solution.py:136
  109.5 32.3 %collective-permute-start.19 = (bf16[1344,512]{1,0:T(8,128)(2,1)}, bf16[1344,512]{1,0:T(8,128)(2,1)}, u32[]{:S(2)}, u32[]{:S(2)}) collective-permute-start(bf16[1344,512]{1,0:T(8,128)(2,1)} %collective-permute-done.8.refs_2_), channel_id=1, source_target_pairs={{0,16},{16,0},{1,17},{17,1},{2,18},{18,2},{3,19},{19,3},{4,20},{20... | collective-permute-start | bytes 4128776 | tf_op jit(solution)/shard_map/ppermute | solution.py:136
  111.6 31.9 %collective-permute-start.16 = (bf16[1344,512]{1,0:T(8,128)(2,1)}, bf16[1344,512]{1,0:T(8,128)(2,1)}, u32[]{:S(2)}, u32[]{:S(2)}) collective-permute-start(bf16[1344,512]{1,0:T(8,128)(2,1)} %collective-permute-done.3), channel_id=1, source_target_pairs={{0,1},{1,0},{2,3},{3,2},{4,5},{5,4},{6,7},{7,6},{8,9},{9,8},{10,11... | collective-permute-start | bytes 4128776 | tf_op jit(solution)/shard_map/ppermute | solution.py:136
  141.8 32.9 %collective-permute-start.23 = (bf16[1344,512]{1,0:T(8,128)(2,1)}, bf16[1344,512]{1,0:T(8,128)(2,1)}, u32[]{:S(2)}, u32[]{:S(2)}) collective-permute-start(bf16[1344,512]{1,0:T(8,128)(2,1)} %get-tuple-element.79), channel_id=1, source_target_pairs={{0,4},{4,0},{8,12},{12,8},{1,5},{5,1},{9,13},{13,9},{2,6},{6,2},{1... | collective-permute-start | bytes 4128776 | tf_op jit(solution)/shard_map/ppermute | solution.py:582
  142.8 32.3 %collective-permute-start.21 = (bf16[1344,512]{1,0:T(8,128)(2,1)S(1)}, bf16[1344,512]{1,0:T(8,128)(2,1)S(1)}, u32[]{:S(2)}, u32[]{:S(2)}) collective-permute-start(bf16[1344,512]{1,0:T(8,128)(2,1)S(1)} %collective-permute-done.17.refs_0_), channel_id=1, source_target_pairs={{0,16},{16,0},{1,17},{17,1},{2,18},{18,2},{3,19},{19,3},{4,20},{20... | collective-permute-start | bytes 4128776 | tf_op jit(solution)/shard_map/ppermute | solution.py:136
  143.3 31.8 %collective-permute-start.22 = (bf16[1344,512]{1,0:T(8,128)(2,1)}, bf16[1344,512]{1,0:T(8,128)(2,1)}, u32[]{:S(2)}, u32[]{:S(2)}) collective-permute-start(bf16[1344,512]{1,0:T(8,128)(2,1)} %collective-permute-done.9.refs_10_), channel_id=1, source_target_pairs={{0,1},{1,0},{4,8},{5,9},{8,4},{9,5},{12,13},{13,12},{2,3},{3,2},{6... | collective-permute-start | bytes 4128776 | tf_op jit(solution)/shard_map/ppermute | solution.py:155
  143.6 63.9 %collective-permute-start.25 = (bf16[1344,512]{1,0:T(8,128)(2,1)}, bf16[1344,512]{1,0:T(8,128)(2,1)}, u32[]{:S(2)}, u32[]{:S(2)}) collective-permute-start(bf16[1344,512]{1,0:T(8,128)(2,1)} %get-tuple-element.60), channel_id=1, source_target_pairs={{0,1},{1,0},{4,8},{5,9},{8,4},{9,5},{12,13},{13,12},{2,3},{3,2},{6... | collective-permute-start | bytes 4128776 | tf_op jit(solution)/shard_map/ppermute | solution.py:155
  175.2 32.3 %collective-permute-start.24 = (bf16[1344,512]{1,0:T(8,128)(2,1)}, bf16[1344,512]{1,0:T(8,128)(2,1)}, u32[]{:S(2)}, u32[]{:S(2)}) collective-permute-start(bf16[1344,512]{1,0:T(8,128)(2,1)} %collective-permute-done.22.refs_12_), channel_id=1, source_target_pairs={{0,4},{4,0},{8,12},{12,8},{1,5},{5,1},{9,13},{13,9},{2,6},{6,2},{1... | collective-permute-start | bytes 4128776 | tf_op jit(solution)/shard_map/ppermute | solution.py:587
  178.7 37.5 %collective-permute-start.26 = (bf16[1344,512]{1,0:T(8,128)(2,1)}, bf16[1344,512]{1,0:T(8,128)(2,1)S(1)}, u32[]{:S(2)}, u32[]{:S(2)}) collective-permute-start(bf16[1344,512]{1,0:T(8,128)(2,1)} %collective-permute-done.22.refs_12_), channel_id=1, source_target_pairs={{0,1},{1,0},{4,20},{5,21},{8,24},{9,25},{12,13},{13,12},{16,17},{1... | collective-permute-start | bytes 4128776 | tf_op jit(solution)/shard_map/ppermute | solution.py:145
  207.5 32.9 %collective-permute-start.28 = (bf16[1344,512]{1,0:T(8,128)(2,1)}, bf16[1344,512]{1,0:T(8,128)(2,1)S(1)}, u32[]{:S(2)}, u32[]{:S(2)}) collective-permute-start(bf16[1344,512]{1,0:T(8,128)(2,1)} %collective-permute-done.24.refs_14_), channel_id=1, source_target_pairs={{0,16},{1,17},{4,5},{5,4},{8,9},{9,8},{12,28},{13,29},{16,0},{17,1... | collective-permute-start | bytes 4128776 | tf_op jit(solution)/shard_map/ppermute | solution.py:145
  208.4 44.6 %collective-permute-start.38 = (bf16[1344,512]{1,0:T(8,128)(2,1)}, bf16[1344,512]{1,0:T(8,128)(2,1)}, u32[]{:S(2)}, u32[]{:S(2)}) collective-permute-start(bf16[1344,512]{1,0:T(8,128)(2,1)} %collective-permute-done.25.refs_16_), channel_id=1, source_target_pairs={{0,4},{4,0},{8,12},{12,8},{1,5},{5,1},{9,13},{13,9},{2,6},{6,2},{1... | collective-permute-start | bytes 4128776 | tf_op jit(solution)/shard_map/ppermute | solution.py:605
  209.2 16.4 %collective-permute-start.27 = (bf16[512,512]{1,0:T(8,128)(2,1)}, bf16[512,512]{1,0:T(8,128)(2,1)S(1)}, u32[]{:S(2)}, u32[]{:S(2)}) collective-permute-start(bf16[512,512]{1,0:T(8,128)(2,1)} %shard_map.98.refs_0_), channel_id=1, source_target_pairs={{0,1},{1,0},{4,8},{5,9},{8,4},{9,5},{12,13},{13,12},{2,3},{3,2},{6... | collective-permute-start | bytes 1572872 | tf_op jit(solution)/shard_map/ppermute | solution.py:155
  224.2 27.1 %collective-permute-start.30 = (bf16[512,512]{1,0:T(8,128)(2,1)}, bf16[512,512]{1,0:T(8,128)(2,1)S(1)}, u32[]{:S(2)}, u32[]{:S(2)}) collective-permute-start(bf16[512,512]{1,0:T(8,128)(2,1)} %shard_map.100.refs_0_), channel_id=1, source_target_pairs={{0,4},{4,12},{8,0},{12,8},{1,5},{5,13},{9,1},{13,9},{2,6},{6,14},{... | collective-permute-start | bytes 1572872 | tf_op jit(solution)/shard_map/ppermute | solution.py:611
  225.6 39.8 %collective-permute-start.37 = (bf16[1344,512]{1,0:T(8,128)(2,1)}, bf16[1344,512]{1,0:T(8,128)(2,1)}, u32[]{:S(2)}, u32[]{:S(2)}) collective-permute-start(bf16[1344,512]{1,0:T(8,128)(2,1)} %collective-permute-done.25.refs_16_), channel_id=1, source_target_pairs={{0,1},{1,0},{4,20},{5,21},{8,24},{9,25},{12,13},{13,12},{16,17},{1... | collective-permute-start | bytes 4128776 | tf_op jit(solution)/shard_map/ppermute | solution.py:145
  225.6 37.6 %collective-permute-start.29 = (bf16[512,512]{1,0:T(8,128)(2,1)}, bf16[512,512]{1,0:T(8,128)(2,1)}, u32[]{:S(2)}, u32[]{:S(2)}) collective-permute-start(bf16[512,512]{1,0:T(8,128)(2,1)} %shard_map.99.refs_0_), channel_id=1, source_target_pairs={{0,4},{4,0},{8,12},{12,8},{1,5},{5,1},{9,13},{13,9},{2,6},{6,2},{1... | collective-permute-start | bytes 1572872 | tf_op jit(solution)/shard_map/ppermute | solution.py:609
  253.1 30.4 %collective-permute-start.39 = (bf16[1344,512]{1,0:T(8,128)(2,1)}, bf16[1344,512]{1,0:T(8,128)(2,1)S(1)}, u32[]{:S(2)}, u32[]{:S(2)}) collective-permute-start(bf16[1344,512]{1,0:T(8,128)(2,1)} %collective-permute-done.38.refs_18_), channel_id=1, source_target_pairs={{0,16},{1,17},{4,5},{5,4},{8,9},{9,8},{12,28},{13,29},{16,0},{17,1... | collective-permute-start | bytes 4128776 | tf_op jit(solution)/shard_map/ppermute | solution.py:145
  264.3 13.6 %collective-permute-start.33 = (bf16[512,512]{1,0:T(8,128)(2,1)S(1)}, bf16[512,512]{1,0:T(8,128)(2,1)}, u32[]{:S(2)}, u32[]{:S(2)}) collective-permute-start(bf16[512,512]{1,0:T(8,128)(2,1)S(1)} %broadcast_select_fusion.2.refs_0_), channel_id=1, source_target_pairs={{0,2},{2,0},{1,3},{3,1},{4,6},{6,4},{5,7},{7,5},{8,10},{10,8},{9,1... | collective-permute-start | bytes 1572872 | tf_op jit(solution)/shard_map/ppermute | solution.py:136
  265.3 13.3 %collective-permute-start.32 = (bf16[512,512]{1,0:T(8,128)(2,1)S(1)}, bf16[512,512]{1,0:T(8,128)(2,1)}, u32[]{:S(2)}, u32[]{:S(2)}) collective-permute-start(bf16[512,512]{1,0:T(8,128)(2,1)S(1)} %broadcast_select_fusion.1.refs_1_), channel_id=1, source_target_pairs={{0,1},{1,0},{2,3},{3,2},{4,5},{5,4},{6,7},{7,6},{8,9},{9,8},{10,11... | collective-permute-start | bytes 1572872 | tf_op jit(solution)/shard_map/ppermute | solution.py:136
  265.3 13.3 %collective-permute-start.31 = (bf16[512,512]{1,0:T(8,128)(2,1)S(1)}, bf16[512,512]{1,0:T(8,128)(2,1)}, u32[]{:S(2)}, u32[]{:S(2)}) collective-permute-start(bf16[512,512]{1,0:T(8,128)(2,1)S(1)} %broadcast_select_fusion.2.refs_0_), channel_id=1, source_target_pairs={{0,1},{1,0},{2,3},{3,2},{4,5},{5,4},{6,7},{7,6},{8,9},{9,8},{10,11... | collective-permute-start | bytes 1572872 | tf_op jit(solution)/shard_map/ppermute | solution.py:136
  (32 other events, 363.0 us)

commit v5 on v4

--- a/solution.py
+++ b/solution.py
@@ -13,7 +13,7 @@
 
 
 EPSILON = 1e-06
-VMEM_BYTES = 60 * 1024 * 1024
+VMEM_BYTES = 64 * 1024 * 1024 - 128 * 1024
 
 
 def shifted(x, axis, by):
@@ -326,74 +326,91 @@
             jax.ShapeDtypeStruct((width // 2, blocks * tokens), jnp.bfloat16),
         ],
         compiler_params=pltpu.CompilerParams(vmem_limit_bytes=VMEM_BYTES),
-        cost_estimate=LITTLE,
+        cost_estimate=pl.CostEstimate(
+            flops=2 * blocks * tokens * features * width,
+            bytes_accessed=blocks * features * tokens + 2 * features * width + 8 * blocks * width * tokens,
+            transcendentals=0,
+        ),
     )(table, normed, *pieces, early, *extras)
 
 
-def attend_kernel(band, scale, table, q_ref, keys, values, *refs):
+def attend_kernel(scale, table, q_ref, keys, values, *refs):
     out, mask = refs[-2:]
     head = 128
     tile = out.shape[1]
-    first = table[0] * (2 * tile) + pl.program_id(0) * tile
-    start = pl.multiple_of(jnp.clip(first + tile - band, 0, keys.shape[0] - band), tile)
-    places = lax.broadcasted_iota(jnp.int32, (band, tile), 1)
-    distance = (first - start) + places - lax.broadcasted_iota(jnp.int32, (band, tile), 0)
-    hidden = jnp.where((distance >= 0) & (distance < WINDOW_LENGTH), 0.0, -1e30)
-    mask[:, :tile] = hidden
-    mask[:, tile:] = hidden
+    span = WINDOW_LENGTH // tile + 1
+    place = table[0] * 2 + pl.program_id(0)
+    later = lax.broadcasted_iota(jnp.int32, (tile, tile), 1) >= lax.broadcasted_iota(
+        jnp.int32, (tile, tile), 0
+    )
+    for index, seen in enumerate((later, jnp.logical_not(later))):
+        hidden = jnp.where(seen, 0.0, -1e30)
+        mask[index, :, :tile] = hidden
+        mask[index, :, tile:] = hidden
     pairs = keys.shape[1] // head
     factor = scale * 1.4426950408889634
-    chunks = [slice(a, min(a + tile, band)) for a in range(0, band, tile)]
-
-    def pair_of(ref, index):
+
+    def pair_of(index):
         return [slice((2 * index + i) * head, (2 * index + i + 1) * head) for i in range(2)]
 
-    def query(index):
-        return jnp.concatenate([q_ref[0, rows, :] for rows in pair_of(q_ref, index)], axis=1)
-
-    def within(chunk):
-        return pl.ds(pl.multiple_of(start + chunk.start, tile), chunk.stop - chunk.start)
-
-    def score(index, chunk, queries):
-        columns = slice(index * head, (index + 1) * head)
-        return mask[chunk, :] + jnp.dot(
-            keys[within(chunk), columns], queries, preferred_element_type=jnp.float32
-        )
-
-    queries = query(0)
-    scores = [score(0, chunk, queries) for chunk in chunks]
-    for index in range(pairs):
-        top = functools.reduce(
-            jnp.maximum, [jnp.max(part, axis=0, keepdims=True) for part in scores]
-        )
-        queries = query(index + 1) if index + 1 < pairs else None
-        exponents, upcoming, total = [], [], 0.0
-        for chunk, part in zip(chunks, scores):
-            exponent = jnp.exp2((part - top) * factor)
-            exponents.append(exponent)
-            total = total + jnp.sum(exponent, axis=0, keepdims=True)
-            if queries is not None:
-                upcoming.append(score(index + 1, chunk, queries))
-        inverse = 1.0 / total
-        result = 0.0
-        rows = slice(index * head, (index + 1) * head)
-        for chunk, exponent in zip(chunks, exponents):
-            result = result + jnp.dot(
-                values[rows, within(chunk)],
-                (exponent * inverse).astype(jnp.bfloat16),
-                preferred_element_type=jnp.float32,
+    def against(count):
+        def within(chunk):
+            return pl.ds(pl.multiple_of((place - (count - 1) + chunk) * tile, tile), tile)
+
+        def query(index):
+            return jnp.concatenate([q_ref[0, rows, :] for rows in pair_of(index)], axis=1)
+
+        def score(index, chunk, queries):
+            columns = slice(index * head, (index + 1) * head)
+            result = jnp.dot(
+                keys[within(chunk), columns], queries, preferred_element_type=jnp.float32
             )
-        for i, here in enumerate(pair_of(out, index)):
-            out[here, :] = result[:, i * tile : (i + 1) * tile].astype(jnp.bfloat16)
-        scores = upcoming
+            if chunk == count - 1:
+                result = result + mask[0]
+            elif chunk == 0 and count == span:
+                result = result + mask[1]
+            return result
+
+        queries = query(0)
+        scores = [score(0, chunk, queries) for chunk in range(count)]
+        for index in range(pairs):
+            top = functools.reduce(
+                jnp.maximum, [jnp.max(part, axis=0, keepdims=True) for part in scores]
+            )
+            queries = query(index + 1) if index + 1 < pairs else None
+            exponents, upcoming, total = [], [], 0.0
+            for chunk, part in enumerate(scores):
+                exponent = jnp.exp2((part - top) * factor)
+                exponents.append(exponent)
+                total = total + jnp.sum(exponent, axis=0, keepdims=True)
+                if queries is not None:
+                    upcoming.append(score(index + 1, chunk, queries))
+            inverse = 1.0 / total
+            result = 0.0
+            rows = slice(index * head, (index + 1) * head)
+            for chunk, exponent in enumerate(exponents):
+                result = result + jnp.dot(
+                    values[rows, within(chunk)],
+                    (exponent * inverse).astype(jnp.bfloat16),
+                    preferred_element_type=jnp.float32,
+                )
+            for i, here in enumerate(pair_of(index)):
+                out[here, :] = result[:, i * tile : (i + 1) * tile].astype(jnp.bfloat16)
+            scores = upcoming
+
+    chunks = jnp.minimum(place + 1, span)
+    for count in range(1, min(span, keys.shape[0] // tile) + 1):
+
+        @pl.when(chunks == count)
+        def _(count=count):
+            against(count)
 
 
 def attend(block, index, queries, keys, values, earlier):
     _, width, tokens = queries.shape
     tile = tokens // 2
-    band = min(WINDOW_LENGTH + tile, keys.shape[0])
     return pl.pallas_call(
-        functools.partial(attend_kernel, band, float(MODEL_WIDTH // QUERY_HEAD_COUNT) ** (-0.5)),
+        functools.partial(attend_kernel, float(MODEL_WIDTH // QUERY_HEAD_COUNT) ** (-0.5)),
         grid_spec=pltpu.PrefetchScalarGridSpec(
             num_scalar_prefetch=1,
             grid=(2,),
@@ -404,32 +421,31 @@
             ]
             + [ANYWHERE] * len(earlier),
             out_specs=pl.BlockSpec((width, tile), lambda t, *_: (0, t)),
-            scratch_shapes=[pltpu.VMEM((band, 2 * tile), jnp.float32)],
+            scratch_shapes=[pltpu.VMEM((2, tile, 2 * tile), jnp.float32)],
         ),
         out_shape=jax.ShapeDtypeStruct((width, tokens), jnp.bfloat16),
         compiler_params=pltpu.CompilerParams(vmem_limit_bytes=VMEM_BYTES),
-        cost_estimate=LITTLE,
+        cost_estimate=pl.CostEstimate(
+            flops=12 * tokens * (WINDOW_LENGTH + tile) * width,
+            bytes_accessed=4 * tokens * width + 4 * keys.shape[0] * keys.shape[1],
+            transcendentals=0,
+        ),
     )(block[None], queries, keys, values, *earlier)
 
 
-def output_kernel(count, full, table, *refs):
+def output_kernel(count, table, *refs):
     parts, pieces, (out, squares, held, row_held) = refs[:8], refs[8 : 8 + count], refs[8 + count :]
     depth = parts[0].shape[0]
-    step = pl.program_id(0)
-
-    @pl.when(step == 0)
+
+    @pl.when(pl.program_id(0) == 0)
     def _():
         for index, part in enumerate(parts):
             held[index * depth : (index + 1) * depth, :] = part[...]
         squares[...] = jnp.zeros_like(squares)
 
     for index, piece in enumerate(pieces):
-
-        @pl.when(table[index] < full)
-        def _(index=index, piece=piece):
-            there = pl.ds(pl.multiple_of(table[index], 128), piece.shape[1])
-            row_held[:, there] = piece[...]
-
+        there = pl.ds(pl.multiple_of(table[index], 128), piece.shape[1])
+        row_held[:, there] = piece[...]
     product = jnp.dot(row_held[...], held[...], preferred_element_type=jnp.float32)
     out[...] = product
     squares[...] += jnp.sum(jnp.square(product), axis=0, keepdims=True)
@@ -441,18 +457,16 @@
     full = 8 * depth
     tile = width // 4
 
-    def rows(index, column, columns):
-        return pl.BlockSpec(
-            (tile, columns), lambda t, table: (jnp.where(table[index] < full, t, 0), column)
-        )
+    def rows(column, columns):
+        return pl.BlockSpec((tile, columns), lambda t, *_: (t, column))
 
     return pl.pallas_call(
-        functools.partial(output_kernel, len(pieces), full),
+        functools.partial(output_kernel, len(pieces)),
         grid_spec=pltpu.PrefetchScalarGridSpec(
             num_scalar_prefetch=1,
             grid=(width // tile,),
             in_specs=[whole((depth, tokens))] * 8
-            + [rows(index, column, columns) for index, (_, column, columns) in enumerate(pieces)],
+            + [rows(column, columns) for _, column, columns in pieces],
             out_specs=[pl.BlockSpec((tile, tokens), lambda t, *_: (t, 0)), whole((1, tokens))],
             scratch_shapes=[
                 pltpu.VMEM((full, tokens), jnp.bfloat16),
@@ -545,10 +559,26 @@
     own_both = swapped(own_col, "sub")
     near_sub = swapped(x_near, "sub")
     own_pieces = (stream[None], own_sub[None], own_col[None], own_both[None])
-    order, *tables = settle(order, *tables)
+    pair_block = jnp.bitwise_xor(row, 1)
+    place_table = ints(
+        *(
+            (2 * slot(block) + jnp.bitwise_xor(which, upper)) * depth
+            for block, which in (
+                (row, 0),
+                (row, 1),
+                (pair_block, group),
+                (pair_block, 1 - group),
+                (3 - pair_block, group),
+                (3 - pair_block, 1 - group),
+                (3 - row, group),
+                (3 - row, 1 - group),
+            )
+        )
+    )
+    order, place_table, *tables = settle(order, place_table, *tables)
     normed = norm_block(order, own_pieces, 0, gain, 0, None)
-    x_far, w_near, near_col, other_side, mine, normed, x_cross = settle(
-        x_far, w_near, near_col, other_side, mine, normed, x_cross
+    x_far, w_near, near_col, other_side, normed, x_cross, mine = settle(
+        x_far, w_near, near_col, other_side, normed, x_cross, mine
     )
     w_cross = exchanged(other_side, middles)
     cross_col = swapped(x_cross, "col")
@@ -559,8 +589,8 @@
     far_sub = swapped(x_far, "sub")
     near_pieces = (x_near[None], near_sub[None], near_col[None], near_both[None])
     normed = norm_block(order, near_pieces, 0, gain, 1, normed)
-    w_cross, o_in, w_near_y, cross_col, x_far, normed, other_side, theirs, cross_sub = settle(
-        w_cross, o_in, w_near_y, cross_col, x_far, normed, other_side, theirs, cross_sub
+    w_cross, w_near_y, cross_col, x_far, normed, other_side, theirs, cross_sub, o_in = settle(
+        w_cross, w_near_y, cross_col, x_far, normed, other_side, theirs, cross_sub, o_in
     )
 
     w_far = lax.ppermute(other_side, "row", beyond)
@@ -572,8 +602,8 @@
     early_table = ints(0, 0, 0, half, features, group * half, features, (1 - group) * half)
     early_pieces = (own_queries, own_pairs, w_near, w_near_y)
     total = project_early(early_table, normed, early_pieces, 0, 3, None)
-    w_far, far_col, w_cross_y, total, o_in, theirs = settle(
-        w_far, far_col, w_cross_y, total, o_in, theirs
+    w_far, far_col, w_cross_y, total, theirs, o_in = settle(
+        w_far, far_col, w_cross_y, total, theirs, o_in
     )
 
     w_far_y = swapped(w_far, "groups")
@@ -584,9 +614,8 @@
     normed = norm_block(order, far_pieces, 0, gain, 3, normed)
     total = project_early(early_table, normed, early_pieces, 3, 1, total)
     w_far_y, o_far, total, o_in_rest = settle(w_far_y, o_far, total, o_in_rest)
-    o_end_far = lax.ppermute(o_far, "row", beside)
     o_cross = exchanged(mine, middles)
-    o_far_y = swapped(o_far, "groups", middles)
+    o_far_y = swapped(o_far, "groups")
     here, there = group * half, (1 - group) * half
     queries, keys, values = project_late(
         ints(0, here, 0, there, features, here, features, there, *blocks),
@@ -599,59 +628,48 @@
     def attended(index, *earlier):
         return attend(blocks[index].astype(jnp.int32), index, queries, keys, values, earlier)
 
-    cross_part = attended(2)
-    to_cross = exchanged(cross_part, middles)
-    shown, o_end_far, o_cross = settle(cross_part, o_end_far, o_cross)
-    o_end_cross = lax.ppermute(o_cross, "row", beside)
-    o_end_far_y = swapped(o_end_far, "groups", ends)
-    o_cross_y = swapped(o_cross, "groups", middles)
-    near_part = attended(1, shown)
-    to_near = lax.ppermute(near_part, "row", beside)
-    far_part = attended(3, near_part, o_far_y)
-    to_far = lax.ppermute(far_part, "row", outside)
-    own_part = attended(0, far_part, to_cross, o_end_far_y)
-    this_side = jnp.where(in_middle, own_part, to_near)
-    this_across = swapped(this_side, "col")
-    that_side = jnp.where(in_middle, to_cross, after(to_far, own_part))
-    that_across = swapped(that_side, "col")
-    o_end_cross_y = swapped(after(o_end_cross, own_part), "groups", ends)
-
-    pair_block = jnp.bitwise_xor(row, 1)
-    out_pieces, out_table = [], []
-
-    def put(piece, column, columns, block, which, offset, here):
-        spot = (2 * slot(block) + jnp.bitwise_xor(which, upper)) * depth + offset
-        out_pieces.append((piece, column, columns))
-        out_table.append(spot if here is None else jnp.where(here, spot, 8 * depth))
-
-    for part in range(2):
-        put(turned, part, depth, row, part, 0, None)
-    put(o_in, 0, depth, pair_block, group, 0, None)
-    put(o_in_rest, 0, depth, pair_block, 1 - group, 0, None)
-    put(o_far, 0, depth, 3 - pair_block, group, 0, in_middle)
-    put(o_far_y, 0, depth, 3 - pair_block, 1 - group, 0, in_middle)
-    put(o_end_far, 0, depth, 3 - row, group, 0, ~in_middle)
-    put(o_end_far_y, 0, depth, 3 - row, 1 - group, 0, ~in_middle)
-    put(o_cross, 0, depth, 3 - row, group, 0, in_middle)
-    put(o_cross_y, 0, depth, 3 - row, 1 - group, 0, in_middle)
-    put(o_end_cross, 0, depth, 3 - pair_block, group, 0, ~in_middle)
-    put(o_end_cross_y, 0, depth, 3 - pair_block, 1 - group, 0, ~in_middle)
-
-    parts = (
-        this_side,
-        that_side,
-        swapped(this_side, "sub"),
-        swapped(that_side, "sub"),
-        this_across,
-        that_across,
-        swapped(this_across, "sub"),
-        swapped(that_across, "sub"),
-    )
-    branch, squares = output_product(ints(*out_table), parts, out_pieces)
-    diagonal = lax.ppermute(squares, ("col", "sub"), [(0, 3), (1, 2), (2, 1), (3, 0)])
-    squares = squares + swapped(squares, "sub") + swapped(squares, "col") + diagonal
-    scaled = branch * lax.rsqrt(squares / MODEL_WIDTH + EPSILON) * post_gain[:, None]
-    return (stream.astype(jnp.float32) + scaled).astype(jnp.bfloat16).T
+    far_part = attended(3)
+    got_far = exchanged(far_part, middles)
+    near_part = attended(1, far_part, o_far_y)
+    near_col, near_sub = swapped(near_part, "col"), swapped(near_part, "sub")
+    o_cross_y = swapped(after(o_cross, far_part), "groups")
+    cross_part = attended(2, near_part)
+    got_cross = exchanged(cross_part, middles)
+    own_part = attended(0, cross_part)
+    got_far = after(got_far, cross_part, near_col)
+    far_col, far_sub = swapped(got_far, "col"), swapped(got_far, "sub")
+    far_both = swapped(after(far_col, got_cross, own_part, o_cross_y), "sub")
+    cross_col, cross_sub = swapped(got_cross, "col"), swapped(got_cross, "sub")
+    own_col, own_sub = swapped(own_part, "col"), swapped(own_part, "sub")
+
+    pieces = (turned, turned, o_in, o_in_rest, o_far, o_far_y, o_cross, o_cross_y)
+    out_pieces = [(piece, int(index == 1), depth) for index, piece in enumerate(pieces)]
+
+    def projected(table, residual, this_side, that_side, *earlier):
+        parts = [part for pair in zip(this_side, that_side) for part in pair]
+        branch, squares = output_product(table, parts, out_pieces)
+        diagonal = lax.ppermute(squares, ("col", "sub"), [(0, 3), (1, 2), (2, 1), (3, 0)])
+        total = squares + swapped(squares, "sub") + swapped(squares, "col") + diagonal
+        if earlier:
+            total = after(total, *earlier)
+        scaled = branch * lax.rsqrt(total / MODEL_WIDTH + EPSILON) * post_gain[:, None]
+        return (residual.astype(jnp.float32) + scaled).astype(jnp.bfloat16), branch
+
+    near_out, near_branch = projected(
+        after(place_table, own_part),
+        x_near,
+        (near_part, near_sub, near_col, swapped(near_col, "sub")),
+        (got_far, far_sub, far_col, far_both),
+        cross_col,
+    )
+    outer = lax.ppermute(near_out, "row", beside)
+    own_out, _ = projected(
+        after(place_table, near_branch),
+        stream,
+        (own_part, own_sub, own_col, swapped(own_col, "sub")),
+        (got_cross, cross_sub, cross_col, swapped(cross_col, "sub")),
+    )
+    return jnp.where(in_middle, own_out, outer).T
 
 
 def on_device(*args):
@@ -662,6 +680,7 @@
         sizes == (2, 4, 2, 2)
         and head == 128
         and tokens % 256 == 0
+        and WINDOW_LENGTH % (tokens // 2) == 0
         and key_matrix.shape[1] % (2 * head) == 0
         and query_weight.shape[1] == 2 * key_matrix.shape[1]
         and value_matrix.shape[1] == key_matrix.shape[1]

time: 307 us -> 305 us (level); the launches traced: 306 us -> 300 us
  waiting for transfers between devices: 131 us -> 113 us
  Pallas kernels: 115 us -> 122 us
  other arithmetic: 11.9 us -> 16 us
    ppermute x9 -> x3, waiting for transfers between devices: 31.4 us -> 4.28 us  [the longest x1 2.92 us: middle_form(): outer = lax.ppermute(near_out, 'row', beside)]
    ppermute x23 -> x33, waiting for transfers between devices: 42.8 us -> 66.2 us  [swapped(): return lax.ppermute(x, axis, [(0, 1), (1, 0)])]
    ppermute x1, waiting for transfers between devices: 20.7 us -> 1.36 us  [middle_form(): o_in = lax.ppermute(mine, 'row', beside)]
    ppermute x1, waiting for transfers between devices: 1.57 us -> 20.1 us  [middle_form(): x_near = lax.ppermute(stream, 'row', beside)]
    ppermute x1, waiting for transfers between devices: 13.4 us -> 1.52 us  [middle_form(): o_in_rest = lax.ppermute(theirs, 'row', beside)]
    pallas_call x5 -> x6, Pallas kernels: 41.4 us -> 48.6 us  [the longest x2 25 us: output_product(): pl.pallas_call(functools.partial(output_kernel, len(pieces)), grid_spec=p...]
    ppermute x9 -> x3, starting transfers between devices: 8.91 us -> 2.51 us  [the longest x2 2.17 us: projected(): lax.ppermute(squares, ('col', 'sub'), [(0, 3), (1, 2), (2, 1), (3, 0)])]
    ppermute x23 -> x33, starting transfers between devices: 14.7 us -> 19.3 us  [swapped(): return lax.ppermute(x, axis, [(0, 1), (1, 0)])]
  transfers between devices with their start and end apart: 43 -> 48, of which waited for: 23 -> 22; matrix products, arithmetic and copies ran while one was open for 6% -> 7% of each run, Pallas kernels for 33% -> 41%
where the time goes in v5:
time: 305 us; the launch traced here: 300 us
  Pallas kernels  122 us (40%)
  waiting for transfers between devices  113 us (37%)
  starting transfers between devices  33.2 us (11%)
  other arithmetic  16 us (5%)
  local copies, waits for them, and re-layouts  14.2 us (5%)
    ppermute x33, waiting for transfers between devices, swapped(): return lax.ppermute(x, axis, [(0, 1), (1, 0)])  66.2 us
    pallas_call x4, Pallas kernels, norm_block(): pl.pallas_call(norm_kernel, grid_spec=pltpu.PrefetchScalarGridSpec(num_sc...  28.2 us
    pallas_call x2, Pallas kernels, output_product(): pl.pallas_call(functools.partial(output_kernel, len(pieces)), grid_spec=p...  25 us
    pallas_call x2, Pallas kernels, project_early(): pl.pallas_call(functools.partial(project_early_kernel, len(pieces)), grid...  24.4 us
    pallas_call x4, Pallas kernels, attend(): pl.pallas_call(functools.partial(attend_kernel, float(MODEL_WIDTH // QUER...  23.6 us
    pallas_call x1, Pallas kernels, project_late(): pl.pallas_call(functools.partial(project_late_kernel, count), grid_spec=p...  21 us
    ppermute x1, waiting for transfers between devices, middle_form(): x_near = lax.ppermute(stream, 'row', beside)  20.1 us
    ppermute x33, starting transfers between devices, swapped(): return lax.ppermute(x, axis, [(0, 1), (1, 0)])  19.3 us
  transfers between devices with their start and end apart: 48, of which 22 were waited for; matrix products, arithmetic and copies ran while one was open for 7% of the time, Pallas kernels for 41%

profile of v5, /device:TPU:0, one launch (start us, length us, event | category | flops | bytes accessed | tf_op | source)
XLA Modules:
  0.0 299.7 jit_solution(8560338274319951803)
XLA Ops:
  0.5 4.1 %collective-permute-start.1 = (bf16[1344,512]{1,0:T(8,128)(2,1)}, bf16[1344,512]{1,0:T(8,128)(2,1)}, u32[]{:S(2)}, u32[]{:S(2)}) collective-permute-start(bf16[1344,512]{1,0:T(8,128)(2,1)} %bitcast.49), channel_id=1, source_target_pairs={{0,4},{4,0},{8,12},{12,8},{1,5},{5,1},{9,13},{13,9},{2,6},{6,2},{1... | collective-permute-start | bytes 4128776 | tf_op jit(solution)/shard_map/ppermute | solution.py:549
  6.1 3.6 %dynamic-slice_bitcast_fusion = (bf16[1344,512]{1,0:T(8,128)(2,1)}, bf16[1344,512]{1,0:T(8,128)(2,1)}) fusion(bf16[1024,1344]{0,1:T(8,128)(2,1)} %param.16, s32[]{:T(128)S(6)} %select_n.107, s32[]{:T(128)S(6)} %select_n.102), kind=kLoop, calls=%fused_computation.6 | loop fusion | bytes 5505032 | tf_op jit(solution)/shard_map/dynamic_slice | solution.py:532
  11.5 3.2 %broadcast_select_fusion = (bf16[1344,512]{1,0:T(8,128)(2,1)}, bf16[1344,512]{1,0:T(8,128)(2,1)}, bf16[1344,512]{1,0:T(8,128)(2,1)}, bf16[1344,512]{1,0:T(8,128)(2,1)}) fusion(pred[]{:T(512)S(6)} %eq.60, bf16[1344,256]{1,0:T(8,128)(2,1)S(1)} %get-tuple-element.116, bf16[1344,256]{1,0:T(8,128)(2,1)S(1)} %get-tuple-element.123, ...), kind=kLoop, calls=%fused_computation.8 | loop fusion | flops 6881280 | bytes 11010057 | tf_op jit(solution)/shard_map/jit(_where)/select_n | solution.py:527
  14.7 20.1 %collective-permute-done.1 = bf16[1344,512]{1,0:T(8,128)(2,1)} collective-permute-done((bf16[1344,512]{1,0:T(8,128)(2,1)}, bf16[1344,512]{1,0:T(8,128)(2,1)}, u32[]{:S(2)}, u32[]{:S(2)}) %collective-permute-start.1) | collective-permute-done | bytes 1376288 | tf_op jit(solution)/shard_map/ppermute | solution.py:549
  36.7 2.0 collective-permute-start.4
  41.5 2.8 multiply_sine_fusion
  45.9 2.3 copy.14.refs_4_.refs_5_
  49.3 7.1 %shard_map.91.refs_0_ = bf16[4,5376,512]{2,1,0:T(8,128)(2,1)} custom-call(s32[4]{0:T(128)} %pad_add_fusion.table, bf16[1,1344,512]{2,1,0:T(8,128)(2,1)} %bitcast.52, bf16[1,1344,512]{2,1,0:T(8,128)(2,1)} %bitcast.58, bf16[1,1344,512]{2,1,0:T(8,128)(2,1)} %bitcast.57, bf16[1,1344,512]{2,1,0:T(8,128)(2,1)} %bitcast.23.refs_3_, f32[4,1344,1]{2,1,0:T(8,128)} %copy.14.refs_4_.refs_5_), custom_call_target="tpu_custom_call" | custom-call | flops 27525120 | bytes 11010048 | tf_op jit(solution)/shard_map/pallas_call | solution.py:191
  56.4 13.2 %collective-permute-done.4.refs_2_ = bf16[1344,512]{1,0:T(8,128)(2,1)} collective-permute-done((bf16[1344,512]{1,0:T(8,128)(2,1)}, bf16[1344,512]{1,0:T(8,128)(2,1)}, u32[]{:S(2)}, u32[]{:S(2)}) %collective-permute-start.4) | collective-permute-done | bytes 1376288 | tf_op jit(solution)/shard_map/ppermute | solution.py:557
  75.1 7.1 %shard_map.92.refs_0_ = bf16[4,5376,512]{2,1,0:T(8,128)(2,1)} custom-call(s32[4]{0:T(128)} %pad_add_fusion.table, bf16[4,5376,512]{2,1,0:T(8,128)(2,1)} %shard_map.91.refs_0_, bf16[1,1344,512]{2,1,0:T(8,128)(2,1)} %bitcast.25.refs_1_, bf16[1,1344,512]{2,1,0:T(8,128)(2,1)} %bitcast.26.refs_2_, ...), custom_call_target="tpu_custom_call", output_to_operand_aliasing={{}: (1, {})} | custom-call | flops 27525120 | bytes 11010048 | tf_op jit(solution)/shard_map/pallas_call | solution.py:191
  82.1 23.6 %collective-permute-done.9.refs_3_ = bf16[1344,512]{1,0:T(8,128)(2,1)} collective-permute-done((bf16[1344,512]{1,0:T(8,128)(2,1)}, bf16[1344,512]{1,0:T(8,128)(2,1)}, u32[]{:S(2)}, u32[]{:S(2)}) %collective-permute-start.9) | collective-permute-done | bytes 1376288 | tf_op jit(solution)/shard_map/ppermute | solution.py:136
  111.3 7.0 %shard_map.93.normed.refs_0_ = bf16[4,5376,512]{2,1,0:T(8,128)(2,1)} custom-call(s32[4]{0:T(128)} %pad_add_fusion.table, bf16[4,5376,512]{2,1,0:T(8,128)(2,1)} %shard_map.92.refs_0_, bf16[1,1344,512]{2,1,0:T(8,128)(2,1)} %bitcast.30.refs_1_, bf16[1,1344,512]{2,1,0:T(8,128)(2,1)} %bitcast.31.refs_2_, ...), custom_call_target="tpu_custom_call", output_to_operand_aliasing={{}: (1, {})} | custom-call | flops 27525120 | bytes 11010048 | tf_op jit(solution)/shard_map/pallas_call | solution.py:191
  118.4 15.4 %shard_map.94.refs_4_ = f32[4,1024,512]{2,1,0:T(8,128)} custom-call(s32[8]{0:T(128)} %stack.88.table, bf16[4,5376,512]{2,1,0:T(8,128)(2,1)} %shard_map.93.normed.refs_0_, bf16[1344,512]{1,0:T(8,128)(2,1)} %get-tuple-element.108.refs_0_, bf16[1344,512]{1,0:T(8,128)(2,1)} %get-tuple-element.112.refs_1_, bf16[1344,512]{1,0:T(8,128)(2,1)} %collective-permute-done.4.refs_2_, ...), custom_call_target="tpu_custom_call" | custom-call | flops 8455716864 | bytes 20054016 | tf_op jit(solution)/shard_map/pallas_call | solution.py:235
  133.8 6.7 %collective-permute-done.17.refs_0_ = bf16[1344,512]{1,0:T(8,128)(2,1)} collective-permute-done((bf16[1344,512]{1,0:T(8,128)(2,1)}, bf16[1344,512]{1,0:T(8,128)(2,1)}, u32[]{:S(2)}, u32[]{:S(2)}) %collective-permute-start.17) | collective-permute-done | bytes 1376288 | tf_op jit(solution)/shard_map/ppermute | solution.py:596
  143.5 1.7 collective-permute-start.23
  145.9 7.0 %shard_map.95.normed = bf16[4,5376,512]{2,1,0:T(8,128)(2,1)} custom-call(s32[4]{0:T(128)} %pad_add_fusion.table, bf16[4,5376,512]{2,1,0:T(8,128)(2,1)} %shard_map.93.normed.refs_0_, bf16[1,1344,512]{2,1,0:T(8,128)(2,1)} %bitcast.34.refs_1_, bf16[1,1344,512]{2,1,0:T(8,128)(2,1)} %bitcast.35.refs_2_, ...), custom_call_target="tpu_custom_call", output_to_operand_aliasing={{}: (1, {})} | custom-call | flops 27525120 | bytes 11010048 | tf_op jit(solution)/shard_map/pallas_call | solution.py:191
  152.9 9.0 %shard_map.96.refs_4_ = f32[4,1024,512]{2,1,0:T(8,128)} custom-call(s32[8]{0:T(128)} %stack.88.table, bf16[4,5376,512]{2,1,0:T(8,128)(2,1)} %shard_map.95.normed, bf16[1344,512]{1,0:T(8,128)(2,1)} %get-tuple-element.108.refs_0_, bf16[1344,512]{1,0:T(8,128)(2,1)} %get-tuple-element.112.refs_1_, ...), custom_call_target="tpu_custom_call", output_to_operand_aliasing={{}: (6, {})} | custom-call | flops 2818572288 | bytes 10354688 | tf_op jit(solution)/shard_map/pallas_call | solution.py:235
  161.9 12.8 %collective-permute-done.21.refs_1_ = bf16[1344,512]{1,0:T(8,128)(2,1)} collective-permute-done((bf16[1344,512]{1,0:T(8,128)(2,1)}, bf16[1344,512]{1,0:T(8,128)(2,1)}, u32[]{:S(2)}, u32[]{:S(2)}) %collective-permute-start.21) | collective-permute-done | bytes 1376288 | tf_op jit(solution)/shard_map/ppermute | solution.py:136
  176.7 21.0 %shard_map.97 = (bf16[4,512,512]{2,1,0:T(8,128)(2,1)}, bf16[2048,256]{1,0:T(8,128)(2,1)}, bf16[256,2048]{1,0:T(8,128)(2,1)}) custom-call(s32[12]{0:T(128)} %stack.87.table, bf16[4,5376,512]{2,1,0:T(8,128)(2,1)} %shard_map.95.normed, bf16[1344,512]{1,0:T(8,128)(2,1)} %collective-permute-done.17.refs_0_, bf16[1344,512]{1,0:T(8,128)(2,1)} %collective-permute-done.21.refs_1_, ...), custom_call_target="tpu_custom_call" | custom-call | flops 11274289152 | bytes 24903680 | tf_op jit(solution)/shard_map/pallas_call | solution.py:299
  197.7 7.2 %shard_map.98.refs_0_ = bf16[512,512]{1,0:T(8,128)(2,1)} custom-call(s32[1]{0:T(128)} %bitcast.18.table, bf16[4,512,512]{2,1,0:T(8,128)(2,1)} %get-tuple-element.92.q_ref, bf16[2048,256]{1,0:T(8,128)(2,1)} %get-tuple-element.93.keys, bf16[256,2048]{1,0:T(8,128)(2,1)} %get-tuple-element.94.values), custom_call_target="tpu_custom_call" | custom-call | flops 4026531840 | bytes 3145728 | tf_op jit(solution)/shard_map/pallas_call | solution.py:412
  208.0 4.6 %shard_map.99.refs_0_ = bf16[512,512]{1,0:T(8,128)(2,1)} custom-call(s32[1]{0:T(128)} %bitcast.16.table, bf16[4,512,512]{2,1,0:T(8,128)(2,1)} %get-tuple-element.92.q_ref, bf16[2048,256]{1,0:T(8,128)(2,1)} %get-tuple-element.93.keys, bf16[256,2048]{1,0:T(8,128)(2,1)} %get-tuple-element.94.values, bf16[512,512]{1,0:T(8,128)(2,1)} %shard_map.98.refs_0_, ...), custom_call_target="tpu_custom_call" | custom-call | flops 4026531840 | bytes 3145728 | tf_op jit(solution)/shard_map/pallas_call | solution.py:412
  213.2 7.3 %shard_map.100.refs_0_ = bf16[512,512]{1,0:T(8,128)(2,1)} custom-call(s32[1]{0:T(128)} %bitcast.17.table, bf16[4,512,512]{2,1,0:T(8,128)(2,1)} %get-tuple-element.92.q_ref, bf16[2048,256]{1,0:T(8,128)(2,1)} %get-tuple-element.93.keys, bf16[256,2048]{1,0:T(8,128)(2,1)} %get-tuple-element.94.values, bf16[512,512]{1,0:T(8,128)(2,1)} %shard_map.99.refs_0_), custom_call_target="tpu_custom_call" | custom-call | flops 4026531840 | bytes 3145728 | tf_op jit(solution)/shard_map/pallas_call | solution.py:412
  220.4 4.9 %collective-permute-done.26.refs_4_ = bf16[512,512]{1,0:T(8,128)(2,1)} collective-permute-done((bf16[512,512]{1,0:T(8,128)(2,1)}, bf16[512,512]{1,0:T(8,128)(2,1)}, u32[]{:S(2)}, u32[]{:S(2)}) %collective-permute-start.26) | collective-permute-done | bytes 524320 | tf_op jit(solution)/shard_map/ppermute | solution.py:136
  225.8 4.6 %shard_map.101.refs_0_ = bf16[512,512]{1,0:T(8,128)(2,1)} custom-call(s32[1]{0:T(128)} %bitcast.13.table, bf16[4,512,512]{2,1,0:T(8,128)(2,1)} %get-tuple-element.92.q_ref, bf16[2048,256]{1,0:T(8,128)(2,1)} %get-tuple-element.93.keys, bf16[256,2048]{1,0:T(8,128)(2,1)} %get-tuple-element.94.values, bf16[512,512]{1,0:T(8,128)(2,1)} %shard_map.100.refs_0_), custom_call_target="tpu_custom_call" | custom-call | flops 4026531840 | bytes 3145728 | tf_op jit(solution)/shard_map/pallas_call | solution.py:412
  231.0 6.8 %collective-permute-done.33.refs_15_ = bf16[1344,512]{1,0:T(8,128)(2,1)} collective-permute-done((bf16[1344,512]{1,0:T(8,128)(2,1)}, bf16[1344,512]{1,0:T(8,128)(2,1)}, u32[]{:S(2)}, u32[]{:S(2)}) %collective-permute-start.33) | collective-permute-done | bytes 1376288 | tf_op jit(solution)/shard_map/ppermute | solution.py:136
  241.5 12.6 %shard_map.102 = (f32[1344,512]{1,0:T(8,128)}, f32[1,512]{1,0:T(1,128)}) custom-call(s32[8]{0:T(128)} %stack.81.table, bf16[512,512]{1,0:T(8,128)(2,1)} %shard_map.99.refs_0_, bf16[512,512]{1,0:T(8,128)(2,1)} %collective-permute-done.25.refs_1_, bf16[512,512]{1,0:T(8,128)(2,1)} %collective-permute-done.27.refs_2_, bf16[512,512]{1,0:T(8,128)(2,1)} %copy-done.11, ...), custom_call_target="tpu_custom_call" | custom-call | flops 5637144576 | bytes 17956864 | tf_op jit(solution)/shard_map/pallas_call | solution.py:463
  259.6 3.8 %add_convert_fusion = bf16[1344,512]{1,0:T(8,128)(2,1)} fusion(f32[1344,512]{1,0:T(8,128)} %get-tuple-element.101, bf16[1344,512]{1,0:T(8,128)(2,1)} %collective-permute-done.1, f32[512]{0:T(512)S(1)} %bitcast.60, f32[1344]{0:T(1024)S(1)} %copy-done.5), kind=kLoop, calls=%fused_computation | loop fusion | flops 3440640 | bytes 5512448 | tf_op jit(solution)/shard_map/convert_element_type | solution.py:656
  264.3 6.2 %collective-permute-done.37.refs_4_ = bf16[512,512]{1,0:T(8,128)(2,1)S(1)} collective-permute-done((bf16[512,512]{1,0:T(8,128)(2,1)}, bf16[512,512]{1,0:T(8,128)(2,1)S(1)}, u32[]{:S(2)}, u32[]{:S(2)}) %collective-permute-start.37) | collective-permute-done | bytes 524320 | tf_op jit(solution)/shard_map/ppermute | solution.py:136
  271.3 1.8 collective-permute-done.39.refs_6_
  273.9 12.4 %shard_map.103 = (f32[1344,512]{1,0:T(8,128)}, f32[1,512]{1,0:T(1,128)}) custom-call(s32[8]{0:T(128)} %stack.81.table, bf16[512,512]{1,0:T(8,128)(2,1)} %shard_map.101.refs_0_, bf16[512,512]{1,0:T(8,128)(2,1)} %collective-permute-done.31.refs_1_, bf16[512,512]{1,0:T(8,128)(2,1)} %copy-done.12, bf16[512,512]{1,0:T(8,128)(2,1)} %copy-done.13, ...), custom_call_target="tpu_custom_call" | custom-call | flops 5637144576 | bytes 17956864 | tf_op jit(solution)/shard_map/pallas_call | solution.py:463
  291.9 2.9 collective-permute-done.47
  294.9 4.3 %fusion.1 = bf16[512,1344]{0,1:T(8,128)(2,1)} fusion(bf16[1344,512]{1,0:T(8,128)(2,1)} %collective-permute-done.47, f32[1344,512]{1,0:T(8,128)} %get-tuple-element.103, f32[1344]{0:T(1024)S(1)} %copy-done.5, f32[512]{0:T(512)S(1)} %bitcast.59, pred[]{:T(512)S(6)} %or.3, bf16[512,1344]{0,1:T(8,128)(2,1)} %param.9), kind=kLoop, calls=%fused_computation.3 | loop fusion | flops 4128768 | bytes 6888705 | tf_op jit(solution)/shard_map/transpose | solution.py:672
  (133 shorter events, 49.9 us)
Async XLA Ops:
  0.0 14.7 %collective-permute-start = (bf16[1344,512]{1,0:T(8,128)(2,1)}, bf16[1344,512]{1,0:T(8,128)(2,1)}, u32[]{:S(2)}, u32[]{:S(2)}) collective-permute-start(bf16[1344,512]{1,0:T(8,128)(2,1)} %bitcast.48), channel_id=1, source_target_pairs={{0,1},{1,0},{4,8},{5,9},{8,4},{9,5},{12,13},{13,12},{2,3},{3,2},{6... | collective-permute-start | bytes 4128776 | tf_op jit(solution)/shard_map/ppermute | solution.py:155
  0.5 34.4 %collective-permute-start.1 = (bf16[1344,512]{1,0:T(8,128)(2,1)}, bf16[1344,512]{1,0:T(8,128)(2,1)}, u32[]{:S(2)}, u32[]{:S(2)}) collective-permute-start(bf16[1344,512]{1,0:T(8,128)(2,1)} %bitcast.49), channel_id=1, source_target_pairs={{0,4},{4,0},{8,12},{12,8},{1,5},{5,1},{9,13},{13,9},{2,6},{6,2},{1... | collective-permute-start | bytes 4128776 | tf_op jit(solution)/shard_map/ppermute | solution.py:549
  4.6 31.6 %collective-permute-start.2 = (bf16[1344,512]{1,0:T(8,128)(2,1)}, bf16[1344,512]{1,0:T(8,128)(2,1)S(1)}, u32[]{:S(2)}, u32[]{:S(2)}) collective-permute-start(bf16[1344,512]{1,0:T(8,128)(2,1)} %bitcast.50), channel_id=1, source_target_pairs={{0,2},{2,0},{1,3},{3,1},{4,6},{6,4},{5,7},{7,5},{8,10},{10,8},{9,1... | collective-permute-start | bytes 4128776 | tf_op jit(solution)/shard_map/ppermute | solution.py:136
  6.1 42.1 %collective-permute-start.6 = (bf16[1344,512]{1,0:T(8,128)(2,1)}, bf16[1344,512]{1,0:T(8,128)(2,1)S(1)}, u32[]{:S(2)}, u32[]{:S(2)}) collective-permute-start(bf16[1344,512]{1,0:T(8,128)(2,1)} %bitcast.51), channel_id=1, source_target_pairs={{0,1},{1,0},{2,3},{3,2},{4,5},{5,4},{6,7},{7,6},{8,9},{9,8},{10,11... | collective-permute-start | bytes 4128776 | tf_op jit(solution)/shard_map/ppermute | solution.py:136
  36.2 12.1 %collective-permute-start.7 = (bf16[1344,512]{1,0:T(8,128)(2,1)S(1)}, bf16[1344,512]{1,0:T(8,128)(2,1)}, u32[]{:S(2)}, u32[]{:S(2)}) collective-permute-start(bf16[1344,512]{1,0:T(8,128)(2,1)S(1)} %collective-permute-done.2), channel_id=1, source_target_pairs={{0,1},{1,0},{2,3},{3,2},{4,5},{5,4},{6,7},{7,6},{8,9},{9,8},{10,11... | collective-permute-start | bytes 4128776 | tf_op jit(solution)/shard_map/ppermute | solution.py:136
  36.2 20.2 %collective-permute-start.3 = (bf16[1344,512]{1,0:T(8,128)(2,1)}, bf16[1344,512]{1,0:T(8,128)(2,1)}, u32[]{:S(2)}, u32[]{:S(2)}) collective-permute-start(bf16[1344,512]{1,0:T(8,128)(2,1)} %collective-permute-done.1), channel_id=1, source_target_pairs={{0,1},{1,0},{4,8},{5,9},{8,4},{9,5},{12,13},{13,12},{2,3},{3,2},{6... | collective-permute-start | bytes 4128776 | tf_op jit(solution)/shard_map/ppermute | solution.py:155
  36.7 32.9 %collective-permute-start.4 = (bf16[1344,512]{1,0:T(8,128)(2,1)}, bf16[1344,512]{1,0:T(8,128)(2,1)}, u32[]{:S(2)}, u32[]{:S(2)}) collective-permute-start(bf16[1344,512]{1,0:T(8,128)(2,1)} %get-tuple-element.59), channel_id=1, source_target_pairs={{0,4},{4,0},{8,12},{12,8},{1,5},{5,1},{9,13},{13,9},{2,6},{6,2},{1... | collective-permute-start | bytes 4128776 | tf_op jit(solution)/shard_map/ppermute | solution.py:557
  38.7 32.3 %collective-permute-start.5 = (bf16[1344,512]{1,0:T(8,128)(2,1)}, bf16[1344,512]{1,0:T(8,128)(2,1)}, u32[]{:S(2)}, u32[]{:S(2)}) collective-permute-start(bf16[1344,512]{1,0:T(8,128)(2,1)} %collective-permute-done.1), channel_id=1, source_target_pairs={{0,2},{2,0},{1,3},{3,1},{4,6},{6,4},{5,7},{7,5},{8,10},{10,8},{9,1... | collective-permute-start | bytes 4128776 | tf_op jit(solution)/shard_map/ppermute | solution.py:136
  48.2 24.8 %collective-permute-start.11 = (bf16[1344,512]{1,0:T(8,128)(2,1)}, bf16[1344,512]{1,0:T(8,128)(2,1)}, u32[]{:S(2)}, u32[]{:S(2)}) collective-permute-start(bf16[1344,512]{1,0:T(8,128)(2,1)} %collective-permute-done.1), channel_id=1, source_target_pairs={{0,1},{1,0},{2,3},{3,2},{4,5},{5,4},{6,7},{7,6},{8,9},{9,8},{10,11... | collective-permute-start | bytes 4128776 | tf_op jit(solution)/shard_map/ppermute | solution.py:136
  71.1 34.6 %collective-permute-start.10 = (bf16[1344,512]{1,0:T(8,128)(2,1)}, bf16[1344,512]{1,0:T(8,128)(2,1)}, u32[]{:S(2)}, u32[]{:S(2)}) collective-permute-start(bf16[1344,512]{1,0:T(8,128)(2,1)} %collective-permute-done), channel_id=1, source_target_pairs={{0,2},{2,0},{1,3},{3,1},{4,6},{6,4},{5,7},{7,5},{8,10},{10,8},{9,1... | collective-permute-start | bytes 4128776 | tf_op jit(solution)/shard_map/ppermute | solution.py:136
  72.6 33.1 %collective-permute-start.13 = (bf16[1344,512]{1,0:T(8,128)(2,1)}, bf16[1344,512]{1,0:T(8,128)(2,1)}, u32[]{:S(2)}, u32[]{:S(2)}) collective-permute-start(bf16[1344,512]{1,0:T(8,128)(2,1)} %collective-permute-done), channel_id=1, source_target_pairs={{0,1},{1,0},{2,3},{3,2},{4,5},{5,4},{6,7},{7,6},{8,9},{9,8},{10,11... | collective-permute-start | bytes 4128776 | tf_op jit(solution)/shard_map/ppermute | solution.py:136
  72.8 9.3 %collective-permute-start.8 = (bf16[1344,512]{1,0:T(8,128)(2,1)}, bf16[1344,512]{1,0:T(8,128)(2,1)}, u32[]{:S(2)}, u32[]{:S(2)}) collective-permute-start(bf16[1344,512]{1,0:T(8,128)(2,1)} %get-tuple-element.75), channel_id=1, source_target_pairs={{0,1},{1,0},{4,8},{5,9},{8,4},{9,5},{12,13},{13,12},{2,3},{3,2},{6... | collective-permute-start | bytes 4128776 | tf_op jit(solution)/shard_map/ppermute | solution.py:155
  73.1 32.6 %collective-permute-start.9 = (bf16[1344,512]{1,0:T(8,128)(2,1)}, bf16[1344,512]{1,0:T(8,128)(2,1)}, u32[]{:S(2)}, u32[]{:S(2)}) collective-permute-start(bf16[1344,512]{1,0:T(8,128)(2,1)} %collective-permute-done.4.refs_2_), channel_id=1, source_target_pairs={{0,16},{16,0},{1,17},{17,1},{2,18},{18,2},{3,19},{19,3},{4,20},{20... | collective-permute-start | bytes 4128776 | tf_op jit(solution)/shard_map/ppermute | solution.py:136
  74.6 32.5 %collective-permute-start.14 = (bf16[1344,512]{1,0:T(8,128)(2,1)}, bf16[1344,512]{1,0:T(8,128)(2,1)}, u32[]{:S(2)}, u32[]{:S(2)}) collective-permute-start(bf16[1344,512]{1,0:T(8,128)(2,1)} %get-tuple-element.70), channel_id=1, source_target_pairs={{0,4},{4,0},{8,12},{12,8},{1,5},{5,1},{9,13},{13,9},{2,6},{6,2},{1... | collective-permute-start | bytes 4128776 | tf_op jit(solution)/shard_map/ppermute | solution.py:585
  107.1 33.4 %collective-permute-start.17 = (bf16[1344,512]{1,0:T(8,128)(2,1)}, bf16[1344,512]{1,0:T(8,128)(2,1)}, u32[]{:S(2)}, u32[]{:S(2)}) collective-permute-start(bf16[1344,512]{1,0:T(8,128)(2,1)} %get-tuple-element.75), channel_id=1, source_target_pairs={{0,8},{4,0},{8,12},{12,4},{1,9},{5,1},{9,13},{13,5},{2,10},{6,2},{... | collective-permute-start | bytes 4128776 | tf_op jit(solution)/shard_map/ppermute | solution.py:596
  108.6 32.6 %collective-permute-start.18 = (bf16[1344,512]{1,0:T(8,128)(2,1)}, bf16[1344,512]{1,0:T(8,128)(2,1)}, u32[]{:S(2)}, u32[]{:S(2)}) collective-permute-start(bf16[1344,512]{1,0:T(8,128)(2,1)} %collective-permute-done.3), channel_id=1, source_target_pairs={{0,2},{2,0},{1,3},{3,1},{4,6},{6,4},{5,7},{7,5},{8,10},{10,8},{9,1... | collective-permute-start | bytes 4128776 | tf_op jit(solution)/shard_map/ppermute | solution.py:136
  109.2 32.6 %collective-permute-start.19 = (bf16[1344,512]{1,0:T(8,128)(2,1)}, bf16[1344,512]{1,0:T(8,128)(2,1)}, u32[]{:S(2)}, u32[]{:S(2)}) collective-permute-start(bf16[1344,512]{1,0:T(8,128)(2,1)} %collective-permute-done.8.refs_2_), channel_id=1, source_target_pairs={{0,16},{16,0},{1,17},{17,1},{2,18},{18,2},{3,19},{19,3},{4,20},{20... | collective-permute-start | bytes 4128776 | tf_op jit(solution)/shard_map/ppermute | solution.py:136
  111.3 34.6 %collective-permute-start.16 = (bf16[1344,512]{1,0:T(8,128)(2,1)}, bf16[1344,512]{1,0:T(8,128)(2,1)}, u32[]{:S(2)}, u32[]{:S(2)}) collective-permute-start(bf16[1344,512]{1,0:T(8,128)(2,1)} %collective-permute-done.3), channel_id=1, source_target_pairs={{0,1},{1,0},{2,3},{3,2},{4,5},{5,4},{6,7},{7,6},{8,9},{9,8},{10,11... | collective-permute-start | bytes 4128776 | tf_op jit(solution)/shard_map/ppermute | solution.py:136
  141.7 32.9 %collective-permute-start.21 = (bf16[1344,512]{1,0:T(8,128)(2,1)}, bf16[1344,512]{1,0:T(8,128)(2,1)}, u32[]{:S(2)}, u32[]{:S(2)}) collective-permute-start(bf16[1344,512]{1,0:T(8,128)(2,1)} %collective-permute-done.17.refs_0_), channel_id=1, source_target_pairs={{0,16},{16,0},{1,17},{17,1},{2,18},{18,2},{3,19},{19,3},{4,20},{20... | collective-permute-start | bytes 4128776 | tf_op jit(solution)/shard_map/ppermute | solution.py:136
  143.3 31.4 %collective-permute-start.22 = (bf16[1344,512]{1,0:T(8,128)(2,1)}, bf16[1344,512]{1,0:T(8,128)(2,1)}, u32[]{:S(2)}, u32[]{:S(2)}) collective-permute-start(bf16[1344,512]{1,0:T(8,128)(2,1)} %collective-permute-done.14.refs_10_), channel_id=1, source_target_pairs={{0,1},{1,0},{4,8},{5,9},{8,4},{9,5},{12,13},{13,12},{2,3},{3,2},{6... | collective-permute-start | bytes 4128776 | tf_op jit(solution)/shard_map/ppermute | solution.py:155
  143.5 32.7 %collective-permute-start.23 = (bf16[1344,512]{1,0:T(8,128)(2,1)}, bf16[1344,512]{1,0:T(8,128)(2,1)}, u32[]{:S(2)}, u32[]{:S(2)}) collective-permute-start(bf16[1344,512]{1,0:T(8,128)(2,1)} %get-tuple-element.84), channel_id=1, source_target_pairs={{0,4},{4,0},{8,12},{12,8},{1,5},{5,1},{9,13},{13,9},{2,6},{6,2},{1... | collective-permute-start | bytes 4128776 | tf_op jit(solution)/shard_map/ppermute | solution.py:612
  145.9 59.0 %collective-permute-start.32 = (bf16[1344,512]{1,0:T(8,128)(2,1)}, bf16[1344,512]{1,0:T(8,128)(2,1)}, u32[]{:S(2)}, u32[]{:S(2)}) collective-permute-start(bf16[1344,512]{1,0:T(8,128)(2,1)} %get-tuple-element.70), channel_id=1, source_target_pairs={{0,1},{1,0},{4,8},{5,9},{8,4},{9,5},{12,13},{13,12},{2,3},{3,2},{6... | collective-permute-start | bytes 4128776 | tf_op jit(solution)/shard_map/ppermute | solution.py:155
  176.2 31.9 %collective-permute-start.24 = (bf16[1344,512]{1,0:T(8,128)(2,1)}, bf16[1344,512]{1,0:T(8,128)(2,1)}, u32[]{:S(2)}, u32[]{:S(2)}) collective-permute-start(bf16[1344,512]{1,0:T(8,128)(2,1)} %collective-permute-done.22.refs_12_), channel_id=1, source_target_pairs={{0,16},{16,0},{1,17},{17,1},{2,18},{18,2},{3,19},{19,3},{4,20},{20... | collective-permute-start | bytes 4128776 | tf_op jit(solution)/shard_map/ppermute | solution.py:136
  204.8 15.6 %collective-permute-start.25 = (bf16[512,512]{1,0:T(8,128)(2,1)}, bf16[512,512]{1,0:T(8,128)(2,1)}, u32[]{:S(2)}, u32[]{:S(2)}) collective-permute-start(bf16[512,512]{1,0:T(8,128)(2,1)} %shard_map.98.refs_0_), channel_id=1, source_target_pairs={{0,1},{1,0},{4,8},{5,9},{8,4},{9,5},{12,13},{13,12},{2,3},{3,2},{6... | collective-permute-start | bytes 1572872 | tf_op jit(solution)/shard_map/ppermute | solution.py:155
  204.8 32.9 %collective-permute-start.33 = (bf16[1344,512]{1,0:T(8,128)(2,1)}, bf16[1344,512]{1,0:T(8,128)(2,1)}, u32[]{:S(2)}, u32[]{:S(2)}) collective-permute-start(bf16[1344,512]{1,0:T(8,128)(2,1)} %collective-permute-done.32.refs_14_), channel_id=1, source_target_pairs={{0,16},{16,0},{1,17},{17,1},{2,18},{18,2},{3,19},{19,3},{4,20},{20... | collective-permute-start | bytes 4128776 | tf_op jit(solution)/shard_map/ppermute | solution.py:136
  212.6 12.7 %collective-permute-start.26 = (bf16[512,512]{1,0:T(8,128)(2,1)}, bf16[512,512]{1,0:T(8,128)(2,1)}, u32[]{:S(2)}, u32[]{:S(2)}) collective-permute-start(bf16[512,512]{1,0:T(8,128)(2,1)} %shard_map.99.refs_0_), channel_id=1, source_target_pairs={{0,2},{2,0},{1,3},{3,1},{4,6},{6,4},{5,7},{7,5},{8,10},{10,8},{9,1... | collective-permute-start | bytes 1572872 | tf_op jit(solution)/shard_map/ppermute | solution.py:136
  220.4 17.3 %collective-permute-start.31 = (bf16[512,512]{1,0:T(8,128)(2,1)}, bf16[512,512]{1,0:T(8,128)(2,1)}, u32[]{:S(2)}, u32[]{:S(2)}) collective-permute-start(bf16[512,512]{1,0:T(8,128)(2,1)} %shard_map.100.refs_0_), channel_id=1, source_target_pairs={{0,1},{1,0},{4,8},{5,9},{8,4},{9,5},{12,13},{13,12},{2,3},{3,2},{6... | collective-permute-start | bytes 1572872 | tf_op jit(solution)/shard_map/ppermute | solution.py:155
  225.3 12.4 %collective-permute-start.29 = (bf16[512,512]{1,0:T(8,128)(2,1)}, bf16[512,512]{1,0:T(8,128)(2,1)}, u32[]{:S(2)}, u32[]{:S(2)}) collective-permute-start(bf16[512,512]{1,0:T(8,128)(2,1)} %collective-permute-done.25.refs_1_), channel_id=1, source_target_pairs={{0,2},{2,0},{1,3},{3,1},{4,6},{6,4},{5,7},{7,5},{8,10},{10,8},{9,1... | collective-permute-start | bytes 1572872 | tf_op jit(solution)/shard_map/ppermute | solution.py:136
  225.8 13.7 %collective-permute-start.27 = (bf16[512,512]{1,0:T(8,128)(2,1)}, bf16[512,512]{1,0:T(8,128)(2,1)}, u32[]{:S(2)}, u32[]{:S(2)}) collective-permute-start(bf16[512,512]{1,0:T(8,128)(2,1)} %shard_map.99.refs_0_), channel_id=1, source_target_pairs={{0,1},{1,0},{2,3},{3,2},{4,5},{5,4},{6,7},{7,6},{8,9},{9,8},{10,11... | collective-permute-start | bytes 1572872 | tf_op jit(solution)/shard_map/ppermute | solution.py:136
  238.3 21.3 %collective-permute-start.38 = (bf16[512,512]{1,0:T(8,128)(2,1)}, bf16[512,512]{1,0:T(8,128)(2,1)}, u32[]{:S(2)}, u32[]{:S(2)}) collective-permute-start(bf16[512,512]{1,0:T(8,128)(2,1)} %collective-permute-done.31.refs_1_), channel_id=1, source_target_pairs={{0,2},{2,0},{1,3},{3,1},{4,6},{6,4},{5,7},{7,5},{8,10},{10,8},{9,1... | collective-permute-start | bytes 1572872 | tf_op jit(solution)/shard_map/ppermute | solution.py:136
  256.0 14.5 %collective-permute-start.37 = (bf16[512,512]{1,0:T(8,128)(2,1)}, bf16[512,512]{1,0:T(8,128)(2,1)S(1)}, u32[]{:S(2)}, u32[]{:S(2)}) collective-permute-start(bf16[512,512]{1,0:T(8,128)(2,1)} %shard_map.101.refs_0_), channel_id=1, source_target_pairs={{0,2},{2,0},{1,3},{3,1},{4,6},{6,4},{5,7},{7,5},{8,10},{10,8},{9,1... | collective-permute-start | bytes 1572872 | tf_op jit(solution)/shard_map/ppermute | solution.py:136
  263.4 31.5 %collective-permute-start.47 = (bf16[1344,512]{1,0:T(8,128)(2,1)}, bf16[1344,512]{1,0:T(8,128)(2,1)}, u32[]{:S(2)}, u32[]{:S(2)}) collective-permute-start(bf16[1344,512]{1,0:T(8,128)(2,1)} %add_convert_fusion), channel_id=1, source_target_pairs={{0,4},{4,0},{8,12},{12,8},{1,5},{5,1},{9,13},{13,9},{2,6},{6,2},{1... | collective-permute-start | bytes 4128776 | tf_op jit(solution)/shard_map/ppermute | solution.py:665
  (33 other events, 216.6 us)

commit v6 on v5

--- a/solution.py
+++ b/solution.py
@@ -13,7 +13,7 @@
 
 
 EPSILON = 1e-06
-VMEM_BYTES = 64 * 1024 * 1024 - 128 * 1024
+MIB = 1024 * 1024
 
 
 def shifted(x, axis, by):
@@ -200,7 +200,7 @@
         ),
         out_shape=jax.ShapeDtypeStruct(shape, jnp.bfloat16),
         input_output_aliases={1: 0} if before else {},
-        compiler_params=pltpu.CompilerParams(vmem_limit_bytes=VMEM_BYTES),
+        compiler_params=pltpu.CompilerParams(vmem_limit_bytes=44 * MIB),
         cost_estimate=pl.CostEstimate(
             flops=40 * depth * tokens, bytes_accessed=16 * depth * tokens, transcendentals=0
         ),
@@ -245,7 +245,7 @@
         ),
         out_shape=jax.ShapeDtypeStruct((4, width, tokens), jnp.float32),
         input_output_aliases={2 + len(pieces): 0} if before else {},
-        compiler_params=pltpu.CompilerParams(vmem_limit_bytes=VMEM_BYTES),
+        compiler_params=pltpu.CompilerParams(vmem_limit_bytes=44 * MIB),
         cost_estimate=pl.CostEstimate(
             flops=2 * blocks * tokens * features // 2 * width,
             bytes_accessed=blocks * features * tokens + features * width + 4 * blocks * width * tokens,
@@ -325,7 +325,7 @@
             jax.ShapeDtypeStruct((blocks * tokens, width // 2), jnp.bfloat16),
             jax.ShapeDtypeStruct((width // 2, blocks * tokens), jnp.bfloat16),
         ],
-        compiler_params=pltpu.CompilerParams(vmem_limit_bytes=VMEM_BYTES),
+        compiler_params=pltpu.CompilerParams(vmem_limit_bytes=48 * MIB),
         cost_estimate=pl.CostEstimate(
             flops=2 * blocks * tokens * features * width,
             bytes_accessed=blocks * features * tokens + 2 * features * width + 8 * blocks * width * tokens,
@@ -424,7 +424,7 @@
             scratch_shapes=[pltpu.VMEM((2, tile, 2 * tile), jnp.float32)],
         ),
         out_shape=jax.ShapeDtypeStruct((width, tokens), jnp.bfloat16),
-        compiler_params=pltpu.CompilerParams(vmem_limit_bytes=VMEM_BYTES),
+        compiler_params=pltpu.CompilerParams(vmem_limit_bytes=28 * MIB),
         cost_estimate=pl.CostEstimate(
             flops=12 * tokens * (WINDOW_LENGTH + tile) * width,
             bytes_accessed=4 * tokens * width + 4 * keys.shape[0] * keys.shape[1],
@@ -477,7 +477,7 @@
             jax.ShapeDtypeStruct((width, tokens), jnp.float32),
             jax.ShapeDtypeStruct((1, tokens), jnp.float32),
         ],
-        compiler_params=pltpu.CompilerParams(vmem_limit_bytes=VMEM_BYTES),
+        compiler_params=pltpu.CompilerParams(vmem_limit_bytes=32 * MIB),
         cost_estimate=pl.CostEstimate(
             flops=2 * tokens * full * width,
             bytes_accessed=2 * full * (tokens + width) + 4 * tokens * width,

time: 305 us -> 299 us (0.980)
  Pallas kernels: 122 us -> 98.4 us
  waiting for transfers between devices: 113 us -> 130 us
  other arithmetic: 16 us -> 12.9 us
    ppermute x33, waiting for transfers between devices: 66.2 us -> 77.4 us  [swapped(): return lax.ppermute(x, axis, [(0, 1), (1, 0)])]
    pallas_call x4, Pallas kernels: 23.6 us -> 15.8 us  [attend(): pl.pallas_call(functools.partial(attend_kernel, float(MODEL_WIDTH // QUER...]
    unnamed x34 -> x52, local copies, waits for them, and re-layouts: 4.56 us -> 11 us
    pallas_call x2, Pallas kernels: 25 us -> 18.8 us  [output_product(): pl.pallas_call(functools.partial(output_kernel, len(pieces)), grid_spec=p...]
    pallas_call x4, Pallas kernels: 28.2 us -> 22.3 us  [norm_block(): pl.pallas_call(norm_kernel, grid_spec=pltpu.PrefetchScalarGridSpec(num_sc...]
    ppermute x1, waiting for transfers between devices: 13.2 us -> 18.2 us  [middle_form(): w_near = lax.ppermute(own_side, 'row', beside)]
  transfers between devices with their start and end apart: 48 -> 48, of which waited for: 22 -> 22; matrix products, arithmetic and copies ran while one was open for 7% -> 5% of each run, Pallas kernels for 41% -> 33%
where the time goes in v6:
time: 299 us; the launch traced here: 294 us
  waiting for transfers between devices  130 us (43%)
  Pallas kernels  98.4 us (33%)
  starting transfers between devices  35.5 us (12%)
  local copies, waits for them, and re-layouts  16.1 us (5%)
  other arithmetic  12.9 us (4%)
    ppermute x33, waiting for transfers between devices, swapped(): return lax.ppermute(x, axis, [(0, 1), (1, 0)])  77.4 us
    pallas_call x4, Pallas kernels, norm_block(): pl.pallas_call(norm_kernel, grid_spec=pltpu.PrefetchScalarGridSpec(num_sc...  22.3 us
    pallas_call x2, Pallas kernels, project_early(): pl.pallas_call(functools.partial(project_early_kernel, len(pieces)), grid...  21.7 us
    ppermute x33, starting transfers between devices, swapped(): return lax.ppermute(x, axis, [(0, 1), (1, 0)])  21.4 us
    ppermute x1, waiting for transfers between devices, middle_form(): x_near = lax.ppermute(stream, 'row', beside)  20.1 us
    pallas_call x1, Pallas kernels, project_late(): pl.pallas_call(functools.partial(project_late_kernel, count), grid_spec=p...  19.9 us
    pallas_call x2, Pallas kernels, output_product(): pl.pallas_call(functools.partial(output_kernel, len(pieces)), grid_spec=p...  18.8 us
    ppermute x1, waiting for transfers between devices, middle_form(): w_near = lax.ppermute(own_side, 'row', beside)  18.2 us
  transfers between devices with their start and end apart: 48, of which 22 were waited for; matrix products, arithmetic and copies ran while one was open for 5% of the time, Pallas kernels for 33%

profile of v6, /device:TPU:0, one launch (start us, length us, event | category | flops | bytes accessed | tf_op | source)
XLA Modules:
  0.0 294.2 jit_solution(4232040003620128877)
XLA Ops:
  0.5 4.1 %collective-permute-start.1 = (bf16[1344,512]{1,0:T(8,128)(2,1)}, bf16[1344,512]{1,0:T(8,128)(2,1)}, u32[]{:S(2)}, u32[]{:S(2)}) collective-permute-start(bf16[1344,512]{1,0:T(8,128)(2,1)} %bitcast.49), channel_id=1, source_target_pairs={{0,4},{4,0},{8,12},{12,8},{1,5},{5,1},{9,13},{13,9},{2,6},{6,2},{1... | collective-permute-start | bytes 4128776 | tf_op jit(solution)/shard_map/ppermute | solution.py:549
  6.1 3.6 %dynamic-slice_bitcast_fusion = (bf16[1344,512]{1,0:T(8,128)(2,1)}, bf16[1344,512]{1,0:T(8,128)(2,1)}) fusion(bf16[1024,1344]{0,1:T(8,128)(2,1)} %param.16, s32[]{:T(128)S(6)} %select_n.107, s32[]{:T(128)S(6)} %select_n.102), kind=kLoop, calls=%fused_computation.6 | loop fusion | bytes 5505032 | tf_op jit(solution)/shard_map/dynamic_slice | solution.py:532
  11.5 3.2 %broadcast_select_fusion = (bf16[1344,512]{1,0:T(8,128)(2,1)}, bf16[1344,512]{1,0:T(8,128)(2,1)}, bf16[1344,512]{1,0:T(8,128)(2,1)}, bf16[1344,512]{1,0:T(8,128)(2,1)}) fusion(pred[]{:T(512)S(6)} %eq.60, bf16[1344,256]{1,0:T(8,128)(2,1)S(1)} %get-tuple-element.116, bf16[1344,256]{1,0:T(8,128)(2,1)S(1)} %get-tuple-element.123, ...), kind=kLoop, calls=%fused_computation.8 | loop fusion | flops 6881280 | bytes 11010057 | tf_op jit(solution)/shard_map/jit(_where)/select_n | solution.py:527
  14.8 20.1 %collective-permute-done.1 = bf16[1344,512]{1,0:T(8,128)(2,1)} collective-permute-done((bf16[1344,512]{1,0:T(8,128)(2,1)}, bf16[1344,512]{1,0:T(8,128)(2,1)}, u32[]{:S(2)}, u32[]{:S(2)}) %collective-permute-start.1) | collective-permute-done | bytes 1376288 | tf_op jit(solution)/shard_map/ppermute | solution.py:549
  36.8 2.0 collective-permute-start.4
  40.5 2.7 multiply_sine_fusion
  45.8 5.7 %shard_map.91.refs_0_ = bf16[4,5376,512]{2,1,0:T(8,128)(2,1)} custom-call(s32[4]{0:T(128)S(1)} %pad_add_fusion.table, bf16[1,1344,512]{2,1,0:T(8,128)(2,1)S(1)} %bitcast.52, bf16[1,1344,512]{2,1,0:T(8,128)(2,1)} %bitcast.21.refs_1_, bf16[1,1344,512]{2,1,0:T(8,128)(2,1)} %bitcast.22.refs_2_, bf16[1,1344,512]{2,1,0:T(8,128)(2,1)} %bitcast.23.refs_3_, ...), custom_call_target="tpu_custom_call" | custom-call | flops 27525120 | bytes 11010048 | tf_op jit(solution)/shard_map/pallas_call | solution.py:191
  51.5 18.2 %collective-permute-done.4.refs_2_ = bf16[1344,512]{1,0:T(8,128)(2,1)} collective-permute-done((bf16[1344,512]{1,0:T(8,128)(2,1)}, bf16[1344,512]{1,0:T(8,128)(2,1)}, u32[]{:S(2)}, u32[]{:S(2)}) %collective-permute-start.4) | collective-permute-done | bytes 1376288 | tf_op jit(solution)/shard_map/ppermute | solution.py:557
  75.0 5.2 %shard_map.92.refs_0_ = bf16[4,5376,512]{2,1,0:T(8,128)(2,1)} custom-call(s32[4]{0:T(128)S(1)} %pad_add_fusion.table, bf16[4,5376,512]{2,1,0:T(8,128)(2,1)} %shard_map.91.refs_0_, bf16[1,1344,512]{2,1,0:T(8,128)(2,1)} %bitcast.25.refs_1_, bf16[1,1344,512]{2,1,0:T(8,128)(2,1)S(1)} %bitcast.59, ...), custom_call_target="tpu_custom_call", output_to_operand_aliasing={{}: (1, {})} | custom-call | flops 27525120 | bytes 11010048 | tf_op jit(solution)/shard_map/pallas_call | solution.py:191
  80.2 25.5 %collective-permute-done.9.refs_3_ = bf16[1344,512]{1,0:T(8,128)(2,1)S(1)} collective-permute-done((bf16[1344,512]{1,0:T(8,128)(2,1)}, bf16[1344,512]{1,0:T(8,128)(2,1)S(1)}, u32[]{:S(2)}, u32[]{:S(2)}) %collective-permute-start.9) | collective-permute-done | bytes 1376288 | tf_op jit(solution)/shard_map/ppermute | solution.py:136
  107.9 1.8 collective-permute-start.17
  114.5 5.6 %shard_map.93.normed.refs_0_ = bf16[4,5376,512]{2,1,0:T(8,128)(2,1)} custom-call(s32[4]{0:T(128)S(1)} %pad_add_fusion.table, bf16[4,5376,512]{2,1,0:T(8,128)(2,1)} %shard_map.92.refs_0_, bf16[1,1344,512]{2,1,0:T(8,128)(2,1)S(1)} %bitcast.57, bf16[1,1344,512]{2,1,0:T(8,128)(2,1)S(1)} %bitcast.58, ...), custom_call_target="tpu_custom_call", output_to_operand_aliasing={{}: (1, {})} | custom-call | flops 27525120 | bytes 11010048 | tf_op jit(solution)/shard_map/pallas_call | solution.py:191
  120.1 14.1 %shard_map.94.refs_4_ = f32[4,1024,512]{2,1,0:T(8,128)} custom-call(s32[8]{0:T(128)S(1)} %stack.88.table, bf16[4,5376,512]{2,1,0:T(8,128)(2,1)} %shard_map.93.normed.refs_0_, bf16[1344,512]{1,0:T(8,128)(2,1)S(1)} %copy-done, bf16[1344,512]{1,0:T(8,128)(2,1)S(1)} %copy-done.2, bf16[1344,512]{1,0:T(8,128)(2,1)} %collective-permute-done.4.refs_2_, ...), custom_call_target="tpu_custom_call" | custom-call | flops 8455716864 | bytes 20054016 | tf_op jit(solution)/shard_map/pallas_call | solution.py:235
  134.2 7.1 %collective-permute-done.17.refs_0_ = bf16[1344,512]{1,0:T(8,128)(2,1)} collective-permute-done((bf16[1344,512]{1,0:T(8,128)(2,1)}, bf16[1344,512]{1,0:T(8,128)(2,1)}, u32[]{:S(2)}, u32[]{:S(2)}) %collective-permute-start.17) | collective-permute-done | bytes 1376288 | tf_op jit(solution)/shard_map/ppermute | solution.py:596
  146.0 5.9 %shard_map.95.normed = bf16[4,5376,512]{2,1,0:T(8,128)(2,1)} custom-call(s32[4]{0:T(128)S(1)} %pad_add_fusion.table, bf16[4,5376,512]{2,1,0:T(8,128)(2,1)} %shard_map.93.normed.refs_0_, bf16[1,1344,512]{2,1,0:T(8,128)(2,1)} %bitcast.34.refs_1_, bf16[1,1344,512]{2,1,0:T(8,128)(2,1)} %bitcast.35.refs_2_, ...), custom_call_target="tpu_custom_call", output_to_operand_aliasing={{}: (1, {})} | custom-call | flops 27525120 | bytes 11010048 | tf_op jit(solution)/shard_map/pallas_call | solution.py:191
  151.9 7.6 %shard_map.96.refs_4_ = f32[4,1024,512]{2,1,0:T(8,128)} custom-call(s32[8]{0:T(128)S(1)} %stack.88.table, bf16[4,5376,512]{2,1,0:T(8,128)(2,1)} %shard_map.95.normed, bf16[1344,512]{1,0:T(8,128)(2,1)S(1)} %copy-done.1, bf16[1344,512]{1,0:T(8,128)(2,1)S(1)} %copy-done.3, ...), custom_call_target="tpu_custom_call", output_to_operand_aliasing={{}: (6, {})} | custom-call | flops 2818572288 | bytes 10354688 | tf_op jit(solution)/shard_map/pallas_call | solution.py:235
  159.6 15.9 %collective-permute-done.21.refs_1_ = bf16[1344,512]{1,0:T(8,128)(2,1)} collective-permute-done((bf16[1344,512]{1,0:T(8,128)(2,1)}, bf16[1344,512]{1,0:T(8,128)(2,1)}, u32[]{:S(2)}, u32[]{:S(2)}) %collective-permute-start.21) | collective-permute-done | bytes 1376288 | tf_op jit(solution)/shard_map/ppermute | solution.py:136
  177.5 19.9 %shard_map.97 = (bf16[4,512,512]{2,1,0:T(8,128)(2,1)}, bf16[2048,256]{1,0:T(8,128)(2,1)S(1)}, bf16[256,2048]{1,0:T(8,128)(2,1)S(1)}) custom-call(s32[12]{0:T(128)S(1)} %stack.87.table, bf16[4,5376,512]{2,1,0:T(8,128)(2,1)} %shard_map.95.normed, bf16[1344,512]{1,0:T(8,128)(2,1)} %collective-permute-done.17.refs_0_, ...), custom_call_target="tpu_custom_call" | custom-call | flops 11274289152 | bytes 24903680 | tf_op jit(solution)/shard_map/pallas_call | solution.py:299
  199.0 4.9 %shard_map.98.refs_0_ = bf16[512,512]{1,0:T(8,128)(2,1)S(1)} custom-call(s32[1]{0:T(128)} %bitcast.18.table, bf16[4,512,512]{2,1,0:T(8,128)(2,1)S(1)} %copy-done.17, bf16[2048,256]{1,0:T(8,128)(2,1)S(1)} %get-tuple-element.93.keys, bf16[256,2048]{1,0:T(8,128)(2,1)S(1)} %get-tuple-element.94.values), custom_call_target="tpu_custom_call" | custom-call | flops 4026531840 | bytes 3145728 | tf_op jit(solution)/shard_map/pallas_call | solution.py:412
  205.6 4.7 %collective-permute-done.24.refs_1_.refs_13_ = bf16[1344,512]{1,0:T(8,128)(2,1)S(1)} collective-permute-done((bf16[1344,512]{1,0:T(8,128)(2,1)}, bf16[1344,512]{1,0:T(8,128)(2,1)S(1)}, u32[]{:S(2)}, u32[]{:S(2)}) %collective-permute-start.24) | collective-permute-done | bytes 1376288 | tf_op jit(solution)/shard_map/ppermute | solution.py:136
  210.3 2.3 shard_map.99.refs_0_
  214.2 6.2 %shard_map.100.refs_0_ = bf16[512,512]{1,0:T(8,128)(2,1)S(1)} custom-call(s32[1]{0:T(128)} %bitcast.17.table, bf16[4,512,512]{2,1,0:T(8,128)(2,1)S(1)} %copy-done.17, bf16[2048,256]{1,0:T(8,128)(2,1)S(1)} %get-tuple-element.93.keys, bf16[256,2048]{1,0:T(8,128)(2,1)S(1)} %get-tuple-element.94.values, bf16[512,512]{1,0:T(8,128)(2,1)S(1)} %shard_map.99.refs_0_), custom_call_target="tpu_custom_call" | custom-call | flops 4026531840 | bytes 3145728 | tf_op jit(solution)/shard_map/pallas_call | solution.py:412
  220.5 3.0 %collective-permute-done.26.refs_4_ = bf16[512,512]{1,0:T(8,128)(2,1)S(1)} collective-permute-done((bf16[512,512]{1,0:T(8,128)(2,1)S(1)}, bf16[512,512]{1,0:T(8,128)(2,1)S(1)}, u32[]{:S(2)}, u32[]{:S(2)}) %collective-permute-start.26) | collective-permute-done | bytes 524320 | tf_op jit(solution)/shard_map/ppermute | solution.py:136
  225.0 2.4 shard_map.101.refs_0_
  227.9 10.3 %collective-permute-done.33.refs_15_ = bf16[1344,512]{1,0:T(8,128)(2,1)S(1)} collective-permute-done((bf16[1344,512]{1,0:T(8,128)(2,1)S(1)}, bf16[1344,512]{1,0:T(8,128)(2,1)S(1)}, u32[]{:S(2)}, u32[]{:S(2)}) %collective-permute-start.33) | collective-permute-done | bytes 1376288 | tf_op jit(solution)/shard_map/ppermute | solution.py:136
  240.9 9.4 %shard_map.102 = (f32[1344,512]{1,0:T(8,128)S(1)}, f32[1,512]{1,0:T(1,128)S(1)}) custom-call(s32[8]{0:T(128)S(1)} %stack.81.table, bf16[512,512]{1,0:T(8,128)(2,1)S(1)} %shard_map.99.refs_0_, bf16[512,512]{1,0:T(8,128)(2,1)S(1)} %collective-permute-done.25.refs_1_, bf16[512,512]{1,0:T(8,128)(2,1)S(1)} %collective-permute-done.27.refs_2_, ...), custom_call_target="tpu_custom_call" | custom-call | flops 5637144576 | bytes 17956864 | tf_op jit(solution)/shard_map/pallas_call | solution.py:463
  255.2 2.9 add_convert_fusion
  259.0 7.4 %collective-permute-done.37.refs_4_ = bf16[512,512]{1,0:T(8,128)(2,1)S(1)} collective-permute-done((bf16[512,512]{1,0:T(8,128)(2,1)S(1)}, bf16[512,512]{1,0:T(8,128)(2,1)S(1)}, u32[]{:S(2)}, u32[]{:S(2)}) %collective-permute-start.37) | collective-permute-done | bytes 524320 | tf_op jit(solution)/shard_map/ppermute | solution.py:136
  269.2 9.4 %shard_map.103 = (f32[1344,512]{1,0:T(8,128)S(1)}, f32[1,512]{1,0:T(1,128)S(1)}) custom-call(s32[8]{0:T(128)S(1)} %stack.81.table, bf16[512,512]{1,0:T(8,128)(2,1)S(1)} %shard_map.101.refs_0_, bf16[512,512]{1,0:T(8,128)(2,1)S(1)} %collective-permute-done.31.refs_1_, bf16[512,512]{1,0:T(8,128)(2,1)S(1)} %collective-permute-done.35.refs_2_, ...), custom_call_target="tpu_custom_call" | custom-call | flops 5637144576 | bytes 17956864 | tf_op jit(solution)/shard_map/pallas_call | solution.py:463
  283.1 1.8 collective-permute-done.42
  285.0 4.8 %collective-permute-done.47 = bf16[1344,512]{1,0:T(8,128)(2,1)} collective-permute-done((bf16[1344,512]{1,0:T(8,128)(2,1)}, bf16[1344,512]{1,0:T(8,128)(2,1)}, u32[]{:S(2)}, u32[]{:S(2)}) %collective-permute-start.47) | collective-permute-done | bytes 1376288 | tf_op jit(solution)/shard_map/ppermute | solution.py:665
  289.8 3.9 %fusion.1 = bf16[512,1344]{0,1:T(8,128)(2,1)} fusion(bf16[1344,512]{1,0:T(8,128)(2,1)} %collective-permute-done.47, f32[1344,512]{1,0:T(8,128)} %copy-done.9, f32[1344]{0:T(1024)S(1)} %copy-done.22, f32[512]{0:T(512)S(1)} %bitcast.61, pred[]{:T(512)S(6)} %or.3, bf16[512,1344]{0,1:T(8,128)(2,1)S(1)} %copy-done.8), kind=kLoop, calls=%fused_computation.3 | loop fusion | flops 4128768 | bytes 6888705 | tf_op jit(solution)/shard_map/transpose | solution.py:672
  (151 shorter events, 51.6 us)
Async XLA Ops:
  0.0 14.8 %collective-permute-start = (bf16[1344,512]{1,0:T(8,128)(2,1)}, bf16[1344,512]{1,0:T(8,128)(2,1)S(1)}, u32[]{:S(2)}, u32[]{:S(2)}) collective-permute-start(bf16[1344,512]{1,0:T(8,128)(2,1)} %bitcast.48), channel_id=1, source_target_pairs={{0,1},{1,0},{4,8},{5,9},{8,4},{9,5},{12,13},{13,12},{2,3},{3,2},{6... | collective-permute-start | bytes 4128776 | tf_op jit(solution)/shard_map/ppermute | solution.py:155
  0.5 34.4 %collective-permute-start.1 = (bf16[1344,512]{1,0:T(8,128)(2,1)}, bf16[1344,512]{1,0:T(8,128)(2,1)}, u32[]{:S(2)}, u32[]{:S(2)}) collective-permute-start(bf16[1344,512]{1,0:T(8,128)(2,1)} %bitcast.49), channel_id=1, source_target_pairs={{0,4},{4,0},{8,12},{12,8},{1,5},{5,1},{9,13},{13,9},{2,6},{6,2},{1... | collective-permute-start | bytes 4128776 | tf_op jit(solution)/shard_map/ppermute | solution.py:549
  4.6 31.7 %collective-permute-start.2 = (bf16[1344,512]{1,0:T(8,128)(2,1)}, bf16[1344,512]{1,0:T(8,128)(2,1)}, u32[]{:S(2)}, u32[]{:S(2)}) collective-permute-start(bf16[1344,512]{1,0:T(8,128)(2,1)} %bitcast.50), channel_id=1, source_target_pairs={{0,2},{2,0},{1,3},{3,1},{4,6},{6,4},{5,7},{7,5},{8,10},{10,8},{9,1... | collective-permute-start | bytes 4128776 | tf_op jit(solution)/shard_map/ppermute | solution.py:136
  6.1 38.3 %collective-permute-start.6 = (bf16[1344,512]{1,0:T(8,128)(2,1)}, bf16[1344,512]{1,0:T(8,128)(2,1)}, u32[]{:S(2)}, u32[]{:S(2)}) collective-permute-start(bf16[1344,512]{1,0:T(8,128)(2,1)} %bitcast.51), channel_id=1, source_target_pairs={{0,1},{1,0},{2,3},{3,2},{4,5},{5,4},{6,7},{7,6},{8,9},{9,8},{10,11... | collective-permute-start | bytes 4128776 | tf_op jit(solution)/shard_map/ppermute | solution.py:136
  36.3 15.2 %collective-permute-start.3 = (bf16[1344,512]{1,0:T(8,128)(2,1)}, bf16[1344,512]{1,0:T(8,128)(2,1)}, u32[]{:S(2)}, u32[]{:S(2)}) collective-permute-start(bf16[1344,512]{1,0:T(8,128)(2,1)} %collective-permute-done.1), channel_id=1, source_target_pairs={{0,1},{1,0},{4,8},{5,9},{8,4},{9,5},{12,13},{13,12},{2,3},{3,2},{6... | collective-permute-start | bytes 4128776 | tf_op jit(solution)/shard_map/ppermute | solution.py:155
  36.8 32.9 %collective-permute-start.4 = (bf16[1344,512]{1,0:T(8,128)(2,1)}, bf16[1344,512]{1,0:T(8,128)(2,1)}, u32[]{:S(2)}, u32[]{:S(2)}) collective-permute-start(bf16[1344,512]{1,0:T(8,128)(2,1)} %get-tuple-element.59), channel_id=1, source_target_pairs={{0,4},{4,0},{8,12},{12,8},{1,5},{5,1},{9,13},{13,9},{2,6},{6,2},{1... | collective-permute-start | bytes 4128776 | tf_op jit(solution)/shard_map/ppermute | solution.py:557
  38.8 32.3 %collective-permute-start.5 = (bf16[1344,512]{1,0:T(8,128)(2,1)}, bf16[1344,512]{1,0:T(8,128)(2,1)}, u32[]{:S(2)}, u32[]{:S(2)}) collective-permute-start(bf16[1344,512]{1,0:T(8,128)(2,1)} %collective-permute-done.1), channel_id=1, source_target_pairs={{0,2},{2,0},{1,3},{3,1},{4,6},{6,4},{5,7},{7,5},{8,10},{10,8},{9,1... | collective-permute-start | bytes 4128776 | tf_op jit(solution)/shard_map/ppermute | solution.py:136
  44.4 28.8 %collective-permute-start.11 = (bf16[1344,512]{1,0:T(8,128)(2,1)}, bf16[1344,512]{1,0:T(8,128)(2,1)S(1)}, u32[]{:S(2)}, u32[]{:S(2)}) collective-permute-start(bf16[1344,512]{1,0:T(8,128)(2,1)} %collective-permute-done.1), channel_id=1, source_target_pairs={{0,1},{1,0},{2,3},{3,2},{4,5},{5,4},{6,7},{7,6},{8,9},{9,8},{10,11... | collective-permute-start | bytes 4128776 | tf_op jit(solution)/shard_map/ppermute | solution.py:136
  71.2 35.6 %collective-permute-start.10 = (bf16[1344,512]{1,0:T(8,128)(2,1)S(1)}, bf16[1344,512]{1,0:T(8,128)(2,1)}, u32[]{:S(2)}, u32[]{:S(2)}) collective-permute-start(bf16[1344,512]{1,0:T(8,128)(2,1)S(1)} %copy-done.12), channel_id=1, source_target_pairs={{0,2},{2,0},{1,3},{3,1},{4,6},{6,4},{5,7},{7,5},{8,10},{10,8},{9,1... | collective-permute-start | bytes 4128776 | tf_op jit(solution)/shard_map/ppermute | solution.py:136
  72.7 34.1 %collective-permute-start.13 = (bf16[1344,512]{1,0:T(8,128)(2,1)S(1)}, bf16[1344,512]{1,0:T(8,128)(2,1)S(1)}, u32[]{:S(2)}, u32[]{:S(2)}) collective-permute-start(bf16[1344,512]{1,0:T(8,128)(2,1)S(1)} %copy-done.12), channel_id=1, source_target_pairs={{0,1},{1,0},{2,3},{3,2},{4,5},{5,4},{6,7},{7,6},{8,9},{9,8},{10,11... | collective-permute-start | bytes 4128776 | tf_op jit(solution)/shard_map/ppermute | solution.py:136
  73.2 32.5 %collective-permute-start.9 = (bf16[1344,512]{1,0:T(8,128)(2,1)}, bf16[1344,512]{1,0:T(8,128)(2,1)S(1)}, u32[]{:S(2)}, u32[]{:S(2)}) collective-permute-start(bf16[1344,512]{1,0:T(8,128)(2,1)} %collective-permute-done.4.refs_2_), channel_id=1, source_target_pairs={{0,16},{16,0},{1,17},{17,1},{2,18},{18,2},{3,19},{19,3},{4,20},{20... | collective-permute-start | bytes 4128776 | tf_op jit(solution)/shard_map/ppermute | solution.py:136
  74.7 33.2 %collective-permute-start.14 = (bf16[1344,512]{1,0:T(8,128)(2,1)S(1)}, bf16[1344,512]{1,0:T(8,128)(2,1)}, u32[]{:S(2)}, u32[]{:S(2)}) collective-permute-start(bf16[1344,512]{1,0:T(8,128)(2,1)S(1)} %copy-done.21), channel_id=1, source_target_pairs={{0,4},{4,0},{8,12},{12,8},{1,5},{5,1},{9,13},{13,9},{2,6},{6,2},{1... | collective-permute-start | bytes 4128776 | tf_op jit(solution)/shard_map/ppermute | solution.py:585
  107.9 33.4 %collective-permute-start.17 = (bf16[1344,512]{1,0:T(8,128)(2,1)}, bf16[1344,512]{1,0:T(8,128)(2,1)}, u32[]{:S(2)}, u32[]{:S(2)}) collective-permute-start(bf16[1344,512]{1,0:T(8,128)(2,1)} %get-tuple-element.75), channel_id=1, source_target_pairs={{0,8},{4,0},{8,12},{12,4},{1,9},{5,1},{9,13},{13,5},{2,10},{6,2},{... | collective-permute-start | bytes 4128776 | tf_op jit(solution)/shard_map/ppermute | solution.py:596
  109.7 32.6 %collective-permute-start.18 = (bf16[1344,512]{1,0:T(8,128)(2,1)}, bf16[1344,512]{1,0:T(8,128)(2,1)}, u32[]{:S(2)}, u32[]{:S(2)}) collective-permute-start(bf16[1344,512]{1,0:T(8,128)(2,1)} %collective-permute-done.3), channel_id=1, source_target_pairs={{0,2},{2,0},{1,3},{3,1},{4,6},{6,4},{5,7},{7,5},{8,10},{10,8},{9,1... | collective-permute-start | bytes 4128776 | tf_op jit(solution)/shard_map/ppermute | solution.py:136
  110.2 32.3 %collective-permute-start.19 = (bf16[1344,512]{1,0:T(8,128)(2,1)}, bf16[1344,512]{1,0:T(8,128)(2,1)}, u32[]{:S(2)}, u32[]{:S(2)}) collective-permute-start(bf16[1344,512]{1,0:T(8,128)(2,1)} %collective-permute-done.8.refs_2_), channel_id=1, source_target_pairs={{0,16},{16,0},{1,17},{17,1},{2,18},{18,2},{3,19},{19,3},{4,20},{20... | collective-permute-start | bytes 4128776 | tf_op jit(solution)/shard_map/ppermute | solution.py:136
  111.8 33.9 %collective-permute-start.16 = (bf16[1344,512]{1,0:T(8,128)(2,1)}, bf16[1344,512]{1,0:T(8,128)(2,1)}, u32[]{:S(2)}, u32[]{:S(2)}) collective-permute-start(bf16[1344,512]{1,0:T(8,128)(2,1)} %collective-permute-done.3), channel_id=1, source_target_pairs={{0,1},{1,0},{2,3},{3,2},{4,5},{5,4},{6,7},{7,6},{8,9},{9,8},{10,11... | collective-permute-start | bytes 4128776 | tf_op jit(solution)/shard_map/ppermute | solution.py:136
  142.5 32.9 %collective-permute-start.21 = (bf16[1344,512]{1,0:T(8,128)(2,1)}, bf16[1344,512]{1,0:T(8,128)(2,1)}, u32[]{:S(2)}, u32[]{:S(2)}) collective-permute-start(bf16[1344,512]{1,0:T(8,128)(2,1)} %collective-permute-done.17.refs_0_), channel_id=1, source_target_pairs={{0,16},{16,0},{1,17},{17,1},{2,18},{18,2},{3,19},{19,3},{4,20},{20... | collective-permute-start | bytes 4128776 | tf_op jit(solution)/shard_map/ppermute | solution.py:136
  144.1 31.4 %collective-permute-start.22 = (bf16[1344,512]{1,0:T(8,128)(2,1)}, bf16[1344,512]{1,0:T(8,128)(2,1)}, u32[]{:S(2)}, u32[]{:S(2)}) collective-permute-start(bf16[1344,512]{1,0:T(8,128)(2,1)} %collective-permute-done.14.refs_10_), channel_id=1, source_target_pairs={{0,1},{1,0},{4,8},{5,9},{8,4},{9,5},{12,13},{13,12},{2,3},{3,2},{6... | collective-permute-start | bytes 4128776 | tf_op jit(solution)/shard_map/ppermute | solution.py:155
  144.3 32.7 %collective-permute-start.23 = (bf16[1344,512]{1,0:T(8,128)(2,1)}, bf16[1344,512]{1,0:T(8,128)(2,1)}, u32[]{:S(2)}, u32[]{:S(2)}) collective-permute-start(bf16[1344,512]{1,0:T(8,128)(2,1)} %get-tuple-element.84), channel_id=1, source_target_pairs={{0,4},{4,0},{8,12},{12,8},{1,5},{5,1},{9,13},{13,9},{2,6},{6,2},{1... | collective-permute-start | bytes 4128776 | tf_op jit(solution)/shard_map/ppermute | solution.py:612
  145.7 58.3 %collective-permute-start.32 = (bf16[1344,512]{1,0:T(8,128)(2,1)}, bf16[1344,512]{1,0:T(8,128)(2,1)S(1)}, u32[]{:S(2)}, u32[]{:S(2)}) collective-permute-start(bf16[1344,512]{1,0:T(8,128)(2,1)} %get-tuple-element.70), channel_id=1, source_target_pairs={{0,1},{1,0},{4,8},{5,9},{8,4},{9,5},{12,13},{13,12},{2,3},{3,2},{6... | collective-permute-start | bytes 4128776 | tf_op jit(solution)/shard_map/ppermute | solution.py:155
  177.0 33.3 %collective-permute-start.24 = (bf16[1344,512]{1,0:T(8,128)(2,1)}, bf16[1344,512]{1,0:T(8,128)(2,1)S(1)}, u32[]{:S(2)}, u32[]{:S(2)}) collective-permute-start(bf16[1344,512]{1,0:T(8,128)(2,1)} %collective-permute-done.22.refs_12_), channel_id=1, source_target_pairs={{0,16},{16,0},{1,17},{17,1},{2,18},{18,2},{3,19},{19,3},{4,20},{20... | collective-permute-start | bytes 4128776 | tf_op jit(solution)/shard_map/ppermute | solution.py:136
  203.9 16.5 %collective-permute-start.25 = (bf16[512,512]{1,0:T(8,128)(2,1)S(1)}, bf16[512,512]{1,0:T(8,128)(2,1)S(1)}, u32[]{:S(2)}, u32[]{:S(2)}) collective-permute-start(bf16[512,512]{1,0:T(8,128)(2,1)S(1)} %shard_map.98.refs_0_), channel_id=1, source_target_pairs={{0,1},{1,0},{4,8},{5,9},{8,4},{9,5},{12,13},{13,12},{2,3},{3,2},{6... | collective-permute-start | bytes 1572872 | tf_op jit(solution)/shard_map/ppermute | solution.py:155
  204.0 34.2 %collective-permute-start.33 = (bf16[1344,512]{1,0:T(8,128)(2,1)S(1)}, bf16[1344,512]{1,0:T(8,128)(2,1)S(1)}, u32[]{:S(2)}, u32[]{:S(2)}) collective-permute-start(bf16[1344,512]{1,0:T(8,128)(2,1)S(1)} %collective-permute-done.32.refs_14_), channel_id=1, source_target_pairs={{0,16},{16,0},{1,17},{17,1},{2,18},{18,2},{3,19},{19,3},{4,20},{20... | collective-permute-start | bytes 4128776 | tf_op jit(solution)/shard_map/ppermute | solution.py:136
  212.6 10.9 %collective-permute-start.26 = (bf16[512,512]{1,0:T(8,128)(2,1)S(1)}, bf16[512,512]{1,0:T(8,128)(2,1)S(1)}, u32[]{:S(2)}, u32[]{:S(2)}) collective-permute-start(bf16[512,512]{1,0:T(8,128)(2,1)S(1)} %shard_map.99.refs_0_), channel_id=1, source_target_pairs={{0,2},{2,0},{1,3},{3,1},{4,6},{6,4},{5,7},{7,5},{8,10},{10,8},{9,1... | collective-permute-start | bytes 1572872 | tf_op jit(solution)/shard_map/ppermute | solution.py:136
  220.4 17.9 %collective-permute-start.31 = (bf16[512,512]{1,0:T(8,128)(2,1)S(1)}, bf16[512,512]{1,0:T(8,128)(2,1)S(1)}, u32[]{:S(2)}, u32[]{:S(2)}) collective-permute-start(bf16[512,512]{1,0:T(8,128)(2,1)S(1)} %shard_map.100.refs_0_), channel_id=1, source_target_pairs={{0,1},{1,0},{4,8},{5,9},{8,4},{9,5},{12,13},{13,12},{2,3},{3,2},{6... | collective-permute-start | bytes 1572872 | tf_op jit(solution)/shard_map/ppermute | solution.py:155
  223.5 14.8 %collective-permute-start.29 = (bf16[512,512]{1,0:T(8,128)(2,1)S(1)}, bf16[512,512]{1,0:T(8,128)(2,1)S(1)}, u32[]{:S(2)}, u32[]{:S(2)}) collective-permute-start(bf16[512,512]{1,0:T(8,128)(2,1)S(1)} %collective-permute-done.25.refs_1_), channel_id=1, source_target_pairs={{0,2},{2,0},{1,3},{3,1},{4,6},{6,4},{5,7},{7,5},{8,10},{10,8},{9,1... | collective-permute-start | bytes 1572872 | tf_op jit(solution)/shard_map/ppermute | solution.py:136
  225.0 15.3 %collective-permute-start.27 = (bf16[512,512]{1,0:T(8,128)(2,1)S(1)}, bf16[512,512]{1,0:T(8,128)(2,1)S(1)}, u32[]{:S(2)}, u32[]{:S(2)}) collective-permute-start(bf16[512,512]{1,0:T(8,128)(2,1)S(1)} %shard_map.99.refs_0_), channel_id=1, source_target_pairs={{0,1},{1,0},{2,3},{3,2},{4,5},{5,4},{6,7},{7,6},{8,9},{9,8},{10,11... | collective-permute-start | bytes 1572872 | tf_op jit(solution)/shard_map/ppermute | solution.py:136
  227.4 12.9 %collective-permute-start.28 = (bf16[512,512]{1,0:T(8,128)(2,1)S(1)}, bf16[512,512]{1,0:T(8,128)(2,1)S(1)}, u32[]{:S(2)}, u32[]{:S(2)}) collective-permute-start(bf16[512,512]{1,0:T(8,128)(2,1)S(1)} %collective-permute-done.25.refs_1_), channel_id=1, source_target_pairs={{0,1},{1,0},{2,3},{3,2},{4,5},{5,4},{6,7},{7,6},{8,9},{9,8},{10,11... | collective-permute-start | bytes 1572872 | tf_op jit(solution)/shard_map/ppermute | solution.py:136
  238.8 16.4 %collective-permute-start.38 = (bf16[512,512]{1,0:T(8,128)(2,1)S(1)}, bf16[512,512]{1,0:T(8,128)(2,1)S(1)}, u32[]{:S(2)}, u32[]{:S(2)}) collective-permute-start(bf16[512,512]{1,0:T(8,128)(2,1)S(1)} %collective-permute-done.31.refs_1_), channel_id=1, source_target_pairs={{0,2},{2,0},{1,3},{3,1},{4,6},{6,4},{5,7},{7,5},{8,10},{10,8},{9,1... | collective-permute-start | bytes 1572872 | tf_op jit(solution)/shard_map/ppermute | solution.py:136
  252.2 14.3 %collective-permute-start.37 = (bf16[512,512]{1,0:T(8,128)(2,1)S(1)}, bf16[512,512]{1,0:T(8,128)(2,1)S(1)}, u32[]{:S(2)}, u32[]{:S(2)}) collective-permute-start(bf16[512,512]{1,0:T(8,128)(2,1)S(1)} %shard_map.101.refs_0_), channel_id=1, source_target_pairs={{0,2},{2,0},{1,3},{3,1},{4,6},{6,4},{5,7},{7,5},{8,10},{10,8},{9,1... | collective-permute-start | bytes 1572872 | tf_op jit(solution)/shard_map/ppermute | solution.py:136
  258.2 31.6 %collective-permute-start.47 = (bf16[1344,512]{1,0:T(8,128)(2,1)}, bf16[1344,512]{1,0:T(8,128)(2,1)}, u32[]{:S(2)}, u32[]{:S(2)}) collective-permute-start(bf16[1344,512]{1,0:T(8,128)(2,1)} %add_convert_fusion), channel_id=1, source_target_pairs={{0,4},{4,0},{8,12},{12,8},{1,5},{5,1},{9,13},{13,9},{2,6},{6,2},{1... | collective-permute-start | bytes 4128776 | tf_op jit(solution)/shard_map/ppermute | solution.py:665
  258.5 8.5 %collective-permute-start.35 = (bf16[512,512]{1,0:T(8,128)(2,1)S(1)}, bf16[512,512]{1,0:T(8,128)(2,1)S(1)}, u32[]{:S(2)}, u32[]{:S(2)}) collective-permute-start(bf16[512,512]{1,0:T(8,128)(2,1)S(1)} %shard_map.101.refs_0_), channel_id=1, source_target_pairs={{0,1},{1,0},{2,3},{3,2},{4,5},{5,4},{6,7},{7,6},{8,9},{9,8},{10,11... | collective-permute-start | bytes 1572872 | tf_op jit(solution)/shard_map/ppermute | solution.py:136
  (42 other events, 383.9 us)

commit v7 on v6

--- a/solution.py
+++ b/solution.py
@@ -200,7 +200,7 @@
         ),
         out_shape=jax.ShapeDtypeStruct(shape, jnp.bfloat16),
         input_output_aliases={1: 0} if before else {},
-        compiler_params=pltpu.CompilerParams(vmem_limit_bytes=44 * MIB),
+        compiler_params=pltpu.CompilerParams(vmem_limit_bytes=63 * MIB),
         cost_estimate=pl.CostEstimate(
             flops=40 * depth * tokens, bytes_accessed=16 * depth * tokens, transcendentals=0
         ),
@@ -245,7 +245,7 @@
         ),
         out_shape=jax.ShapeDtypeStruct((4, width, tokens), jnp.float32),
         input_output_aliases={2 + len(pieces): 0} if before else {},
-        compiler_params=pltpu.CompilerParams(vmem_limit_bytes=44 * MIB),
+        compiler_params=pltpu.CompilerParams(vmem_limit_bytes=63 * MIB),
         cost_estimate=pl.CostEstimate(
             flops=2 * blocks * tokens * features // 2 * width,
             bytes_accessed=blocks * features * tokens + features * width + 4 * blocks * width * tokens,
@@ -589,6 +589,7 @@
     far_sub = swapped(x_far, "sub")
     near_pieces = (x_near[None], near_sub[None], near_col[None], near_both[None])
     normed = norm_block(order, near_pieces, 0, gain, 1, normed)
+    w_cross_y = swapped(after(w_cross, w_near_y), "groups")
     w_cross, w_near_y, cross_col, x_far, normed, other_side, theirs, cross_sub, o_in = settle(
         w_cross, w_near_y, cross_col, x_far, normed, other_side, theirs, cross_sub, o_in
     )
@@ -596,7 +597,6 @@
     w_far = lax.ppermute(other_side, "row", beyond)
     far_col = swapped(x_far, "col")
     cross_both = swapped(cross_col, "sub")
-    w_cross_y = swapped(w_cross, "groups")
     cross_pieces = (x_cross[None], cross_sub[None], cross_col[None], cross_both[None])
     normed = norm_block(order, cross_pieces, 0, gain, 2, normed)
     early_table = ints(0, 0, 0, half, features, group * half, features, (1 - group) * half)

time: 299 us -> 298 us (level)
  Pallas kernels: 98.4 us -> 108 us
  local copies, waits for them, and re-layouts: 16.1 us -> 11.4 us
  waiting for transfers between devices: 130 us -> 126 us
    unnamed x52 -> x24, local copies, waits for them, and re-layouts: 11 us -> 4.25 us
    pallas_call x4, Pallas kernels: 22.3 us -> 28.2 us  [norm_block(): pl.pallas_call(norm_kernel, grid_spec=pltpu.PrefetchScalarGridSpec(num_sc...]
    ppermute x33, waiting for transfers between devices: 77.4 us -> 72.3 us  [swapped(): return lax.ppermute(x, axis, [(0, 1), (1, 0)])]
  transfers between devices with their start and end apart: 48 -> 48, of which waited for: 22 -> 24; matrix products, arithmetic and copies ran while one was open for 5% -> 6% of each run, Pallas kernels for 33% -> 37%
where the time goes in v7:
time: 298 us; the launch traced here: 292 us
  waiting for transfers between devices  126 us (42%)
  Pallas kernels  108 us (36%)
  starting transfers between devices  33 us (11%)
  other arithmetic  13 us (4%)
  local copies, waits for them, and re-layouts  11.4 us (4%)
    ppermute x33, waiting for transfers between devices, swapped(): return lax.ppermute(x, axis, [(0, 1), (1, 0)])  72.3 us
    pallas_call x4, Pallas kernels, norm_block(): pl.pallas_call(norm_kernel, grid_spec=pltpu.PrefetchScalarGridSpec(num_sc...  28.2 us
    pallas_call x2, Pallas kernels, project_early(): pl.pallas_call(functools.partial(project_early_kernel, len(pieces)), grid...  24.4 us
    ppermute x1, waiting for transfers between devices, middle_form(): x_near = lax.ppermute(stream, 'row', beside)  20.1 us
    pallas_call x1, Pallas kernels, project_late(): pl.pallas_call(functools.partial(project_late_kernel, count), grid_spec=p...  19.9 us
    ppermute x33, starting transfers between devices, swapped(): return lax.ppermute(x, axis, [(0, 1), (1, 0)])  19.1 us
    pallas_call x2, Pallas kernels, output_product(): pl.pallas_call(functools.partial(output_kernel, len(pieces)), grid_spec=p...  19 us
    pallas_call x4, Pallas kernels, attend(): pl.pallas_call(functools.partial(attend_kernel, float(MODEL_WIDTH // QUER...  17 us
  transfers between devices with their start and end apart: 48, of which 24 were waited for; matrix products, arithmetic and copies ran while one was open for 6% of the time, Pallas kernels for 37%

profile of v7, /device:TPU:0, one launch (start us, length us, event | category | flops | bytes accessed | tf_op | source)
XLA Modules:
  0.0 292.4 jit_solution(10820134995672893205)
XLA Ops:
  0.5 4.1 %collective-permute-start.1 = (bf16[1344,512]{1,0:T(8,128)(2,1)}, bf16[1344,512]{1,0:T(8,128)(2,1)}, u32[]{:S(2)}, u32[]{:S(2)}) collective-permute-start(bf16[1344,512]{1,0:T(8,128)(2,1)} %bitcast.53), channel_id=1, source_target_pairs={{0,4},{4,0},{8,12},{12,8},{1,5},{5,1},{9,13},{13,9},{2,6},{6,2},{1... | collective-permute-start | bytes 4128776 | tf_op jit(solution)/shard_map/ppermute | solution.py:549
  6.1 3.6 %dynamic-slice_bitcast_fusion = (bf16[1344,512]{1,0:T(8,128)(2,1)}, bf16[1344,512]{1,0:T(8,128)(2,1)}) fusion(bf16[1024,1344]{0,1:T(8,128)(2,1)} %param.16, s32[]{:T(128)S(6)} %select_n.107, s32[]{:T(128)S(6)} %select_n.102), kind=kLoop, calls=%fused_computation.6 | loop fusion | bytes 5505032 | tf_op jit(solution)/shard_map/dynamic_slice | solution.py:532
  11.5 3.2 %broadcast_select_fusion = (bf16[1344,512]{1,0:T(8,128)(2,1)}, bf16[1344,512]{1,0:T(8,128)(2,1)}, bf16[1344,512]{1,0:T(8,128)(2,1)}, bf16[1344,512]{1,0:T(8,128)(2,1)}) fusion(pred[]{:T(512)S(6)} %eq.60, bf16[1344,256]{1,0:T(8,128)(2,1)S(1)} %get-tuple-element.118, bf16[1344,256]{1,0:T(8,128)(2,1)S(1)} %get-tuple-element.125, ...), kind=kLoop, calls=%fused_computation.8 | loop fusion | flops 6881280 | bytes 11010057 | tf_op jit(solution)/shard_map/jit(_where)/select_n | solution.py:527
  14.8 20.1 %collective-permute-done.1 = bf16[1344,512]{1,0:T(8,128)(2,1)} collective-permute-done((bf16[1344,512]{1,0:T(8,128)(2,1)}, bf16[1344,512]{1,0:T(8,128)(2,1)}, u32[]{:S(2)}, u32[]{:S(2)}) %collective-permute-start.1) | collective-permute-done | bytes 1376288 | tf_op jit(solution)/shard_map/ppermute | solution.py:549
  36.7 2.0 collective-permute-start.4
  40.9 2.7 multiply_sine_fusion
  44.0 2.3 copy.14.refs_4_.refs_5_
  46.3 7.1 %shard_map.91.refs_0_ = bf16[4,5376,512]{2,1,0:T(8,128)(2,1)} custom-call(s32[4]{0:T(128)} %pad_add_fusion.table, bf16[1,1344,512]{2,1,0:T(8,128)(2,1)} %bitcast.56, bf16[1,1344,512]{2,1,0:T(8,128)(2,1)} %bitcast.21.refs_1_, bf16[1,1344,512]{2,1,0:T(8,128)(2,1)} %bitcast.57, bf16[1,1344,512]{2,1,0:T(8,128)(2,1)} %bitcast.23.refs_3_, ...), custom_call_target="tpu_custom_call" | custom-call | flops 27525120 | bytes 11010048 | tf_op jit(solution)/shard_map/pallas_call | solution.py:191
  53.4 16.2 %collective-permute-done.4.refs_2_ = bf16[1344,512]{1,0:T(8,128)(2,1)} collective-permute-done((bf16[1344,512]{1,0:T(8,128)(2,1)}, bf16[1344,512]{1,0:T(8,128)(2,1)}, u32[]{:S(2)}, u32[]{:S(2)}) %collective-permute-start.4) | collective-permute-done | bytes 1376288 | tf_op jit(solution)/shard_map/ppermute | solution.py:557
  75.1 7.1 %shard_map.92.refs_0_ = bf16[4,5376,512]{2,1,0:T(8,128)(2,1)} custom-call(s32[4]{0:T(128)} %pad_add_fusion.table, bf16[4,5376,512]{2,1,0:T(8,128)(2,1)} %shard_map.91.refs_0_, bf16[1,1344,512]{2,1,0:T(8,128)(2,1)} %bitcast.25.refs_1_, bf16[1,1344,512]{2,1,0:T(8,128)(2,1)} %bitcast.26.refs_2_, ...), custom_call_target="tpu_custom_call", output_to_operand_aliasing={{}: (1, {})} | custom-call | flops 27525120 | bytes 11010048 | tf_op jit(solution)/shard_map/pallas_call | solution.py:191
  82.1 23.6 %collective-permute-done.9.refs_3_ = bf16[1344,512]{1,0:T(8,128)(2,1)} collective-permute-done((bf16[1344,512]{1,0:T(8,128)(2,1)}, bf16[1344,512]{1,0:T(8,128)(2,1)}, u32[]{:S(2)}, u32[]{:S(2)}) %collective-permute-start.9) | collective-permute-done | bytes 1376288 | tf_op jit(solution)/shard_map/ppermute | solution.py:136
  111.3 7.0 %shard_map.93.normed.refs_0_ = bf16[4,5376,512]{2,1,0:T(8,128)(2,1)} custom-call(s32[4]{0:T(128)} %pad_add_fusion.table, bf16[4,5376,512]{2,1,0:T(8,128)(2,1)} %shard_map.92.refs_0_, bf16[1,1344,512]{2,1,0:T(8,128)(2,1)} %bitcast.58, bf16[1,1344,512]{2,1,0:T(8,128)(2,1)} %bitcast.31.refs_2_, ...), custom_call_target="tpu_custom_call", output_to_operand_aliasing={{}: (1, {})} | custom-call | flops 27525120 | bytes 11010048 | tf_op jit(solution)/shard_map/pallas_call | solution.py:191
  118.4 15.4 %shard_map.94.refs_4_ = f32[4,1024,512]{2,1,0:T(8,128)} custom-call(s32[8]{0:T(128)} %stack.88.table, bf16[4,5376,512]{2,1,0:T(8,128)(2,1)} %shard_map.93.normed.refs_0_, bf16[1344,512]{1,0:T(8,128)(2,1)} %get-tuple-element.110.refs_0_, bf16[1344,512]{1,0:T(8,128)(2,1)} %get-tuple-element.114.refs_1_, bf16[1344,512]{1,0:T(8,128)(2,1)} %collective-permute-done.4.refs_2_, ...), custom_call_target="tpu_custom_call" | custom-call | flops 8455716864 | bytes 20054016 | tf_op jit(solution)/shard_map/pallas_call | solution.py:235
  133.7 6.7 %collective-permute-done.17.refs_0_ = bf16[1344,512]{1,0:T(8,128)(2,1)} collective-permute-done((bf16[1344,512]{1,0:T(8,128)(2,1)}, bf16[1344,512]{1,0:T(8,128)(2,1)}, u32[]{:S(2)}, u32[]{:S(2)}) %collective-permute-start.17) | collective-permute-done | bytes 1376288 | tf_op jit(solution)/shard_map/ppermute | solution.py:597
  143.5 1.7 collective-permute-start.23
  145.4 7.0 %shard_map.95.normed = bf16[4,5376,512]{2,1,0:T(8,128)(2,1)} custom-call(s32[4]{0:T(128)} %pad_add_fusion.table, bf16[4,5376,512]{2,1,0:T(8,128)(2,1)} %shard_map.93.normed.refs_0_, bf16[1,1344,512]{2,1,0:T(8,128)(2,1)} %bitcast.34.refs_1_, bf16[1,1344,512]{2,1,0:T(8,128)(2,1)} %bitcast.35.refs_2_, ...), custom_call_target="tpu_custom_call", output_to_operand_aliasing={{}: (1, {})} | custom-call | flops 27525120 | bytes 11010048 | tf_op jit(solution)/shard_map/pallas_call | solution.py:191
  152.4 9.0 %shard_map.96.refs_4_ = f32[4,1024,512]{2,1,0:T(8,128)} custom-call(s32[8]{0:T(128)} %stack.88.table, bf16[4,5376,512]{2,1,0:T(8,128)(2,1)} %shard_map.95.normed, bf16[1344,512]{1,0:T(8,128)(2,1)} %get-tuple-element.110.refs_0_, bf16[1344,512]{1,0:T(8,128)(2,1)} %get-tuple-element.114.refs_1_, ...), custom_call_target="tpu_custom_call", output_to_operand_aliasing={{}: (6, {})} | custom-call | flops 2818572288 | bytes 10354688 | tf_op jit(solution)/shard_map/pallas_call | solution.py:235
  161.4 13.2 %collective-permute-done.21.refs_1_ = bf16[1344,512]{1,0:T(8,128)(2,1)} collective-permute-done((bf16[1344,512]{1,0:T(8,128)(2,1)}, bf16[1344,512]{1,0:T(8,128)(2,1)}, u32[]{:S(2)}, u32[]{:S(2)}) %collective-permute-start.21) | collective-permute-done | bytes 1376288 | tf_op jit(solution)/shard_map/ppermute | solution.py:136
  177.7 19.9 %shard_map.97 = (bf16[4,512,512]{2,1,0:T(8,128)(2,1)}, bf16[2048,256]{1,0:T(8,128)(2,1)S(1)}, bf16[256,2048]{1,0:T(8,128)(2,1)S(1)}) custom-call(s32[12]{0:T(128)S(1)} %stack.87.table, bf16[4,5376,512]{2,1,0:T(8,128)(2,1)} %shard_map.95.normed, bf16[1344,512]{1,0:T(8,128)(2,1)} %collective-permute-done.17.refs_0_, ...), custom_call_target="tpu_custom_call" | custom-call | flops 11274289152 | bytes 24903680 | tf_op jit(solution)/shard_map/pallas_call | solution.py:299
  199.2 4.9 %shard_map.98.refs_0_ = bf16[512,512]{1,0:T(8,128)(2,1)S(1)} custom-call(s32[1]{0:T(128)} %bitcast.18.table, bf16[4,512,512]{2,1,0:T(8,128)(2,1)S(1)} %copy-done.2, bf16[2048,256]{1,0:T(8,128)(2,1)S(1)} %get-tuple-element.95.keys, bf16[256,2048]{1,0:T(8,128)(2,1)S(1)} %get-tuple-element.96.values), custom_call_target="tpu_custom_call" | custom-call | flops 4026531840 | bytes 3145728 | tf_op jit(solution)/shard_map/pallas_call | solution.py:412
  205.9 2.4 collective-permute-done.24.refs_1_.refs_13_
  208.3 2.3 shard_map.99.refs_0_
  210.8 7.4 %shard_map.100.refs_0_ = bf16[512,512]{1,0:T(8,128)(2,1)S(1)} custom-call(s32[1]{0:T(128)} %bitcast.17.table, bf16[4,512,512]{2,1,0:T(8,128)(2,1)S(1)} %copy-done.2, bf16[2048,256]{1,0:T(8,128)(2,1)S(1)} %get-tuple-element.95.keys, bf16[256,2048]{1,0:T(8,128)(2,1)S(1)} %get-tuple-element.96.values, bf16[512,512]{1,0:T(8,128)(2,1)S(1)} %shard_map.99.refs_0_), custom_call_target="tpu_custom_call" | custom-call | flops 4026531840 | bytes 3145728 | tf_op jit(solution)/shard_map/pallas_call | solution.py:412
  218.4 4.3 %collective-permute-done.26.refs_4_ = bf16[512,512]{1,0:T(8,128)(2,1)S(1)} collective-permute-done((bf16[512,512]{1,0:T(8,128)(2,1)S(1)}, bf16[512,512]{1,0:T(8,128)(2,1)S(1)}, u32[]{:S(2)}, u32[]{:S(2)}) %collective-permute-start.26) | collective-permute-done | bytes 524320 | tf_op jit(solution)/shard_map/ppermute | solution.py:136
  223.2 2.4 shard_map.101.refs_0_
  226.2 11.3 %collective-permute-done.33.refs_15_ = bf16[1344,512]{1,0:T(8,128)(2,1)S(1)} collective-permute-done((bf16[1344,512]{1,0:T(8,128)(2,1)}, bf16[1344,512]{1,0:T(8,128)(2,1)S(1)}, u32[]{:S(2)}, u32[]{:S(2)}) %collective-permute-start.33) | collective-permute-done | bytes 1376288 | tf_op jit(solution)/shard_map/ppermute | solution.py:136
  240.1 9.5 %shard_map.102 = (f32[1344,512]{1,0:T(8,128)S(1)}, f32[1,512]{1,0:T(1,128)S(1)}) custom-call(s32[8]{0:T(128)S(1)} %stack.81.table, bf16[512,512]{1,0:T(8,128)(2,1)S(1)} %shard_map.99.refs_0_, bf16[512,512]{1,0:T(8,128)(2,1)S(1)} %collective-permute-done.25.refs_1_, bf16[512,512]{1,0:T(8,128)(2,1)S(1)} %collective-permute-done.27.refs_2_, ...), custom_call_target="tpu_custom_call" | custom-call | flops 5637144576 | bytes 17956864 | tf_op jit(solution)/shard_map/pallas_call | solution.py:463
  253.9 2.9 add_convert_fusion
  258.3 7.5 %collective-permute-done.37.refs_4_ = bf16[512,512]{1,0:T(8,128)(2,1)S(1)} collective-permute-done((bf16[512,512]{1,0:T(8,128)(2,1)S(1)}, bf16[512,512]{1,0:T(8,128)(2,1)S(1)}, u32[]{:S(2)}, u32[]{:S(2)}) %collective-permute-start.37) | collective-permute-done | bytes 524320 | tf_op jit(solution)/shard_map/ppermute | solution.py:136
  268.5 9.5 %shard_map.103 = (f32[1344,512]{1,0:T(8,128)S(1)}, f32[1,512]{1,0:T(1,128)S(1)}) custom-call(s32[8]{0:T(128)S(1)} %stack.81.table, bf16[512,512]{1,0:T(8,128)(2,1)S(1)} %shard_map.101.refs_0_, bf16[512,512]{1,0:T(8,128)(2,1)S(1)} %collective-permute-done.31.refs_1_, bf16[512,512]{1,0:T(8,128)(2,1)S(1)} %collective-permute-done.35.refs_2_, ...), custom_call_target="tpu_custom_call" | custom-call | flops 5637144576 | bytes 17956864 | tf_op jit(solution)/shard_map/pallas_call | solution.py:463
  282.2 6.2 %collective-permute-done.47 = bf16[1344,512]{1,0:T(8,128)(2,1)} collective-permute-done((bf16[1344,512]{1,0:T(8,128)(2,1)}, bf16[1344,512]{1,0:T(8,128)(2,1)}, u32[]{:S(2)}, u32[]{:S(2)}) %collective-permute-start.47) | collective-permute-done | bytes 1376288 | tf_op jit(solution)/shard_map/ppermute | solution.py:665
  288.5 3.5 %fusion.1 = bf16[512,1344]{0,1:T(8,128)(2,1)} fusion(bf16[1344,512]{1,0:T(8,128)(2,1)} %collective-permute-done.47, f32[1344,512]{1,0:T(8,128)S(1)} %get-tuple-element.105, f32[1344]{0:T(1024)S(1)} %copy-done.8, f32[512]{0:T(512)S(1)} %bitcast.59, pred[]{:T(512)S(6)} %or.3, bf16[512,1344]{0,1:T(8,128)(2,1)} %param.9), kind=kLoop, calls=%fused_computation.3 | loop fusion | flops 4128768 | bytes 6888705 | tf_op jit(solution)/shard_map/transpose | solution.py:672
  (123 shorter events, 45.5 us)
Async XLA Ops:
  0.0 14.8 %collective-permute-start = (bf16[1344,512]{1,0:T(8,128)(2,1)}, bf16[1344,512]{1,0:T(8,128)(2,1)S(1)}, u32[]{:S(2)}, u32[]{:S(2)}) collective-permute-start(bf16[1344,512]{1,0:T(8,128)(2,1)} %bitcast.52), channel_id=1, source_target_pairs={{0,1},{1,0},{4,8},{5,9},{8,4},{9,5},{12,13},{13,12},{2,3},{3,2},{6... | collective-permute-start | bytes 4128776 | tf_op jit(solution)/shard_map/ppermute | solution.py:155
  0.5 34.4 %collective-permute-start.1 = (bf16[1344,512]{1,0:T(8,128)(2,1)}, bf16[1344,512]{1,0:T(8,128)(2,1)}, u32[]{:S(2)}, u32[]{:S(2)}) collective-permute-start(bf16[1344,512]{1,0:T(8,128)(2,1)} %bitcast.53), channel_id=1, source_target_pairs={{0,4},{4,0},{8,12},{12,8},{1,5},{5,1},{9,13},{13,9},{2,6},{6,2},{1... | collective-permute-start | bytes 4128776 | tf_op jit(solution)/shard_map/ppermute | solution.py:549
  4.6 31.6 %collective-permute-start.2 = (bf16[1344,512]{1,0:T(8,128)(2,1)}, bf16[1344,512]{1,0:T(8,128)(2,1)S(1)}, u32[]{:S(2)}, u32[]{:S(2)}) collective-permute-start(bf16[1344,512]{1,0:T(8,128)(2,1)} %bitcast.54), channel_id=1, source_target_pairs={{0,2},{2,0},{1,3},{3,1},{4,6},{6,4},{5,7},{7,5},{8,10},{10,8},{9,1... | collective-permute-start | bytes 4128776 | tf_op jit(solution)/shard_map/ppermute | solution.py:136
  6.1 40.2 %collective-permute-start.6 = (bf16[1344,512]{1,0:T(8,128)(2,1)}, bf16[1344,512]{1,0:T(8,128)(2,1)}, u32[]{:S(2)}, u32[]{:S(2)}) collective-permute-start(bf16[1344,512]{1,0:T(8,128)(2,1)} %bitcast.55), channel_id=1, source_target_pairs={{0,1},{1,0},{2,3},{3,2},{4,5},{5,4},{6,7},{7,6},{8,9},{9,8},{10,11... | collective-permute-start | bytes 4128776 | tf_op jit(solution)/shard_map/ppermute | solution.py:136
  36.2 10.1 %collective-permute-start.7 = (bf16[1344,512]{1,0:T(8,128)(2,1)S(1)}, bf16[1344,512]{1,0:T(8,128)(2,1)}, u32[]{:S(2)}, u32[]{:S(2)}) collective-permute-start(bf16[1344,512]{1,0:T(8,128)(2,1)S(1)} %collective-permute-done.2), channel_id=1, source_target_pairs={{0,1},{1,0},{2,3},{3,2},{4,5},{5,4},{6,7},{7,6},{8,9},{9,8},{10,11... | collective-permute-start | bytes 4128776 | tf_op jit(solution)/shard_map/ppermute | solution.py:136
  36.2 17.2 %collective-permute-start.3 = (bf16[1344,512]{1,0:T(8,128)(2,1)}, bf16[1344,512]{1,0:T(8,128)(2,1)}, u32[]{:S(2)}, u32[]{:S(2)}) collective-permute-start(bf16[1344,512]{1,0:T(8,128)(2,1)} %collective-permute-done.1), channel_id=1, source_target_pairs={{0,1},{1,0},{4,8},{5,9},{8,4},{9,5},{12,13},{13,12},{2,3},{3,2},{6... | collective-permute-start | bytes 4128776 | tf_op jit(solution)/shard_map/ppermute | solution.py:155
  36.7 32.9 %collective-permute-start.4 = (bf16[1344,512]{1,0:T(8,128)(2,1)}, bf16[1344,512]{1,0:T(8,128)(2,1)}, u32[]{:S(2)}, u32[]{:S(2)}) collective-permute-start(bf16[1344,512]{1,0:T(8,128)(2,1)} %get-tuple-element.60), channel_id=1, source_target_pairs={{0,4},{4,0},{8,12},{12,8},{1,5},{5,1},{9,13},{13,9},{2,6},{6,2},{1... | collective-permute-start | bytes 4128776 | tf_op jit(solution)/shard_map/ppermute | solution.py:557
  38.7 32.3 %collective-permute-start.5 = (bf16[1344,512]{1,0:T(8,128)(2,1)}, bf16[1344,512]{1,0:T(8,128)(2,1)}, u32[]{:S(2)}, u32[]{:S(2)}) collective-permute-start(bf16[1344,512]{1,0:T(8,128)(2,1)} %collective-permute-done.1), channel_id=1, source_target_pairs={{0,2},{2,0},{1,3},{3,1},{4,6},{6,4},{5,7},{7,5},{8,10},{10,8},{9,1... | collective-permute-start | bytes 4128776 | tf_op jit(solution)/shard_map/ppermute | solution.py:136
  46.3 26.8 %collective-permute-start.11 = (bf16[1344,512]{1,0:T(8,128)(2,1)}, bf16[1344,512]{1,0:T(8,128)(2,1)}, u32[]{:S(2)}, u32[]{:S(2)}) collective-permute-start(bf16[1344,512]{1,0:T(8,128)(2,1)} %collective-permute-done.1), channel_id=1, source_target_pairs={{0,1},{1,0},{2,3},{3,2},{4,5},{5,4},{6,7},{7,6},{8,9},{9,8},{10,11... | collective-permute-start | bytes 4128776 | tf_op jit(solution)/shard_map/ppermute | solution.py:136
  71.1 34.6 %collective-permute-start.10 = (bf16[1344,512]{1,0:T(8,128)(2,1)}, bf16[1344,512]{1,0:T(8,128)(2,1)}, u32[]{:S(2)}, u32[]{:S(2)}) collective-permute-start(bf16[1344,512]{1,0:T(8,128)(2,1)} %copy-done.7), channel_id=1, source_target_pairs={{0,2},{2,0},{1,3},{3,1},{4,6},{6,4},{5,7},{7,5},{8,10},{10,8},{9,1... | collective-permute-start | bytes 4128776 | tf_op jit(solution)/shard_map/ppermute | solution.py:136
  72.6 33.1 %collective-permute-start.13 = (bf16[1344,512]{1,0:T(8,128)(2,1)}, bf16[1344,512]{1,0:T(8,128)(2,1)}, u32[]{:S(2)}, u32[]{:S(2)}) collective-permute-start(bf16[1344,512]{1,0:T(8,128)(2,1)} %copy-done.7), channel_id=1, source_target_pairs={{0,1},{1,0},{2,3},{3,2},{4,5},{5,4},{6,7},{7,6},{8,9},{9,8},{10,11... | collective-permute-start | bytes 4128776 | tf_op jit(solution)/shard_map/ppermute | solution.py:136
  73.1 32.6 %collective-permute-start.9 = (bf16[1344,512]{1,0:T(8,128)(2,1)}, bf16[1344,512]{1,0:T(8,128)(2,1)}, u32[]{:S(2)}, u32[]{:S(2)}) collective-permute-start(bf16[1344,512]{1,0:T(8,128)(2,1)} %collective-permute-done.4.refs_2_), channel_id=1, source_target_pairs={{0,16},{16,0},{1,17},{17,1},{2,18},{18,2},{3,19},{19,3},{4,20},{20... | collective-permute-start | bytes 4128776 | tf_op jit(solution)/shard_map/ppermute | solution.py:136
  74.6 32.5 %collective-permute-start.14 = (bf16[1344,512]{1,0:T(8,128)(2,1)}, bf16[1344,512]{1,0:T(8,128)(2,1)}, u32[]{:S(2)}, u32[]{:S(2)}) collective-permute-start(bf16[1344,512]{1,0:T(8,128)(2,1)} %get-tuple-element.71), channel_id=1, source_target_pairs={{0,4},{4,0},{8,12},{12,8},{1,5},{5,1},{9,13},{13,9},{2,6},{6,2},{1... | collective-permute-start | bytes 4128776 | tf_op jit(solution)/shard_map/ppermute | solution.py:585
  107.1 33.4 %collective-permute-start.17 = (bf16[1344,512]{1,0:T(8,128)(2,1)}, bf16[1344,512]{1,0:T(8,128)(2,1)}, u32[]{:S(2)}, u32[]{:S(2)}) collective-permute-start(bf16[1344,512]{1,0:T(8,128)(2,1)} %get-tuple-element.76), channel_id=1, source_target_pairs={{0,8},{4,0},{8,12},{12,4},{1,9},{5,1},{9,13},{13,5},{2,10},{6,2},{... | collective-permute-start | bytes 4128776 | tf_op jit(solution)/shard_map/ppermute | solution.py:597
  108.6 32.6 %collective-permute-start.18 = (bf16[1344,512]{1,0:T(8,128)(2,1)}, bf16[1344,512]{1,0:T(8,128)(2,1)}, u32[]{:S(2)}, u32[]{:S(2)}) collective-permute-start(bf16[1344,512]{1,0:T(8,128)(2,1)} %collective-permute-done.3), channel_id=1, source_target_pairs={{0,2},{2,0},{1,3},{3,1},{4,6},{6,4},{5,7},{7,5},{8,10},{10,8},{9,1... | collective-permute-start | bytes 4128776 | tf_op jit(solution)/shard_map/ppermute | solution.py:136
  109.2 32.6 %collective-permute-start.19 = (bf16[1344,512]{1,0:T(8,128)(2,1)}, bf16[1344,512]{1,0:T(8,128)(2,1)}, u32[]{:S(2)}, u32[]{:S(2)}) collective-permute-start(bf16[1344,512]{1,0:T(8,128)(2,1)} %collective-permute-done.8.refs_2_), channel_id=1, source_target_pairs={{0,16},{16,0},{1,17},{17,1},{2,18},{18,2},{3,19},{19,3},{4,20},{20... | collective-permute-start | bytes 4128776 | tf_op jit(solution)/shard_map/ppermute | solution.py:136
  111.3 34.0 %collective-permute-start.16 = (bf16[1344,512]{1,0:T(8,128)(2,1)}, bf16[1344,512]{1,0:T(8,128)(2,1)}, u32[]{:S(2)}, u32[]{:S(2)}) collective-permute-start(bf16[1344,512]{1,0:T(8,128)(2,1)} %collective-permute-done.3), channel_id=1, source_target_pairs={{0,1},{1,0},{2,3},{3,2},{4,5},{5,4},{6,7},{7,6},{8,9},{9,8},{10,11... | collective-permute-start | bytes 4128776 | tf_op jit(solution)/shard_map/ppermute | solution.py:136
  141.7 32.9 %collective-permute-start.21 = (bf16[1344,512]{1,0:T(8,128)(2,1)}, bf16[1344,512]{1,0:T(8,128)(2,1)}, u32[]{:S(2)}, u32[]{:S(2)}) collective-permute-start(bf16[1344,512]{1,0:T(8,128)(2,1)} %collective-permute-done.17.refs_0_), channel_id=1, source_target_pairs={{0,16},{16,0},{1,17},{17,1},{2,18},{18,2},{3,19},{19,3},{4,20},{20... | collective-permute-start | bytes 4128776 | tf_op jit(solution)/shard_map/ppermute | solution.py:136
  143.3 31.4 %collective-permute-start.22 = (bf16[1344,512]{1,0:T(8,128)(2,1)}, bf16[1344,512]{1,0:T(8,128)(2,1)}, u32[]{:S(2)}, u32[]{:S(2)}) collective-permute-start(bf16[1344,512]{1,0:T(8,128)(2,1)} %collective-permute-done.14.refs_10_), channel_id=1, source_target_pairs={{0,1},{1,0},{4,8},{5,9},{8,4},{9,5},{12,13},{13,12},{2,3},{3,2},{6... | collective-permute-start | bytes 4128776 | tf_op jit(solution)/shard_map/ppermute | solution.py:155
  143.5 32.7 %collective-permute-start.23 = (bf16[1344,512]{1,0:T(8,128)(2,1)}, bf16[1344,512]{1,0:T(8,128)(2,1)}, u32[]{:S(2)}, u32[]{:S(2)}) collective-permute-start(bf16[1344,512]{1,0:T(8,128)(2,1)} %get-tuple-element.85), channel_id=1, source_target_pairs={{0,4},{4,0},{8,12},{12,8},{1,5},{5,1},{9,13},{13,9},{2,6},{6,2},{1... | collective-permute-start | bytes 4128776 | tf_op jit(solution)/shard_map/ppermute | solution.py:612
  145.3 58.9 %collective-permute-start.32 = (bf16[1344,512]{1,0:T(8,128)(2,1)}, bf16[1344,512]{1,0:T(8,128)(2,1)}, u32[]{:S(2)}, u32[]{:S(2)}) collective-permute-start(bf16[1344,512]{1,0:T(8,128)(2,1)} %get-tuple-element.71), channel_id=1, source_target_pairs={{0,1},{1,0},{4,8},{5,9},{8,4},{9,5},{12,13},{13,12},{2,3},{3,2},{6... | collective-permute-start | bytes 4128776 | tf_op jit(solution)/shard_map/ppermute | solution.py:155
  176.2 32.1 %collective-permute-start.24 = (bf16[1344,512]{1,0:T(8,128)(2,1)}, bf16[1344,512]{1,0:T(8,128)(2,1)S(1)}, u32[]{:S(2)}, u32[]{:S(2)}) collective-permute-start(bf16[1344,512]{1,0:T(8,128)(2,1)} %collective-permute-done.22.refs_12_), channel_id=1, source_target_pairs={{0,16},{16,0},{1,17},{17,1},{2,18},{18,2},{3,19},{19,3},{4,20},{20... | collective-permute-start | bytes 4128776 | tf_op jit(solution)/shard_map/ppermute | solution.py:136
  204.1 14.2 %collective-permute-start.25 = (bf16[512,512]{1,0:T(8,128)(2,1)S(1)}, bf16[512,512]{1,0:T(8,128)(2,1)S(1)}, u32[]{:S(2)}, u32[]{:S(2)}) collective-permute-start(bf16[512,512]{1,0:T(8,128)(2,1)S(1)} %shard_map.98.refs_0_), channel_id=1, source_target_pairs={{0,1},{1,0},{4,8},{5,9},{8,4},{9,5},{12,13},{13,12},{2,3},{3,2},{6... | collective-permute-start | bytes 1572872 | tf_op jit(solution)/shard_map/ppermute | solution.py:155
  204.2 33.2 %collective-permute-start.33 = (bf16[1344,512]{1,0:T(8,128)(2,1)}, bf16[1344,512]{1,0:T(8,128)(2,1)S(1)}, u32[]{:S(2)}, u32[]{:S(2)}) collective-permute-start(bf16[1344,512]{1,0:T(8,128)(2,1)} %collective-permute-done.32.refs_14_), channel_id=1, source_target_pairs={{0,16},{16,0},{1,17},{17,1},{2,18},{18,2},{3,19},{19,3},{4,20},{20... | collective-permute-start | bytes 4128776 | tf_op jit(solution)/shard_map/ppermute | solution.py:136
  210.6 12.2 %collective-permute-start.26 = (bf16[512,512]{1,0:T(8,128)(2,1)S(1)}, bf16[512,512]{1,0:T(8,128)(2,1)S(1)}, u32[]{:S(2)}, u32[]{:S(2)}) collective-permute-start(bf16[512,512]{1,0:T(8,128)(2,1)S(1)} %shard_map.99.refs_0_), channel_id=1, source_target_pairs={{0,2},{2,0},{1,3},{3,1},{4,6},{6,4},{5,7},{7,5},{8,10},{10,8},{9,1... | collective-permute-start | bytes 1572872 | tf_op jit(solution)/shard_map/ppermute | solution.py:136
  218.3 19.1 %collective-permute-start.31 = (bf16[512,512]{1,0:T(8,128)(2,1)S(1)}, bf16[512,512]{1,0:T(8,128)(2,1)S(1)}, u32[]{:S(2)}, u32[]{:S(2)}) collective-permute-start(bf16[512,512]{1,0:T(8,128)(2,1)S(1)} %shard_map.100.refs_0_), channel_id=1, source_target_pairs={{0,1},{1,0},{4,8},{5,9},{8,4},{9,5},{12,13},{13,12},{2,3},{3,2},{6... | collective-permute-start | bytes 1572872 | tf_op jit(solution)/shard_map/ppermute | solution.py:155
  222.7 14.7 %collective-permute-start.29 = (bf16[512,512]{1,0:T(8,128)(2,1)S(1)}, bf16[512,512]{1,0:T(8,128)(2,1)S(1)}, u32[]{:S(2)}, u32[]{:S(2)}) collective-permute-start(bf16[512,512]{1,0:T(8,128)(2,1)S(1)} %collective-permute-done.25.refs_1_), channel_id=1, source_target_pairs={{0,2},{2,0},{1,3},{3,1},{4,6},{6,4},{5,7},{7,5},{8,10},{10,8},{9,1... | collective-permute-start | bytes 1572872 | tf_op jit(solution)/shard_map/ppermute | solution.py:136
  223.2 15.6 %collective-permute-start.27 = (bf16[512,512]{1,0:T(8,128)(2,1)S(1)}, bf16[512,512]{1,0:T(8,128)(2,1)S(1)}, u32[]{:S(2)}, u32[]{:S(2)}) collective-permute-start(bf16[512,512]{1,0:T(8,128)(2,1)S(1)} %shard_map.99.refs_0_), channel_id=1, source_target_pairs={{0,1},{1,0},{2,3},{3,2},{4,5},{5,4},{6,7},{7,6},{8,9},{9,8},{10,11... | collective-permute-start | bytes 1572872 | tf_op jit(solution)/shard_map/ppermute | solution.py:136
  225.6 13.2 %collective-permute-start.28 = (bf16[512,512]{1,0:T(8,128)(2,1)S(1)}, bf16[512,512]{1,0:T(8,128)(2,1)S(1)}, u32[]{:S(2)}, u32[]{:S(2)}) collective-permute-start(bf16[512,512]{1,0:T(8,128)(2,1)S(1)} %collective-permute-done.25.refs_1_), channel_id=1, source_target_pairs={{0,1},{1,0},{2,3},{3,2},{4,5},{5,4},{6,7},{7,6},{8,9},{9,8},{10,11... | collective-permute-start | bytes 1572872 | tf_op jit(solution)/shard_map/ppermute | solution.py:136
  238.0 15.9 %collective-permute-start.38 = (bf16[512,512]{1,0:T(8,128)(2,1)S(1)}, bf16[512,512]{1,0:T(8,128)(2,1)S(1)}, u32[]{:S(2)}, u32[]{:S(2)}) collective-permute-start(bf16[512,512]{1,0:T(8,128)(2,1)S(1)} %collective-permute-done.31.refs_1_), channel_id=1, source_target_pairs={{0,2},{2,0},{1,3},{3,1},{4,6},{6,4},{5,7},{7,5},{8,10},{10,8},{9,1... | collective-permute-start | bytes 1572872 | tf_op jit(solution)/shard_map/ppermute | solution.py:136
  251.5 14.3 %collective-permute-start.37 = (bf16[512,512]{1,0:T(8,128)(2,1)S(1)}, bf16[512,512]{1,0:T(8,128)(2,1)S(1)}, u32[]{:S(2)}, u32[]{:S(2)}) collective-permute-start(bf16[512,512]{1,0:T(8,128)(2,1)S(1)} %shard_map.101.refs_0_), channel_id=1, source_target_pairs={{0,2},{2,0},{1,3},{3,1},{4,6},{6,4},{5,7},{7,5},{8,10},{10,8},{9,1... | collective-permute-start | bytes 1572872 | tf_op jit(solution)/shard_map/ppermute | solution.py:136
  256.8 31.6 %collective-permute-start.47 = (bf16[1344,512]{1,0:T(8,128)(2,1)}, bf16[1344,512]{1,0:T(8,128)(2,1)}, u32[]{:S(2)}, u32[]{:S(2)}) collective-permute-start(bf16[1344,512]{1,0:T(8,128)(2,1)} %add_convert_fusion), channel_id=1, source_target_pairs={{0,4},{4,0},{8,12},{12,8},{1,5},{5,1},{9,13},{13,9},{2,6},{6,2},{1... | collective-permute-start | bytes 4128776 | tf_op jit(solution)/shard_map/ppermute | solution.py:665
  (28 other events, 242.0 us)

commit v8 on v7

--- a/solution.py
+++ b/solution.py
@@ -640,7 +640,7 @@
     far_col, far_sub = swapped(got_far, "col"), swapped(got_far, "sub")
     far_both = swapped(after(far_col, got_cross, own_part, o_cross_y), "sub")
     cross_col, cross_sub = swapped(got_cross, "col"), swapped(got_cross, "sub")
-    own_col, own_sub = swapped(own_part, "col"), swapped(own_part, "sub")
+    own_col, own_sub = swapped(after(own_part, far_both), "col"), swapped(own_part, "sub")
 
     pieces = (turned, turned, o_in, o_in_rest, o_far, o_far_y, o_cross, o_cross_y)
     out_pieces = [(piece, int(index == 1), depth) for index, piece in enumerate(pieces)]
@@ -668,8 +668,9 @@
         stream,
         (own_part, own_sub, own_col, swapped(own_col, "sub")),
         (got_cross, cross_sub, cross_col, swapped(cross_col, "sub")),
-    )
-    return jnp.where(in_middle, own_out, outer).T
+        near_out,
+    )
+    return jnp.where(in_middle, lax.optimization_barrier(own_out), outer).T
 
 
 def on_device(*args):

time: 298 us -> 308 us (1.034)
  waiting for transfers between devices: 126 us -> 134 us
    ppermute x33, waiting for transfers between devices: 72.3 us -> 61.6 us  [swapped(): return lax.ppermute(x, axis, [(0, 1), (1, 0)])]
    ppermute x1, waiting for transfers between devices: 6.21 us -> 16 us  [middle_form(): outer = lax.ppermute(near_out, 'row', beside)]
    ppermute x2, waiting for transfers between devices: 1.41 us -> 10.4 us  [projected(): lax.ppermute(squares, ('col', 'sub'), [(0, 3), (1, 2), (2, 1), (3, 0)])]
  transfers between devices with their start and end apart: 48 -> 48, of which waited for: 24 -> 21; matrix products, arithmetic and copies ran while one was open for 6% -> 6% of each run, Pallas kernels for 37% -> 36%
where the time goes in v8:
time: 308 us; the launch traced here: 303 us
  waiting for transfers between devices  134 us (44%)
  Pallas kernels  108 us (35%)
  starting transfers between devices  34.3 us (11%)
  other arithmetic  13.9 us (5%)
  local copies, waits for them, and re-layouts  11.4 us (4%)
    ppermute x33, waiting for transfers between devices, swapped(): return lax.ppermute(x, axis, [(0, 1), (1, 0)])  61.6 us
    pallas_call x4, Pallas kernels, norm_block(): pl.pallas_call(norm_kernel, grid_spec=pltpu.PrefetchScalarGridSpec(num_sc...  28.2 us
    pallas_call x2, Pallas kernels, project_early(): pl.pallas_call(functools.partial(project_early_kernel, len(pieces)), grid...  24.4 us
    ppermute x33, starting transfers between devices, swapped(): return lax.ppermute(x, axis, [(0, 1), (1, 0)])  20.6 us
    ppermute x1, waiting for transfers between devices, middle_form(): x_near = lax.ppermute(stream, 'row', beside)  20.1 us
    pallas_call x1, Pallas kernels, project_late(): pl.pallas_call(functools.partial(project_late_kernel, count), grid_spec=p...  19.9 us
    pallas_call x2, Pallas kernels, output_product(): pl.pallas_call(functools.partial(output_kernel, len(pieces)), grid_spec=p...  19 us
    pallas_call x4, Pallas kernels, attend(): pl.pallas_call(functools.partial(attend_kernel, float(MODEL_WIDTH // QUER...  17 us
  transfers between devices with their start and end apart: 48, of which 21 were waited for; matrix products, arithmetic and copies ran while one was open for 6% of the time, Pallas kernels for 36%

profile of v8, /device:TPU:0, one launch (start us, length us, event | category | flops | bytes accessed | tf_op | source)
XLA Modules:
  0.0 302.8 jit_solution(13766076377748080598)
XLA Ops:
  0.5 4.1 %collective-permute-start.1 = (bf16[1344,512]{1,0:T(8,128)(2,1)}, bf16[1344,512]{1,0:T(8,128)(2,1)}, u32[]{:S(2)}, u32[]{:S(2)}) collective-permute-start(bf16[1344,512]{1,0:T(8,128)(2,1)} %bitcast.53), channel_id=1, source_target_pairs={{0,4},{4,0},{8,12},{12,8},{1,5},{5,1},{9,13},{13,9},{2,6},{6,2},{1... | collective-permute-start | bytes 4128776 | tf_op jit(solution)/shard_map/ppermute | solution.py:549
  6.1 3.6 %dynamic-slice_bitcast_fusion = (bf16[1344,512]{1,0:T(8,128)(2,1)}, bf16[1344,512]{1,0:T(8,128)(2,1)}) fusion(bf16[1024,1344]{0,1:T(8,128)(2,1)} %param.16, s32[]{:T(128)S(6)} %select_n.107, s32[]{:T(128)S(6)} %select_n.102), kind=kLoop, calls=%fused_computation.5 | loop fusion | bytes 5505032 | tf_op jit(solution)/shard_map/dynamic_slice | solution.py:532
  11.5 3.2 %broadcast_select_fusion = (bf16[1344,512]{1,0:T(8,128)(2,1)}, bf16[1344,512]{1,0:T(8,128)(2,1)}, bf16[1344,512]{1,0:T(8,128)(2,1)}, bf16[1344,512]{1,0:T(8,128)(2,1)}) fusion(pred[]{:T(512)S(6)} %eq.60, bf16[1344,256]{1,0:T(8,128)(2,1)S(1)} %get-tuple-element.122, bf16[1344,256]{1,0:T(8,128)(2,1)S(1)} %get-tuple-element.129, ...), kind=kLoop, calls=%fused_computation.7 | loop fusion | flops 6881280 | bytes 11010057 | tf_op jit(solution)/shard_map/jit(_where)/select_n | solution.py:527
  14.8 20.1 %collective-permute-done.1 = bf16[1344,512]{1,0:T(8,128)(2,1)} collective-permute-done((bf16[1344,512]{1,0:T(8,128)(2,1)}, bf16[1344,512]{1,0:T(8,128)(2,1)}, u32[]{:S(2)}, u32[]{:S(2)}) %collective-permute-start.1) | collective-permute-done | bytes 1376288 | tf_op jit(solution)/shard_map/ppermute | solution.py:549
  36.7 2.0 collective-permute-start.4
  40.9 2.7 multiply_sine_fusion
  44.0 2.3 copy.14.refs_4_.refs_5_
  46.3 7.1 %shard_map.91.refs_0_ = bf16[4,5376,512]{2,1,0:T(8,128)(2,1)} custom-call(s32[4]{0:T(128)} %pad_add_fusion.table, bf16[1,1344,512]{2,1,0:T(8,128)(2,1)} %bitcast.56, bf16[1,1344,512]{2,1,0:T(8,128)(2,1)} %bitcast.21.refs_1_, bf16[1,1344,512]{2,1,0:T(8,128)(2,1)} %bitcast.57, bf16[1,1344,512]{2,1,0:T(8,128)(2,1)} %bitcast.23.refs_3_, ...), custom_call_target="tpu_custom_call" | custom-call | flops 27525120 | bytes 11010048 | tf_op jit(solution)/shard_map/pallas_call | solution.py:191
  53.4 16.2 %collective-permute-done.4.refs_2_ = bf16[1344,512]{1,0:T(8,128)(2,1)} collective-permute-done((bf16[1344,512]{1,0:T(8,128)(2,1)}, bf16[1344,512]{1,0:T(8,128)(2,1)}, u32[]{:S(2)}, u32[]{:S(2)}) %collective-permute-start.4) | collective-permute-done | bytes 1376288 | tf_op jit(solution)/shard_map/ppermute | solution.py:557
  75.1 7.1 %shard_map.92.refs_0_ = bf16[4,5376,512]{2,1,0:T(8,128)(2,1)} custom-call(s32[4]{0:T(128)} %pad_add_fusion.table, bf16[4,5376,512]{2,1,0:T(8,128)(2,1)} %shard_map.91.refs_0_, bf16[1,1344,512]{2,1,0:T(8,128)(2,1)} %bitcast.25.refs_1_, bf16[1,1344,512]{2,1,0:T(8,128)(2,1)} %bitcast.26.refs_2_, ...), custom_call_target="tpu_custom_call", output_to_operand_aliasing={{}: (1, {})} | custom-call | flops 27525120 | bytes 11010048 | tf_op jit(solution)/shard_map/pallas_call | solution.py:191
  82.1 23.6 %collective-permute-done.9.refs_3_ = bf16[1344,512]{1,0:T(8,128)(2,1)} collective-permute-done((bf16[1344,512]{1,0:T(8,128)(2,1)}, bf16[1344,512]{1,0:T(8,128)(2,1)}, u32[]{:S(2)}, u32[]{:S(2)}) %collective-permute-start.9) | collective-permute-done | bytes 1376288 | tf_op jit(solution)/shard_map/ppermute | solution.py:136
  111.3 7.0 %shard_map.93.normed.refs_0_ = bf16[4,5376,512]{2,1,0:T(8,128)(2,1)} custom-call(s32[4]{0:T(128)} %pad_add_fusion.table, bf16[4,5376,512]{2,1,0:T(8,128)(2,1)} %shard_map.92.refs_0_, bf16[1,1344,512]{2,1,0:T(8,128)(2,1)} %bitcast.58, bf16[1,1344,512]{2,1,0:T(8,128)(2,1)} %bitcast.31.refs_2_, ...), custom_call_target="tpu_custom_call", output_to_operand_aliasing={{}: (1, {})} | custom-call | flops 27525120 | bytes 11010048 | tf_op jit(solution)/shard_map/pallas_call | solution.py:191
  118.4 15.4 %shard_map.94.refs_4_ = f32[4,1024,512]{2,1,0:T(8,128)} custom-call(s32[8]{0:T(128)} %stack.88.table, bf16[4,5376,512]{2,1,0:T(8,128)(2,1)} %shard_map.93.normed.refs_0_, bf16[1344,512]{1,0:T(8,128)(2,1)} %get-tuple-element.114.refs_0_, bf16[1344,512]{1,0:T(8,128)(2,1)} %get-tuple-element.118.refs_1_, bf16[1344,512]{1,0:T(8,128)(2,1)} %collective-permute-done.4.refs_2_, ...), custom_call_target="tpu_custom_call" | custom-call | flops 8455716864 | bytes 20054016 | tf_op jit(solution)/shard_map/pallas_call | solution.py:235
  133.7 6.7 %collective-permute-done.17.refs_0_ = bf16[1344,512]{1,0:T(8,128)(2,1)} collective-permute-done((bf16[1344,512]{1,0:T(8,128)(2,1)}, bf16[1344,512]{1,0:T(8,128)(2,1)}, u32[]{:S(2)}, u32[]{:S(2)}) %collective-permute-start.17) | collective-permute-done | bytes 1376288 | tf_op jit(solution)/shard_map/ppermute | solution.py:597
  145.4 7.0 %shard_map.95.normed = bf16[4,5376,512]{2,1,0:T(8,128)(2,1)} custom-call(s32[4]{0:T(128)} %pad_add_fusion.table, bf16[4,5376,512]{2,1,0:T(8,128)(2,1)} %shard_map.93.normed.refs_0_, bf16[1,1344,512]{2,1,0:T(8,128)(2,1)} %bitcast.34.refs_1_, bf16[1,1344,512]{2,1,0:T(8,128)(2,1)} %bitcast.35.refs_2_, ...), custom_call_target="tpu_custom_call", output_to_operand_aliasing={{}: (1, {})} | custom-call | flops 27525120 | bytes 11010048 | tf_op jit(solution)/shard_map/pallas_call | solution.py:191
  152.4 9.0 %shard_map.96.refs_4_ = f32[4,1024,512]{2,1,0:T(8,128)} custom-call(s32[8]{0:T(128)} %stack.88.table, bf16[4,5376,512]{2,1,0:T(8,128)(2,1)} %shard_map.95.normed, bf16[1344,512]{1,0:T(8,128)(2,1)} %get-tuple-element.114.refs_0_, bf16[1344,512]{1,0:T(8,128)(2,1)} %get-tuple-element.118.refs_1_, ...), custom_call_target="tpu_custom_call", output_to_operand_aliasing={{}: (6, {})} | custom-call | flops 2818572288 | bytes 10354688 | tf_op jit(solution)/shard_map/pallas_call | solution.py:235
  161.4 13.2 %collective-permute-done.21.refs_1_ = bf16[1344,512]{1,0:T(8,128)(2,1)} collective-permute-done((bf16[1344,512]{1,0:T(8,128)(2,1)}, bf16[1344,512]{1,0:T(8,128)(2,1)}, u32[]{:S(2)}, u32[]{:S(2)}) %collective-permute-start.21) | collective-permute-done | bytes 1376288 | tf_op jit(solution)/shard_map/ppermute | solution.py:136
  177.7 19.9 %shard_map.97 = (bf16[4,512,512]{2,1,0:T(8,128)(2,1)}, bf16[2048,256]{1,0:T(8,128)(2,1)S(1)}, bf16[256,2048]{1,0:T(8,128)(2,1)S(1)}) custom-call(s32[12]{0:T(128)S(1)} %stack.87.table, bf16[4,5376,512]{2,1,0:T(8,128)(2,1)} %shard_map.95.normed, bf16[1344,512]{1,0:T(8,128)(2,1)} %collective-permute-done.17.refs_0_, ...), custom_call_target="tpu_custom_call" | custom-call | flops 11274289152 | bytes 24903680 | tf_op jit(solution)/shard_map/pallas_call | solution.py:299
  199.2 4.9 %shard_map.98.refs_0_ = bf16[512,512]{1,0:T(8,128)(2,1)S(1)} custom-call(s32[1]{0:T(128)} %bitcast.18.table, bf16[4,512,512]{2,1,0:T(8,128)(2,1)S(1)} %copy-done.2, bf16[2048,256]{1,0:T(8,128)(2,1)S(1)} %get-tuple-element.97.keys, bf16[256,2048]{1,0:T(8,128)(2,1)S(1)} %get-tuple-element.98.values), custom_call_target="tpu_custom_call" | custom-call | flops 4026531840 | bytes 3145728 | tf_op jit(solution)/shard_map/pallas_call | solution.py:412
  205.9 2.4 collective-permute-done.24.refs_1_.refs_13_
  208.3 2.3 shard_map.99.refs_0_
  210.8 7.4 %shard_map.100.refs_0_ = bf16[512,512]{1,0:T(8,128)(2,1)S(1)} custom-call(s32[1]{0:T(128)} %bitcast.17.table, bf16[4,512,512]{2,1,0:T(8,128)(2,1)S(1)} %copy-done.2, bf16[2048,256]{1,0:T(8,128)(2,1)S(1)} %get-tuple-element.97.keys, bf16[256,2048]{1,0:T(8,128)(2,1)S(1)} %get-tuple-element.98.values, bf16[512,512]{1,0:T(8,128)(2,1)S(1)} %shard_map.99.refs_0_), custom_call_target="tpu_custom_call" | custom-call | flops 4026531840 | bytes 3145728 | tf_op jit(solution)/shard_map/pallas_call | solution.py:412
  218.3 4.4 %collective-permute-done.26.refs_4_ = bf16[512,512]{1,0:T(8,128)(2,1)S(1)} collective-permute-done((bf16[512,512]{1,0:T(8,128)(2,1)S(1)}, bf16[512,512]{1,0:T(8,128)(2,1)S(1)}, u32[]{:S(2)}, u32[]{:S(2)}) %collective-permute-start.26) | collective-permute-done | bytes 524320 | tf_op jit(solution)/shard_map/ppermute | solution.py:136
  223.2 2.4 shard_map.101.refs_0_
  225.6 11.8 %collective-permute-done.33.refs_15_ = bf16[1344,512]{1,0:T(8,128)(2,1)S(1)} collective-permute-done((bf16[1344,512]{1,0:T(8,128)(2,1)}, bf16[1344,512]{1,0:T(8,128)(2,1)S(1)}, u32[]{:S(2)}, u32[]{:S(2)}) %collective-permute-start.33) | collective-permute-done | bytes 1376288 | tf_op jit(solution)/shard_map/ppermute | solution.py:136
  241.6 9.5 %shard_map.102 = (f32[1344,512]{1,0:T(8,128)S(1)}, f32[1,512]{1,0:T(1,128)S(1)}) custom-call(s32[8]{0:T(128)S(1)} %stack.81.table, bf16[512,512]{1,0:T(8,128)(2,1)S(1)} %shard_map.99.refs_0_, bf16[512,512]{1,0:T(8,128)(2,1)S(1)} %collective-permute-done.25.refs_1_, bf16[512,512]{1,0:T(8,128)(2,1)S(1)} %collective-permute-done.27.refs_2_, ...), custom_call_target="tpu_custom_call" | custom-call | flops 5637144576 | bytes 17956864 | tf_op jit(solution)/shard_map/pallas_call | solution.py:463
  253.5 9.3 %collective-permute-done.46 = f32[1,512]{1,0:T(1,128)S(1)} collective-permute-done((f32[1,512]{1,0:T(1,128)S(1)}, f32[1,512]{1,0:T(1,128)S(1)}, u32[]{:S(2)}, u32[]{:S(2)}) %collective-permute-start.46) | collective-permute-done | bytes 2080 | tf_op jit(solution)/shard_map/ppermute | solution.py:651
  264.4 2.9 add_convert_fusion.1
  268.6 9.5 %shard_map.103 = (f32[1344,512]{1,0:T(8,128)S(1)}, f32[1,512]{1,0:T(1,128)S(1)}) custom-call(s32[8]{0:T(128)S(1)} %stack.81.table, bf16[512,512]{1,0:T(8,128)(2,1)S(1)} %shard_map.101.refs_0_, bf16[512,512]{1,0:T(8,128)(2,1)S(1)} %collective-permute-done.31.refs_1_, bf16[512,512]{1,0:T(8,128)(2,1)S(1)} %collective-permute-done.35.refs_2_, ...), custom_call_target="tpu_custom_call" | custom-call | flops 5637144576 | bytes 17956864 | tf_op jit(solution)/shard_map/pallas_call | solution.py:463
  281.9 1.8 add_convert_fusion
  283.7 16.0 %collective-permute-done.47 = bf16[1344,512]{1,0:T(8,128)(2,1)} collective-permute-done((bf16[1344,512]{1,0:T(8,128)(2,1)}, bf16[1344,512]{1,0:T(8,128)(2,1)}, u32[]{:S(2)}, u32[]{:S(2)}) %collective-permute-start.47) | collective-permute-done | bytes 1376288 | tf_op jit(solution)/shard_map/ppermute | solution.py:665
  299.7 2.6 select_bitcast_fusion
  (125 shorter events, 44.5 us)
Async XLA Ops:
  0.0 14.8 %collective-permute-start = (bf16[1344,512]{1,0:T(8,128)(2,1)}, bf16[1344,512]{1,0:T(8,128)(2,1)S(1)}, u32[]{:S(2)}, u32[]{:S(2)}) collective-permute-start(bf16[1344,512]{1,0:T(8,128)(2,1)} %bitcast.52), channel_id=1, source_target_pairs={{0,1},{1,0},{4,8},{5,9},{8,4},{9,5},{12,13},{13,12},{2,3},{3,2},{6... | collective-permute-start | bytes 4128776 | tf_op jit(solution)/shard_map/ppermute | solution.py:155
  0.5 34.4 %collective-permute-start.1 = (bf16[1344,512]{1,0:T(8,128)(2,1)}, bf16[1344,512]{1,0:T(8,128)(2,1)}, u32[]{:S(2)}, u32[]{:S(2)}) collective-permute-start(bf16[1344,512]{1,0:T(8,128)(2,1)} %bitcast.53), channel_id=1, source_target_pairs={{0,4},{4,0},{8,12},{12,8},{1,5},{5,1},{9,13},{13,9},{2,6},{6,2},{1... | collective-permute-start | bytes 4128776 | tf_op jit(solution)/shard_map/ppermute | solution.py:549
  4.6 31.6 %collective-permute-start.2 = (bf16[1344,512]{1,0:T(8,128)(2,1)}, bf16[1344,512]{1,0:T(8,128)(2,1)S(1)}, u32[]{:S(2)}, u32[]{:S(2)}) collective-permute-start(bf16[1344,512]{1,0:T(8,128)(2,1)} %bitcast.54), channel_id=1, source_target_pairs={{0,2},{2,0},{1,3},{3,1},{4,6},{6,4},{5,7},{7,5},{8,10},{10,8},{9,1... | collective-permute-start | bytes 4128776 | tf_op jit(solution)/shard_map/ppermute | solution.py:136
  6.1 40.2 %collective-permute-start.6 = (bf16[1344,512]{1,0:T(8,128)(2,1)}, bf16[1344,512]{1,0:T(8,128)(2,1)}, u32[]{:S(2)}, u32[]{:S(2)}) collective-permute-start(bf16[1344,512]{1,0:T(8,128)(2,1)} %bitcast.55), channel_id=1, source_target_pairs={{0,1},{1,0},{2,3},{3,2},{4,5},{5,4},{6,7},{7,6},{8,9},{9,8},{10,11... | collective-permute-start | bytes 4128776 | tf_op jit(solution)/shard_map/ppermute | solution.py:136
  36.2 17.2 %collective-permute-start.3 = (bf16[1344,512]{1,0:T(8,128)(2,1)}, bf16[1344,512]{1,0:T(8,128)(2,1)}, u32[]{:S(2)}, u32[]{:S(2)}) collective-permute-start(bf16[1344,512]{1,0:T(8,128)(2,1)} %collective-permute-done.1), channel_id=1, source_target_pairs={{0,1},{1,0},{4,8},{5,9},{8,4},{9,5},{12,13},{13,12},{2,3},{3,2},{6... | collective-permute-start | bytes 4128776 | tf_op jit(solution)/shard_map/ppermute | solution.py:155
  36.7 32.9 %collective-permute-start.4 = (bf16[1344,512]{1,0:T(8,128)(2,1)}, bf16[1344,512]{1,0:T(8,128)(2,1)}, u32[]{:S(2)}, u32[]{:S(2)}) collective-permute-start(bf16[1344,512]{1,0:T(8,128)(2,1)} %get-tuple-element.62), channel_id=1, source_target_pairs={{0,4},{4,0},{8,12},{12,8},{1,5},{5,1},{9,13},{13,9},{2,6},{6,2},{1... | collective-permute-start | bytes 4128776 | tf_op jit(solution)/shard_map/ppermute | solution.py:557
  38.7 32.3 %collective-permute-start.5 = (bf16[1344,512]{1,0:T(8,128)(2,1)}, bf16[1344,512]{1,0:T(8,128)(2,1)}, u32[]{:S(2)}, u32[]{:S(2)}) collective-permute-start(bf16[1344,512]{1,0:T(8,128)(2,1)} %collective-permute-done.1), channel_id=1, source_target_pairs={{0,2},{2,0},{1,3},{3,1},{4,6},{6,4},{5,7},{7,5},{8,10},{10,8},{9,1... | collective-permute-start | bytes 4128776 | tf_op jit(solution)/shard_map/ppermute | solution.py:136
  46.3 26.8 %collective-permute-start.11 = (bf16[1344,512]{1,0:T(8,128)(2,1)}, bf16[1344,512]{1,0:T(8,128)(2,1)}, u32[]{:S(2)}, u32[]{:S(2)}) collective-permute-start(bf16[1344,512]{1,0:T(8,128)(2,1)} %collective-permute-done.1), channel_id=1, source_target_pairs={{0,1},{1,0},{2,3},{3,2},{4,5},{5,4},{6,7},{7,6},{8,9},{9,8},{10,11... | collective-permute-start | bytes 4128776 | tf_op jit(solution)/shard_map/ppermute | solution.py:136
  71.1 34.6 %collective-permute-start.10 = (bf16[1344,512]{1,0:T(8,128)(2,1)}, bf16[1344,512]{1,0:T(8,128)(2,1)}, u32[]{:S(2)}, u32[]{:S(2)}) collective-permute-start(bf16[1344,512]{1,0:T(8,128)(2,1)} %copy-done.7), channel_id=1, source_target_pairs={{0,2},{2,0},{1,3},{3,1},{4,6},{6,4},{5,7},{7,5},{8,10},{10,8},{9,1... | collective-permute-start | bytes 4128776 | tf_op jit(solution)/shard_map/ppermute | solution.py:136
  72.6 33.1 %collective-permute-start.13 = (bf16[1344,512]{1,0:T(8,128)(2,1)}, bf16[1344,512]{1,0:T(8,128)(2,1)}, u32[]{:S(2)}, u32[]{:S(2)}) collective-permute-start(bf16[1344,512]{1,0:T(8,128)(2,1)} %copy-done.7), channel_id=1, source_target_pairs={{0,1},{1,0},{2,3},{3,2},{4,5},{5,4},{6,7},{7,6},{8,9},{9,8},{10,11... | collective-permute-start | bytes 4128776 | tf_op jit(solution)/shard_map/ppermute | solution.py:136
  73.1 32.6 %collective-permute-start.9 = (bf16[1344,512]{1,0:T(8,128)(2,1)}, bf16[1344,512]{1,0:T(8,128)(2,1)}, u32[]{:S(2)}, u32[]{:S(2)}) collective-permute-start(bf16[1344,512]{1,0:T(8,128)(2,1)} %collective-permute-done.4.refs_2_), channel_id=1, source_target_pairs={{0,16},{16,0},{1,17},{17,1},{2,18},{18,2},{3,19},{19,3},{4,20},{20... | collective-permute-start | bytes 4128776 | tf_op jit(solution)/shard_map/ppermute | solution.py:136
  74.6 32.5 %collective-permute-start.14 = (bf16[1344,512]{1,0:T(8,128)(2,1)}, bf16[1344,512]{1,0:T(8,128)(2,1)}, u32[]{:S(2)}, u32[]{:S(2)}) collective-permute-start(bf16[1344,512]{1,0:T(8,128)(2,1)} %get-tuple-element.73), channel_id=1, source_target_pairs={{0,4},{4,0},{8,12},{12,8},{1,5},{5,1},{9,13},{13,9},{2,6},{6,2},{1... | collective-permute-start | bytes 4128776 | tf_op jit(solution)/shard_map/ppermute | solution.py:585
  107.1 33.4 %collective-permute-start.17 = (bf16[1344,512]{1,0:T(8,128)(2,1)}, bf16[1344,512]{1,0:T(8,128)(2,1)}, u32[]{:S(2)}, u32[]{:S(2)}) collective-permute-start(bf16[1344,512]{1,0:T(8,128)(2,1)} %get-tuple-element.78), channel_id=1, source_target_pairs={{0,8},{4,0},{8,12},{12,4},{1,9},{5,1},{9,13},{13,5},{2,10},{6,2},{... | collective-permute-start | bytes 4128776 | tf_op jit(solution)/shard_map/ppermute | solution.py:597
  108.6 32.6 %collective-permute-start.18 = (bf16[1344,512]{1,0:T(8,128)(2,1)}, bf16[1344,512]{1,0:T(8,128)(2,1)}, u32[]{:S(2)}, u32[]{:S(2)}) collective-permute-start(bf16[1344,512]{1,0:T(8,128)(2,1)} %collective-permute-done.3), channel_id=1, source_target_pairs={{0,2},{2,0},{1,3},{3,1},{4,6},{6,4},{5,7},{7,5},{8,10},{10,8},{9,1... | collective-permute-start | bytes 4128776 | tf_op jit(solution)/shard_map/ppermute | solution.py:136
  109.2 32.6 %collective-permute-start.19 = (bf16[1344,512]{1,0:T(8,128)(2,1)}, bf16[1344,512]{1,0:T(8,128)(2,1)}, u32[]{:S(2)}, u32[]{:S(2)}) collective-permute-start(bf16[1344,512]{1,0:T(8,128)(2,1)} %collective-permute-done.8.refs_2_), channel_id=1, source_target_pairs={{0,16},{16,0},{1,17},{17,1},{2,18},{18,2},{3,19},{19,3},{4,20},{20... | collective-permute-start | bytes 4128776 | tf_op jit(solution)/shard_map/ppermute | solution.py:136
  111.3 34.0 %collective-permute-start.16 = (bf16[1344,512]{1,0:T(8,128)(2,1)}, bf16[1344,512]{1,0:T(8,128)(2,1)}, u32[]{:S(2)}, u32[]{:S(2)}) collective-permute-start(bf16[1344,512]{1,0:T(8,128)(2,1)} %collective-permute-done.3), channel_id=1, source_target_pairs={{0,1},{1,0},{2,3},{3,2},{4,5},{5,4},{6,7},{7,6},{8,9},{9,8},{10,11... | collective-permute-start | bytes 4128776 | tf_op jit(solution)/shard_map/ppermute | solution.py:136
  141.7 32.9 %collective-permute-start.21 = (bf16[1344,512]{1,0:T(8,128)(2,1)}, bf16[1344,512]{1,0:T(8,128)(2,1)}, u32[]{:S(2)}, u32[]{:S(2)}) collective-permute-start(bf16[1344,512]{1,0:T(8,128)(2,1)} %collective-permute-done.17.refs_0_), channel_id=1, source_target_pairs={{0,16},{16,0},{1,17},{17,1},{2,18},{18,2},{3,19},{19,3},{4,20},{20... | collective-permute-start | bytes 4128776 | tf_op jit(solution)/shard_map/ppermute | solution.py:136
  143.3 31.4 %collective-permute-start.22 = (bf16[1344,512]{1,0:T(8,128)(2,1)}, bf16[1344,512]{1,0:T(8,128)(2,1)}, u32[]{:S(2)}, u32[]{:S(2)}) collective-permute-start(bf16[1344,512]{1,0:T(8,128)(2,1)} %collective-permute-done.14.refs_10_), channel_id=1, source_target_pairs={{0,1},{1,0},{4,8},{5,9},{8,4},{9,5},{12,13},{13,12},{2,3},{3,2},{6... | collective-permute-start | bytes 4128776 | tf_op jit(solution)/shard_map/ppermute | solution.py:155
  143.5 32.7 %collective-permute-start.23 = (bf16[1344,512]{1,0:T(8,128)(2,1)}, bf16[1344,512]{1,0:T(8,128)(2,1)}, u32[]{:S(2)}, u32[]{:S(2)}) collective-permute-start(bf16[1344,512]{1,0:T(8,128)(2,1)} %get-tuple-element.87), channel_id=1, source_target_pairs={{0,4},{4,0},{8,12},{12,8},{1,5},{5,1},{9,13},{13,9},{2,6},{6,2},{1... | collective-permute-start | bytes 4128776 | tf_op jit(solution)/shard_map/ppermute | solution.py:612
  145.3 58.9 %collective-permute-start.32 = (bf16[1344,512]{1,0:T(8,128)(2,1)}, bf16[1344,512]{1,0:T(8,128)(2,1)}, u32[]{:S(2)}, u32[]{:S(2)}) collective-permute-start(bf16[1344,512]{1,0:T(8,128)(2,1)} %get-tuple-element.73), channel_id=1, source_target_pairs={{0,1},{1,0},{4,8},{5,9},{8,4},{9,5},{12,13},{13,12},{2,3},{3,2},{6... | collective-permute-start | bytes 4128776 | tf_op jit(solution)/shard_map/ppermute | solution.py:155
  176.2 32.1 %collective-permute-start.24 = (bf16[1344,512]{1,0:T(8,128)(2,1)}, bf16[1344,512]{1,0:T(8,128)(2,1)S(1)}, u32[]{:S(2)}, u32[]{:S(2)}) collective-permute-start(bf16[1344,512]{1,0:T(8,128)(2,1)} %collective-permute-done.22.refs_12_), channel_id=1, source_target_pairs={{0,16},{16,0},{1,17},{17,1},{2,18},{18,2},{3,19},{19,3},{4,20},{20... | collective-permute-start | bytes 4128776 | tf_op jit(solution)/shard_map/ppermute | solution.py:136
  204.1 14.2 %collective-permute-start.25 = (bf16[512,512]{1,0:T(8,128)(2,1)S(1)}, bf16[512,512]{1,0:T(8,128)(2,1)S(1)}, u32[]{:S(2)}, u32[]{:S(2)}) collective-permute-start(bf16[512,512]{1,0:T(8,128)(2,1)S(1)} %shard_map.98.refs_0_), channel_id=1, source_target_pairs={{0,1},{1,0},{4,8},{5,9},{8,4},{9,5},{12,13},{13,12},{2,3},{3,2},{6... | collective-permute-start | bytes 1572872 | tf_op jit(solution)/shard_map/ppermute | solution.py:155
  204.2 33.2 %collective-permute-start.33 = (bf16[1344,512]{1,0:T(8,128)(2,1)}, bf16[1344,512]{1,0:T(8,128)(2,1)S(1)}, u32[]{:S(2)}, u32[]{:S(2)}) collective-permute-start(bf16[1344,512]{1,0:T(8,128)(2,1)} %collective-permute-done.32.refs_14_), channel_id=1, source_target_pairs={{0,16},{16,0},{1,17},{17,1},{2,18},{18,2},{3,19},{19,3},{4,20},{20... | collective-permute-start | bytes 4128776 | tf_op jit(solution)/shard_map/ppermute | solution.py:136
  210.6 12.2 %collective-permute-start.26 = (bf16[512,512]{1,0:T(8,128)(2,1)S(1)}, bf16[512,512]{1,0:T(8,128)(2,1)S(1)}, u32[]{:S(2)}, u32[]{:S(2)}) collective-permute-start(bf16[512,512]{1,0:T(8,128)(2,1)S(1)} %shard_map.99.refs_0_), channel_id=1, source_target_pairs={{0,2},{2,0},{1,3},{3,1},{4,6},{6,4},{5,7},{7,5},{8,10},{10,8},{9,1... | collective-permute-start | bytes 1572872 | tf_op jit(solution)/shard_map/ppermute | solution.py:136
  218.3 19.2 %collective-permute-start.31 = (bf16[512,512]{1,0:T(8,128)(2,1)S(1)}, bf16[512,512]{1,0:T(8,128)(2,1)S(1)}, u32[]{:S(2)}, u32[]{:S(2)}) collective-permute-start(bf16[512,512]{1,0:T(8,128)(2,1)S(1)} %shard_map.100.refs_0_), channel_id=1, source_target_pairs={{0,1},{1,0},{4,8},{5,9},{8,4},{9,5},{12,13},{13,12},{2,3},{3,2},{6... | collective-permute-start | bytes 1572872 | tf_op jit(solution)/shard_map/ppermute | solution.py:155
  222.7 14.7 %collective-permute-start.29 = (bf16[512,512]{1,0:T(8,128)(2,1)S(1)}, bf16[512,512]{1,0:T(8,128)(2,1)S(1)}, u32[]{:S(2)}, u32[]{:S(2)}) collective-permute-start(bf16[512,512]{1,0:T(8,128)(2,1)S(1)} %collective-permute-done.25.refs_1_), channel_id=1, source_target_pairs={{0,2},{2,0},{1,3},{3,1},{4,6},{6,4},{5,7},{7,5},{8,10},{10,8},{9,1... | collective-permute-start | bytes 1572872 | tf_op jit(solution)/shard_map/ppermute | solution.py:136
  238.5 14.8 %collective-permute-start.38 = (bf16[512,512]{1,0:T(8,128)(2,1)S(1)}, bf16[512,512]{1,0:T(8,128)(2,1)S(1)}, u32[]{:S(2)}, u32[]{:S(2)}) collective-permute-start(bf16[512,512]{1,0:T(8,128)(2,1)S(1)} %collective-permute-done.31.refs_1_), channel_id=1, source_target_pairs={{0,2},{2,0},{1,3},{3,1},{4,6},{6,4},{5,7},{7,5},{8,10},{10,8},{9,1... | collective-permute-start | bytes 1572872 | tf_op jit(solution)/shard_map/ppermute | solution.py:136
  239.4 24.5 %collective-permute-start.37 = (bf16[512,512]{1,0:T(8,128)(2,1)S(1)}, bf16[512,512]{1,0:T(8,128)(2,1)S(1)}, u32[]{:S(2)}, u32[]{:S(2)}) collective-permute-start(bf16[512,512]{1,0:T(8,128)(2,1)S(1)} %shard_map.101.refs_0_), channel_id=1, source_target_pairs={{0,2},{2,0},{1,3},{3,1},{4,6},{6,4},{5,7},{7,5},{8,10},{10,8},{9,1... | collective-permute-start | bytes 1572872 | tf_op jit(solution)/shard_map/ppermute | solution.py:136
  251.1 11.7 %collective-permute-start.46 = (f32[1,512]{1,0:T(1,128)S(1)}, f32[1,512]{1,0:T(1,128)S(1)}, u32[]{:S(2)}, u32[]{:S(2)}) collective-permute-start(f32[1,512]{1,0:T(1,128)S(1)} %get-tuple-element.110), channel_id=1, source_target_pairs={{0,3},{1,2},{2,1},{3,0},{4,7},{5,6},{6,5},{7,4},{8,11},{9,10},{10,... | collective-permute-start | bytes 6152 | tf_op jit(solution)/shard_map/ppermute | solution.py:651
  251.8 12.0 %collective-permute-start.45 = (f32[1,512]{1,0:T(1,128)S(1)}, f32[1,512]{1,0:T(1,128)S(1)}, u32[]{:S(2)}, u32[]{:S(2)}) collective-permute-start(f32[1,512]{1,0:T(1,128)S(1)} %get-tuple-element.110), channel_id=1, source_target_pairs={{0,2},{2,0},{1,3},{3,1},{4,6},{6,4},{5,7},{7,5},{8,10},{10,8},{9,1... | collective-permute-start | bytes 6152 | tf_op jit(solution)/shard_map/ppermute | solution.py:136
  253.2 15.4 %collective-permute-start.35 = (bf16[512,512]{1,0:T(8,128)(2,1)S(1)}, bf16[512,512]{1,0:T(8,128)(2,1)S(1)}, u32[]{:S(2)}, u32[]{:S(2)}) collective-permute-start(bf16[512,512]{1,0:T(8,128)(2,1)S(1)} %shard_map.101.refs_0_), channel_id=1, source_target_pairs={{0,1},{1,0},{2,3},{3,2},{4,5},{5,4},{6,7},{7,6},{8,9},{9,8},{10,11... | collective-permute-start | bytes 1572872 | tf_op jit(solution)/shard_map/ppermute | solution.py:136
  267.3 32.4 %collective-permute-start.47 = (bf16[1344,512]{1,0:T(8,128)(2,1)}, bf16[1344,512]{1,0:T(8,128)(2,1)}, u32[]{:S(2)}, u32[]{:S(2)}) collective-permute-start(bf16[1344,512]{1,0:T(8,128)(2,1)} %add_convert_fusion.1), channel_id=1, source_target_pairs={{0,4},{4,0},{8,12},{12,8},{1,5},{5,1},{9,13},{13,9},{2,6},{6,2},{1... | collective-permute-start | bytes 4128776 | tf_op jit(solution)/shard_map/ppermute | solution.py:665
  (28 other events, 265.0 us)
